TPU v7x, 256 devices: a whole 4x4x8 slice. The times are simulated.
256 devices in a mesh: dp: 32 (over z, y), ha: 2 (over x_lo), wa: 4 (over x_hi, core).
Axes of the slice: x: 4 (x_hi: 2, x_lo: 2; x = x_hi * 2 + x_lo), y: 4, z: 8, core: 2. Of those that a mesh axis runs over, the one named last changes fastest.
Arguments:
- activations: bfloat16 [32, 4, 24, 64, 256], P('dp', None, 'ha', 'wa'), may hold values from -6 to 6
- saved_hidden: bfloat16 [32, 4, 24, 64, 256], P('dp', None, 'ha', 'wa'), may hold values from -6 to 6
- cotangent: bfloat16 [32, 4, 24, 64, 256], P('dp', None, 'ha', 'wa'), may hold values from -6 to 6
- conv_one: bfloat16 [256, 3, 3, 3, 256], replicated, may hold values from -0.078125 to 0.078125
- conv_two: bfloat16 [256, 3, 3, 3, 256], replicated, may hold values from -0.078125 to 0.078125
- film_table: float32 [1000, 512], replicated, may hold values from -3 to 3
- timesteps: int32 [32], P('dp'), may hold values from 0 to 999
Outputs:
- grad_input: bfloat16 [32, 4, 24, 64, 256], P('dp', None, 'ha', 'wa')
- grad_conv_one: float32 [256, 3, 3, 3, 256], P(('ha', 'wa'), None, None, None, 'dp')
- grad_conv_two: float32 [256, 3, 3, 3, 256], P(('ha', 'wa'), None, None, None, 'dp')
All inputs are finite; a program needn't handle non-finite values.
Results may differ from a plain program's by a relative error of at most 0.003.
Values may be sent and summed in bfloat16 or wider, within the bound.
No kernel may reach another device: no remote copies, remote signals or barrier semaphores. Data moves between devices by JAX's collectives and lax.ppermute only.
A program may use at most 320 MiB of HBM per device.

v0:
```python
import jax
import jax.numpy as jnp
from jax import lax
from jax.sharding import PartitionSpec as P


def with_halo(block, sides, width):
    for axis, dim in sides:
        count = lax.axis_size(axis)
        forward = [(i, i + 1) for i in range(count - 1)]
        backward = [(target, source) for source, target in forward]
        low = lax.ppermute(
            lax.slice_in_dim(block, block.shape[dim] - width, None, axis=dim), axis, forward
        )
        high = lax.ppermute(lax.slice_in_dim(block, 0, width, axis=dim), axis, backward)
        block = jnp.concatenate([low, block, high], axis=dim)
    return block


def weight_grad(padded_in, cotan_in):
    num_frames, num_rows, num_cols, outs_count = cotan_in.shape
    cot_rows = cotan_in.reshape(-1, outs_count)
    blocks_list = []
    for offset in range(27):
        tshift, hshift, wshift = (offset // 9, offset // 3 % 3, offset % 3)
        window = padded_in[
            tshift : tshift + num_frames, hshift : hshift + num_rows, wshift : wshift + num_cols
        ]
        window = window.reshape(-1, padded_in.shape[-1])
        blocks_list.append(
            lax.dot_general(
                window, cot_rows, (((0,), (0,)), ((), ())), preferred_element_type=jnp.float32
            )
        )
    return jnp.stack(blocks_list, 1).reshape(padded_in.shape[-1], 3, 3, 3, outs_count)


def conv_transpose(padded_cot, weight):
    num_frames = padded_cot.shape[0] - 2
    num_rows = padded_cot.shape[1] - 2
    num_cols = padded_cot.shape[2] - 2
    accum_sum = jnp.zeros((num_frames * num_rows * num_cols, weight.shape[0]), jnp.float32)
    for offset in range(27):
        tshift, hshift, wshift = (offset // 9, offset // 3 % 3, offset % 3)
        window = padded_cot[
            2 - tshift : 2 - tshift + num_frames,
            2 - hshift : 2 - hshift + num_rows,
            2 - wshift : 2 - wshift + num_cols,
        ]
        window = window.reshape(-1, padded_cot.shape[-1])
        accum_sum = accum_sum + lax.dot_general(
            window,
            weight[:, tshift, hshift, wshift, :],
            (((1,), (1,)), ((), ())),
            preferred_element_type=jnp.float32,
        )
    return accum_sum.reshape(num_frames, num_rows, num_cols, weight.shape[0])


def reduce_grad(padded_in, cotan_in):
    partial_value = weight_grad(padded_in, cotan_in)
    data_half = lax.psum_scatter(partial_value, "dp", scatter_dimension=4, tiled=True)
    summed = lax.psum_scatter(data_half, ("ha", "wa"), scatter_dimension=0, tiled=True)
    return summed


def shards(activations, saved_hidden, cotangent, conv_one, conv_two, film_table, timesteps):
    inputs = activations[0]
    hidden_pre = saved_hidden[0]
    upstream = cotangent[0]
    channels = inputs.shape[-1]
    one_hot = (
        lax.broadcasted_iota(jnp.int32, (1, film_table.shape[0]), 1) == timesteps[:, None]
    ).astype(jnp.float32)
    film_rows = jnp.dot(
        one_hot, film_table, precision=lax.Precision.HIGHEST, preferred_element_type=jnp.float32
    )[0]
    film_scale = 1.0 + film_rows[:channels]
    film_shift = film_rows[channels:]
    shifted = hidden_pre.astype(jnp.float32) * film_scale + film_shift
    sigma = jax.nn.sigmoid(shifted)
    activated = (shifted * sigma).astype(jnp.bfloat16)
    stacked = jnp.stack([inputs, activated, upstream])
    rimmed = with_halo(stacked, (("ha", 2), ("wa", 3)), 1)
    cot_pad = jnp.pad(rimmed[2], ((0, 2), (0, 0), (0, 0), (0, 0)))
    grad_act = conv_transpose(cot_pad, conv_two)
    grad_hidden = (grad_act * film_scale * sigma * (1.0 + shifted * (1.0 - sigma))).astype(
        jnp.bfloat16
    )
    act_pad = jnp.pad(rimmed[1], ((2, 0), (0, 0), (0, 0), (0, 0)))
    grad_two = reduce_grad(act_pad, upstream)
    hid_rim = with_halo(grad_hidden, (("ha", 1), ("wa", 2)), 1)
    hid_pad = jnp.pad(hid_rim, ((0, 2), (0, 0), (0, 0), (0, 0)))
    grad_input = (upstream.astype(jnp.float32) + conv_transpose(hid_pad, conv_one)).astype(
        jnp.bfloat16
    )
    inp_pad = jnp.pad(rimmed[0], ((2, 0), (0, 0), (0, 0), (0, 0)))
    grad_one = reduce_grad(inp_pad, grad_hidden)
    all_rows = (
        lax.axis_size("dp")
        * lax.axis_size("ha")
        * lax.axis_size("wa")
        * inputs.shape[0]
        * inputs.shape[1]
        * inputs.shape[2]
    )
    factor = float(all_rows) ** (-0.5)
    return (grad_input[None], grad_one * factor, grad_two * factor)


def solution(mesh):
    placed = (
        P("dp", None, "ha", "wa", None),
        P("dp", None, "ha", "wa", None),
        P("dp", None, "ha", "wa", None),
        P(),
        P(),
        P(),
        P("dp"),
    )
    return jax.shard_map(
        shards,
        mesh=mesh,
        in_specs=placed,
        out_specs=(
            P("dp", None, "ha", "wa", None),
            P(("ha", "wa"), None, None, None, "dp"),
            P(("ha", "wa"), None, None, None, "dp"),
        ),
        check_vma=False,
    )
```

profile of v0, /device:TPU:24, one launch (start us, length us, event | category | flops | bytes accessed | tf_op | source)
XLA Modules:
  0.0 620.5 jit_solution(15118405864311239598)
XLA Ops:
  11.6 1.3 collective-permute-start.1
  12.9 4.6 collective-permute-start
  18.1 1.5 collective-permute-done
  19.7 1.5 pad_maximum_fusion.8
  21.2 1.3 collective-permute-start.3
  22.5 3.0 collective-permute-start.2
  26.5 2.6 pad_maximum_fusion
  29.3 1.7 fusion.211
  31.1 2.0 fusion.208
  70.0 8.1 %copy.12 = f32[256,3,3,3,256]{0,4,3,2,1:T(8,128)} copy(f32[256,3,3,3,256]{4,0,3,2,1:T(8,128)} %bitcast.196) | data formatting | bytes 14155776 | tf_op jit(solution)/shard_map/reshape | solution.py:35
  80.1 2.2 fusion.207
  108.6 8.1 %copy.13 = f32[256,3,3,3,256]{0,4,3,2,1:T(8,128)} copy(f32[256,3,3,3,256]{4,0,3,2,1:T(8,128)} %bitcast.253) | data formatting | bytes 14155776 | tf_op jit(solution)/shard_map/reshape | solution.py:35
  116.8 1.6 collective-permute-start.5
  118.4 4.5 collective-permute-start.4
  122.9 1.6 collective-permute-done.4
  125.9 5.4 collective-permute-start.6
  133.4 2.0 fusion.206
  143.7 168.0 %reduce-scatter.9.cloned.1.call-done = f32[256,3,3,3,8]{0,4,3,2,1:T(8,128)} async-done(((f32[256,3,3,3,256]{0,4,3,2,1:T(8,128)}), f32[256,3,3,3,8]{0,4,3,2,1:T(8,128)}) %reduce-scatter.9.cloned.1.call-update) | async-done | bytes 221200 | tf_op jit(solution)/shard_map/reduce_scatter | solution.py:62
  311.7 1.8 copy.45
  314.7 1.6 fusion.5
  316.4 224.2 %reduce-scatter.11.cloned.1.call-done = f32[256,3,3,3,8]{0,4,3,2,1:T(8,128)} async-done(((f32[256,3,3,3,256]{0,4,3,2,1:T(8,128)}), f32[256,3,3,3,8]{0,4,3,2,1:T(8,128)}) %reduce-scatter.11.cloned.1.call-update) | async-done | bytes 221200 | tf_op jit(solution)/shard_map/reduce_scatter | solution.py:62
  540.5 1.8 copy.47
  543.2 33.0 %reduce-scatter.13.cloned.1.call-done = f32[32,216]{1,0:T(8,128)} async-done(((f32[256,216]{1,0:T(8,128)}), f32[32,216]{1,0:T(8,128)}) %reduce-scatter.13.cloned.1.call-update) | async-done | bytes 27664
  577.7 34.7 %reduce-scatter.15.cloned.1.call-done = f32[32,216]{1,0:T(8,128)} async-done(((f32[256,216]{1,0:T(8,128)}), f32[32,216]{1,0:T(8,128)}) %reduce-scatter.15.cloned.1.call-update) | async-done | bytes 27664
  (164 shorter events, 87.2 us)
Async XLA Ops:
  7.2 1.6 copy-start
  7.2 304.5 %reduce-scatter.9.cloned.1.call-start = ((), (), s32[]{:S(2)}) async-start(), calls=%async_computation.4 | async-start | bytes 7299072 | tf_op jit(solution)/shard_map/reduce_scatter | solution.py:62
  11.6 6.5 %collective-permute-start.1 = (bf16[3,4,1,16,256]{4,3,2,1,0:T(8,128)(2,1)S(1)}, bf16[3,4,1,16,256]{4,3,2,1,0:T(8,128)(2,1)S(1)}, u32[]{:S(2)}, u32[]{:S(2)}) collective-permute-start(bf16[3,4,1,16,256]{4,3,2,1,0:T(8,128)(2,1)S(1)} %get-tuple-element.9), channel_id=1, source_target_pairs={{4,0},{5,1},{6,2},{7,3},{12,8},{13,9},{14,10},{15,11},{20,16},{21,... | collective-permute-start | bytes 294920 | tf_op jit(solution)/shard_map/ppermute | solution.py:15
  12.9 6.8 %collective-permute-start = (bf16[3,4,1,16,256]{4,3,2,1,0:T(8,128)(2,1)S(1)}, bf16[3,4,1,16,256]{4,3,2,1,0:T(8,128)(2,1)S(1)}, u32[]{:S(2)}, u32[]{:S(2)}) collective-permute-start(bf16[3,4,1,16,256]{4,3,2,1,0:T(8,128)(2,1)S(1)} %get-tuple-element.8), channel_id=1, source_target_pairs={{0,4},{1,5},{2,6},{3,7},{8,12},{9,13},{10,14},{11,15},{16,20},{17,... | collective-permute-start | bytes 294920 | tf_op jit(solution)/shard_map/ppermute | solution.py:12
  21.2 4.4 collective-permute-start.3
  22.5 4.1 collective-permute-start.2
  31.1 2.7 copy-start.4
  39.5 2.1 copy-start.10
  78.1 1.0 copy-start.2
  78.1 462.4 %reduce-scatter.11.cloned.1.call-start = ((), (), s32[]{:S(2)}) async-start(), calls=%async_computation.5 | async-start | bytes 7299072 | tf_op jit(solution)/shard_map/reduce_scatter | solution.py:62
  86.4 13.1 %copy-start.9 = (bf16[4,12,16,256]{3,2,1,0:T(8,128)(2,1)S(1)}, bf16[4,12,16,256]{3,2,1,0:T(8,128)(2,1)}, u32[]{:S(2)}) copy-start(bf16[4,12,16,256]{3,2,1,0:T(8,128)(2,1)} %get-tuple-element.53) | copy-start | bytes 1179652
  87.4 13.1 %copy-start.8 = (bf16[4,12,16,256]{3,2,1,0:T(8,128)(2,1)S(1)}, bf16[4,12,16,256]{3,2,1,0:T(8,128)(2,1)}, u32[]{:S(2)}) copy-start(bf16[4,12,16,256]{3,2,1,0:T(8,128)(2,1)} %get-tuple-element.52) | copy-start | bytes 1179652
  88.4 13.2 %copy-start.7 = (bf16[4,12,16,256]{3,2,1,0:T(8,128)(2,1)S(1)}, bf16[4,12,16,256]{3,2,1,0:T(8,128)(2,1)}, u32[]{:S(2)}) copy-start(bf16[4,12,16,256]{3,2,1,0:T(8,128)(2,1)} %get-tuple-element.51) | copy-start | bytes 1179652
  89.4 13.1 %copy-start.6 = (bf16[4,12,16,256]{3,2,1,0:T(8,128)(2,1)S(1)}, bf16[4,12,16,256]{3,2,1,0:T(8,128)(2,1)}, u32[]{:S(2)}) copy-start(bf16[4,12,16,256]{3,2,1,0:T(8,128)(2,1)} %get-tuple-element.50) | copy-start | bytes 1179652
  90.4 13.2 %copy-start.5 = (bf16[4,12,16,256]{3,2,1,0:T(8,128)(2,1)S(1)}, bf16[4,12,16,256]{3,2,1,0:T(8,128)(2,1)}, u32[]{:S(2)}) copy-start(bf16[4,12,16,256]{3,2,1,0:T(8,128)(2,1)} %get-tuple-element.49) | copy-start | bytes 1179652
  116.7 459.5 %reduce-scatter.13.cloned.1.call-start = ((), (), s32[]{:S(2)}) async-start(), calls=%async_computation.6 | async-start | bytes 294912
  116.8 16.3 %copy-start.3 = (bf16[256,3,3,3,256]{4,0,3,2,1:T(8,128)(2,1)S(1)}, bf16[256,3,3,3,256]{4,0,3,2,1:T(8,128)(2,1)}, u32[]{:S(2)}) copy-start(bf16[256,3,3,3,256]{4,0,3,2,1:T(8,128)(2,1)} %param.10) | copy-start | bytes 10616836
  116.8 6.1 collective-permute-start.5
  118.4 6.1 collective-permute-start.4
  124.6 7.5 %collective-permute-start.7 = (bf16[4,14,1,256]{3,2,1,0:T(2,128)(2,1)S(1)}, bf16[4,14,1,256]{3,2,1,0:T(2,128)(2,1)S(1)}, u32[]{:S(2)}, u32[]{:S(2)}) collective-permute-start(bf16[4,14,1,256]{3,2,1,0:T(2,128)(2,1)S(1)} %get-tuple-element.90), channel_id=1, source_target_pairs={{1,0},{2,1},{3,2},{5,4},{6,5},{7,6},{9,8},{10,9},{11,10},{13,12},{... | collective-permute-start | bytes 86024 | tf_op jit(solution)/shard_map/ppermute | solution.py:15
  125.9 6.2 %collective-permute-start.6 = (bf16[4,14,1,256]{3,2,1,0:T(2,128)(2,1)S(1)}, bf16[4,14,1,256]{3,2,1,0:T(2,128)(2,1)S(1)}, u32[]{:S(2)}, u32[]{:S(2)}) collective-permute-start(bf16[4,14,1,256]{3,2,1,0:T(2,128)(2,1)S(1)} %get-tuple-element.91), channel_id=1, source_target_pairs={{0,1},{1,2},{2,3},{4,5},{5,6},{6,7},{8,9},{9,10},{10,11},{12,13},{... | collective-permute-start | bytes 86024 | tf_op jit(solution)/shard_map/ppermute | solution.py:12
  141.9 472.1 %copy-start.1 = (f32[1000,512]{1,0:T(8,128)S(1)}, f32[1000,512]{1,0:T(8,128)}, u32[]{:S(2)}) copy-start(f32[1000,512]{1,0:T(8,128)} %param.12) | copy-start | bytes 6144004
  313.5 299.0 %reduce-scatter.15.cloned.1.call-start = ((), (), s32[]{:S(2)}) async-start(), calls=%async_computation.7 | async-start | bytes 294912
Sparse Core Ops, SparseCore 0:
  78.2 233.4 reduce-scatter.8
  316.3 224.2 reduce-scatter.10
  543.0 33.1 reduce-scatter.12
  578.7 33.7 reduce-scatter.14
where the time goes:
time: 623 us; the launch traced here: 620 us
  waiting for transfers between devices  465 us (75%)
  matrix products  74.7 us (12%)
  local copies, waits for them, and re-layouts  32.1 us (5%)
  starting transfers between devices  23.1 us (4%)
  between operations  15.2 us (2%)
  other arithmetic  10.5 us (2%)
    reduce_scatter x2, waiting for transfers between devices, reduce_grad(): lax.psum_scatter(partial_value, 'dp', scatter_dimension=4, tiled=True)  392 us
    unnamed x6, waiting for transfers between devices  67.8 us
    dot_general x54, matrix products, weight_grad(): lax.dot_general(window, cot_rows, (((0,), (0,)), ((), ())), preferred_ele...  54.7 us
    dot_general x54, matrix products, conv_transpose(): lax.dot_general(window, weight[:, tshift, hshift, wshift, :], (((1,), (1,...  19.3 us
    ppermute x4, starting transfers between devices, with_halo(): lax.ppermute(lax.slice_in_dim(block, block.shape[dim] - width, None, axis...  17.5 us
    reshape x2, local copies, waits for them, and re-layouts, weight_grad(): jnp.stack(blocks_list, 1).reshape(padded_in.shape[-1], 3, 3, 3, outs_count)  16.2 us
  transfers between devices with their start and end apart: 12, of which 9 were waited for; matrix products, arithmetic and copies ran while one was open for 9% of the time, Pallas kernels for 0%

commit v1 on v0

v1 whole, which is shorter than its diff:
```python
import functools

import jax
import jax.numpy as jnp
from jax import lax
from jax.experimental import pallas as pl
from jax.experimental.pallas import tpu as pltpu
from jax.sharding import Mesh
from jax.sharding import PartitionSpec as P

BF = jnp.bfloat16
F32 = jnp.float32
AX = ("z", "y", "ha", "xh", "core")
SIZES = (8, 4, 2, 2, 2)
PARAMS = pltpu.CompilerParams(vmem_limit_bytes=56 * 2**20)
VM = pl.BlockSpec(memory_space=pltpu.VMEM)
SM = pl.BlockSpec(memory_space=pltpu.SMEM)
HB = pl.BlockSpec(memory_space=pl.ANY)
NT = (((1,), (1,)), ((), ()))
TN = (((0,), (0,)), ((), ()))
SDS = jax.ShapeDtypeStruct


def split_index(i):
    core, xh, ha, y, z = i % 2, i // 2 % 2, i // 4 % 2, i // 8 % 4, i // 32
    return z, y, xh * 2 + ha, core


def join_index(z, y, x, core):
    return (((z % 8) * 4 + y % 4) * 4 + (x % 2) * 2 + x % 4 // 2) * 2 + core


def ring_pairs(dx=0, dy=0, dc=0):
    pairs = []
    for i in range(256):
        z, y, x, core = split_index(i)
        pairs.append((i, join_index(z, y + dy, x + dx, core ^ dc)))
    return pairs


def block_pairs(dh, dw):
    pairs = []
    for i in range(256):
        ha, wa, dp = i // 4 % 2, i % 4, i // 8
        if 0 <= wa + dw < 4:
            pairs.append((i, dp * 8 + (ha ^ dh) * 4 + wa + dw))
    return pairs


def send(value, pairs):
    return lax.ppermute(value, AX, pairs)


def halo(block, ha):
    near = lax.dynamic_index_in_dim(block, 11 * (1 - ha), 1, keepdims=False)
    row = send(near, block_pairs(1, 0))
    left = send(block[:, :, 15, :], block_pairs(0, 1))
    right = send(block[:, :, 0, :], block_pairs(0, -1))
    corner_left = send(near[:, 15, :], block_pairs(1, 1))
    corner_right = send(near[:, 0, :], block_pairs(1, -1))
    return row, left, right, corner_left, corner_right


def build_shifted(wide, block, row, left, right, corner_left, corner_right, ha):
    col = lax.broadcasted_iota(jnp.int32, (16, 256), 0)
    is_top, is_low = (ha == 1).astype(F32), (ha == 0).astype(F32)
    for f in range(4):
        edge = row[f].astype(F32)
        lefts, rights = left[f].astype(F32), right[f].astype(F32)
        cl, cr = corner_left[f : f + 1].astype(F32), corner_right[f : f + 1].astype(F32)
        for r in range(14):
            if r in (0, 13):
                keep = is_top if r == 0 else is_low
                cells, lo, hi = edge * keep, cl * keep, cr * keep
                wide[f, r, :, 256:512] = cells.astype(BF)
            else:
                cells = block[f, r - 1].astype(F32)
                lo, hi = lefts[r - 1 : r], rights[r - 1 : r]
                wide[f, r, :, 256:512] = block[f, r - 1]
            wide[f, r, :, 512:768] = jnp.where(col == 0, lo, pltpu.roll(cells, 1, 0)).astype(BF)
            wide[f, r, :, 0:256] = jnp.where(col == 15, hi, pltpu.roll(cells, 15, 0)).astype(BF)


def weight_copies(weight, held, sem):
    return [
        pltpu.make_async_copy(weight.at[pl.ds(a * 9, 9)], held.at[pl.ds(a * 9, 9)], sem.at[a])
        for a in range(3)
    ]


def conv_sum(wide, held, copies, total):
    for a in (2, 1, 0):
        frames = a + 2
        copies[a].wait()
        for b in range(3):
            window = wide[2 - a : 4, 2 - b : 14 - b].reshape(frames * 192, 768)
            part = None
            for e in range(3):
                one = lax.dot_general(
                    window[:, e * 256 : (e + 1) * 256],
                    held[(a * 3 + b) * 3 + e],
                    NT,
                    preferred_element_type=F32,
                )
                part = one if part is None else part + one
            if a == 2 and b == 0:
                total[...] = part
            else:
                total[0 : frames * 192] += part


def first_kernel(
    place, block, row, left, right, cl, cr, hidden, inputs, film, weight,
    act_out, inp_out, wide, hid_out, held, total, sem,
):
    copies = weight_copies(weight, held, sem)
    for a in (2, 1, 0):
        copies[a].start()
    x, core, ha = place[0], place[2], place[3]
    lane = lax.broadcasted_iota(jnp.int32, (256, 256), 1)
    goal = (x + ((lane >> 5) & 3)) & 3
    kept = core ^ (lane >> 7)
    source = ((goal & 1) << 7) + ((goal >> 1) << 6) + (kept << 5) + (lane & 31)
    order = (lax.broadcasted_iota(jnp.int32, (256, 256), 0) == source).astype(BF)
    inp_out[...] = jnp.dot(
        inputs[...].reshape(768, 256), order, preferred_element_type=F32
    ).astype(BF)
    scale, shift = 1.0 + film[0:1, 0:256], film[0:1, 256:512]
    shifted = hidden[...].reshape(768, 256).astype(F32) * scale + shift
    sigma = jax.nn.sigmoid(shifted)
    activated = (shifted * sigma).astype(BF)
    act_out[...] = jnp.dot(activated, order, preferred_element_type=F32).astype(BF)
    build_shifted(wide, block, row, left, right, cl, cr, ha)
    conv_sum(wide, held, copies, total)
    shifted = hidden[...].reshape(768, 256).astype(F32) * scale + shift
    sigma = jax.nn.sigmoid(shifted)
    grad = total[...] * scale * sigma * (1.0 + shifted * (1.0 - sigma))
    hid_out[...] = grad.astype(BF).reshape(4, 12, 16, 256)


def second_grad_kernel(wide, act, own, pair):
    b = pl.program_id(0)
    for a in range(3):
        rows = (a + 2) * 192
        window = wide[2 - a : 4, pl.ds(2 - b, 12)].reshape(rows, 768)
        grad = lax.dot_general(act[0:rows], window, TN, preferred_element_type=F32)
        own[a, 0] = grad[0:128]
        pair[a, 0] = grad[128:256]


def second_pair_kernel(own, pair, keep, one, two, three):
    for a in range(3):
        total = own[a, 0] + pair[a, 0]
        keep[a, 0] = total[0:32]
        one[a, 0] = total[32:64].astype(BF)
        two[a, 0] = total[64:96].astype(BF)
        three[a, 0] = total[96:128].astype(BF)


def second_x_kernel(place, own, got1, got2, got3, keep, one, two, three, held):
    y = place[1]
    outs = (keep, one, two, three)

    def tap(t):
        ab, lanes = t // 3, slice(t % 3 * 256, t % 3 * 256 + 256)
        at = (ab // 3, ab % 3, slice(None), lanes)
        return own[at] + got1[at].astype(F32) + got2[at].astype(F32) + got3[at].astype(F32)

    for g in range(7):
        parts = [tap(t) if t < 27 else jnp.zeros((32, 256), F32) for t in range(4 * g, 4 * g + 4)]
        held[...] = jnp.concatenate(parts, axis=0).T.reshape(8, 4, 8, 128)
        for q in range(4):
            piece = held[:, (y + q) & 3].reshape(64, 128)
            outs[q][g] = piece.astype(outs[q].dtype)


def first_grad_kernel(
    place, block, row, left, right, cl, cr, inp, wide, own, pair, held
):
    b = pl.program_id(0)
    y = place[1]

    @pl.when(b == 0)
    def _():
        build_shifted(wide, block, row, left, right, cl, cr, place[3])

    for a in range(3):
        rows = (a + 2) * 192
        window = wide[2 - a : 4, pl.ds(2 - b, 12)].reshape(rows, 768)
        grad = lax.dot_general(window, inp[0:rows], TN, preferred_element_type=F32)
        held[...] = grad.reshape(3, 8, 4, 8, 256)
        for q in range(4):
            piece = held[:, :, (y + q) & 3].reshape(3, 64, 256)
            own[q, a, 0] = piece[:, :, 0:128]
            pair[q, a, 0] = piece[:, :, 128:256]


def first_pair_kernel(own, pair, keep, one, two, three):
    for q, out in enumerate((keep, one, two, three)):
        out[...] = (own[q] + pair[q]).astype(out.dtype)


def first_y_kernel(own, got1, got2, got3, keep, one, two, three):
    outs = (keep, one, two, three)

    def tap(t):
        at = (t // 9, t // 3 % 3, t % 3)
        return own[at] + got1[at].astype(F32) + got2[at].astype(F32) + got3[at].astype(F32)

    for g in range(7):
        taps = [tap(t) if t < 27 else jnp.zeros((64, 128), F32) for t in range(4 * g, 4 * g + 4)]
        for q in range(4):
            piece = jnp.concatenate([v[:, q * 32 : q * 32 + 32] for v in taps], axis=1)
            outs[q][g] = piece.astype(outs[q].dtype)


def last_stage_kernel(a0, a1, a2, a3, b0, b1, b2, b3, out):
    sums = []
    for own, got in ((a0, (a1, a2, a3)), (b0, (b1, b2, b3))):
        total = own[...]
        for ref in got:
            total = total + ref[...].astype(F32)
        sums.append(total)
    for z in range(8):
        parts = [total[:, z * 8 : z * 8 + 8].reshape(56, 128) for total in sums]
        out[z] = jnp.concatenate(parts, axis=0).astype(BF)


def final_kernel(factor, got, one, two):
    total = got[0].astype(F32)
    for z in range(1, 8):
        total = total + got[z].astype(F32)
    total = (total * factor).reshape(2, 7, 8, 128)
    for out, which in ((two, 0), (one, 1)):
        for t in range(27):
            out[t] = total[which, t // 4, :, t % 4 * 32 : t % 4 * 32 + 32]


def input_conv_kernel(wide, block, weight, out, held, total, sem):
    copies = weight_copies(weight, held, sem)
    for a in (2, 1, 0):
        copies[a].start()
    conv_sum(wide, held, copies, total)
    grad = block[...].reshape(768, 256).astype(F32) + total[...]
    out[...] = grad.astype(BF).reshape(4, 12, 16, 256)


def shards(activations, saved_hidden, cotangent, conv_one, conv_two, film_table, timesteps):
    inputs, hidden, block = activations[0], saved_hidden[0], cotangent[0]
    ha, xh = lax.axis_index("ha"), lax.axis_index("xh")
    y, core = lax.axis_index("y"), lax.axis_index("core")
    place = jnp.stack([xh * 2 + ha, y, core, ha]).astype(jnp.int32)
    film = lax.dynamic_slice(film_table, (timesteps[0], 0), (1, 512))
    taps_one = conv_one.transpose(1, 2, 3, 0, 4).reshape(27, 256, 256)
    taps_two = conv_two.transpose(1, 2, 3, 0, 4).reshape(27, 256, 256)
    conv_scratch = [
        pltpu.VMEM((27, 256, 256), BF),
        pltpu.VMEM((768, 256), F32),
        pltpu.SemaphoreType.DMA((3,)),
    ]
    whole = lambda shape: pl.BlockSpec(shape, lambda b: (0,) * len(shape))

    cot_halo = halo(block, ha)
    act, inp, wide_cot, grad_hidden = pl.pallas_call(
        first_kernel,
        out_shape=(
            SDS((768, 256), BF),
            SDS((768, 256), BF),
            SDS((4, 14, 16, 768), BF),
            SDS((4, 12, 16, 256), BF),
        ),
        in_specs=[SM] + [VM] * 9 + [HB],
        out_specs=[VM] * 4,
        scratch_shapes=conv_scratch,
        compiler_params=PARAMS,
        name="conv_two_back",
    )(place, block, *cot_halo, hidden, inputs, film, taps_two)

    hid_halo = halo(grad_hidden, ha)

    tall = pl.BlockSpec((3, 1, 128, 768), lambda b: (0, b, 0, 0))
    low = pl.BlockSpec((3, 1, 32, 768), lambda b: (0, b, 0, 0))
    own, pair = pl.pallas_call(
        second_grad_kernel,
        grid=(3,),
        out_shape=(SDS((3, 3, 128, 768), F32),) * 2,
        in_specs=[whole((4, 14, 16, 768)), whole((768, 256))],
        out_specs=[tall, tall],
        compiler_params=PARAMS,
        name="grad_two",
    )(wide_cot, act)
    pair = send(pair, ring_pairs(dc=1))
    pieces = pl.pallas_call(
        second_pair_kernel,
        grid=(3,),
        out_shape=(SDS((3, 3, 32, 768), F32),) + (SDS((3, 3, 32, 768), BF),) * 3,
        in_specs=[tall, tall],
        out_specs=[low] * 4,
        compiler_params=PARAMS,
        name="grad_two_pair",
    )(own, pair)
    got = [send(pieces[d], ring_pairs(dx=d)) for d in (2, 1, 3)]
    quads = (SDS((7, 64, 128), F32),) + (SDS((7, 64, 128), BF),) * 3
    pieces = pl.pallas_call(
        second_x_kernel,
        out_shape=quads,
        in_specs=[SM] + [VM] * 4,
        out_specs=[VM] * 4,
        scratch_shapes=[pltpu.VMEM((8, 4, 8, 128), F32)],
        compiler_params=PARAMS,
        name="grad_two_x",
    )(place, pieces[0], *got)
    parts_two = [pieces[0]] + [send(pieces[d], ring_pairs(dy=d)) for d in (2, 1, 3)]

    wide_spec = whole((4, 14, 16, 768))
    split = pl.BlockSpec((4, 3, 1, 3, 64, 128), lambda b: (0, 0, b, 0, 0, 0))
    part = pl.BlockSpec((3, 1, 3, 64, 128), lambda b: (0, b, 0, 0, 0))
    wide_hid, own, pair = pl.pallas_call(
        first_grad_kernel,
        grid=(3,),
        out_shape=(SDS((4, 14, 16, 768), BF),) + (SDS((4, 3, 3, 3, 64, 128), F32),) * 2,
        in_specs=[
            SM,
            whole((4, 12, 16, 256)),
            whole((4, 16, 256)),
            whole((4, 12, 256)),
            whole((4, 12, 256)),
            whole((4, 256)),
            whole((4, 256)),
            whole((768, 256)),
        ],
        out_specs=[wide_spec, split, split],
        scratch_shapes=[pltpu.VMEM((3, 8, 4, 8, 256), F32)],
        compiler_params=PARAMS,
        name="grad_one",
    )(place, grad_hidden, *hid_halo, inp)
    pair = send(pair, ring_pairs(dc=1))
    pieces = pl.pallas_call(
        first_pair_kernel,
        grid=(3,),
        out_shape=(SDS((3, 3, 3, 64, 128), F32),) + (SDS((3, 3, 3, 64, 128), BF),) * 3,
        in_specs=[split, split],
        out_specs=[part] * 4,
        compiler_params=PARAMS,
        name="grad_one_pair",
    )(own, pair)
    got = [send(pieces[d], ring_pairs(dy=d)) for d in (2, 1, 3)]
    pieces = pl.pallas_call(
        first_y_kernel,
        out_shape=quads,
        in_specs=[VM] * 4,
        out_specs=[VM] * 4,
        compiler_params=PARAMS,
        name="grad_one_y",
    )(pieces[0], *got)
    parts_one = [pieces[0]] + [send(pieces[d], ring_pairs(dx=d)) for d in (2, 1, 3)]

    grad_input = pl.pallas_call(
        input_conv_kernel,
        out_shape=SDS((4, 12, 16, 256), BF),
        in_specs=[VM, VM, HB],
        out_specs=VM,
        scratch_shapes=conv_scratch,
        compiler_params=PARAMS,
        name="conv_one_back",
    )(wide_hid, block, taps_one)

    planes = pl.pallas_call(
        last_stage_kernel,
        out_shape=SDS((8, 112, 128), BF),
        in_specs=[VM] * 8,
        out_specs=VM,
        compiler_params=PARAMS,
        name="last_stage",
    )(*parts_two, *parts_one)
    planes = lax.all_to_all(planes, "z", 0, 0, tiled=True)
    factor = float(256 * 768) ** (-0.5)
    grad_one, grad_two = pl.pallas_call(
        functools.partial(final_kernel, factor),
        out_shape=(SDS((27, 8, 32), F32),) * 2,
        in_specs=[VM],
        out_specs=[VM] * 2,
        compiler_params=PARAMS,
        name="final_sum",
    )(planes)
    shape = lambda g: g.transpose(2, 0, 1).reshape(32, 3, 3, 3, 8)
    return grad_input[None], shape(grad_one), shape(grad_two)


def solution(mesh):
    fine = Mesh(mesh.devices.reshape(SIZES), AX)
    clip = ("z", "y")
    placed = P(clip, None, "ha", ("xh", "core"), None)
    weight = P(("ha", "xh", "core"), None, None, None, clip)
    return jax.shard_map(
        shards,
        mesh=fine,
        in_specs=(placed, placed, placed, P(), P(), P(), P(clip)),
        out_specs=(placed, weight, weight),
        check_vma=False,
    )
```

time: 623 us -> 141 us (0.23)
  waiting for transfers between devices: 465 us -> 23.5 us
  matrix products: 74.7 us -> 0 us
  Pallas kernels: 0 us -> 49.3 us
  starting transfers between devices: 23.1 us -> 53.7 us
  local copies, waits for them, and re-layouts: 32.1 us -> 11.7 us
  between operations: 15.2 us -> 1.6 us
  other arithmetic: 10.5 us -> 0.65 us
    reduce_scatter x2 -> x0, waiting for transfers between devices: 392 us -> none  [reduce_grad(): lax.psum_scatter(partial_value, 'dp', scatter_dimension=4, tiled=True)]
    dot_general x109 -> x0, matrix products: 74.7 us -> none  [the longest x54 54.7 us: weight_grad(): lax.dot_general(window, cot_rows, (((0,), (0,)), ((), ())), preferred_ele...]
    unnamed x6 -> x0, waiting for transfers between devices: 67.8 us -> none
    pallas_call x0 -> x10, Pallas kernels: none -> 49.3 us  [the longest x1 8.2 us: shards(): pl.pallas_call(first_kernel, out_shape=(SDS((768, 256), BF), SDS((768, 25...]
    ppermute x8 -> x24, starting transfers between devices: 22.9 us -> 45.2 us  [send(): return lax.ppermute(value, AX, pairs)]
    reshape x2 -> x0, local copies, waits for them, and re-layouts: 16.2 us -> none  [weight_grad(): jnp.stack(blocks_list, 1).reshape(padded_in.shape[-1], 3, 3, 3, outs_count)]
    ppermute x8 -> x24, waiting for transfers between devices: 4.83 us -> 20.3 us  [send(): return lax.ppermute(value, AX, pairs)]
    all_to_all x0 -> x1, starting transfers between devices: none -> 8.46 us  [shards(): planes = lax.all_to_all(planes, 'z', 0, 0, tiled=True)]
  transfers between devices with their start and end apart: 12 -> 25, of which waited for: 9 -> 10; matrix products, arithmetic and copies ran while one was open for 9% -> 3% of each run, Pallas kernels for 0% -> 27%
where the time goes in v1:
time: 141 us; the launch traced here: 140 us
  starting transfers between devices  53.7 us (38%)
  Pallas kernels  49.3 us (35%)
  waiting for transfers between devices  23.5 us (17%)
  local copies, waits for them, and re-layouts  11.7 us (8%)
  between operations  1.6 us (1%)
    ppermute x24, starting transfers between devices, send(): return lax.ppermute(value, AX, pairs)  45.2 us
    ppermute x24, waiting for transfers between devices, send(): return lax.ppermute(value, AX, pairs)  20.3 us
    all_to_all x1, starting transfers between devices, shards(): planes = lax.all_to_all(planes, 'z', 0, 0, tiled=True)  8.46 us
    pallas_call x1, Pallas kernels, shards(): pl.pallas_call(first_kernel, out_shape=(SDS((768, 256), BF), SDS((768, 25...  8.2 us
    pallas_call x1, Pallas kernels, shards(): pl.pallas_call(input_conv_kernel, out_shape=SDS((4, 12, 16, 256), BF), in...  7.88 us
    pallas_call x1, Pallas kernels, shards(): pl.pallas_call(first_grad_kernel, grid=(3,), out_shape=(SDS((4, 14, 16, 7...  7.42 us
    pallas_call x1, Pallas kernels, shards(): pl.pallas_call(second_grad_kernel, grid=(3,), out_shape=(SDS((3, 3, 128,...  6.22 us
    unnamed x46, local copies, waits for them, and re-layouts  5.92 us
  transfers between devices with their start and end apart: 25, of which 10 were waited for; matrix products, arithmetic and copies ran while one was open for 3% of the time, Pallas kernels for 27%

profile of v1, /device:TPU:24, one launch (start us, length us, event | category | flops | bytes accessed | tf_op | source)
XLA Modules:
  0.0 140.5 jit_solution(11053946482608106044)
XLA Ops:
  4.5 4.3 %collective-permute-start.3 = (bf16[4,256]{1,0:T(4,128)(2,1)S(1)}, bf16[4,256]{1,0:T(4,128)(2,1)S(1)}, u32[]{:S(2)}, u32[]{:S(2)}) collective-permute-start(bf16[4,256]{1,0:T(4,128)(2,1)S(1)} %get-tuple-element.64), channel_id=1, source_target_pairs={{0,5},{1,6},{2,7},{4,1},{5,2},{6,3},{8,13},{9,14},{10,15},{12,9},{... | collective-permute-start | bytes 6152 | tf_op jit(solution)/shard_map/ppermute | solution.py:51
  9.9 2.7 %collective-permute-start.1 = (bf16[4,12,256]{2,1,0:T(8,128)(2,1)S(1)}, bf16[4,12,256]{2,1,0:T(8,128)(2,1)S(1)}, u32[]{:S(2)}, u32[]{:S(2)}) collective-permute-start(bf16[4,12,256]{2,1,0:T(8,128)(2,1)S(1)} %copy.18), channel_id=1, source_target_pairs={{0,1},{1,2},{2,3},{4,5},{5,6},{6,7},{8,9},{9,10},{10,11},{12,13},{... | collective-permute-start | bytes 73736 | tf_op jit(solution)/shard_map/ppermute | solution.py:51
  17.9 8.2 %conv_two_back.1 = (bf16[768,256]{1,0:T(8,128)(2,1)}, bf16[768,256]{1,0:T(8,128)(2,1)}, bf16[4,14,16,768]{3,2,1,0:T(8,128)(2,1)}, bf16[4,12,16,256]{3,2,1,0:T(8,128)(2,1)}) custom-call(s32[4]{0:T(128)} %pad_add_fusion.place, bf16[4,12,16,256]{3,2,1,0:T(8,128)(2,1)} %bitcast.51, bf16[4,16,256]{2,1,0:T(8,128)(2,1)} %copy.21.row, ...), custom_call_target="tpu_custom_call" | custom-call | tf_op jit(solution)/shard_map/conv_two_back/pallas_call | solution.py:264
  28.3 6.2 %grad_two.1 = (f32[3,3,128,768]{3,2,1,0:T(8,128)}, f32[3,3,128,768]{3,2,1,0:T(8,128)}) custom-call(bf16[4,14,16,768]{3,2,1,0:T(8,128)(2,1)} %get-tuple-element.33.wide, bf16[768,256]{1,0:T(8,128)(2,1)} %get-tuple-element.34.act), custom_call_target="tpu_custom_call" | custom-call | tf_op jit(solution)/shard_map/grad_two/pallas_call | solution.py:283
  34.5 4.0 %collective-permute-start.10 = (f32[3,3,128,768]{3,2,1,0:T(8,128)}, f32[3,3,128,768]{3,2,1,0:T(8,128)S(1)}, u32[]{:S(2)}, u32[]{:S(2)}) collective-permute-start(f32[3,3,128,768]{3,2,1,0:T(8,128)} %get-tuple-element.36), channel_id=1, source_target_pairs={{0,1},{1,0},{2,3},{3,2},{4,5},{5,4},{6,7},{7,6},{8,9},{9,8},{10,11... | collective-permute-start | bytes 10616840 | tf_op jit(solution)/shard_map/ppermute | solution.py:51
  39.8 3.0 %collective-permute-start.6 = (bf16[4,12,256]{2,1,0:T(8,128)(2,1)S(1)}, bf16[4,12,256]{2,1,0:T(8,128)(2,1)S(1)}, u32[]{:S(2)}, u32[]{:S(2)}) collective-permute-start(bf16[4,12,256]{2,1,0:T(8,128)(2,1)S(1)} %get-tuple-element.58), channel_id=1, source_target_pairs={{0,1},{1,2},{2,3},{4,5},{5,6},{6,7},{8,9},{9,10},{10,11},{12,13},{... | collective-permute-start | bytes 73736 | tf_op jit(solution)/shard_map/ppermute | solution.py:51
  44.2 6.6 %collective-permute-start.8 = (bf16[4,256]{1,0:T(4,128)(2,1)S(1)}, bf16[4,256]{1,0:T(4,128)(2,1)S(1)}, u32[]{:S(2)}, u32[]{:S(2)}) collective-permute-start(bf16[4,256]{1,0:T(4,128)(2,1)S(1)} %get-tuple-element.62), channel_id=1, source_target_pairs={{0,5},{1,6},{2,7},{4,1},{5,2},{6,3},{8,13},{9,14},{10,15},{12,9},{... | collective-permute-start | bytes 6152 | tf_op jit(solution)/shard_map/ppermute | solution.py:51
  52.7 7.4 %grad_one.1 = (bf16[4,14,16,768]{3,2,1,0:T(8,128)(2,1)}, f32[4,3,3,3,64,128]{5,4,3,2,1,0:T(8,128)}, f32[4,3,3,3,64,128]{5,4,3,2,1,0:T(8,128)}) custom-call(s32[4]{0:T(128)} %pad_add_fusion.place, bf16[4,12,16,256]{3,2,1,0:T(8,128)(2,1)} %get-tuple-element.30.block, bf16[4,16,256]{2,1,0:T(8,128)(2,1)} %copy.25.row, bf16[4,12,256]{2,1,0:T(8,128)(2,1)} %copy-done.18, ...), custom_call_target="tpu_custom_call" | custom-call | tf_op jit(solution)/shard_map/grad_one/pallas_call | solution.py:318
  61.2 1.8 %copy-done.1 = f32[3,3,128,768]{3,2,1,0:T(8,128)} copy-done((f32[3,3,128,768]{3,2,1,0:T(8,128)}, f32[3,3,128,768]{3,2,1,0:T(8,128)S(1)}, u32[]{:S(2)}) %copy-start.1) | copy-done | bytes 3538968
  62.9 5.1 %grad_two_pair.1 = (f32[3,3,32,768]{3,2,1,0:T(8,128)}, bf16[3,3,32,768]{3,2,1,0:T(8,128)(2,1)}, bf16[3,3,32,768]{3,2,1,0:T(8,128)(2,1)}, bf16[3,3,32,768]{3,2,1,0:T(8,128)(2,1)}) custom-call(f32[3,3,128,768]{3,2,1,0:T(8,128)} %get-tuple-element.35.own, f32[3,3,128,768]{3,2,1,0:T(8,128)} %copy-done.1), custom_call_target="tpu_custom_call" | custom-call | tf_op jit(solution)/shard_map/grad_two_pair/pallas_call | solution.py:293
  68.0 2.7 %collective-permute-start.11 = (bf16[3,3,32,768]{3,2,1,0:T(8,128)(2,1)}, bf16[3,3,32,768]{3,2,1,0:T(8,128)(2,1)S(1)}, u32[]{:S(2)}, u32[]{:S(2)}) collective-permute-start(bf16[3,3,32,768]{3,2,1,0:T(8,128)(2,1)} %get-tuple-element.38), channel_id=1, source_target_pairs={{0,2},{1,3},{2,0},{3,1},{4,6},{5,7},{6,4},{7,5},{8,10},{9,11},{10,... | collective-permute-start | bytes 1327112 | tf_op jit(solution)/shard_map/ppermute | solution.py:51
  74.0 5.1 %grad_one_pair.1 = (f32[3,3,3,64,128]{4,3,2,1,0:T(8,128)}, bf16[3,3,3,64,128]{4,3,2,1,0:T(8,128)(2,1)}, bf16[3,3,3,64,128]{4,3,2,1,0:T(8,128)(2,1)}, bf16[3,3,3,64,128]{4,3,2,1,0:T(8,128)(2,1)}) custom-call(f32[4,3,3,3,64,128]{5,4,3,2,1,0:T(8,128)} %get-tuple-element.45.own, f32[4,3,3,3,64,128]{5,4,3,2,1,0:T(8,128)} %collective-permute-done.17.pair), custom_call_target="tpu_custom_call" | custom-call | tf_op jit(solution)/shard_map/grad_one_pair/pallas_call | solution.py:338
  80.2 2.2 %collective-permute-start.19 = (bf16[3,3,3,64,128]{4,3,2,1,0:T(8,128)(2,1)}, bf16[3,3,3,64,128]{4,3,2,1,0:T(8,128)(2,1)S(1)}, u32[]{:S(2)}, u32[]{:S(2)}) collective-permute-start(bf16[3,3,3,64,128]{4,3,2,1,0:T(8,128)(2,1)} %get-tuple-element.49), channel_id=1, source_target_pairs={{0,8},{1,9},{2,10},{3,11},{4,12},{5,13},{6,14},{7,15},{8,16},{9,17... | collective-permute-start | bytes 1327112 | tf_op jit(solution)/shard_map/ppermute | solution.py:51
  83.5 7.8 %collective-permute-done.12.got2 = bf16[3,3,32,768]{3,2,1,0:T(8,128)(2,1)S(1)} collective-permute-done((bf16[3,3,32,768]{3,2,1,0:T(8,128)(2,1)}, bf16[3,3,32,768]{3,2,1,0:T(8,128)(2,1)S(1)}, u32[]{:S(2)}, u32[]{:S(2)}) %collective-permute-start.12) | collective-permute-done | bytes 442400 | tf_op jit(solution)/shard_map/ppermute | solution.py:51
  93.3 2.8 %grad_two_x.1 = (f32[7,64,128]{2,1,0:T(8,128)}, bf16[7,64,128]{2,1,0:T(8,128)(2,1)}, bf16[7,64,128]{2,1,0:T(8,128)(2,1)}, bf16[7,64,128]{2,1,0:T(8,128)(2,1)}) custom-call(s32[4]{0:T(128)} %pad_add_fusion.place, f32[3,3,32,768]{3,2,1,0:T(8,128)} %get-tuple-element.37.own, bf16[3,3,32,768]{3,2,1,0:T(8,128)(2,1)} %copy-done.3, ...), custom_call_target="tpu_custom_call" | custom-call | tf_op jit(solution)/shard_map/grad_two_x/pallas_call | solution.py:304
  97.2 2.2 %collective-permute-start.15 = (bf16[7,64,128]{2,1,0:T(8,128)(2,1)}, bf16[7,64,128]{2,1,0:T(8,128)(2,1)S(1)}, u32[]{:S(2)}, u32[]{:S(2)}) collective-permute-start(bf16[7,64,128]{2,1,0:T(8,128)(2,1)} %get-tuple-element.43), channel_id=1, source_target_pairs={{0,8},{1,9},{2,10},{3,11},{4,12},{5,13},{6,14},{7,15},{8,16},{9,17... | collective-permute-start | bytes 344072 | tf_op jit(solution)/shard_map/ppermute | solution.py:51
  100.7 2.6 %collective-permute-done.20.got3 = bf16[3,3,3,64,128]{4,3,2,1,0:T(8,128)(2,1)S(1)} collective-permute-done((bf16[3,3,3,64,128]{4,3,2,1,0:T(8,128)(2,1)}, bf16[3,3,3,64,128]{4,3,2,1,0:T(8,128)(2,1)S(1)}, u32[]{:S(2)}, u32[]{:S(2)}) %collective-permute-start.20) | collective-permute-done | bytes 442400 | tf_op jit(solution)/shard_map/ppermute | solution.py:51
  104.1 2.8 %grad_one_y.1 = (f32[7,64,128]{2,1,0:T(8,128)}, bf16[7,64,128]{2,1,0:T(8,128)(2,1)}, bf16[7,64,128]{2,1,0:T(8,128)(2,1)}, bf16[7,64,128]{2,1,0:T(8,128)(2,1)}) custom-call(f32[3,3,3,64,128]{4,3,2,1,0:T(8,128)} %get-tuple-element.47.own, bf16[3,3,3,64,128]{4,3,2,1,0:T(8,128)(2,1)} %copy-done.6, bf16[3,3,3,64,128]{4,3,2,1,0:T(8,128)(2,1)} %copy-done.7, ...), custom_call_target="tpu_custom_call" | custom-call | tf_op jit(solution)/shard_map/grad_one_y/pallas_call | solution.py:348
  107.3 2.9 %collective-permute-start.23 = (bf16[7,64,128]{2,1,0:T(8,128)(2,1)}, bf16[7,64,128]{2,1,0:T(8,128)(2,1)S(1)}, u32[]{:S(2)}, u32[]{:S(2)}) collective-permute-start(bf16[7,64,128]{2,1,0:T(8,128)(2,1)} %get-tuple-element.54), channel_id=1, source_target_pairs={{0,6},{1,7},{2,4},{3,5},{4,0},{5,1},{6,2},{7,3},{8,14},{9,15},{10,... | collective-permute-start | bytes 344072 | tf_op jit(solution)/shard_map/ppermute | solution.py:51
  110.2 4.5 %collective-permute-done.21.b1 = bf16[7,64,128]{2,1,0:T(8,128)(2,1)S(1)} collective-permute-done((bf16[7,64,128]{2,1,0:T(8,128)(2,1)}, bf16[7,64,128]{2,1,0:T(8,128)(2,1)S(1)}, u32[]{:S(2)}, u32[]{:S(2)}) %collective-permute-start.21) | collective-permute-done | bytes 114720 | tf_op jit(solution)/shard_map/ppermute | solution.py:51
  116.4 2.1 %last_stage.1 = bf16[8,112,128]{2,1,0:T(8,128)(2,1)} custom-call(f32[7,64,128]{2,1,0:T(8,128)} %get-tuple-element.41.a0, bf16[7,64,128]{2,1,0:T(8,128)(2,1)} %copy-done.9, bf16[7,64,128]{2,1,0:T(8,128)(2,1)} %copy-done.10, bf16[7,64,128]{2,1,0:T(8,128)(2,1)} %copy-done.11, f32[7,64,128]{2,1,0:T(8,128)} %get-tuple-element.51.b0, ...), custom_call_target="tpu_custom_call" | custom-call | tf_op jit(solution)/shard_map/last_stage/pallas_call | solution.py:368
  118.6 8.5 %all-to-all-start = ((bf16[8,112,128]{2,1,0:T(8,128)(2,1)}), bf16[8,112,128]{2,1,0:T(8,128)(2,1)S(1)}, u32[]{:S(2)}, u32[]{:S(2)}) async-start(bf16[8,112,128]{2,1,0:T(8,128)(2,1)} %last_stage.1), calls=%async_computation | async-start | bytes 458752 | tf_op jit(solution)/shard_map/all_to_all | solution.py:376
  127.0 7.9 %conv_one_back.1 = bf16[4,12,16,256]{3,2,1,0:T(8,128)(2,1)} custom-call(bf16[4,14,16,768]{3,2,1,0:T(8,128)(2,1)} %get-tuple-element.32.wide, bf16[4,12,16,256]{3,2,1,0:T(8,128)(2,1)} %bitcast.52, bf16[27,256,256]{2,1,0:T(8,128)(2,1)} %bitcast.49), custom_call_target="tpu_custom_call" | custom-call | tf_op jit(solution)/shard_map/conv_one_back/pallas_call | solution.py:358
  134.9 3.2 %all-to-all-done.got = bf16[8,112,128]{2,1,0:T(8,128)(2,1)S(1)} async-done(((bf16[8,112,128]{2,1,0:T(8,128)(2,1)}), bf16[8,112,128]{2,1,0:T(8,128)(2,1)S(1)}, u32[]{:S(2)}, u32[]{:S(2)}) %all-to-all-start) | async-done | bytes 229408 | tf_op jit(solution)/shard_map/all_to_all | solution.py:376
  (99 shorter events, 32.5 us)
Async XLA Ops:
  1.6 14.2 %collective-permute-start = (bf16[4,16,256]{2,0,1:T(4,128)(2,1)S(1)}, bf16[4,16,256]{2,0,1:T(4,128)(2,1)S(1)}, u32[]{:S(2)}, u32[]{:S(2)}) collective-permute-start(bf16[4,16,256]{2,0,1:T(4,128)(2,1)S(1)} %bitcast.58), channel_id=1, source_target_pairs={{0,4},{1,5},{2,6},{3,7},{4,0},{5,1},{6,2},{7,3},{8,12},{9,13},{10,... | collective-permute-start | bytes 98312 | tf_op jit(solution)/shard_map/ppermute | solution.py:51
  3.2 13.3 %collective-permute-start.4 = (bf16[4,256]{1,0:T(4,128)(2,1)S(1)}, bf16[4,256]{1,0:T(4,128)(2,1)S(1)}, u32[]{:S(2)}, u32[]{:S(2)}) collective-permute-start(bf16[4,256]{1,0:T(4,128)(2,1)S(1)} %get-tuple-element.63), channel_id=1, source_target_pairs={{1,4},{2,5},{3,6},{5,0},{6,1},{7,2},{9,12},{10,13},{11,14},{13,8},... | collective-permute-start | bytes 6152 | tf_op jit(solution)/shard_map/ppermute | solution.py:51
  4.5 12.0 %collective-permute-start.3 = (bf16[4,256]{1,0:T(4,128)(2,1)S(1)}, bf16[4,256]{1,0:T(4,128)(2,1)S(1)}, u32[]{:S(2)}, u32[]{:S(2)}) collective-permute-start(bf16[4,256]{1,0:T(4,128)(2,1)S(1)} %get-tuple-element.64), channel_id=1, source_target_pairs={{0,5},{1,6},{2,7},{4,1},{5,2},{6,3},{8,13},{9,14},{10,15},{12,9},{... | collective-permute-start | bytes 6152 | tf_op jit(solution)/shard_map/ppermute | solution.py:51
  9.9 6.6 %collective-permute-start.1 = (bf16[4,12,256]{2,1,0:T(8,128)(2,1)S(1)}, bf16[4,12,256]{2,1,0:T(8,128)(2,1)S(1)}, u32[]{:S(2)}, u32[]{:S(2)}) collective-permute-start(bf16[4,12,256]{2,1,0:T(8,128)(2,1)S(1)} %copy.18), channel_id=1, source_target_pairs={{0,1},{1,2},{2,3},{4,5},{5,6},{6,7},{8,9},{9,10},{10,11},{12,13},{... | collective-permute-start | bytes 73736 | tf_op jit(solution)/shard_map/ppermute | solution.py:51
  28.0 16.1 %collective-permute-start.5 = (bf16[4,16,256]{2,0,1:T(4,128)(2,1)S(1)}, bf16[4,16,256]{2,0,1:T(4,128)(2,1)S(1)}, u32[]{:S(2)}, u32[]{:S(2)}) collective-permute-start(bf16[4,16,256]{2,0,1:T(4,128)(2,1)S(1)} %bitcast.60), channel_id=1, source_target_pairs={{0,4},{1,5},{2,6},{3,7},{4,0},{5,1},{6,2},{7,3},{8,12},{9,13},{10,... | collective-permute-start | bytes 98312 | tf_op jit(solution)/shard_map/ppermute | solution.py:51
  34.5 26.6 %collective-permute-start.10 = (f32[3,3,128,768]{3,2,1,0:T(8,128)}, f32[3,3,128,768]{3,2,1,0:T(8,128)S(1)}, u32[]{:S(2)}, u32[]{:S(2)}) collective-permute-start(f32[3,3,128,768]{3,2,1,0:T(8,128)} %get-tuple-element.36), channel_id=1, source_target_pairs={{0,1},{1,0},{2,3},{3,2},{4,5},{5,4},{6,7},{7,6},{8,9},{9,8},{10,11... | collective-permute-start | bytes 10616840 | tf_op jit(solution)/shard_map/ppermute | solution.py:51
  38.5 13.6 %collective-permute-start.7 = (bf16[4,12,256]{2,1,0:T(8,128)(2,1)S(1)}, bf16[4,12,256]{2,1,0:T(8,128)(2,1)S(1)}, u32[]{:S(2)}, u32[]{:S(2)}) collective-permute-start(bf16[4,12,256]{2,1,0:T(8,128)(2,1)S(1)} %get-tuple-element.57), channel_id=1, source_target_pairs={{1,0},{2,1},{3,2},{5,4},{6,5},{7,6},{9,8},{10,9},{11,10},{13,12},{... | collective-permute-start | bytes 73736 | tf_op jit(solution)/shard_map/ppermute | solution.py:51
  39.8 12.3 %collective-permute-start.6 = (bf16[4,12,256]{2,1,0:T(8,128)(2,1)S(1)}, bf16[4,12,256]{2,1,0:T(8,128)(2,1)S(1)}, u32[]{:S(2)}, u32[]{:S(2)}) collective-permute-start(bf16[4,12,256]{2,1,0:T(8,128)(2,1)S(1)} %get-tuple-element.58), channel_id=1, source_target_pairs={{0,1},{1,2},{2,3},{4,5},{5,6},{6,7},{8,9},{9,10},{10,11},{12,13},{... | collective-permute-start | bytes 73736 | tf_op jit(solution)/shard_map/ppermute | solution.py:51
  42.8 8.5 %collective-permute-start.9 = (bf16[4,256]{1,0:T(4,128)(2,1)S(1)}, bf16[4,256]{1,0:T(4,128)(2,1)S(1)}, u32[]{:S(2)}, u32[]{:S(2)}) collective-permute-start(bf16[4,256]{1,0:T(4,128)(2,1)S(1)} %get-tuple-element.61), channel_id=1, source_target_pairs={{1,4},{2,5},{3,6},{5,0},{6,1},{7,2},{9,12},{10,13},{11,14},{13,8},... | collective-permute-start | bytes 6152 | tf_op jit(solution)/shard_map/ppermute | solution.py:51
  44.2 7.9 %collective-permute-start.8 = (bf16[4,256]{1,0:T(4,128)(2,1)S(1)}, bf16[4,256]{1,0:T(4,128)(2,1)S(1)}, u32[]{:S(2)}, u32[]{:S(2)}) collective-permute-start(bf16[4,256]{1,0:T(4,128)(2,1)S(1)} %get-tuple-element.62), channel_id=1, source_target_pairs={{0,5},{1,6},{2,7},{4,1},{5,2},{6,3},{8,13},{9,14},{10,15},{12,9},{... | collective-permute-start | bytes 6152 | tf_op jit(solution)/shard_map/ppermute | solution.py:51
  60.1 13.9 %collective-permute-start.17 = (f32[4,3,3,3,64,128]{5,4,3,2,1,0:T(8,128)}, f32[4,3,3,3,64,128]{5,4,3,2,1,0:T(8,128)}, u32[]{:S(2)}, u32[]{:S(2)}) collective-permute-start(f32[4,3,3,3,64,128]{5,4,3,2,1,0:T(8,128)} %get-tuple-element.46), channel_id=1, source_target_pairs={{0,1},{1,0},{2,3},{3,2},{4,5},{5,4},{6,7},{7,6},{8,9},{9,8},{10,11... | collective-permute-start | bytes 10616840 | tf_op jit(solution)/shard_map/ppermute | solution.py:51
  68.0 14.8 %collective-permute-start.11 = (bf16[3,3,32,768]{3,2,1,0:T(8,128)(2,1)}, bf16[3,3,32,768]{3,2,1,0:T(8,128)(2,1)S(1)}, u32[]{:S(2)}, u32[]{:S(2)}) collective-permute-start(bf16[3,3,32,768]{3,2,1,0:T(8,128)(2,1)} %get-tuple-element.38), channel_id=1, source_target_pairs={{0,2},{1,3},{2,0},{3,1},{4,6},{5,7},{6,4},{7,5},{8,10},{9,11},{10,... | collective-permute-start | bytes 1327112 | tf_op jit(solution)/shard_map/ppermute | solution.py:51
  70.7 20.6 %collective-permute-start.12 = (bf16[3,3,32,768]{3,2,1,0:T(8,128)(2,1)}, bf16[3,3,32,768]{3,2,1,0:T(8,128)(2,1)S(1)}, u32[]{:S(2)}, u32[]{:S(2)}) collective-permute-start(bf16[3,3,32,768]{3,2,1,0:T(8,128)(2,1)} %get-tuple-element.39), channel_id=1, source_target_pairs={{0,4},{1,5},{2,6},{3,7},{4,2},{5,3},{6,0},{7,1},{8,12},{9,13},{10,... | collective-permute-start | bytes 1327112 | tf_op jit(solution)/shard_map/ppermute | solution.py:51
  72.3 20.3 %collective-permute-start.13 = (bf16[3,3,32,768]{3,2,1,0:T(8,128)(2,1)}, bf16[3,3,32,768]{3,2,1,0:T(8,128)(2,1)S(1)}, u32[]{:S(2)}, u32[]{:S(2)}) collective-permute-start(bf16[3,3,32,768]{3,2,1,0:T(8,128)(2,1)} %get-tuple-element.40), channel_id=1, source_target_pairs={{0,6},{1,7},{2,4},{3,5},{4,0},{5,1},{6,2},{7,3},{8,14},{9,15},{10,... | collective-permute-start | bytes 1327112 | tf_op jit(solution)/shard_map/ppermute | solution.py:51
  79.0 20.4 %collective-permute-start.18 = (bf16[3,3,3,64,128]{4,3,2,1,0:T(8,128)(2,1)}, bf16[3,3,3,64,128]{4,3,2,1,0:T(8,128)(2,1)S(1)}, u32[]{:S(2)}, u32[]{:S(2)}) collective-permute-start(bf16[3,3,3,64,128]{4,3,2,1,0:T(8,128)(2,1)} %get-tuple-element.48), channel_id=1, source_target_pairs={{0,16},{1,17},{2,18},{3,19},{4,20},{5,21},{6,22},{7,23},{8,24},{9,... | collective-permute-start | bytes 1327112 | tf_op jit(solution)/shard_map/ppermute | solution.py:51
  80.2 20.6 %collective-permute-start.19 = (bf16[3,3,3,64,128]{4,3,2,1,0:T(8,128)(2,1)}, bf16[3,3,3,64,128]{4,3,2,1,0:T(8,128)(2,1)S(1)}, u32[]{:S(2)}, u32[]{:S(2)}) collective-permute-start(bf16[3,3,3,64,128]{4,3,2,1,0:T(8,128)(2,1)} %get-tuple-element.49), channel_id=1, source_target_pairs={{0,8},{1,9},{2,10},{3,11},{4,12},{5,13},{6,14},{7,15},{8,16},{9,17... | collective-permute-start | bytes 1327112 | tf_op jit(solution)/shard_map/ppermute | solution.py:51
  82.8 20.5 %collective-permute-start.20 = (bf16[3,3,3,64,128]{4,3,2,1,0:T(8,128)(2,1)}, bf16[3,3,3,64,128]{4,3,2,1,0:T(8,128)(2,1)S(1)}, u32[]{:S(2)}, u32[]{:S(2)}) collective-permute-start(bf16[3,3,3,64,128]{4,3,2,1,0:T(8,128)(2,1)} %get-tuple-element.50), channel_id=1, source_target_pairs={{0,24},{1,25},{2,26},{3,27},{4,28},{5,29},{6,30},{7,31},{8,0},{9,1... | collective-permute-start | bytes 1327112 | tf_op jit(solution)/shard_map/ppermute | solution.py:51
  96.1 11.2 %collective-permute-start.14 = (bf16[7,64,128]{2,1,0:T(8,128)(2,1)}, bf16[7,64,128]{2,1,0:T(8,128)(2,1)S(1)}, u32[]{:S(2)}, u32[]{:S(2)}) collective-permute-start(bf16[7,64,128]{2,1,0:T(8,128)(2,1)} %get-tuple-element.42), channel_id=1, source_target_pairs={{0,16},{1,17},{2,18},{3,19},{4,20},{5,21},{6,22},{7,23},{8,24},{9,... | collective-permute-start | bytes 344072 | tf_op jit(solution)/shard_map/ppermute | solution.py:51
  97.2 13.0 %collective-permute-start.15 = (bf16[7,64,128]{2,1,0:T(8,128)(2,1)}, bf16[7,64,128]{2,1,0:T(8,128)(2,1)S(1)}, u32[]{:S(2)}, u32[]{:S(2)}) collective-permute-start(bf16[7,64,128]{2,1,0:T(8,128)(2,1)} %get-tuple-element.43), channel_id=1, source_target_pairs={{0,8},{1,9},{2,10},{3,11},{4,12},{5,13},{6,14},{7,15},{8,16},{9,17... | collective-permute-start | bytes 344072 | tf_op jit(solution)/shard_map/ppermute | solution.py:51
  99.5 10.7 %collective-permute-start.16 = (bf16[7,64,128]{2,1,0:T(8,128)(2,1)}, bf16[7,64,128]{2,1,0:T(8,128)(2,1)S(1)}, u32[]{:S(2)}, u32[]{:S(2)}) collective-permute-start(bf16[7,64,128]{2,1,0:T(8,128)(2,1)} %get-tuple-element.44), channel_id=1, source_target_pairs={{0,24},{1,25},{2,26},{3,27},{4,28},{5,29},{6,30},{7,31},{8,0},{9,1... | collective-permute-start | bytes 344072 | tf_op jit(solution)/shard_map/ppermute | solution.py:51
  106.9 7.7 %collective-permute-start.21 = (bf16[7,64,128]{2,1,0:T(8,128)(2,1)}, bf16[7,64,128]{2,1,0:T(8,128)(2,1)S(1)}, u32[]{:S(2)}, u32[]{:S(2)}) collective-permute-start(bf16[7,64,128]{2,1,0:T(8,128)(2,1)} %get-tuple-element.52), channel_id=1, source_target_pairs={{0,2},{1,3},{2,0},{3,1},{4,6},{5,7},{6,4},{7,5},{8,10},{9,11},{10,... | collective-permute-start | bytes 344072 | tf_op jit(solution)/shard_map/ppermute | solution.py:51
  106.9 8.8 %collective-permute-start.22 = (bf16[7,64,128]{2,1,0:T(8,128)(2,1)}, bf16[7,64,128]{2,1,0:T(8,128)(2,1)S(1)}, u32[]{:S(2)}, u32[]{:S(2)}) collective-permute-start(bf16[7,64,128]{2,1,0:T(8,128)(2,1)} %get-tuple-element.53), channel_id=1, source_target_pairs={{0,4},{1,5},{2,6},{3,7},{4,2},{5,3},{6,0},{7,1},{8,12},{9,13},{10,... | collective-permute-start | bytes 344072 | tf_op jit(solution)/shard_map/ppermute | solution.py:51
  107.3 8.5 %collective-permute-start.23 = (bf16[7,64,128]{2,1,0:T(8,128)(2,1)}, bf16[7,64,128]{2,1,0:T(8,128)(2,1)S(1)}, u32[]{:S(2)}, u32[]{:S(2)}) collective-permute-start(bf16[7,64,128]{2,1,0:T(8,128)(2,1)} %get-tuple-element.54), channel_id=1, source_target_pairs={{0,6},{1,7},{2,4},{3,5},{4,0},{5,1},{6,2},{7,3},{8,14},{9,15},{10,... | collective-permute-start | bytes 344072 | tf_op jit(solution)/shard_map/ppermute | solution.py:51
  118.6 19.5 %all-to-all-start = ((bf16[8,112,128]{2,1,0:T(8,128)(2,1)}), bf16[8,112,128]{2,1,0:T(8,128)(2,1)S(1)}, u32[]{:S(2)}, u32[]{:S(2)}) async-start(bf16[8,112,128]{2,1,0:T(8,128)(2,1)} %last_stage.1), calls=%async_computation | async-start | bytes 458752 | tf_op jit(solution)/shard_map/all_to_all | solution.py:376
  (24 other events, 67.8 us)

commit v2 on v0

v2 whole, which is shorter than its diff:
```python
import functools

import jax
import jax.numpy as jnp
from jax import lax
from jax.experimental import pallas as pl
from jax.experimental.pallas import tpu as pltpu
from jax.sharding import Mesh
from jax.sharding import PartitionSpec as P

BF = jnp.bfloat16
F32 = jnp.float32
AX = ("z", "y", "ha", "xh", "core")
SIZES = (8, 4, 2, 2, 2)
VM = pl.BlockSpec(memory_space=pltpu.VMEM)
HB = pl.BlockSpec(memory_space=pl.ANY)
SM = pl.BlockSpec(memory_space=pltpu.SMEM)
NT = (((1,), (1,)), ((), ()))
TN = (((0,), (0,)), ((), ()))


def core_pairs():
    return [(i, i ^ 1) for i in range(256)]


def block_pairs(dh, dw):
    pairs = []
    for i in range(256):
        ha, wa, dp = i // 4 % 2, i % 4, i // 8
        if 0 <= wa + dw < 4:
            pairs.append((i, dp * 8 + (ha ^ dh) * 4 + wa + dw))
    return pairs


def send(value, pairs):
    return lax.ppermute(value, AX, pairs)


def call(kernel, name, args, spaces, outs, scratch=(), limit=16):
    args = [
        pltpu.with_memory_space_constraint(a, pltpu.VMEM) if s == "v" else a
        for a, s in zip(args, spaces)
    ]
    specs = {"v": VM, "c": VM, "h": HB, "s": SM}
    return pl.pallas_call(
        kernel,
        out_shape=tuple(outs),
        in_specs=[specs[s] for s in spaces],
        out_specs=tuple(VM for _ in outs),
        scratch_shapes=list(scratch),
        compiler_params=pltpu.CompilerParams(vmem_limit_bytes=limit * 2**20),
        name=name,
    )(*args)


def pack_kernel(count, *refs):
    blocks, (row, hi, lo, corner_hi, corner_lo, wide) = refs[:count], refs[count:]
    ha = lax.axis_index("ha")
    edge = 11 * (1 - ha)
    for n, block in enumerate(blocks):
        flat = block[...].reshape(768, 256).astype(F32)
        wide[0] = flat[:, 0:128]
        wide[1] = flat[:, 128:256]
        for f in range(4):
            row[n, f] = block[f, edge]
            for j, out, corner in ((15, hi, corner_hi), (0, lo, corner_lo)):
                for h in range(2):
                    lanes = slice(h * 128, h * 128 + 128)
                    cells = wide[h, pl.ds(f * 192 + j, 12, stride=16), :]
                    cells = jnp.concatenate([cells, jnp.zeros((4, 128), F32)], axis=0)
                    out[n, f, :, lanes] = cells.astype(BF)
                    cell = wide[h, pl.ds(f * 192 + edge * 16 + j, 1), :]
                    corner[n, f, :, lanes] = jnp.broadcast_to(cell, (16, 128)).astype(BF)


def halo(name, blocks, space):
    n = len(blocks)
    side = pltpu.VMEM((n, 4, 16, 256), BF)
    row, hi, lo, corner_hi, corner_lo = call(
        functools.partial(pack_kernel, n),
        name,
        blocks,
        space * n,
        [side] * 5,
        [pltpu.VMEM((2, 768, 128), F32)],
    )
    return (
        send(row, block_pairs(1, 0)),
        send(hi, block_pairs(0, 1)),
        send(lo, block_pairs(0, -1)),
        send(corner_hi, block_pairs(1, 1)),
        send(corner_lo, block_pairs(1, -1)),
    )


def build_shifted(wide, block, row, left, right, corner_left, corner_right, ha, from_left):
    col = lax.broadcasted_iota(jnp.int32, (16, 256), 0)
    is_top, is_low = (ha == 1).astype(F32), (ha == 0).astype(F32)
    at_left, at_right = (0, 512) if from_left else (512, 0)
    for f in range(4):
        edge = row(f).astype(F32)
        lefts, rights = left(f).astype(F32), right(f).astype(F32)
        cl, cr = corner_left(f).astype(F32), corner_right(f).astype(F32)
        for r in range(14):
            if r in (0, 13):
                keep = is_top if r == 0 else is_low
                cells, lo, hi = edge * keep, cl * keep, cr * keep
            else:
                cells = block(f, r - 1).astype(F32)
                lo, hi = lefts[r - 1 : r], rights[r - 1 : r]
            wide[f, r, :, 256:512] = cells.astype(BF)
            shifted = jnp.where(col == 0, lo, pltpu.roll(cells, 1, 0))
            wide[f, r, :, at_left : at_left + 256] = shifted.astype(BF)
            shifted = jnp.where(col == 15, hi, pltpu.roll(cells, 15, 0))
            wide[f, r, :, at_right : at_right + 256] = shifted.astype(BF)


def weight_copies(weight, held, sem):
    return [
        pltpu.make_async_copy(weight.at[pl.ds(a * 9, 9)], held.at[pl.ds(a * 9, 9)], sem.at[a])
        for a in range(3)
    ]


def conv_sum(wide, held, copies, total):
    for a in (2, 1, 0):
        frames = a + 2
        copies[a].wait()
        for b in range(3):
            window = wide[2 - a : 4, 2 - b : 14 - b].reshape(frames * 192, 768)
            part = None
            for e in range(3):
                one = lax.dot_general(
                    window[:, e * 256 : (e + 1) * 256],
                    held[(a * 3 + b) * 3 + e],
                    NT,
                    preferred_element_type=F32,
                )
                part = one if part is None else part + one
            if a == 2 and b == 0:
                total[...] = part
            else:
                total[0 : frames * 192] += part


CONV_SCRATCH = [
    pltpu.VMEM((27, 256, 256), BF),
    pltpu.VMEM((768, 256), F32),
    pltpu.SemaphoreType.DMA((4,)),
]


def first_kernel(
    step, block, inputs, hidden, row, left, right, corner_left, corner_right, table, weight,
    act_out, wide_in, wide, hid_out, held, total, sem, film, side,
):
    start = step[0]
    whole = pl.multiple_of(start // 8 * 8, 8)
    film_copy = pltpu.make_async_copy(table.at[pl.ds(whole, 8)], film, sem.at[3])
    film_copy.start()
    copies = weight_copies(weight, held, sem)
    for a in (2, 1, 0):
        copies[a].start()
    ha, core = lax.axis_index("ha"), lax.axis_index("core")

    lane = lax.broadcasted_iota(jnp.int32, (256, 256), 1)
    goal = (lane >> 5) & 3
    source = ((goal & 1) << 7) + ((goal >> 1) << 6) + ((core ^ (lane >> 7)) << 5) + (lane & 31)
    order = (lax.broadcasted_iota(jnp.int32, (256, 256), 0) == source).astype(BF)

    def sort(value):
        return jnp.dot(value, order, preferred_element_type=F32)

    build_shifted(
        wide,
        lambda f, r: block[f, r],
        lambda f: row[0, f],
        lambda f: left[0, f],
        lambda f: right[0, f],
        lambda f: corner_left[0, f],
        lambda f: corner_right[0, f],
        ha,
        False,
    )
    film_copy.wait()
    line = film[pl.ds(start - whole, 1), :]
    scale, shift = 1.0 + line[:, 0:256], line[:, 256:512]
    shifted = hidden[...].reshape(768, 256).astype(F32) * scale + shift
    sigma = jax.nn.sigmoid(shifted)
    act_out[...] = sort((shifted * sigma).astype(BF)).astype(BF)
    total[...] = sort(inputs[...].reshape(768, 256))
    for n, ref in enumerate((row, left, right, corner_left, corner_right)):
        side[n] = sort(ref[1].reshape(64, 256)).reshape(4, 16, 256)
    build_shifted(
        wide_in,
        lambda f, r: total[(f * 12 + r) * 16 : (f * 12 + r) * 16 + 16],
        lambda f: side[0, f],
        lambda f: side[1, f],
        lambda f: side[2, f],
        lambda f: side[3, f],
        lambda f: side[4, f],
        ha,
        True,
    )
    conv_sum(wide, held, copies, total)
    shifted = hidden[...].reshape(768, 256).astype(F32) * scale + shift
    sigma = jax.nn.sigmoid(shifted)
    grad = total[...] * scale * sigma * (1.0 + shifted * (1.0 - sigma))
    hid_out[...] = grad.astype(BF).reshape(4, 12, 16, 256)


def input_conv_kernel(
    hid, block, row, left, right, corner_left, corner_right, weight,
    out, held, total, sem, wide,
):
    copies = weight_copies(weight, held, sem)
    for a in (2, 1, 0):
        copies[a].start()
    build_shifted(
        wide,
        lambda f, r: hid[f, r],
        lambda f: row[0, f],
        lambda f: left[0, f],
        lambda f: right[0, f],
        lambda f: corner_left[0, f],
        lambda f: corner_right[0, f],
        lax.axis_index("ha"),
        False,
    )
    conv_sum(wide, held, copies, total)
    grad = block[...].reshape(768, 256).astype(F32) + total[...]
    out[...] = grad.astype(BF).reshape(4, 12, 16, 256)


def second_grad_kernel(wide, act, own, pair):
    for a in range(3):
        rows = (a + 2) * 192
        for b in range(3):
            window = wide[2 - a : 4, 2 - b : 14 - b].reshape(rows, 768)
            grad = lax.dot_general(act[0:rows], window, TN, preferred_element_type=F32)
            own[a * 3 + b] = grad[0:128]
            pair[a * 3 + b] = grad[128:256]


def second_pair_kernel(own, pair, out, keep):
    x = lax.axis_index("xh") * 2 + lax.axis_index("ha")
    mine = pl.ds(pl.multiple_of(x * 32, 32), 32)
    for ab in range(9):
        for q in range(4):
            rows = slice(q * 32, q * 32 + 32)
            out[q, ab] = (own[ab, rows] + pair[ab, rows]).astype(BF)
        keep[ab] = own[ab, mine] + pair[ab, mine]


def second_x_kernel(got, own, out, keep, held):
    x = lax.axis_index("xh") * 2 + lax.axis_index("ha")
    y = lax.axis_index("y")

    def tap(t):
        ab, lanes = t // 3, slice(t % 3 * 256, t % 3 * 256 + 256)
        total = own[ab, :, lanes]
        for d in range(1, 4):
            total = total + got[(x + d) & 3, ab, :, lanes].astype(F32)
        return total

    for g in range(7):
        parts = [tap(t) if t < 27 else jnp.zeros((32, 256), F32) for t in range(4 * g, 4 * g + 4)]
        held[...] = jnp.concatenate(parts, axis=0).T.reshape(8, 4, 8, 128)
        for q in range(4):
            out[q, g] = held[:, q].reshape(64, 128).astype(BF)
        keep[g] = held[:, y].reshape(64, 128)


def first_grad_kernel(hid, wide, own, pair):
    for a in range(3):
        rows = (a + 2) * 192
        left = hid[2 - a : 4].reshape(rows, 256)
        for b in range(3):
            window = wide[0 : a + 2, b : b + 12].reshape(rows, 768)
            grad = lax.dot_general(left, window, TN, preferred_element_type=F32)
            grad = grad.reshape(8, 4, 8, 768)
            for q in range(4):
                piece = grad[:, q].reshape(64, 768)
                for e in range(3):
                    t = (a * 3 + b) * 3 + e
                    own[q, t] = piece[:, e * 256 : e * 256 + 128]
                    pair[q, t] = piece[:, e * 256 + 128 : e * 256 + 256]


def first_pair_kernel(own, pair, out, keep):
    y = lax.axis_index("y")
    for q in range(4):
        out[q] = (own[q] + pair[q]).astype(BF)
    keep[...] = own[y] + pair[y]


def first_y_kernel(got, own, out, keep, held):
    y = lax.axis_index("y")
    x = lax.axis_index("xh") * 2 + lax.axis_index("ha")

    def tap(t):
        total = own[t]
        for d in range(1, 4):
            total = total + got[(y + d) & 3, t].astype(F32)
        return total

    for g in range(7):
        taps = [tap(t) if t < 27 else jnp.zeros((64, 128), F32) for t in range(4 * g, 4 * g + 4)]
        for q in range(4):
            piece = jnp.concatenate([v[:, q * 32 : q * 32 + 32] for v in taps], axis=1)
            held[q] = piece
            out[q, g] = piece.astype(BF)
        keep[g] = held[x]


def last_kernel(got_two, own_two, got_one, own_one, out, keep, held):
    x = lax.axis_index("xh") * 2 + lax.axis_index("ha")
    y, z = lax.axis_index("y"), lax.axis_index("z")
    for n, (own, got, me) in enumerate(((own_two, got_two, y), (own_one, got_one, x))):
        total = own[...]
        for d in range(1, 4):
            total = total + got[(me + d) & 3].astype(F32)
        held[n] = total.reshape(7, 8, 8, 128)

    def plane(z):
        return jnp.concatenate([held[n, :, z].reshape(56, 128) for n in range(2)], axis=0)

    for q in range(8):
        out[q] = plane(q).astype(BF)
    keep[...] = plane(z)


def final_kernel(factor, got, own, one, two):
    z = lax.axis_index("z")
    total = own[...]
    for d in range(1, 8):
        total = total + got[(z + d) & 7].astype(F32)
    total = (total * factor).reshape(2, 7, 8, 128)
    for out, which in ((two, 0), (one, 1)):
        for t in range(27):
            out[t] = total[which, t // 4, :, t % 4 * 32 : t % 4 * 32 + 32]


def shards(activations, saved_hidden, cotangent, conv_one, conv_two, film_table, timesteps):
    inputs, hidden, block = activations[0], saved_hidden[0], cotangent[0]
    taps_one = conv_one.transpose(1, 2, 3, 0, 4).reshape(27, 256, 256)
    taps_two = conv_two.transpose(1, 2, 3, 0, 4).reshape(27, 256, 256)
    to_x = lambda v: lax.all_to_all(v, ("xh", "ha"), 0, 0, tiled=True)
    to_y = lambda v: lax.all_to_all(v, "y", 0, 0, tiled=True)
    wide = pltpu.VMEM((4, 14, 16, 768), BF)
    quads = [pltpu.VMEM((4, 7, 64, 128), BF), pltpu.VMEM((7, 64, 128), F32)]

    sides = halo("pack_first", [block, inputs], "c")
    act, wide_in, wide_cot, grad_hidden = call(
        first_kernel,
        "conv_two_back",
        (timesteps, block, inputs, hidden, *sides, film_table, taps_two),
        "sccc" + "v" * 5 + "hh",
        [pltpu.VMEM((768, 256), BF), wide, wide, pltpu.VMEM((4, 12, 16, 256), BF)],
        [*CONV_SCRATCH, pltpu.VMEM((8, 512), F32), pltpu.VMEM((5, 4, 16, 256), F32)],
    )

    tall = pltpu.VMEM((9, 128, 768), F32)
    own, pair = call(second_grad_kernel, "grad_two", (wide_cot, act), "vv", [tall, tall])
    pair = send(pair, core_pairs())
    out, own_two = call(
        second_pair_kernel,
        "grad_two_pair",
        (own, pair),
        "vv",
        [pltpu.VMEM((4, 9, 32, 768), BF), pltpu.VMEM((9, 32, 768), F32)],
    )
    got_two = to_x(out)

    split = pltpu.VMEM((4, 27, 64, 128), F32)
    own, pair = call(first_grad_kernel, "grad_one", (grad_hidden, wide_in), "vv", [split, split])
    pair = send(pair, core_pairs())
    out, own_one = call(
        first_pair_kernel,
        "grad_one_pair",
        (own, pair),
        "vv",
        [pltpu.VMEM((4, 27, 64, 128), BF), pltpu.VMEM((27, 64, 128), F32)],
    )
    got_one = to_y(out)

    sides = halo("pack_second", [grad_hidden], "v")
    (grad_input,) = call(
        input_conv_kernel,
        "conv_one_back",
        (grad_hidden, block, *sides, taps_one),
        "vc" + "v" * 5 + "h",
        [jax.ShapeDtypeStruct((4, 12, 16, 256), BF)],
        [*CONV_SCRATCH, pltpu.VMEM((4, 14, 16, 768), BF)],
    )

    out, own_two = call(
        second_x_kernel, "grad_two_x", (got_two, own_two), "vv", quads,
        [pltpu.VMEM((8, 4, 8, 128), F32)],
    )
    got_two = to_y(out)
    out, own_one = call(
        first_y_kernel, "grad_one_y", (got_one, own_one), "vv", quads,
        [pltpu.VMEM((4, 64, 128), F32)],
    )
    got_one = to_x(out)

    out, own = call(
        last_kernel,
        "last_stage",
        (got_two, own_two, got_one, own_one),
        "vvvv",
        [pltpu.VMEM((8, 112, 128), BF), pltpu.VMEM((112, 128), F32)],
        [pltpu.VMEM((2, 7, 8, 8, 128), F32)],
    )
    planes = lax.all_to_all(out, "z", 0, 0, tiled=True)
    factor = float(256 * 768) ** (-0.5)
    result = jax.ShapeDtypeStruct((27, 8, 32), F32)
    grad_one, grad_two = call(
        functools.partial(final_kernel, factor),
        "final_sum",
        (planes, own),
        "vv",
        [result, result],
    )
    shape = lambda g: g.transpose(2, 0, 1).reshape(32, 3, 3, 3, 8)
    return grad_input[None], shape(grad_one), shape(grad_two)


def solution(mesh):
    fine = Mesh(mesh.devices.reshape(SIZES), AX)
    clip = ("z", "y")
    placed = P(clip, None, "ha", ("xh", "core"), None)
    weight = P(("ha", "xh", "core"), None, None, None, clip)
    return jax.shard_map(
        shards,
        mesh=fine,
        in_specs=(placed, placed, placed, P(), P(), P(), P(clip)),
        out_specs=(placed, weight, weight),
        check_vma=False,
    )
```

time: 623 us -> 161 us (0.26)
  the two profiles are of different devices: /device:TPU:24 before, /device:TPU:1 now
where the time goes in v2:
time: 161 us; the launch traced here: 159 us
  starting transfers between devices  52.2 us (32%)
  waiting for transfers between devices  47.3 us (29%)
  Pallas kernels  26.7 us (17%)
  local copies, waits for them, and re-layouts  22.8 us (14%)
  blocking collectives  8.95 us (6%)
    ppermute x12, starting transfers between devices, send(): return lax.ppermute(value, AX, pairs)  32.6 us
    pallas_call x12, Pallas kernels, call(): pl.pallas_call(kernel, out_shape=tuple(outs), in_specs=[specs[s] for s in...  26.7 us
    unnamed x44, local copies, waits for them, and re-layouts  22.8 us
    all_to_all x2, waiting for transfers between devices, shards(): to_x = lambda v: lax.all_to_all(v, ('xh', 'ha'), 0, 0, tiled=True)  22.5 us
    all_to_all x1, waiting for transfers between devices, shards(): to_y = lambda v: lax.all_to_all(v, 'y', 0, 0, tiled=True)  16.1 us
    all_to_all x1, blocking collectives, shards(): to_y = lambda v: lax.all_to_all(v, 'y', 0, 0, tiled=True)  8.95 us
    ppermute x12, waiting for transfers between devices, send(): return lax.ppermute(value, AX, pairs)  8.68 us
    all_to_all x1, starting transfers between devices, shards(): planes = lax.all_to_all(out, 'z', 0, 0, tiled=True)  8.19 us
  transfers between devices with their start and end apart: 16, of which 5 were waited for; matrix products, arithmetic and copies ran while one was open for 0% of the time, Pallas kernels for 10%

profile of v2, /device:TPU:1, one launch (start us, length us, event | category | flops | bytes accessed | tf_op | source)
XLA Modules:
  0.0 159.5 jit_solution(6909572147514679337)
XLA Ops:
  2.8 2.1 %collective-permute-start = (bf16[2,4,16,256]{3,2,1,0:T(8,128)(2,1)S(1)}, bf16[2,4,16,256]{3,2,1,0:T(8,128)(2,1)S(1)}, u32[]{:S(2)}, u32[]{:S(2)}) collective-permute-start(bf16[2,4,16,256]{3,2,1,0:T(8,128)(2,1)S(1)} %get-tuple-element.33), channel_id=1, source_target_pairs={{0,4},{1,5},{2,6},{3,7},{4,0},{5,1},{6,2},{7,3},{8,12},{9,13},{10,... | collective-permute-start | bytes 196616 | tf_op jit(solution)/shard_map/ppermute | solution.py:36
  4.9 5.2 %collective-permute-start.1 = (bf16[2,4,16,256]{3,2,1,0:T(8,128)(2,1)S(1)}, bf16[2,4,16,256]{3,2,1,0:T(8,128)(2,1)S(1)}, u32[]{:S(2)}, u32[]{:S(2)}) collective-permute-start(bf16[2,4,16,256]{3,2,1,0:T(8,128)(2,1)S(1)} %get-tuple-element.34), channel_id=1, source_target_pairs={{0,1},{1,2},{2,3},{4,5},{5,6},{6,7},{8,9},{9,10},{10,11},{12,13},{... | collective-permute-start | bytes 196616 | tf_op jit(solution)/shard_map/ppermute | solution.py:36
  10.1 1.9 %collective-permute-start.2 = (bf16[2,4,16,256]{3,2,1,0:T(8,128)(2,1)S(1)}, bf16[2,4,16,256]{3,2,1,0:T(8,128)(2,1)S(1)}, u32[]{:S(2)}, u32[]{:S(2)}) collective-permute-start(bf16[2,4,16,256]{3,2,1,0:T(8,128)(2,1)S(1)} %get-tuple-element.35), channel_id=1, source_target_pairs={{1,0},{2,1},{3,2},{5,4},{6,5},{7,6},{9,8},{10,9},{11,10},{13,12},{... | collective-permute-start | bytes 196616 | tf_op jit(solution)/shard_map/ppermute | solution.py:36
  12.1 4.5 %collective-permute-start.3 = (bf16[2,4,16,256]{3,2,1,0:T(8,128)(2,1)S(1)}, bf16[2,4,16,256]{3,2,1,0:T(8,128)(2,1)S(1)}, u32[]{:S(2)}, u32[]{:S(2)}) collective-permute-start(bf16[2,4,16,256]{3,2,1,0:T(8,128)(2,1)S(1)} %get-tuple-element.36), channel_id=1, source_target_pairs={{0,5},{1,6},{2,7},{4,1},{5,2},{6,3},{8,13},{9,14},{10,15},{12,9},{... | collective-permute-start | bytes 196616 | tf_op jit(solution)/shard_map/ppermute | solution.py:36
  19.2 4.2 %collective-permute-done.4.corner_right = bf16[2,4,16,256]{3,2,1,0:T(8,128)(2,1)S(1)} collective-permute-done((bf16[2,4,16,256]{3,2,1,0:T(8,128)(2,1)S(1)}, bf16[2,4,16,256]{3,2,1,0:T(8,128)(2,1)S(1)}, u32[]{:S(2)}, u32[]{:S(2)}) %collective-permute-start.4) | collective-permute-done | bytes 65568 | tf_op jit(solution)/shard_map/ppermute | solution.py:36
  23.4 2.0 %copy-done.2 = bf16[256,3,3,3,256]{4,0,3,2,1:T(8,128)(2,1)S(1)} copy-done((bf16[256,3,3,3,256]{4,0,3,2,1:T(8,128)(2,1)S(1)}, bf16[256,3,3,3,256]{4,0,3,2,1:T(8,128)(2,1)}, u32[]{:S(2)}) %copy-start.2) | copy-done | bytes 3538968
  29.0 6.5 %conv_two_back.1 = (bf16[768,256]{1,0:T(8,128)(2,1)S(1)}, bf16[4,14,16,768]{3,2,1,0:T(8,128)(2,1)S(1)}, bf16[4,14,16,768]{3,2,1,0:T(8,128)(2,1)S(1)}, bf16[4,12,16,256]{3,2,1,0:T(8,128)(2,1)S(1)}) custom-call(s32[1]{0:T(128)S(6)} %copy.10.step, bf16[4,12,16,256]{3,2,1,0:T(8,128)(2,1)S(1)} %bitcast.17, bf16[4,12,16,256]{3,2,1,0:T(8,128)(2,1)S(1)} %bitcast.22, ...), custom_call_target="tpu_custom_call" | custom-call | tf_op jit(solution)/shard_map/conv_two_back/pallas_call | solution.py:45
  35.5 2.6 %grad_one.1 = (f32[4,27,64,128]{3,2,1,0:T(8,128)S(1)}, f32[4,27,64,128]{3,2,1,0:T(8,128)S(1)}) custom-call(bf16[4,12,16,256]{3,2,1,0:T(8,128)(2,1)S(1)} %get-tuple-element.38.refs_0_.hid, bf16[4,14,16,768]{3,2,1,0:T(8,128)(2,1)S(1)} %get-tuple-element.52.wide), custom_call_target="tpu_custom_call" | custom-call | tf_op jit(solution)/shard_map/grad_one/pallas_call | solution.py:45
  38.2 4.4 %grad_two.1 = (f32[9,128,768]{2,1,0:T(8,128)S(1)}, f32[9,128,768]{2,1,0:T(8,128)}) custom-call(bf16[4,14,16,768]{3,2,1,0:T(8,128)(2,1)S(1)} %get-tuple-element.44.wide, bf16[768,256]{1,0:T(8,128)(2,1)S(1)} %get-tuple-element.45.act), custom_call_target="tpu_custom_call" | custom-call | tf_op jit(solution)/shard_map/grad_two/pallas_call | solution.py:45
  47.5 4.2 %all-to-all-start.2 = ((bf16[4,27,64,128]{3,2,1,0:T(8,128)(2,1)}), bf16[4,27,64,128]{3,2,1,0:T(8,128)(2,1)S(1)}, u32[]{:S(2)}, u32[]{:S(2)}) async-start(bf16[4,27,64,128]{3,2,1,0:T(8,128)(2,1)} %get-tuple-element.55), calls=%async_computation.2 | async-start | bytes 3538944 | tf_op jit(solution)/shard_map/all_to_all | solution.py:349
  51.7 2.0 %copy-done.7 = f32[9,128,768]{2,1,0:T(8,128)S(1)} copy-done((f32[9,128,768]{2,1,0:T(8,128)S(1)}, f32[9,128,768]{2,1,0:T(8,128)}, u32[]{:S(2)}) %copy-start.7) | copy-done | bytes 3538968
  53.7 2.4 %grad_two_pair.1 = (bf16[4,9,32,768]{3,2,1,0:T(8,128)(2,1)S(1)}, f32[9,32,768]{2,1,0:T(8,128)S(1)}) custom-call(f32[9,128,768]{2,1,0:T(8,128)S(1)} %copy-done.7, f32[9,128,768]{2,1,0:T(8,128)} %collective-permute-done.10.pair), custom_call_target="tpu_custom_call" | custom-call | tf_op jit(solution)/shard_map/grad_two_pair/pallas_call | solution.py:45
  58.3 16.1 %all-to-all-done.2.got = bf16[4,27,64,128]{3,2,1,0:T(8,128)(2,1)S(1)} async-done(((bf16[4,27,64,128]{3,2,1,0:T(8,128)(2,1)}), bf16[4,27,64,128]{3,2,1,0:T(8,128)(2,1)S(1)}, u32[]{:S(2)}, u32[]{:S(2)}) %all-to-all-start.2) | async-done | bytes 1769504 | tf_op jit(solution)/shard_map/all_to_all | solution.py:349
  74.3 3.6 %all-to-all-start = ((bf16[4,9,32,768]{3,2,1,0:T(8,128)(2,1)}), bf16[4,9,32,768]{3,2,1,0:T(8,128)(2,1)S(1)}, u32[]{:S(2)}, u32[]{:S(2)}) async-start(bf16[4,9,32,768]{3,2,1,0:T(8,128)(2,1)} %copy-done.9), calls=%async_computation | async-start | bytes 3538944 | tf_op jit(solution)/shard_map/all_to_all | solution.py:348
  81.3 18.3 %all-to-all-done.got = bf16[4,9,32,768]{3,2,1,0:T(8,128)(2,1)S(1)} async-done(((bf16[4,9,32,768]{3,2,1,0:T(8,128)(2,1)}), bf16[4,9,32,768]{3,2,1,0:T(8,128)(2,1)S(1)}, u32[]{:S(2)}, u32[]{:S(2)}) %all-to-all-start) | async-done | bytes 1769504 | tf_op jit(solution)/shard_map/all_to_all | solution.py:348
  99.6 3.6 %all-to-all-start.3 = ((bf16[4,7,64,128]{3,2,1,0:T(8,128)(2,1)}), bf16[4,7,64,128]{3,2,1,0:T(8,128)(2,1)S(1)}, u32[]{:S(2)}, u32[]{:S(2)}) async-start(bf16[4,7,64,128]{3,2,1,0:T(8,128)(2,1)} %copy-done.16), calls=%async_computation.3 | async-start | bytes 917504 | tf_op jit(solution)/shard_map/all_to_all | solution.py:348
  105.4 4.2 %all-to-all-done.3.got_one = bf16[4,7,64,128]{3,2,1,0:T(8,128)(2,1)S(1)} async-done(((bf16[4,7,64,128]{3,2,1,0:T(8,128)(2,1)}), bf16[4,7,64,128]{3,2,1,0:T(8,128)(2,1)S(1)}, u32[]{:S(2)}, u32[]{:S(2)}) %all-to-all-start.3) | async-done | bytes 458784 | tf_op jit(solution)/shard_map/all_to_all | solution.py:348
  109.7 8.9 %all_to_all.25.got_two = bf16[4,7,64,128]{3,2,1,0:T(8,128)(2,1)S(1)} all-to-all(bf16[4,7,64,128]{3,2,1,0:T(8,128)(2,1)S(1)} %get-tuple-element.50), channel_id=1, replica_groups=mesh['z'=8,'y'=4,'ha'=2,'xh'=2,'core'=2] {'y'}, dimensions={0} | all-to-all | bytes 917504 | tf_op jit(solution)/shard_map/all_to_all | solution.py:349
  121.3 8.2 %all-to-all-start.4 = ((bf16[8,112,128]{2,1,0:T(8,128)(2,1)}), bf16[8,112,128]{2,1,0:T(8,128)(2,1)S(1)}, u32[]{:S(2)}, u32[]{:S(2)}) async-start(bf16[8,112,128]{2,1,0:T(8,128)(2,1)} %get-tuple-element.59), calls=%async_computation.4 | async-start | bytes 458752 | tf_op jit(solution)/shard_map/all_to_all | solution.py:416
  130.0 8.4 %collective-permute-start.6 = (bf16[1,4,16,256]{3,2,1,0:T(8,128)(2,1)S(1)}, bf16[1,4,16,256]{3,2,1,0:T(8,128)(2,1)S(1)}, u32[]{:S(2)}, u32[]{:S(2)}) collective-permute-start(bf16[1,4,16,256]{3,2,1,0:T(8,128)(2,1)S(1)} %get-tuple-element.40), channel_id=1, source_target_pairs={{0,1},{1,2},{2,3},{4,5},{5,6},{6,7},{8,9},{9,10},{10,11},{12,13},{... | collective-permute-start | bytes 98312 | tf_op jit(solution)/shard_map/ppermute | solution.py:36
  140.4 3.7 %collective-permute-start.8 = (bf16[1,4,16,256]{3,2,1,0:T(8,128)(2,1)S(1)}, bf16[1,4,16,256]{3,2,1,0:T(8,128)(2,1)S(1)}, u32[]{:S(2)}, u32[]{:S(2)}) collective-permute-start(bf16[1,4,16,256]{3,2,1,0:T(8,128)(2,1)S(1)} %get-tuple-element.42), channel_id=1, source_target_pairs={{0,5},{1,6},{2,7},{4,1},{5,2},{6,3},{8,13},{9,14},{10,15},{12,9},{... | collective-permute-start | bytes 98312 | tf_op jit(solution)/shard_map/ppermute | solution.py:36
  146.1 4.5 %collective-permute-done.9.corner_right = bf16[1,4,16,256]{3,2,1,0:T(8,128)(2,1)S(1)} collective-permute-done((bf16[1,4,16,256]{3,2,1,0:T(8,128)(2,1)S(1)}, bf16[1,4,16,256]{3,2,1,0:T(8,128)(2,1)S(1)}, u32[]{:S(2)}, u32[]{:S(2)}) %collective-permute-start.9) | collective-permute-done | bytes 32800 | tf_op jit(solution)/shard_map/ppermute | solution.py:36
  150.5 2.0 %copy-done.5 = bf16[256,3,3,3,256]{4,0,3,2,1:T(8,128)(2,1)S(1)} copy-done((bf16[256,3,3,3,256]{4,0,3,2,1:T(8,128)(2,1)S(1)}, bf16[256,3,3,3,256]{4,0,3,2,1:T(8,128)(2,1)}, u32[]{:S(2)}) %copy-start.5) | copy-done | bytes 3538968
  152.5 6.1 %conv_one_back.1 = bf16[4,12,16,256]{3,2,1,0:T(8,128)(2,1)} custom-call(bf16[4,12,16,256]{3,2,1,0:T(8,128)(2,1)S(1)} %copy-done.4, bf16[4,12,16,256]{3,2,1,0:T(8,128)(2,1)S(1)} %bitcast.18, bf16[1,4,16,256]{3,2,1,0:T(8,128)(2,1)S(1)} %collective-permute-done.5.row, bf16[1,4,16,256]{3,2,1,0:T(8,128)(2,1)S(1)} %collective-permute-done.6.left, ...), custom_call_target="tpu_custom_call" | custom-call | tf_op jit(solution)/shard_map/conv_one_back/pallas_call | solution.py:45
  (65 shorter events, 28.2 us)
Async XLA Ops:
  2.8 16.3 %collective-permute-start = (bf16[2,4,16,256]{3,2,1,0:T(8,128)(2,1)S(1)}, bf16[2,4,16,256]{3,2,1,0:T(8,128)(2,1)S(1)}, u32[]{:S(2)}, u32[]{:S(2)}) collective-permute-start(bf16[2,4,16,256]{3,2,1,0:T(8,128)(2,1)S(1)} %get-tuple-element.33), channel_id=1, source_target_pairs={{0,4},{1,5},{2,6},{3,7},{4,0},{5,1},{6,2},{7,3},{8,12},{9,13},{10,... | collective-permute-start | bytes 196616 | tf_op jit(solution)/shard_map/ppermute | solution.py:36
  4.9 14.2 %collective-permute-start.1 = (bf16[2,4,16,256]{3,2,1,0:T(8,128)(2,1)S(1)}, bf16[2,4,16,256]{3,2,1,0:T(8,128)(2,1)S(1)}, u32[]{:S(2)}, u32[]{:S(2)}) collective-permute-start(bf16[2,4,16,256]{3,2,1,0:T(8,128)(2,1)S(1)} %get-tuple-element.34), channel_id=1, source_target_pairs={{0,1},{1,2},{2,3},{4,5},{5,6},{6,7},{8,9},{9,10},{10,11},{12,13},{... | collective-permute-start | bytes 196616 | tf_op jit(solution)/shard_map/ppermute | solution.py:36
  10.1 9.1 %collective-permute-start.2 = (bf16[2,4,16,256]{3,2,1,0:T(8,128)(2,1)S(1)}, bf16[2,4,16,256]{3,2,1,0:T(8,128)(2,1)S(1)}, u32[]{:S(2)}, u32[]{:S(2)}) collective-permute-start(bf16[2,4,16,256]{3,2,1,0:T(8,128)(2,1)S(1)} %get-tuple-element.35), channel_id=1, source_target_pairs={{1,0},{2,1},{3,2},{5,4},{6,5},{7,6},{9,8},{10,9},{11,10},{13,12},{... | collective-permute-start | bytes 196616 | tf_op jit(solution)/shard_map/ppermute | solution.py:36
  12.1 7.1 %collective-permute-start.3 = (bf16[2,4,16,256]{3,2,1,0:T(8,128)(2,1)S(1)}, bf16[2,4,16,256]{3,2,1,0:T(8,128)(2,1)S(1)}, u32[]{:S(2)}, u32[]{:S(2)}) collective-permute-start(bf16[2,4,16,256]{3,2,1,0:T(8,128)(2,1)S(1)} %get-tuple-element.36), channel_id=1, source_target_pairs={{0,5},{1,6},{2,7},{4,1},{5,2},{6,3},{8,13},{9,14},{10,15},{12,9},{... | collective-permute-start | bytes 196616 | tf_op jit(solution)/shard_map/ppermute | solution.py:36
  16.6 6.8 %collective-permute-start.4 = (bf16[2,4,16,256]{3,2,1,0:T(8,128)(2,1)S(1)}, bf16[2,4,16,256]{3,2,1,0:T(8,128)(2,1)S(1)}, u32[]{:S(2)}, u32[]{:S(2)}) collective-permute-start(bf16[2,4,16,256]{3,2,1,0:T(8,128)(2,1)S(1)} %get-tuple-element.37), channel_id=1, source_target_pairs={{1,4},{2,5},{3,6},{5,0},{6,1},{7,2},{9,12},{10,13},{11,14},{13,8},... | collective-permute-start | bytes 196616 | tf_op jit(solution)/shard_map/ppermute | solution.py:36
  23.4 2.0 %copy-start.2 = (bf16[256,3,3,3,256]{4,0,3,2,1:T(8,128)(2,1)S(1)}, bf16[256,3,3,3,256]{4,0,3,2,1:T(8,128)(2,1)}, u32[]{:S(2)}) copy-start(bf16[256,3,3,3,256]{4,0,3,2,1:T(8,128)(2,1)} %param.11) | copy-start | bytes 10616836
  25.4 1.6 copy-start.8
  35.5 11.1 %copy-start.3 = (bf16[4,12,16,256]{3,2,1,0:T(8,128)(2,1)}, bf16[4,12,16,256]{3,2,1,0:T(8,128)(2,1)S(1)}, u32[]{:S(2)}) copy-start(bf16[4,12,16,256]{3,2,1,0:T(8,128)(2,1)S(1)} %get-tuple-element.38.refs_0_.hid) | copy-start | bytes 1179652
  38.1 6.8 %collective-permute-start.11 = (f32[4,27,64,128]{3,2,1,0:T(8,128)S(1)}, f32[4,27,64,128]{3,2,1,0:T(8,128)S(1)}, u32[]{:S(2)}, u32[]{:S(2)}) collective-permute-start(f32[4,27,64,128]{3,2,1,0:T(8,128)S(1)} %get-tuple-element.54), channel_id=1, source_target_pairs={{0,1},{1,0},{2,3},{3,2},{4,5},{5,4},{6,7},{7,6},{8,9},{9,8},{10,11... | collective-permute-start | bytes 10616840 | tf_op jit(solution)/shard_map/ppermute | solution.py:36
  42.6 1.8 %copy-start.6 = (f32[9,128,768]{2,1,0:T(8,128)}, f32[9,128,768]{2,1,0:T(8,128)S(1)}, u32[]{:S(2)}) copy-start(f32[9,128,768]{2,1,0:T(8,128)S(1)} %get-tuple-element.46.own) | copy-start | bytes 10616836
  44.4 7.3 %collective-permute-start.10 = (f32[9,128,768]{2,1,0:T(8,128)}, f32[9,128,768]{2,1,0:T(8,128)}, u32[]{:S(2)}, u32[]{:S(2)}) collective-permute-start(f32[9,128,768]{2,1,0:T(8,128)} %get-tuple-element.47), channel_id=1, source_target_pairs={{0,1},{1,0},{2,3},{3,2},{4,5},{5,4},{6,7},{7,6},{8,9},{9,8},{10,11... | collective-permute-start | bytes 10616840 | tf_op jit(solution)/shard_map/ppermute | solution.py:36
  47.5 26.8 %all-to-all-start.2 = ((bf16[4,27,64,128]{3,2,1,0:T(8,128)(2,1)}), bf16[4,27,64,128]{3,2,1,0:T(8,128)(2,1)S(1)}, u32[]{:S(2)}, u32[]{:S(2)}) async-start(bf16[4,27,64,128]{3,2,1,0:T(8,128)(2,1)} %get-tuple-element.55), calls=%async_computation.2 | async-start | bytes 3538944 | tf_op jit(solution)/shard_map/all_to_all | solution.py:349
  51.7 2.0 %copy-start.7 = (f32[9,128,768]{2,1,0:T(8,128)S(1)}, f32[9,128,768]{2,1,0:T(8,128)}, u32[]{:S(2)}) copy-start(f32[9,128,768]{2,1,0:T(8,128)} %copy-done.6) | copy-start | bytes 10616836
  74.3 25.3 %all-to-all-start = ((bf16[4,9,32,768]{3,2,1,0:T(8,128)(2,1)}), bf16[4,9,32,768]{3,2,1,0:T(8,128)(2,1)S(1)}, u32[]{:S(2)}, u32[]{:S(2)}) async-start(bf16[4,9,32,768]{3,2,1,0:T(8,128)(2,1)} %copy-done.9), calls=%async_computation | async-start | bytes 3538944 | tf_op jit(solution)/shard_map/all_to_all | solution.py:348
  81.3 48.2 %copy-start.4 = (bf16[4,12,16,256]{3,2,1,0:T(8,128)(2,1)S(1)}, bf16[4,12,16,256]{3,2,1,0:T(8,128)(2,1)}, u32[]{:S(2)}) copy-start(bf16[4,12,16,256]{3,2,1,0:T(8,128)(2,1)} %copy-done.3) | copy-start | bytes 1179652
  81.3 69.2 %copy-start.1 = (bf16[1,4,12,16,256]{4,3,2,1,0:T(8,128)(2,1)S(1)}, bf16[1,4,12,16,256]{4,3,2,1,0:T(8,128)(2,1)}, u32[]{:S(2)}) copy-start(bf16[1,4,12,16,256]{4,3,2,1,0:T(8,128)(2,1)} %param.9) | copy-start | bytes 1179652
  99.6 10.0 %all-to-all-start.3 = ((bf16[4,7,64,128]{3,2,1,0:T(8,128)(2,1)}), bf16[4,7,64,128]{3,2,1,0:T(8,128)(2,1)S(1)}, u32[]{:S(2)}, u32[]{:S(2)}) async-start(bf16[4,7,64,128]{3,2,1,0:T(8,128)(2,1)} %copy-done.16), calls=%async_computation.3 | async-start | bytes 917504 | tf_op jit(solution)/shard_map/all_to_all | solution.py:348
  121.3 37.4 %all-to-all-start.4 = ((bf16[8,112,128]{2,1,0:T(8,128)(2,1)}), bf16[8,112,128]{2,1,0:T(8,128)(2,1)S(1)}, u32[]{:S(2)}, u32[]{:S(2)}) async-start(bf16[8,112,128]{2,1,0:T(8,128)(2,1)} %get-tuple-element.59), calls=%async_computation.4 | async-start | bytes 458752 | tf_op jit(solution)/shard_map/all_to_all | solution.py:416
  129.6 16.4 %collective-permute-start.5 = (bf16[1,4,16,256]{3,2,1,0:T(8,128)(2,1)S(1)}, bf16[1,4,16,256]{3,2,1,0:T(8,128)(2,1)S(1)}, u32[]{:S(2)}, u32[]{:S(2)}) collective-permute-start(bf16[1,4,16,256]{3,2,1,0:T(8,128)(2,1)S(1)} %get-tuple-element.39), channel_id=1, source_target_pairs={{0,4},{1,5},{2,6},{3,7},{4,0},{5,1},{6,2},{7,3},{8,12},{9,13},{10,... | collective-permute-start | bytes 98312 | tf_op jit(solution)/shard_map/ppermute | solution.py:36
  130.0 16.0 %collective-permute-start.6 = (bf16[1,4,16,256]{3,2,1,0:T(8,128)(2,1)S(1)}, bf16[1,4,16,256]{3,2,1,0:T(8,128)(2,1)S(1)}, u32[]{:S(2)}, u32[]{:S(2)}) collective-permute-start(bf16[1,4,16,256]{3,2,1,0:T(8,128)(2,1)S(1)} %get-tuple-element.40), channel_id=1, source_target_pairs={{0,1},{1,2},{2,3},{4,5},{5,6},{6,7},{8,9},{9,10},{10,11},{12,13},{... | collective-permute-start | bytes 98312 | tf_op jit(solution)/shard_map/ppermute | solution.py:36
  138.4 7.6 %collective-permute-start.7 = (bf16[1,4,16,256]{3,2,1,0:T(8,128)(2,1)S(1)}, bf16[1,4,16,256]{3,2,1,0:T(8,128)(2,1)S(1)}, u32[]{:S(2)}, u32[]{:S(2)}) collective-permute-start(bf16[1,4,16,256]{3,2,1,0:T(8,128)(2,1)S(1)} %get-tuple-element.41), channel_id=1, source_target_pairs={{1,0},{2,1},{3,2},{5,4},{6,5},{7,6},{9,8},{10,9},{11,10},{13,12},{... | collective-permute-start | bytes 98312 | tf_op jit(solution)/shard_map/ppermute | solution.py:36
  140.4 5.7 %collective-permute-start.8 = (bf16[1,4,16,256]{3,2,1,0:T(8,128)(2,1)S(1)}, bf16[1,4,16,256]{3,2,1,0:T(8,128)(2,1)S(1)}, u32[]{:S(2)}, u32[]{:S(2)}) collective-permute-start(bf16[1,4,16,256]{3,2,1,0:T(8,128)(2,1)S(1)} %get-tuple-element.42), channel_id=1, source_target_pairs={{0,5},{1,6},{2,7},{4,1},{5,2},{6,3},{8,13},{9,14},{10,15},{12,9},{... | collective-permute-start | bytes 98312 | tf_op jit(solution)/shard_map/ppermute | solution.py:36
  144.1 6.4 %collective-permute-start.9 = (bf16[1,4,16,256]{3,2,1,0:T(8,128)(2,1)S(1)}, bf16[1,4,16,256]{3,2,1,0:T(8,128)(2,1)S(1)}, u32[]{:S(2)}, u32[]{:S(2)}) collective-permute-start(bf16[1,4,16,256]{3,2,1,0:T(8,128)(2,1)S(1)} %get-tuple-element.43), channel_id=1, source_target_pairs={{1,4},{2,5},{3,6},{5,0},{6,1},{7,2},{9,12},{10,13},{11,14},{13,8},... | collective-permute-start | bytes 98312 | tf_op jit(solution)/shard_map/ppermute | solution.py:36
  150.5 2.0 %copy-start.5 = (bf16[256,3,3,3,256]{4,0,3,2,1:T(8,128)(2,1)S(1)}, bf16[256,3,3,3,256]{4,0,3,2,1:T(8,128)(2,1)}, u32[]{:S(2)}) copy-start(bf16[256,3,3,3,256]{4,0,3,2,1:T(8,128)(2,1)} %param.10) | copy-start | bytes 10616836
  (14 other events, 13.5 us)

commit v3 on v2

v3 whole, which is shorter than its diff:
```python
import functools

import jax
import jax.numpy as jnp
from jax import lax
from jax.experimental import pallas as pl
from jax.experimental.pallas import tpu as pltpu
from jax.sharding import Mesh
from jax.sharding import PartitionSpec as P

BF = jnp.bfloat16
F32 = jnp.float32
AX = ("z", "y", "ha", "xh", "core")
SIZES = (8, 4, 2, 2, 2)
VM = pl.BlockSpec(memory_space=pltpu.VMEM)
HB = pl.BlockSpec(memory_space=pl.ANY)
SM = pl.BlockSpec(memory_space=pltpu.SMEM)
NT = (((1,), (1,)), ((), ()))
TN = (((0,), (0,)), ((), ()))


def core_pairs():
    return [(i, i ^ 1) for i in range(256)]


def block_pairs(dh, dw):
    return [(i, i // 8 * 8 + (i // 4 % 2 ^ dh) * 4 + (i + dw) % 4) for i in range(256)]


def ring_pairs(dx, dy):
    pairs = []
    for i in range(256):
        core, xh, ha, y, z = i % 2, i // 2 % 2, i // 4 % 2, i // 8 % 4, i // 32
        x = (xh * 2 + ha + dx) % 4
        pairs.append((i, ((z * 4 + (y + dy) % 4) * 2 + x % 2) * 4 + x // 2 * 2 + core))
    return pairs


def send(value, pairs):
    return lax.ppermute(value, AX, pairs)


def call(kernel, name, args, spaces, outs, scratch=(), limit=16):
    where = {"v": pltpu.VMEM, "p": pltpu.HBM, "h": pltpu.HBM}
    args = [
        pltpu.with_memory_space_constraint(a, where[s]) if s in where else a
        for a, s in zip(args, spaces)
    ]
    specs = {"v": VM, "p": VM, "h": HB, "s": SM}
    return pl.pallas_call(
        kernel,
        out_shape=tuple(o for o, _ in outs),
        in_specs=[specs[s] for s in spaces],
        out_specs=tuple(specs[s] for _, s in outs),
        scratch_shapes=list(scratch),
        compiler_params=pltpu.CompilerParams(vmem_limit_bytes=limit * 2**20),
        name=name,
    )(*args)


def near(shape, dtype):
    return pltpu.VMEM(shape, dtype), "v"


def far(shape, dtype):
    return pltpu.HBM(shape, dtype), "h"


def x_place():
    return lax.axis_index("xh") * 2 + lax.axis_index("ha")


def column(wide, lanes_half, f, j):
    cells = wide[lanes_half, pl.ds(f * 192 + j, 12, stride=16), :]
    return jnp.concatenate([cells, jnp.zeros((4, 128), F32)], axis=0).astype(BF)


def spread(wide, block):
    flat = block[...].reshape(768, 256).astype(F32)
    wide[0] = flat[:, 0:128]
    wide[1] = flat[:, 128:256]


def pack_kernel(one, two, row, hi, lo, corner_hi, corner_lo, wide):
    edge = 11 * (1 - lax.axis_index("ha"))
    for n, block in enumerate((one, two)):
        spread(wide, block)
        for f in range(4):
            row[n, f] = block[f, edge]
            for j, out, corner in ((15, hi, corner_hi), (0, lo, corner_lo)):
                for h in range(2):
                    lanes = slice(h * 128, h * 128 + 128)
                    out[n, f, :, lanes] = column(wide, h, f, j)
                    cell = wide[h, pl.ds(f * 192 + edge * 16 + j, 1), :]
                    corner[n, f, :, lanes] = jnp.broadcast_to(cell, (16, 128)).astype(BF)


def pack_columns_kernel(block, after, hi, lo, wide):
    del after
    spread(wide, block)
    for f in range(4):
        for j, out in ((15, hi), (0, lo)):
            for h in range(2):
                out[f, :, h * 128 : h * 128 + 128] = column(wide, h, f, j)


def pack_rows_kernel(block, left, right, row):
    edge = 11 * (1 - lax.axis_index("ha"))
    for f in range(4):
        row[0, f] = block[f, edge]
        for n, side in ((1, left), (2, right)):
            cells = side[f].astype(F32)
            cell = jnp.where(edge == 0, cells[0:1], cells[11:12])
            row[n, f] = jnp.broadcast_to(cell, (16, 256)).astype(BF)


def build_shifted(put, cell_row, row, left, right, corner_left, corner_right):
    ha, wa = lax.axis_index("ha"), lax.axis_index("xh") * 2 + lax.axis_index("core")
    col = lax.broadcasted_iota(jnp.int32, (16, 256), 0)
    is_top, is_low = (ha == 1).astype(F32), (ha == 0).astype(F32)
    has_left, has_right = (wa > 0).astype(F32), (wa < 3).astype(F32)
    for f in range(4):
        edge = row(f).astype(F32)
        lefts, rights = left(f).astype(F32) * has_left, right(f).astype(F32) * has_right
        cl = corner_left(f).astype(F32)[0:1] * has_left
        cr = corner_right(f).astype(F32)[0:1] * has_right
        for r in range(14):
            if r in (0, 13):
                keep = is_top if r == 0 else is_low
                cells, lo, hi = edge * keep, cl * keep, cr * keep
            else:
                cells = cell_row(f, r - 1).astype(F32)
                lo, hi = lefts[r - 1 : r], rights[r - 1 : r]
            put(f, r, 1, cells.astype(BF))
            put(f, r, 0, jnp.where(col == 0, lo, pltpu.roll(cells, 1, 0)).astype(BF))
            put(f, r, 2, jnp.where(col == 15, hi, pltpu.roll(cells, 15, 0)).astype(BF))


def put_back(wide):
    def put(f, r, which, cells):
        wide[f, r, :, (2 - which) * 256 : (3 - which) * 256] = cells

    return put


def weight_copies(weight, held, sem):
    return [
        pltpu.make_async_copy(weight.at[pl.ds(a * 9, 9)], held.at[pl.ds(a * 9, 9)], sem.at[a])
        for a in range(3)
    ]


def conv_sum(wide, held, copies, total):
    for a in (2, 1, 0):
        frames = a + 2
        copies[a].wait()
        for b in range(3):
            window = wide[2 - a : 4, 2 - b : 14 - b].reshape(frames * 192, 768)
            part = None
            for e in range(3):
                one = lax.dot_general(
                    window[:, e * 256 : (e + 1) * 256],
                    held[(a * 3 + b) * 3 + e],
                    NT,
                    preferred_element_type=F32,
                )
                part = one if part is None else part + one
            if a == 2 and b == 0:
                total[...] = part
            else:
                total[0 : frames * 192] += part


CONV_SCRATCH = [
    pltpu.VMEM((27, 256, 256), BF),
    pltpu.VMEM((768, 256), F32),
    pltpu.SemaphoreType.DMA((3,)),
]


def channel_order():
    lane = lax.broadcasted_iota(jnp.int32, (256, 256), 1)
    goal, kept = (lane >> 5) & 3, lax.axis_index("core") ^ (lane >> 7)
    source = ((goal & 1) << 7) + ((goal >> 1) << 6) + (kept << 5) + (lane & 31)
    return (lax.broadcasted_iota(jnp.int32, (256, 256), 0) == source).astype(BF)


def film_kernel(step, inputs, hidden, table, act_out, inp_out, slope, film, sem):
    start = step[0]
    whole = pl.multiple_of(start // 8 * 8, 8)
    film_copy = pltpu.make_async_copy(table.at[pl.ds(whole, 8)], film, sem)
    film_copy.start()
    order = channel_order()
    sort = lambda v: jnp.dot(v, order, preferred_element_type=F32).astype(BF)
    inp_out[...] = sort(inputs[...].reshape(768, 256)).reshape(4, 12, 16, 256)
    film_copy.wait()
    line = film[pl.ds(start - whole, 1), :]
    scale, shift = 1.0 + line[:, 0:256], line[:, 256:512]
    shifted = hidden[...].reshape(768, 256).astype(F32) * scale + shift
    sigma = jax.nn.sigmoid(shifted)
    act_out[...] = sort((shifted * sigma).astype(BF))
    slope[...] = scale * sigma * (1.0 + shifted * (1.0 - sigma))


def first_kernel(
    block, inp, slope, row, left, right, corner_left, corner_right, weight,
    wide_in, wide, hid_out, held, total, sem, side,
):
    copies = weight_copies(weight, held, sem)
    for a in (2, 1, 0):
        copies[a].start()
    sides = (row, left, right, corner_left, corner_right)
    build_shifted(
        put_back(wide), lambda f, r: block[f, r], *[lambda f, s=s: s[0, f] for s in sides]
    )
    order = channel_order()
    for n, ref in enumerate(sides):
        cells = jnp.dot(ref[1].reshape(64, 256), order, preferred_element_type=F32)
        side[n] = cells.reshape(4, 16, 256)

    def put(f, r, which, cells):
        at = which * 128
        wide_in[f, r, :, at : at + 128] = cells[:, 0:128]
        wide_in[f, r, :, at + 384 : at + 512] = cells[:, 128:256]

    build_shifted(put, lambda f, r: inp[f, r], *[lambda f, n=n: side[n, f] for n in range(5)])
    conv_sum(wide, held, copies, total)
    hid_out[...] = (total[...] * slope[...]).astype(BF).reshape(4, 12, 16, 256)


def input_conv_kernel(hid, block, row, left, right, weight, out, held, total, sem, wide):
    copies = weight_copies(weight, held, sem)
    for a in (2, 1, 0):
        copies[a].start()
    build_shifted(
        put_back(wide),
        lambda f, r: hid[f, r],
        lambda f: row[0, f],
        lambda f: left[f],
        lambda f: right[f],
        lambda f: row[1, f],
        lambda f: row[2, f],
    )
    conv_sum(wide, held, copies, total)
    grad = block[...].reshape(768, 256).astype(F32) + total[...]
    out[...] = grad.astype(BF).reshape(4, 12, 16, 256)


def second_part(wide, act, half, a, b):
    rows = (a + 2) * 192
    window = wide[2 - a : 4, 2 - b : 14 - b].reshape(rows, 768)
    left = act[0:rows, half * 128 : half * 128 + 128]
    return lax.dot_general(left, window, TN, preferred_element_type=F32)


def second_pair_kernel(wide, act, pair):
    for a in range(3):
        for b in range(3):
            pair[a * 3 + b] = second_part(wide, act, 1, a, b)


def second_own_kernel(wide, act, got, out, keep, held, sem):
    mine = pl.ds(pl.multiple_of(x_place() * 32, 32), 32)
    for a in range(3):
        for b in range(3):
            ab = a * 3 + b
            total = second_part(wide, act, 0, a, b) + got[ab]
            held[ab] = total
            for q in range(4):
                out[q, ab] = total[q * 32 : q * 32 + 32].astype(BF)
    kept = pltpu.make_async_copy(held.at[:, mine], keep, sem)
    kept.start()
    kept.wait()


def second_x_kernel(got, own, after, one, two, three, keep, held):
    del after
    x, y = x_place(), lax.axis_index("y")

    def tap(t):
        ab, lanes = t // 3, slice(t % 3 * 256, t % 3 * 256 + 256)
        total = own[ab, :, lanes]
        for d in range(1, 4):
            total = total + got[(x + d) & 3, ab, :, lanes].astype(F32)
        return total

    for g in range(7):
        parts = [tap(t) if t < 27 else jnp.zeros((32, 256), F32) for t in range(4 * g, 4 * g + 4)]
        held[...] = jnp.concatenate(parts, axis=0).T.reshape(8, 4, 8, 128)
        for d, out in enumerate((keep, one, two, three)):
            out[g] = held[:, (y + d) & 3].reshape(64, 128).astype(out.dtype)


def first_part(hid, wide, half, a, b):
    rows = (a + 2) * 192
    left = hid[2 - a : 4].reshape(rows, 256)
    window = wide[0 : a + 2, b : b + 12, :, half * 384 : half * 384 + 384].reshape(rows, 384)
    return lax.dot_general(left, window, TN, preferred_element_type=F32)


def first_pair_kernel(hid, wide, pair):
    for a in range(3):
        for b in range(3):
            pair[a * 3 + b] = first_part(hid, wide, 1, a, b)


def first_own_kernel(hid, wide, got, one, two, three, keep, held, own, sem):
    y = lax.axis_index("y")
    for a in range(3):
        for b in range(3):
            ab = a * 3 + b
            held[...] = (first_part(hid, wide, 0, a, b) + got[ab]).reshape(8, 4, 8, 384)
            for d, out in enumerate((own, one, two, three)):
                piece = held[:, (y + d) & 3].reshape(64, 384)
                for e in range(3):
                    out[ab * 3 + e] = piece[:, e * 128 : e * 128 + 128].astype(out.dtype)
    kept = pltpu.make_async_copy(own, keep, sem)
    kept.start()
    kept.wait()


def first_y_kernel(got1, got2, got3, own, one, two, three, keep, held):
    x = x_place()

    def tap(t):
        total = own[t]
        for got in (got1, got2, got3):
            total = total + got[t].astype(F32)
        return total

    for g in range(7):
        taps = [tap(t) if t < 27 else jnp.zeros((64, 128), F32) for t in range(4 * g, 4 * g + 4)]
        for q in range(4):
            held[q] = jnp.concatenate([v[:, q * 32 : q * 32 + 32] for v in taps], axis=1)
        for d, out in enumerate((keep, one, two, three)):
            out[g] = held[(x + d) & 3].astype(out.dtype)


def last_kernel(own_two, a1, a2, a3, own_one, b1, b2, b3, out, keep, held):
    for n, (own, got) in enumerate(((own_two, (a1, a2, a3)), (own_one, (b1, b2, b3)))):
        total = own[...]
        for ref in got:
            total = total + ref[...].astype(F32)
        held[n] = total.reshape(7, 8, 8, 128)

    def plane(z):
        return jnp.concatenate([held[n, :, z].reshape(56, 128) for n in range(2)], axis=0)

    for q in range(8):
        out[q] = plane(q).astype(BF)
    keep[...] = plane(lax.axis_index("z"))


def final_kernel(factor, got, own, one, two):
    z = lax.axis_index("z")
    total = own[...]
    for d in range(1, 8):
        total = total + got[(z + d) & 7].astype(F32)
    total = (total * factor).reshape(2, 7, 8, 128)
    for out, which in ((two, 0), (one, 1)):
        for t in range(27):
            out[t] = total[which, t // 4, :, t % 4 * 32 : t % 4 * 32 + 32]


def shards(activations, saved_hidden, cotangent, conv_one, conv_two, film_table, timesteps):
    inputs, hidden, block = activations[0], saved_hidden[0], cotangent[0]
    taps_one = conv_one.transpose(1, 2, 3, 0, 4).reshape(27, 256, 256)
    taps_two = conv_two.transpose(1, 2, 3, 0, 4).reshape(27, 256, 256)
    wide = near((4, 14, 16, 768), BF)
    quads = [near((7, 64, 128), BF)] * 3 + [near((7, 64, 128), F32)]
    to_x = lambda parts: [send(p, ring_pairs(d + 1, 0)) for d, p in enumerate(parts)]
    to_y = lambda parts: [send(p, ring_pairs(0, d + 1)) for d, p in enumerate(parts)]

    packed = call(
        pack_kernel,
        "pack_first",
        (block, inputs),
        "pp",
        [near((2, 4, 16, 256), BF)] * 5,
        [pltpu.VMEM((2, 768, 128), F32)],
    )
    ways = ((1, 0), (0, 1), (0, -1), (1, 1), (1, -1))
    sides = [send(p, block_pairs(*way)) for p, way in zip(packed, ways)]
    act, inp, slope = call(
        film_kernel,
        "film",
        (timesteps, inputs, hidden, film_table),
        "spph",
        [near((768, 256), BF), near((4, 12, 16, 256), BF), near((768, 256), F32)],
        [pltpu.VMEM((8, 512), F32), pltpu.SemaphoreType.DMA],
    )
    wide_in, wide_cot, grad_hidden = call(
        first_kernel,
        "conv_two_back",
        (block, inp, slope, *sides, taps_two),
        "pvv" + "v" * 5 + "h",
        [wide, wide, near((4, 12, 16, 256), BF)],
        [*CONV_SCRATCH, pltpu.VMEM((5, 4, 16, 256), F32)],
    )

    (pair_two,) = call(
        second_pair_kernel, "grad_two_pair", (wide_cot, act), "vv", [near((9, 128, 768), F32)]
    )
    pair_two = send(pair_two, core_pairs())
    (pair_one,) = call(
        first_pair_kernel, "grad_one_pair", (grad_hidden, wide_in), "vv", [near((9, 256, 384), F32)]
    )
    pair_one = send(pair_one, core_pairs())
    out, own_two = call(
        second_own_kernel,
        "grad_two_own",
        (wide_cot, act, pair_two),
        "vvv",
        [near((4, 9, 32, 768), BF), far((9, 32, 768), F32)],
        [pltpu.VMEM((9, 128, 768), F32), pltpu.SemaphoreType.DMA],
    )
    got_two = lax.all_to_all(out, ("xh", "ha"), 0, 0, tiled=True)
    *parts, own_one = call(
        first_own_kernel,
        "grad_one_own",
        (grad_hidden, wide_in, pair_one),
        "vvv",
        [near((27, 64, 128), BF)] * 3 + [far((27, 64, 128), F32)],
        [
            pltpu.VMEM((8, 4, 8, 384), F32),
            pltpu.VMEM((27, 64, 128), F32),
            pltpu.SemaphoreType.DMA,
        ],
    )
    got_one = to_y(parts)

    hi, lo = call(
        pack_columns_kernel,
        "pack_columns",
        (grad_hidden, own_one),
        "vh",
        [near((4, 16, 256), BF)] * 2,
        [pltpu.VMEM((2, 768, 128), F32)],
    )
    left, right = send(hi, block_pairs(0, 1)), send(lo, block_pairs(0, -1))
    (row,) = call(
        pack_rows_kernel, "pack_rows", (grad_hidden, left, right), "vvv", [near((3, 4, 16, 256), BF)]
    )
    row = send(row, block_pairs(1, 0))
    (grad_input,) = call(
        input_conv_kernel,
        "conv_one_back",
        (grad_hidden, block, row, left, right, taps_one),
        "vpvvvh",
        [(jax.ShapeDtypeStruct((4, 12, 16, 256), BF), "v")],
        [*CONV_SCRATCH, pltpu.VMEM((4, 14, 16, 768), BF)],
    )

    *parts, own_two = call(
        second_x_kernel,
        "grad_two_x",
        (got_two, own_two, grad_input),
        "vph",
        quads,
        [pltpu.VMEM((8, 4, 8, 128), F32)],
    )
    got_two = to_y(parts)
    *parts, own_one = call(
        first_y_kernel,
        "grad_one_y",
        (*got_one, own_one),
        "vvvp",
        quads,
        [pltpu.VMEM((4, 64, 128), F32)],
    )
    got_one = to_x(parts)

    out, own = call(
        last_kernel,
        "last_stage",
        (own_two, *got_two, own_one, *got_one),
        "v" * 8,
        [near((8, 112, 128), BF), near((112, 128), F32)],
        [pltpu.VMEM((2, 7, 8, 8, 128), F32)],
    )
    planes = lax.all_to_all(out, "z", 0, 0, tiled=True)
    factor = float(256 * 768) ** (-0.5)
    result = jax.ShapeDtypeStruct((27, 8, 32), F32), "v"
    grad_one, grad_two = call(
        functools.partial(final_kernel, factor), "final_sum", (planes, own), "vv", [result, result]
    )
    shape = lambda g: g.transpose(2, 0, 1).reshape(32, 3, 3, 3, 8)
    return grad_input[None], shape(grad_one), shape(grad_two)


def solution(mesh):
    fine = Mesh(mesh.devices.reshape(SIZES), AX)
    clip = ("z", "y")
    placed = P(clip, None, "ha", ("xh", "core"), None)
    weight = P(("ha", "xh", "core"), None, None, None, clip)
    return jax.shard_map(
        shards,
        mesh=fine,
        in_specs=(placed, placed, placed, P(), P(), P(), P(clip)),
        out_specs=(placed, weight, weight),
        check_vma=False,
    )
```

time: 161 us -> 116 us (0.72)
  the two profiles are of different devices: /device:TPU:1 before, /device:TPU:24 now
where the time goes in v3:
time: 116 us; the launch traced here: 115 us
  Pallas kernels  35.4 us (31%)
  starting transfers between devices  30 us (26%)
  waiting for transfers between devices  28.6 us (25%)
  blocking collectives  18.4 us (16%)
  between operations  1.45 us (1%)
  local copies, waits for them, and re-layouts  1.26 us (1%)
    pallas_call x14, Pallas kernels, call(): pl.pallas_call(kernel, out_shape=tuple((o for o, _ in outs)), in_specs=[s...  35.4 us
    ppermute x19, waiting for transfers between devices, send(): return lax.ppermute(value, AX, pairs)  28.6 us
    ppermute x19, starting transfers between devices, send(): return lax.ppermute(value, AX, pairs)  26.4 us
    all_to_all x1, blocking collectives, shards(): planes = lax.all_to_all(out, 'z', 0, 0, tiled=True)  18.4 us
    all_to_all x1, starting transfers between devices, shards(): got_two = lax.all_to_all(out, ('xh', 'ha'), 0, 0, tiled=True)  3.58 us
  transfers between devices with their start and end apart: 20, of which 8 were waited for; matrix products, arithmetic and copies ran while one was open for 0% of the time, Pallas kernels for 21%

profile of v3, /device:TPU:24, one launch (start us, length us, event | category | flops | bytes accessed | tf_op | source)
XLA Modules:
  0.0 115.2 jit_solution(18198972529295681993)
XLA Ops:
  3.5 3.2 %collective-permute-start.2 = (bf16[2,4,16,256]{3,2,1,0:T(8,128)(2,1)S(1)}, bf16[2,4,16,256]{3,2,1,0:T(8,128)(2,1)S(1)}, u32[]{:S(2)}, u32[]{:S(2)}) collective-permute-start(bf16[2,4,16,256]{3,2,1,0:T(8,128)(2,1)S(1)} %get-tuple-element.38), channel_id=1, source_target_pairs={{0,3},{1,0},{2,1},{3,2},{4,7},{5,4},{6,5},{7,6},{8,11},{9,8},{10,9... | collective-permute-start | bytes 196616 | tf_op jit(solution)/shard_map/ppermute | solution.py:40
  6.8 3.0 %collective-permute-start.4 = (bf16[2,4,16,256]{3,2,1,0:T(8,128)(2,1)S(1)}, bf16[2,4,16,256]{3,2,1,0:T(8,128)(2,1)S(1)}, u32[]{:S(2)}, u32[]{:S(2)}) collective-permute-start(bf16[2,4,16,256]{3,2,1,0:T(8,128)(2,1)S(1)} %get-tuple-element.40), channel_id=1, source_target_pairs={{0,7},{1,4},{2,5},{3,6},{4,3},{5,0},{6,1},{7,2},{8,15},{9,12},{10,... | collective-permute-start | bytes 196616 | tf_op jit(solution)/shard_map/ppermute | solution.py:40
  10.4 2.3 %film.1 = (bf16[768,256]{1,0:T(8,128)(2,1)S(1)}, bf16[4,12,16,256]{3,2,1,0:T(8,128)(2,1)S(1)}, f32[768,256]{1,0:T(8,128)S(1)}) custom-call(s32[1]{0:T(128)S(6)} %copy.10.step, bf16[4,12,16,256]{3,2,1,0:T(8,128)(2,1)} %bitcast.23, bf16[4,12,16,256]{3,2,1,0:T(8,128)(2,1)} %bitcast.24, f32[1000,512]{1,0:T(8,128)} %table.1), custom_call_target="tpu_custom_call" | custom-call | tf_op jit(solution)/shard_map/film/pallas_call | solution.py:50
  12.7 7.0 %conv_two_back.1 = (bf16[4,14,16,768]{3,2,1,0:T(8,128)(2,1)S(1)}, bf16[4,14,16,768]{3,2,1,0:T(8,128)(2,1)S(1)}, bf16[4,12,16,256]{3,2,1,0:T(8,128)(2,1)S(1)}) custom-call(bf16[4,12,16,256]{3,2,1,0:T(8,128)(2,1)} %bitcast.19, bf16[4,12,16,256]{3,2,1,0:T(8,128)(2,1)S(1)} %get-tuple-element.34.inp, f32[768,256]{1,0:T(8,128)S(1)} %get-tuple-element.35.slope, ...), custom_call_target="tpu_custom_call" | custom-call | tf_op jit(solution)/shard_map/conv_two_back/pallas_call | solution.py:50
  22.4 3.5 %grad_one_pair.1 = f32[9,256,384]{2,1,0:T(8,128)} custom-call(bf16[4,12,16,256]{3,2,1,0:T(8,128)(2,1)S(1)} %get-tuple-element.41.hid.block, bf16[4,14,16,768]{3,2,1,0:T(8,128)(2,1)S(1)} %get-tuple-element.42.wide), custom_call_target="tpu_custom_call" | custom-call | tf_op jit(solution)/shard_map/grad_one_pair/pallas_call | solution.py:50
  26.0 2.3 %collective-permute-done.9.got = f32[9,128,768]{2,1,0:T(8,128)S(1)} collective-permute-done((f32[9,128,768]{2,1,0:T(8,128)S(1)}, f32[9,128,768]{2,1,0:T(8,128)S(1)}, u32[]{:S(2)}, u32[]{:S(2)}) %collective-permute-start.9) | collective-permute-done | bytes 3538976 | tf_op jit(solution)/shard_map/ppermute | solution.py:40
  28.3 2.4 %grad_two_own.1 = (bf16[4,9,32,768]{3,2,1,0:T(8,128)(2,1)S(1)}, f32[9,32,768]{2,1,0:T(8,128)}) custom-call(bf16[4,14,16,768]{3,2,1,0:T(8,128)(2,1)S(1)} %get-tuple-element.46.wide, bf16[768,256]{1,0:T(8,128)(2,1)S(1)} %get-tuple-element.47.act, f32[9,128,768]{2,1,0:T(8,128)S(1)} %collective-permute-done.9.got), custom_call_target="tpu_custom_call" | custom-call | tf_op jit(solution)/shard_map/grad_two_own/pallas_call | solution.py:50
  31.9 3.6 %all-to-all-start = ((bf16[4,9,32,768]{3,2,1,0:T(8,128)(2,1)}), bf16[4,9,32,768]{3,2,1,0:T(8,128)(2,1)S(1)}, u32[]{:S(2)}, u32[]{:S(2)}) async-start(bf16[4,9,32,768]{3,2,1,0:T(8,128)(2,1)} %copy-done), calls=%async_computation | async-start | bytes 3538944 | tf_op jit(solution)/shard_map/all_to_all | solution.py:417
  35.5 5.4 %grad_one_own.1 = (bf16[27,64,128]{2,1,0:T(8,128)(2,1)S(1)}, bf16[27,64,128]{2,1,0:T(8,128)(2,1)S(1)}, bf16[27,64,128]{2,1,0:T(8,128)(2,1)S(1)}, f32[27,64,128]{2,1,0:T(8,128)}) custom-call(bf16[4,12,16,256]{3,2,1,0:T(8,128)(2,1)S(1)} %get-tuple-element.41.hid.block, bf16[4,14,16,768]{3,2,1,0:T(8,128)(2,1)S(1)} %get-tuple-element.42.wide, ...), custom_call_target="tpu_custom_call" | custom-call | tf_op jit(solution)/shard_map/grad_one_own/pallas_call | solution.py:50
  41.2 2.6 %collective-permute-start.14 = (bf16[27,64,128]{2,1,0:T(8,128)(2,1)S(1)}, bf16[27,64,128]{2,1,0:T(8,128)(2,1)S(1)}, u32[]{:S(2)}, u32[]{:S(2)}) collective-permute-start(bf16[27,64,128]{2,1,0:T(8,128)(2,1)S(1)} %get-tuple-element.55), channel_id=1, source_target_pairs={{0,16},{1,17},{2,18},{3,19},{4,20},{5,21},{6,22},{7,23},{8,24},{9,... | collective-permute-start | bytes 1327112 | tf_op jit(solution)/shard_map/ppermute | solution.py:40
  44.0 3.2 %collective-permute-start.7 = (bf16[4,16,256]{2,1,0:T(8,128)(2,1)S(1)}, bf16[4,16,256]{2,1,0:T(8,128)(2,1)S(1)}, u32[]{:S(2)}, u32[]{:S(2)}) collective-permute-start(bf16[4,16,256]{2,1,0:T(8,128)(2,1)S(1)} %get-tuple-element.45), channel_id=1, source_target_pairs={{0,3},{1,0},{2,1},{3,2},{4,7},{5,4},{6,5},{7,6},{8,11},{9,8},{10,9... | collective-permute-start | bytes 98312 | tf_op jit(solution)/shard_map/ppermute | solution.py:40
  47.2 6.8 %collective-permute-done.13.got1 = bf16[27,64,128]{2,1,0:T(8,128)(2,1)S(1)} collective-permute-done((bf16[27,64,128]{2,1,0:T(8,128)(2,1)S(1)}, bf16[27,64,128]{2,1,0:T(8,128)(2,1)S(1)}, u32[]{:S(2)}, u32[]{:S(2)}) %collective-permute-start.13) | collective-permute-done | bytes 442400 | tf_op jit(solution)/shard_map/ppermute | solution.py:40
  54.0 1.7 %collective-permute-done.14.got2 = bf16[27,64,128]{2,1,0:T(8,128)(2,1)S(1)} collective-permute-done((bf16[27,64,128]{2,1,0:T(8,128)(2,1)S(1)}, bf16[27,64,128]{2,1,0:T(8,128)(2,1)S(1)}, u32[]{:S(2)}, u32[]{:S(2)}) %collective-permute-start.14) | collective-permute-done | bytes 442400 | tf_op jit(solution)/shard_map/ppermute | solution.py:40
  55.7 8.8 %collective-permute-done.15.got3 = bf16[27,64,128]{2,1,0:T(8,128)(2,1)S(1)} collective-permute-done((bf16[27,64,128]{2,1,0:T(8,128)(2,1)S(1)}, bf16[27,64,128]{2,1,0:T(8,128)(2,1)S(1)}, u32[]{:S(2)}, u32[]{:S(2)}) %collective-permute-start.15) | collective-permute-done | bytes 442400 | tf_op jit(solution)/shard_map/ppermute | solution.py:40
  64.5 2.0 %grad_one_y.1 = (bf16[7,64,128]{2,1,0:T(8,128)(2,1)S(1)}, bf16[7,64,128]{2,1,0:T(8,128)(2,1)S(1)}, bf16[7,64,128]{2,1,0:T(8,128)(2,1)S(1)}, f32[7,64,128]{2,1,0:T(8,128)S(1)}) custom-call(bf16[27,64,128]{2,1,0:T(8,128)(2,1)S(1)} %collective-permute-done.13.got1, bf16[27,64,128]{2,1,0:T(8,128)(2,1)S(1)} %collective-permute-done.14.got2, ...), custom_call_target="tpu_custom_call" | custom-call | tf_op jit(solution)/shard_map/grad_one_y/pallas_call | solution.py:50
  66.5 1.8 %collective-permute-start.16 = (bf16[7,64,128]{2,1,0:T(8,128)(2,1)S(1)}, bf16[7,64,128]{2,1,0:T(8,128)(2,1)S(1)}, u32[]{:S(2)}, u32[]{:S(2)}) collective-permute-start(bf16[7,64,128]{2,1,0:T(8,128)(2,1)S(1)} %get-tuple-element.58), channel_id=1, source_target_pairs={{0,4},{1,5},{2,6},{3,7},{4,2},{5,3},{6,0},{7,1},{8,12},{9,13},{10,... | collective-permute-start | bytes 344072 | tf_op jit(solution)/shard_map/ppermute | solution.py:40
  69.9 3.1 %collective-permute-done.8.row = bf16[3,4,16,256]{3,2,1,0:T(8,128)(2,1)S(1)} collective-permute-done((bf16[3,4,16,256]{3,2,1,0:T(8,128)(2,1)S(1)}, bf16[3,4,16,256]{3,2,1,0:T(8,128)(2,1)S(1)}, u32[]{:S(2)}, u32[]{:S(2)}) %collective-permute-start.8) | collective-permute-done | bytes 98336 | tf_op jit(solution)/shard_map/ppermute | solution.py:40
  73.0 7.5 %conv_one_back.1.after = bf16[4,12,16,256]{3,2,1,0:T(8,128)(2,1)} custom-call(bf16[4,12,16,256]{3,2,1,0:T(8,128)(2,1)S(1)} %get-tuple-element.41.hid.block, bf16[4,12,16,256]{3,2,1,0:T(8,128)(2,1)} %bitcast.20, bf16[3,4,16,256]{3,2,1,0:T(8,128)(2,1)S(1)} %collective-permute-done.8.row, bf16[4,16,256]{2,1,0:T(8,128)(2,1)S(1)} %collective-permute-done.6.left, ...), custom_call_target="tpu_custom_call" | custom-call | tf_op jit(solution)/shard_map/conv_one_back/pallas_call | solution.py:50
  80.5 2.8 %collective-permute-start.17 = (bf16[7,64,128]{2,1,0:T(8,128)(2,1)S(1)}, bf16[7,64,128]{2,1,0:T(8,128)(2,1)S(1)}, u32[]{:S(2)}, u32[]{:S(2)}) collective-permute-start(bf16[7,64,128]{2,1,0:T(8,128)(2,1)S(1)} %get-tuple-element.59), channel_id=1, source_target_pairs={{0,2},{1,3},{2,0},{3,1},{4,6},{5,7},{6,4},{7,5},{8,10},{9,11},{10,... | collective-permute-start | bytes 344072 | tf_op jit(solution)/shard_map/ppermute | solution.py:40
  83.3 2.4 %collective-permute-start.18 = (bf16[7,64,128]{2,1,0:T(8,128)(2,1)S(1)}, bf16[7,64,128]{2,1,0:T(8,128)(2,1)S(1)}, u32[]{:S(2)}, u32[]{:S(2)}) collective-permute-start(bf16[7,64,128]{2,1,0:T(8,128)(2,1)S(1)} %get-tuple-element.60), channel_id=1, source_target_pairs={{0,6},{1,7},{2,4},{3,5},{4,0},{5,1},{6,2},{7,3},{8,14},{9,15},{10,... | collective-permute-start | bytes 344072 | tf_op jit(solution)/shard_map/ppermute | solution.py:40
  87.8 1.7 %collective-permute-start.11 = (bf16[7,64,128]{2,1,0:T(8,128)(2,1)S(1)}, bf16[7,64,128]{2,1,0:T(8,128)(2,1)S(1)}, u32[]{:S(2)}, u32[]{:S(2)}) collective-permute-start(bf16[7,64,128]{2,1,0:T(8,128)(2,1)S(1)} %get-tuple-element.52), channel_id=1, source_target_pairs={{0,16},{1,17},{2,18},{3,19},{4,20},{5,21},{6,22},{7,23},{8,24},{9,... | collective-permute-start | bytes 344072 | tf_op jit(solution)/shard_map/ppermute | solution.py:40
  90.0 2.3 %collective-permute-done.10.a1 = bf16[7,64,128]{2,1,0:T(8,128)(2,1)S(1)} collective-permute-done((bf16[7,64,128]{2,1,0:T(8,128)(2,1)S(1)}, bf16[7,64,128]{2,1,0:T(8,128)(2,1)S(1)}, u32[]{:S(2)}, u32[]{:S(2)}) %collective-permute-start.10) | collective-permute-done | bytes 114720 | tf_op jit(solution)/shard_map/ppermute | solution.py:40
  92.3 2.4 %collective-permute-done.11.a2 = bf16[7,64,128]{2,1,0:T(8,128)(2,1)S(1)} collective-permute-done((bf16[7,64,128]{2,1,0:T(8,128)(2,1)S(1)}, bf16[7,64,128]{2,1,0:T(8,128)(2,1)S(1)}, u32[]{:S(2)}, u32[]{:S(2)}) %collective-permute-start.11) | collective-permute-done | bytes 114720 | tf_op jit(solution)/shard_map/ppermute | solution.py:40
  96.0 18.4 %all_to_all.10.got = bf16[8,112,128]{2,1,0:T(8,128)(2,1)S(1)} all-to-all(bf16[8,112,128]{2,1,0:T(8,128)(2,1)S(1)} %get-tuple-element.61), channel_id=1, replica_groups=mesh['z'=8,'y'=4,'ha'=2,'xh'=2,'core'=2] {'z'}, dimensions={0} | all-to-all | bytes 458752 | tf_op jit(solution)/shard_map/all_to_all | solution.py:481
  (33 shorter events, 13.6 us)
Async XLA Ops:
  1.9 10.7 %collective-permute-start = (bf16[2,4,16,256]{3,2,1,0:T(8,128)(2,1)S(1)}, bf16[2,4,16,256]{3,2,1,0:T(8,128)(2,1)S(1)}, u32[]{:S(2)}, u32[]{:S(2)}) collective-permute-start(bf16[2,4,16,256]{3,2,1,0:T(8,128)(2,1)S(1)} %get-tuple-element.36), channel_id=1, source_target_pairs={{0,4},{1,5},{2,6},{3,7},{4,0},{5,1},{6,2},{7,3},{8,12},{9,13},{10,... | collective-permute-start | bytes 196616 | tf_op jit(solution)/shard_map/ppermute | solution.py:40
  3.5 9.2 %collective-permute-start.1 = (bf16[2,4,16,256]{3,2,1,0:T(8,128)(2,1)S(1)}, bf16[2,4,16,256]{3,2,1,0:T(8,128)(2,1)S(1)}, u32[]{:S(2)}, u32[]{:S(2)}) collective-permute-start(bf16[2,4,16,256]{3,2,1,0:T(8,128)(2,1)S(1)} %get-tuple-element.37), channel_id=1, source_target_pairs={{0,1},{1,2},{2,3},{3,0},{4,5},{5,6},{6,7},{7,4},{8,9},{9,10},{10,1... | collective-permute-start | bytes 196616 | tf_op jit(solution)/shard_map/ppermute | solution.py:40
  3.5 9.2 %collective-permute-start.2 = (bf16[2,4,16,256]{3,2,1,0:T(8,128)(2,1)S(1)}, bf16[2,4,16,256]{3,2,1,0:T(8,128)(2,1)S(1)}, u32[]{:S(2)}, u32[]{:S(2)}) collective-permute-start(bf16[2,4,16,256]{3,2,1,0:T(8,128)(2,1)S(1)} %get-tuple-element.38), channel_id=1, source_target_pairs={{0,3},{1,0},{2,1},{3,2},{4,7},{5,4},{6,5},{7,6},{8,11},{9,8},{10,9... | collective-permute-start | bytes 196616 | tf_op jit(solution)/shard_map/ppermute | solution.py:40
  6.8 5.9 %collective-permute-start.3 = (bf16[2,4,16,256]{3,2,1,0:T(8,128)(2,1)S(1)}, bf16[2,4,16,256]{3,2,1,0:T(8,128)(2,1)S(1)}, u32[]{:S(2)}, u32[]{:S(2)}) collective-permute-start(bf16[2,4,16,256]{3,2,1,0:T(8,128)(2,1)S(1)} %get-tuple-element.39), channel_id=1, source_target_pairs={{0,5},{1,6},{2,7},{3,4},{4,1},{5,2},{6,3},{7,0},{8,13},{9,14},{10,... | collective-permute-start | bytes 196616 | tf_op jit(solution)/shard_map/ppermute | solution.py:40
  6.8 5.9 %collective-permute-start.4 = (bf16[2,4,16,256]{3,2,1,0:T(8,128)(2,1)S(1)}, bf16[2,4,16,256]{3,2,1,0:T(8,128)(2,1)S(1)}, u32[]{:S(2)}, u32[]{:S(2)}) collective-permute-start(bf16[2,4,16,256]{3,2,1,0:T(8,128)(2,1)S(1)} %get-tuple-element.40), channel_id=1, source_target_pairs={{0,7},{1,4},{2,5},{3,6},{4,3},{5,0},{6,1},{7,2},{8,15},{9,12},{10,... | collective-permute-start | bytes 196616 | tf_op jit(solution)/shard_map/ppermute | solution.py:40
  21.2 7.1 %collective-permute-start.9 = (f32[9,128,768]{2,1,0:T(8,128)S(1)}, f32[9,128,768]{2,1,0:T(8,128)S(1)}, u32[]{:S(2)}, u32[]{:S(2)}) collective-permute-start(f32[9,128,768]{2,1,0:T(8,128)S(1)} %grad_two_pair.1), channel_id=1, source_target_pairs={{0,1},{1,0},{2,3},{3,2},{4,5},{5,4},{6,7},{7,6},{8,9},{9,8},{10,11... | collective-permute-start | bytes 10616840 | tf_op jit(solution)/shard_map/ppermute | solution.py:40
  26.0 9.5 %collective-permute-start.5 = (f32[9,256,384]{2,1,0:T(8,128)}, f32[9,256,384]{2,1,0:T(8,128)}, u32[]{:S(2)}, u32[]{:S(2)}) collective-permute-start(f32[9,256,384]{2,1,0:T(8,128)} %grad_one_pair.1), channel_id=1, source_target_pairs={{0,1},{1,0},{2,3},{3,2},{4,5},{5,4},{6,7},{7,6},{8,9},{9,8},{10,11... | collective-permute-start | bytes 10616840 | tf_op jit(solution)/shard_map/ppermute | solution.py:40
  30.6 1.3 %copy-start = (bf16[4,9,32,768]{3,2,1,0:T(8,128)(2,1)}, bf16[4,9,32,768]{3,2,1,0:T(8,128)(2,1)S(1)}, u32[]{:S(2)}) copy-start(bf16[4,9,32,768]{3,2,1,0:T(8,128)(2,1)S(1)} %get-tuple-element.48) | copy-start | bytes 5308420
  31.9 53.8 %all-to-all-start = ((bf16[4,9,32,768]{3,2,1,0:T(8,128)(2,1)}), bf16[4,9,32,768]{3,2,1,0:T(8,128)(2,1)S(1)}, u32[]{:S(2)}, u32[]{:S(2)}) async-start(bf16[4,9,32,768]{3,2,1,0:T(8,128)(2,1)} %copy-done), calls=%async_computation | async-start | bytes 3538944 | tf_op jit(solution)/shard_map/all_to_all | solution.py:417
  40.9 13.1 %collective-permute-start.13 = (bf16[27,64,128]{2,1,0:T(8,128)(2,1)S(1)}, bf16[27,64,128]{2,1,0:T(8,128)(2,1)S(1)}, u32[]{:S(2)}, u32[]{:S(2)}) collective-permute-start(bf16[27,64,128]{2,1,0:T(8,128)(2,1)S(1)} %get-tuple-element.54), channel_id=1, source_target_pairs={{0,8},{1,9},{2,10},{3,11},{4,12},{5,13},{6,14},{7,15},{8,16},{9,17... | collective-permute-start | bytes 1327112 | tf_op jit(solution)/shard_map/ppermute | solution.py:40
  41.2 14.5 %collective-permute-start.14 = (bf16[27,64,128]{2,1,0:T(8,128)(2,1)S(1)}, bf16[27,64,128]{2,1,0:T(8,128)(2,1)S(1)}, u32[]{:S(2)}, u32[]{:S(2)}) collective-permute-start(bf16[27,64,128]{2,1,0:T(8,128)(2,1)S(1)} %get-tuple-element.55), channel_id=1, source_target_pairs={{0,16},{1,17},{2,18},{3,19},{4,20},{5,21},{6,22},{7,23},{8,24},{9,... | collective-permute-start | bytes 1327112 | tf_op jit(solution)/shard_map/ppermute | solution.py:40
  43.8 20.7 %collective-permute-start.15 = (bf16[27,64,128]{2,1,0:T(8,128)(2,1)S(1)}, bf16[27,64,128]{2,1,0:T(8,128)(2,1)S(1)}, u32[]{:S(2)}, u32[]{:S(2)}) collective-permute-start(bf16[27,64,128]{2,1,0:T(8,128)(2,1)S(1)} %get-tuple-element.56), channel_id=1, source_target_pairs={{0,24},{1,25},{2,26},{3,27},{4,28},{5,29},{6,30},{7,31},{8,0},{9,1... | collective-permute-start | bytes 1327112 | tf_op jit(solution)/shard_map/ppermute | solution.py:40
  43.9 24.4 %collective-permute-start.6 = (bf16[4,16,256]{2,1,0:T(8,128)(2,1)S(1)}, bf16[4,16,256]{2,1,0:T(8,128)(2,1)S(1)}, u32[]{:S(2)}, u32[]{:S(2)}) collective-permute-start(bf16[4,16,256]{2,1,0:T(8,128)(2,1)S(1)} %get-tuple-element.44), channel_id=1, source_target_pairs={{0,1},{1,2},{2,3},{3,0},{4,5},{5,6},{6,7},{7,4},{8,9},{9,10},{10,1... | collective-permute-start | bytes 98312 | tf_op jit(solution)/shard_map/ppermute | solution.py:40
  44.0 24.3 %collective-permute-start.7 = (bf16[4,16,256]{2,1,0:T(8,128)(2,1)S(1)}, bf16[4,16,256]{2,1,0:T(8,128)(2,1)S(1)}, u32[]{:S(2)}, u32[]{:S(2)}) collective-permute-start(bf16[4,16,256]{2,1,0:T(8,128)(2,1)S(1)} %get-tuple-element.45), channel_id=1, source_target_pairs={{0,3},{1,0},{2,1},{3,2},{4,7},{5,4},{6,5},{7,6},{8,11},{9,8},{10,9... | collective-permute-start | bytes 98312 | tf_op jit(solution)/shard_map/ppermute | solution.py:40
  66.5 23.0 %collective-permute-start.16 = (bf16[7,64,128]{2,1,0:T(8,128)(2,1)S(1)}, bf16[7,64,128]{2,1,0:T(8,128)(2,1)S(1)}, u32[]{:S(2)}, u32[]{:S(2)}) collective-permute-start(bf16[7,64,128]{2,1,0:T(8,128)(2,1)S(1)} %get-tuple-element.58), channel_id=1, source_target_pairs={{0,4},{1,5},{2,6},{3,7},{4,2},{5,3},{6,0},{7,1},{8,12},{9,13},{10,... | collective-permute-start | bytes 344072 | tf_op jit(solution)/shard_map/ppermute | solution.py:40
  68.3 4.7 %collective-permute-start.8 = (bf16[3,4,16,256]{3,2,1,0:T(8,128)(2,1)S(1)}, bf16[3,4,16,256]{3,2,1,0:T(8,128)(2,1)S(1)}, u32[]{:S(2)}, u32[]{:S(2)}) collective-permute-start(bf16[3,4,16,256]{3,2,1,0:T(8,128)(2,1)S(1)} %pack_rows.1), channel_id=1, source_target_pairs={{0,4},{1,5},{2,6},{3,7},{4,0},{5,1},{6,2},{7,3},{8,12},{9,13},{10,... | collective-permute-start | bytes 294920 | tf_op jit(solution)/shard_map/ppermute | solution.py:40
  80.5 9.5 %collective-permute-start.17 = (bf16[7,64,128]{2,1,0:T(8,128)(2,1)S(1)}, bf16[7,64,128]{2,1,0:T(8,128)(2,1)S(1)}, u32[]{:S(2)}, u32[]{:S(2)}) collective-permute-start(bf16[7,64,128]{2,1,0:T(8,128)(2,1)S(1)} %get-tuple-element.59), channel_id=1, source_target_pairs={{0,2},{1,3},{2,0},{3,1},{4,6},{5,7},{6,4},{7,5},{8,10},{9,11},{10,... | collective-permute-start | bytes 344072 | tf_op jit(solution)/shard_map/ppermute | solution.py:40
  83.3 6.7 %collective-permute-start.18 = (bf16[7,64,128]{2,1,0:T(8,128)(2,1)S(1)}, bf16[7,64,128]{2,1,0:T(8,128)(2,1)S(1)}, u32[]{:S(2)}, u32[]{:S(2)}) collective-permute-start(bf16[7,64,128]{2,1,0:T(8,128)(2,1)S(1)} %get-tuple-element.60), channel_id=1, source_target_pairs={{0,6},{1,7},{2,4},{3,5},{4,0},{5,1},{6,2},{7,3},{8,14},{9,15},{10,... | collective-permute-start | bytes 344072 | tf_op jit(solution)/shard_map/ppermute | solution.py:40
  87.3 5.0 %collective-permute-start.10 = (bf16[7,64,128]{2,1,0:T(8,128)(2,1)S(1)}, bf16[7,64,128]{2,1,0:T(8,128)(2,1)S(1)}, u32[]{:S(2)}, u32[]{:S(2)}) collective-permute-start(bf16[7,64,128]{2,1,0:T(8,128)(2,1)S(1)} %get-tuple-element.51), channel_id=1, source_target_pairs={{0,8},{1,9},{2,10},{3,11},{4,12},{5,13},{6,14},{7,15},{8,16},{9,17... | collective-permute-start | bytes 344072 | tf_op jit(solution)/shard_map/ppermute | solution.py:40
  87.8 6.9 %collective-permute-start.11 = (bf16[7,64,128]{2,1,0:T(8,128)(2,1)S(1)}, bf16[7,64,128]{2,1,0:T(8,128)(2,1)S(1)}, u32[]{:S(2)}, u32[]{:S(2)}) collective-permute-start(bf16[7,64,128]{2,1,0:T(8,128)(2,1)S(1)} %get-tuple-element.52), channel_id=1, source_target_pairs={{0,16},{1,17},{2,18},{3,19},{4,20},{5,21},{6,22},{7,23},{8,24},{9,... | collective-permute-start | bytes 344072 | tf_op jit(solution)/shard_map/ppermute | solution.py:40
  89.5 6.4 %collective-permute-start.12 = (bf16[7,64,128]{2,1,0:T(8,128)(2,1)S(1)}, bf16[7,64,128]{2,1,0:T(8,128)(2,1)S(1)}, u32[]{:S(2)}, u32[]{:S(2)}) collective-permute-start(bf16[7,64,128]{2,1,0:T(8,128)(2,1)S(1)} %get-tuple-element.53), channel_id=1, source_target_pairs={{0,24},{1,25},{2,26},{3,27},{4,28},{5,29},{6,30},{7,31},{8,0},{9,1... | collective-permute-start | bytes 344072 | tf_op jit(solution)/shard_map/ppermute | solution.py:40

commit v4 on v3

--- a/solution.py
+++ b/solution.py
@@ -27,12 +27,12 @@
     return [(i, i // 8 * 8 + (i // 4 % 2 ^ dh) * 4 + (i + dw) % 4) for i in range(256)]
 
 
-def ring_pairs(dx, dy):
+def ring_pairs(dx=0, dy=0, dz=0):
     pairs = []
     for i in range(256):
         core, xh, ha, y, z = i % 2, i // 2 % 2, i // 4 % 2, i // 8 % 4, i // 32
-        x = (xh * 2 + ha + dx) % 4
-        pairs.append((i, ((z * 4 + (y + dy) % 4) * 2 + x % 2) * 4 + x // 2 * 2 + core))
+        x, y, z = (xh * 2 + ha + dx) % 4, (y + dy) % 4, (z + dz) % 8
+        pairs.append((i, ((z * 4 + y) * 2 + x % 2) * 4 + x // 2 * 2 + core))
     return pairs
 
 
@@ -63,7 +63,7 @@
 
 
 def far(shape, dtype):
-    return pltpu.HBM(shape, dtype), "h"
+    return pltpu.HBM(shape, dtype), "p"
 
 
 def x_place():
@@ -104,7 +104,8 @@
                 out[f, :, h * 128 : h * 128 + 128] = column(wide, h, f, j)
 
 
-def pack_rows_kernel(block, left, right, row):
+def pack_rows_kernel(block, left, right, after, row):
+    del after
     edge = 11 * (1 - lax.axis_index("ha"))
     for f in range(4):
         row[0, f] = block[f, edge]
@@ -150,10 +151,9 @@
     ]
 
 
-def conv_sum(wide, held, copies, total):
+def conv_sum(wide, held, total):
     for a in (2, 1, 0):
         frames = a + 2
-        copies[a].wait()
         for b in range(3):
             window = wide[2 - a : 4, 2 - b : 14 - b].reshape(frames * 192, 768)
             part = None
@@ -171,13 +171,6 @@
                 total[0 : frames * 192] += part
 
 
-CONV_SCRATCH = [
-    pltpu.VMEM((27, 256, 256), BF),
-    pltpu.VMEM((768, 256), F32),
-    pltpu.SemaphoreType.DMA((3,)),
-]
-
-
 def channel_order():
     lane = lax.broadcasted_iota(jnp.int32, (256, 256), 1)
     goal, kept = (lane >> 5) & 3, lax.axis_index("core") ^ (lane >> 7)
@@ -185,30 +178,43 @@
     return (lax.broadcasted_iota(jnp.int32, (256, 256), 0) == source).astype(BF)
 
 
-def film_kernel(step, inputs, hidden, table, act_out, inp_out, slope, film, sem):
+def film_kernel(
+    step, inputs, hidden, table, weight, act_out, inp_out, slope, taps,
+    film, blocks, sem, block_sem, tap_sem,
+):
     start = step[0]
     whole = pl.multiple_of(start // 8 * 8, 8)
     film_copy = pltpu.make_async_copy(table.at[pl.ds(whole, 8)], film, sem)
     film_copy.start()
+    block_copies = [
+        pltpu.make_async_copy(ref, blocks.at[n], block_sem.at[n])
+        for n, ref in enumerate((inputs, hidden))
+    ]
+    for copy in block_copies:
+        copy.start()
+    copies = weight_copies(weight, taps, tap_sem)
+    for copy in copies:
+        copy.start()
     order = channel_order()
     sort = lambda v: jnp.dot(v, order, preferred_element_type=F32).astype(BF)
-    inp_out[...] = sort(inputs[...].reshape(768, 256)).reshape(4, 12, 16, 256)
+    for copy in block_copies:
+        copy.wait()
     film_copy.wait()
+    inp_out[...] = sort(blocks[0].reshape(768, 256)).reshape(4, 12, 16, 256)
     line = film[pl.ds(start - whole, 1), :]
     scale, shift = 1.0 + line[:, 0:256], line[:, 256:512]
-    shifted = hidden[...].reshape(768, 256).astype(F32) * scale + shift
+    shifted = blocks[1].reshape(768, 256).astype(F32) * scale + shift
     sigma = jax.nn.sigmoid(shifted)
     act_out[...] = sort((shifted * sigma).astype(BF))
     slope[...] = scale * sigma * (1.0 + shifted * (1.0 - sigma))
+    for copy in copies:
+        copy.wait()
 
 
 def first_kernel(
-    block, inp, slope, row, left, right, corner_left, corner_right, weight,
-    wide_in, wide, hid_out, held, total, sem, side,
+    block, inp, slope, row, left, right, corner_left, corner_right, taps,
+    wide_in, wide, hid_out, total, side,
 ):
-    copies = weight_copies(weight, held, sem)
-    for a in (2, 1, 0):
-        copies[a].start()
     sides = (row, left, right, corner_left, corner_right)
     build_shifted(
         put_back(wide), lambda f, r: block[f, r], *[lambda f, s=s: s[0, f] for s in sides]
@@ -224,14 +230,14 @@
         wide_in[f, r, :, at + 384 : at + 512] = cells[:, 128:256]
 
     build_shifted(put, lambda f, r: inp[f, r], *[lambda f, n=n: side[n, f] for n in range(5)])
-    conv_sum(wide, held, copies, total)
+    conv_sum(wide, taps, total)
     hid_out[...] = (total[...] * slope[...]).astype(BF).reshape(4, 12, 16, 256)
 
 
 def input_conv_kernel(hid, block, row, left, right, weight, out, held, total, sem, wide):
     copies = weight_copies(weight, held, sem)
-    for a in (2, 1, 0):
-        copies[a].start()
+    for copy in copies:
+        copy.start()
     build_shifted(
         put_back(wide),
         lambda f, r: hid[f, r],
@@ -241,7 +247,9 @@
         lambda f: row[1, f],
         lambda f: row[2, f],
     )
-    conv_sum(wide, held, copies, total)
+    for copy in copies:
+        copy.wait()
+    conv_sum(wide, held, total)
     grad = block[...].reshape(768, 256).astype(F32) + total[...]
     out[...] = grad.astype(BF).reshape(4, 12, 16, 256)
 
@@ -253,35 +261,34 @@
     return lax.dot_general(left, window, TN, preferred_element_type=F32)
 
 
-def second_pair_kernel(wide, act, pair):
+def second_pair_kernel(wide, act, after, pair):
+    del after
     for a in range(3):
         for b in range(3):
             pair[a * 3 + b] = second_part(wide, act, 1, a, b)
 
 
-def second_own_kernel(wide, act, got, out, keep, held, sem):
-    mine = pl.ds(pl.multiple_of(x_place() * 32, 32), 32)
+def second_own_kernel(wide, act, got, after, one, two, three, keep, held):
+    del after
+    x = x_place()
     for a in range(3):
         for b in range(3):
             ab = a * 3 + b
-            total = second_part(wide, act, 0, a, b) + got[ab]
-            held[ab] = total
-            for q in range(4):
-                out[q, ab] = total[q * 32 : q * 32 + 32].astype(BF)
-    kept = pltpu.make_async_copy(held.at[:, mine], keep, sem)
-    kept.start()
-    kept.wait()
-
-
-def second_x_kernel(got, own, after, one, two, three, keep, held):
+            held[...] = second_part(wide, act, 0, a, b) + got[ab]
+            for d, out in enumerate((keep, one, two, three)):
+                rows = pl.ds(pl.multiple_of(((x + d) & 3) * 32, 32), 32)
+                out[ab] = held[rows, :].astype(out.dtype)
+
+
+def second_x_kernel(got1, got2, got3, own, after, one, two, three, keep, held):
     del after
-    x, y = x_place(), lax.axis_index("y")
+    y = lax.axis_index("y")
 
     def tap(t):
         ab, lanes = t // 3, slice(t % 3 * 256, t % 3 * 256 + 256)
         total = own[ab, :, lanes]
-        for d in range(1, 4):
-            total = total + got[(x + d) & 3, ab, :, lanes].astype(F32)
+        for got in (got1, got2, got3):
+            total = total + got[ab, :, lanes].astype(F32)
         return total
 
     for g in range(7):
@@ -291,41 +298,37 @@
             out[g] = held[:, (y + d) & 3].reshape(64, 128).astype(out.dtype)
 
 
-def first_part(hid, wide, half, a, b):
-    rows = (a + 2) * 192
-    left = hid[2 - a : 4].reshape(rows, 256)
-    window = wide[0 : a + 2, b : b + 12, :, half * 384 : half * 384 + 384].reshape(rows, 384)
-    return lax.dot_general(left, window, TN, preferred_element_type=F32)
-
-
-def first_pair_kernel(hid, wide, pair):
+def first_grad_kernel(hid, wide, own, pair):
     for a in range(3):
+        rows = (a + 2) * 192
+        left = hid[2 - a : 4].reshape(rows, 256)
         for b in range(3):
-            pair[a * 3 + b] = first_part(hid, wide, 1, a, b)
-
-
-def first_own_kernel(hid, wide, got, one, two, three, keep, held, own, sem):
+            window = wide[0 : a + 2, b : b + 12].reshape(rows, 768)
+            grad = lax.dot_general(left, window, TN, preferred_element_type=F32)
+            grad = grad.reshape(8, 4, 8, 768)
+            for q in range(4):
+                piece = grad[:, q].reshape(64, 768)
+                for e in range(3):
+                    t = (a * 3 + b) * 3 + e
+                    own[q, t] = piece[:, e * 128 : e * 128 + 128]
+                    pair[q, t] = piece[:, e * 128 + 384 : e * 128 + 512]
+
+
+def first_pair_kernel(own, pair, out, keep):
     y = lax.axis_index("y")
-    for a in range(3):
-        for b in range(3):
-            ab = a * 3 + b
-            held[...] = (first_part(hid, wide, 0, a, b) + got[ab]).reshape(8, 4, 8, 384)
-            for d, out in enumerate((own, one, two, three)):
-                piece = held[:, (y + d) & 3].reshape(64, 384)
-                for e in range(3):
-                    out[ab * 3 + e] = piece[:, e * 128 : e * 128 + 128].astype(out.dtype)
-    kept = pltpu.make_async_copy(own, keep, sem)
-    kept.start()
-    kept.wait()
-
-
-def first_y_kernel(got1, got2, got3, own, one, two, three, keep, held):
-    x = x_place()
+    for q in range(4):
+        out[q] = (own[q] + pair[q]).astype(BF)
+    keep[...] = own[y] + pair[y]
+
+
+def first_y_kernel(got, own, after, one, two, three, keep, held):
+    del after
+    x, y = x_place(), lax.axis_index("y")
 
     def tap(t):
         total = own[t]
-        for got in (got1, got2, got3):
-            total = total + got[t].astype(F32)
+        for d in range(1, 4):
+            total = total + got[(y + d) & 3, t].astype(F32)
         return total
 
     for g in range(7):
@@ -336,26 +339,24 @@
             out[g] = held[(x + d) & 3].astype(out.dtype)
 
 
-def last_kernel(own_two, a1, a2, a3, own_one, b1, b2, b3, out, keep, held):
+def last_kernel(own_two, a1, a2, a3, own_one, b1, b2, b3, *rest):
+    outs, held = rest[:8], rest[8]
     for n, (own, got) in enumerate(((own_two, (a1, a2, a3)), (own_one, (b1, b2, b3)))):
         total = own[...]
         for ref in got:
             total = total + ref[...].astype(F32)
         held[n] = total.reshape(7, 8, 8, 128)
-
-    def plane(z):
-        return jnp.concatenate([held[n, :, z].reshape(56, 128) for n in range(2)], axis=0)
-
-    for q in range(8):
-        out[q] = plane(q).astype(BF)
-    keep[...] = plane(lax.axis_index("z"))
-
-
-def final_kernel(factor, got, own, one, two):
     z = lax.axis_index("z")
+    for d, out in enumerate(outs):
+        plane = [held[n, :, (z + d) & 7].reshape(56, 128) for n in range(2)]
+        out[...] = jnp.concatenate(plane, axis=0).astype(out.dtype)
+
+
+def final_kernel(factor, own, *rest):
+    got, (one, two) = rest[:7], rest[7:]
     total = own[...]
-    for d in range(1, 8):
-        total = total + got[(z + d) & 7].astype(F32)
+    for ref in got:
+        total = total + ref[...].astype(F32)
     total = (total * factor).reshape(2, 7, 8, 128)
     for out, which in ((two, 0), (one, 1)):
         for t in range(27):
@@ -368,8 +369,9 @@
     taps_two = conv_two.transpose(1, 2, 3, 0, 4).reshape(27, 256, 256)
     wide = near((4, 14, 16, 768), BF)
     quads = [near((7, 64, 128), BF)] * 3 + [near((7, 64, 128), F32)]
-    to_x = lambda parts: [send(p, ring_pairs(d + 1, 0)) for d, p in enumerate(parts)]
-    to_y = lambda parts: [send(p, ring_pairs(0, d + 1)) for d, p in enumerate(parts)]
+
+    def ring(parts, axis):
+        return [send(p, ring_pairs(**{axis: d + 1})) for d, p in enumerate(parts)]
 
     packed = call(
         pack_kernel,
@@ -381,65 +383,80 @@
     )
     ways = ((1, 0), (0, 1), (0, -1), (1, 1), (1, -1))
     sides = [send(p, block_pairs(*way)) for p, way in zip(packed, ways)]
-    act, inp, slope = call(
+    act, inp, slope, held_two = call(
         film_kernel,
         "film",
-        (timesteps, inputs, hidden, film_table),
-        "spph",
-        [near((768, 256), BF), near((4, 12, 16, 256), BF), near((768, 256), F32)],
-        [pltpu.VMEM((8, 512), F32), pltpu.SemaphoreType.DMA],
+        (timesteps, inputs, hidden, film_table, taps_two),
+        "shhhh",
+        [
+            near((768, 256), BF),
+            near((4, 12, 16, 256), BF),
+            near((768, 256), F32),
+            near((27, 256, 256), BF),
+        ],
+        [
+            pltpu.VMEM((8, 512), F32),
+            pltpu.VMEM((2, 4, 12, 16, 256), BF),
+            pltpu.SemaphoreType.DMA,
+            pltpu.SemaphoreType.DMA((2,)),
+            pltpu.SemaphoreType.DMA((3,)),
+        ],
     )
     wide_in, wide_cot, grad_hidden = call(
         first_kernel,
         "conv_two_back",
-        (block, inp, slope, *sides, taps_two),
-        "pvv" + "v" * 5 + "h",
+        (block, inp, slope, *sides, held_two),
+        "pvv" + "v" * 5 + "v",
         [wide, wide, near((4, 12, 16, 256), BF)],
-        [*CONV_SCRATCH, pltpu.VMEM((5, 4, 16, 256), F32)],
-    )
-
+        [pltpu.VMEM((768, 256), F32), pltpu.VMEM((5, 4, 16, 256), F32)],
+    )
+
+    split = near((4, 27, 64, 128), F32)
+    own_one, pair_one = call(
+        first_grad_kernel, "grad_one", (grad_hidden, wide_in), "vv", [split, split]
+    )
+    got_pair_one = send(pair_one, core_pairs())
     (pair_two,) = call(
-        second_pair_kernel, "grad_two_pair", (wide_cot, act), "vv", [near((9, 128, 768), F32)]
-    )
-    pair_two = send(pair_two, core_pairs())
-    (pair_one,) = call(
-        first_pair_kernel, "grad_one_pair", (grad_hidden, wide_in), "vv", [near((9, 256, 384), F32)]
-    )
-    pair_one = send(pair_one, core_pairs())
-    out, own_two = call(
-        second_own_kernel,
-        "grad_two_own",
-        (wide_cot, act, pair_two),
+        second_pair_kernel,
+        "grad_two_pair",
+        (wide_cot, act, pair_one),
         "vvv",
-        [near((4, 9, 32, 768), BF), far((9, 32, 768), F32)],
-        [pltpu.VMEM((9, 128, 768), F32), pltpu.SemaphoreType.DMA],
-    )
-    got_two = lax.all_to_all(out, ("xh", "ha"), 0, 0, tiled=True)
-    *parts, own_one = call(
-        first_own_kernel,
-        "grad_one_own",
-        (grad_hidden, wide_in, pair_one),
-        "vvv",
-        [near((27, 64, 128), BF)] * 3 + [far((27, 64, 128), F32)],
-        [
-            pltpu.VMEM((8, 4, 8, 384), F32),
-            pltpu.VMEM((27, 64, 128), F32),
-            pltpu.SemaphoreType.DMA,
-        ],
-    )
-    got_one = to_y(parts)
-
+        [near((9, 128, 768), F32)],
+    )
+    got_pair_two = send(pair_two, core_pairs())
     hi, lo = call(
         pack_columns_kernel,
         "pack_columns",
-        (grad_hidden, own_one),
-        "vh",
+        (grad_hidden, pair_two),
+        "vv",
         [near((4, 16, 256), BF)] * 2,
         [pltpu.VMEM((2, 768, 128), F32)],
     )
     left, right = send(hi, block_pairs(0, 1)), send(lo, block_pairs(0, -1))
+    out_one, own_one = call(
+        first_pair_kernel,
+        "grad_one_sum",
+        (own_one, got_pair_one),
+        "vv",
+        [far((4, 27, 64, 128), BF), far((27, 64, 128), F32)],
+    )
+    got_one = lax.all_to_all(out_one, "y", 0, 0, tiled=True)
+    *parts, own_two = call(
+        second_own_kernel,
+        "grad_two_own",
+        (wide_cot, act, got_pair_two, out_one),
+        "vvvh",
+        [near((9, 32, 768), BF)] * 3 + [far((9, 32, 768), F32)],
+        [pltpu.VMEM((128, 768), F32)],
+    )
+    got_two = ring(parts, "dx")
+
     (row,) = call(
-        pack_rows_kernel, "pack_rows", (grad_hidden, left, right), "vvv", [near((3, 4, 16, 256), BF)]
+        pack_rows_kernel,
+        "pack_rows",
+        (grad_hidden, left, right, parts[0]),
+        "vvvv",
+        [near((3, 4, 16, 256), BF)],
     )
     row = send(row, block_pairs(1, 0))
     (grad_input,) = call(
@@ -448,41 +465,50 @@
         (grad_hidden, block, row, left, right, taps_one),
         "vpvvvh",
         [(jax.ShapeDtypeStruct((4, 12, 16, 256), BF), "v")],
-        [*CONV_SCRATCH, pltpu.VMEM((4, 14, 16, 768), BF)],
-    )
-
+        [
+            pltpu.VMEM((27, 256, 256), BF),
+            pltpu.VMEM((768, 256), F32),
+            pltpu.SemaphoreType.DMA((3,)),
+            pltpu.VMEM((4, 14, 16, 768), BF),
+        ],
+    )
+
+    *parts, own_one = call(
+        first_y_kernel,
+        "grad_one_y",
+        (got_one, own_one, grad_input),
+        "vph",
+        quads,
+        [pltpu.VMEM((4, 64, 128), F32)],
+    )
+    got_one = ring(parts, "dx")
     *parts, own_two = call(
         second_x_kernel,
         "grad_two_x",
-        (got_two, own_two, grad_input),
-        "vph",
+        (*got_two, own_two, grad_input),
+        "vvvph",
         quads,
         [pltpu.VMEM((8, 4, 8, 128), F32)],
     )
-    got_two = to_y(parts)
-    *parts, own_one = call(
-        first_y_kernel,
-        "grad_one_y",
-        (*got_one, own_one),
-        "vvvp",
-        quads,
-        [pltpu.VMEM((4, 64, 128), F32)],
-    )
-    got_one = to_x(parts)
-
-    out, own = call(
+    got_two = ring(parts, "dy")
+
+    own, *parts = call(
         last_kernel,
         "last_stage",
         (own_two, *got_two, own_one, *got_one),
         "v" * 8,
-        [near((8, 112, 128), BF), near((112, 128), F32)],
+        [near((112, 128), F32)] + [near((112, 128), BF)] * 7,
         [pltpu.VMEM((2, 7, 8, 8, 128), F32)],
     )
-    planes = lax.all_to_all(out, "z", 0, 0, tiled=True)
+    planes = ring(parts, "dz")
     factor = float(256 * 768) ** (-0.5)
     result = jax.ShapeDtypeStruct((27, 8, 32), F32), "v"
     grad_one, grad_two = call(
-        functools.partial(final_kernel, factor), "final_sum", (planes, own), "vv", [result, result]
+        functools.partial(final_kernel, factor),
+        "final_sum",
+        (own, *planes),
+        "v" * 8,
+        [result, result],
     )
     shape = lambda g: g.transpose(2, 0, 1).reshape(32, 3, 3, 3, 8)
     return grad_input[None], shape(grad_one), shape(grad_two)

time: 116 us -> 117 us (level)
  the two profiles are of different devices: /device:TPU:24 before, /device:TPU:2 now
where the time goes in v4:
time: 117 us; the launch traced here: 116 us
  starting transfers between devices  51.8 us (44%)
  waiting for transfers between devices  30.8 us (26%)
  Pallas kernels  29.6 us (25%)
  local copies, waits for them, and re-layouts  2.4 us (2%)
  between operations  1.53 us (1%)
    ppermute x26, starting transfers between devices, send(): return lax.ppermute(value, AX, pairs)  47.2 us
    ppermute x26, waiting for transfers between devices, send(): return lax.ppermute(value, AX, pairs)  30.8 us
    pallas_call x14, Pallas kernels, call(): pl.pallas_call(kernel, out_shape=tuple((o for o, _ in outs)), in_specs=[s...  29.6 us
    all_to_all x1, starting transfers between devices, shards(): got_one = lax.all_to_all(out_one, 'y', 0, 0, tiled=True)  4.57 us
    unnamed x12, local copies, waits for them, and re-layouts  2.4 us
  transfers between devices with their start and end apart: 27, of which 7 were waited for; matrix products, arithmetic and copies ran while one was open for 0% of the time, Pallas kernels for 18%

profile of v4, /device:TPU:2, one launch (start us, length us, event | category | flops | bytes accessed | tf_op | source)
XLA Modules:
  0.0 116.1 jit_solution(5361329476734541670)
XLA Ops:
  1.9 2.4 %collective-permute-start = (bf16[2,4,16,256]{3,2,1,0:T(8,128)(2,1)S(1)}, bf16[2,4,16,256]{3,2,1,0:T(8,128)(2,1)S(1)}, u32[]{:S(2)}, u32[]{:S(2)}) collective-permute-start(bf16[2,4,16,256]{3,2,1,0:T(8,128)(2,1)S(1)} %get-tuple-element.45), channel_id=1, source_target_pairs={{0,4},{1,5},{2,6},{3,7},{4,0},{5,1},{6,2},{7,3},{8,12},{9,13},{10,... | collective-permute-start | bytes 196616 | tf_op jit(solution)/shard_map/ppermute | solution.py:40
  4.3 3.2 %collective-permute-start.2 = (bf16[2,4,16,256]{3,2,1,0:T(8,128)(2,1)S(1)}, bf16[2,4,16,256]{3,2,1,0:T(8,128)(2,1)S(1)}, u32[]{:S(2)}, u32[]{:S(2)}) collective-permute-start(bf16[2,4,16,256]{3,2,1,0:T(8,128)(2,1)S(1)} %get-tuple-element.47), channel_id=1, source_target_pairs={{0,3},{1,0},{2,1},{3,2},{4,7},{5,4},{6,5},{7,6},{8,11},{9,8},{10,9... | collective-permute-start | bytes 196616 | tf_op jit(solution)/shard_map/ppermute | solution.py:40
  9.9 2.4 %film.1 = (bf16[768,256]{1,0:T(8,128)(2,1)S(1)}, bf16[4,12,16,256]{3,2,1,0:T(8,128)(2,1)S(1)}, f32[768,256]{1,0:T(8,128)S(1)}, bf16[27,256,256]{2,1,0:T(8,128)(2,1)S(1)}) custom-call(s32[1]{0:T(128)S(6)} %copy.10.step, bf16[4,12,16,256]{3,2,1,0:T(8,128)(2,1)} %bitcast.23, bf16[4,12,16,256]{3,2,1,0:T(8,128)(2,1)} %bitcast.24, f32[1000,512]{1,0:T(8,128)} %table.1, ...), custom_call_target="tpu_custom_call" | custom-call | tf_op jit(solution)/shard_map/film/pallas_call | solution.py:50
  12.4 3.8 %conv_two_back.1 = (bf16[4,14,16,768]{3,2,1,0:T(8,128)(2,1)S(1)}, bf16[4,14,16,768]{3,2,1,0:T(8,128)(2,1)S(1)}, bf16[4,12,16,256]{3,2,1,0:T(8,128)(2,1)S(1)}) custom-call(bf16[4,12,16,256]{3,2,1,0:T(8,128)(2,1)} %bitcast.20, bf16[4,12,16,256]{3,2,1,0:T(8,128)(2,1)S(1)} %get-tuple-element.43.inp, f32[768,256]{1,0:T(8,128)S(1)} %get-tuple-element.44.slope, ...), custom_call_target="tpu_custom_call" | custom-call | tf_op jit(solution)/shard_map/conv_two_back/pallas_call | solution.py:50
  16.2 2.6 %grad_one.1 = (f32[4,27,64,128]{3,2,1,0:T(8,128)S(1)}, f32[4,27,64,128]{3,2,1,0:T(8,128)S(1)}) custom-call(bf16[4,12,16,256]{3,2,1,0:T(8,128)(2,1)S(1)} %get-tuple-element.51.hid.block, bf16[4,14,16,768]{3,2,1,0:T(8,128)(2,1)S(1)} %get-tuple-element.54.wide), custom_call_target="tpu_custom_call" | custom-call | tf_op jit(solution)/shard_map/grad_one/pallas_call | solution.py:50
  21.0 4.2 %collective-permute-done.8.pair = f32[4,27,64,128]{3,2,1,0:T(8,128)S(1)} collective-permute-done((f32[4,27,64,128]{3,2,1,0:T(8,128)S(1)}, f32[4,27,64,128]{3,2,1,0:T(8,128)S(1)}, u32[]{:S(2)}, u32[]{:S(2)}) %collective-permute-start.8) | collective-permute-done | bytes 3538976 | tf_op jit(solution)/shard_map/ppermute | solution.py:40
  25.1 1.9 %grad_one_sum.1 = (bf16[4,27,64,128]{3,2,1,0:T(8,128)(2,1)}, f32[27,64,128]{2,1,0:T(8,128)}) custom-call(f32[4,27,64,128]{3,2,1,0:T(8,128)S(1)} %get-tuple-element.58.own, f32[4,27,64,128]{3,2,1,0:T(8,128)S(1)} %collective-permute-done.8.pair), custom_call_target="tpu_custom_call" | custom-call | tf_op jit(solution)/shard_map/grad_one_sum/pallas_call | solution.py:50
  27.0 4.6 %all-to-all-start = ((bf16[4,27,64,128]{3,2,1,0:T(8,128)(2,1)}), bf16[4,27,64,128]{3,2,1,0:T(8,128)(2,1)}, u32[]{:S(2)}, u32[]{:S(2)}) async-start(bf16[4,27,64,128]{3,2,1,0:T(8,128)(2,1)} %get-tuple-element.59.after), calls=%async_computation | async-start | bytes 3538944 | tf_op jit(solution)/shard_map/all_to_all | solution.py:443
  34.0 5.0 %grad_two_own.1 = (bf16[9,32,768]{2,1,0:T(8,128)(2,1)S(1)}, bf16[9,32,768]{2,1,0:T(8,128)(2,1)S(1)}, bf16[9,32,768]{2,1,0:T(8,128)(2,1)S(1)}, f32[9,32,768]{2,1,0:T(8,128)}) custom-call(bf16[4,14,16,768]{3,2,1,0:T(8,128)(2,1)S(1)} %copy-done.3, bf16[768,256]{1,0:T(8,128)(2,1)S(1)} %copy-done.5, f32[9,128,768]{2,1,0:T(8,128)} %collective-permute-done.7.got, ...), custom_call_target="tpu_custom_call" | custom-call | tf_op jit(solution)/shard_map/grad_two_own/pallas_call | solution.py:50
  39.5 3.1 %collective-permute-start.11 = (bf16[9,32,768]{2,1,0:T(8,128)(2,1)S(1)}, bf16[9,32,768]{2,1,0:T(8,128)(2,1)S(1)}, u32[]{:S(2)}, u32[]{:S(2)}) collective-permute-start(bf16[9,32,768]{2,1,0:T(8,128)(2,1)S(1)} %get-tuple-element.61), channel_id=1, source_target_pairs={{0,2},{1,3},{2,0},{3,1},{4,6},{5,7},{6,4},{7,5},{8,10},{9,11},{10,... | collective-permute-start | bytes 1327112 | tf_op jit(solution)/shard_map/ppermute | solution.py:40
  43.7 3.2 %collective-permute-start.6 = (bf16[4,16,256]{2,1,0:T(8,128)(2,1)S(1)}, bf16[4,16,256]{2,1,0:T(8,128)(2,1)S(1)}, u32[]{:S(2)}, u32[]{:S(2)}) collective-permute-start(bf16[4,16,256]{2,1,0:T(8,128)(2,1)S(1)} %get-tuple-element.57), channel_id=1, source_target_pairs={{0,3},{1,0},{2,1},{3,2},{4,7},{5,4},{6,5},{7,6},{8,11},{9,8},{10,9... | collective-permute-start | bytes 98312 | tf_op jit(solution)/shard_map/ppermute | solution.py:40
  47.0 15.6 %collective-permute-done.5.left = bf16[4,16,256]{2,1,0:T(8,128)(2,1)S(1)} collective-permute-done((bf16[4,16,256]{2,1,0:T(8,128)(2,1)S(1)}, bf16[4,16,256]{2,1,0:T(8,128)(2,1)S(1)}, u32[]{:S(2)}, u32[]{:S(2)}) %collective-permute-start.5) | collective-permute-done | bytes 32800 | tf_op jit(solution)/shard_map/ppermute | solution.py:40
  63.8 4.3 %collective-permute-done.9.row = bf16[3,4,16,256]{3,2,1,0:T(8,128)(2,1)S(1)} collective-permute-done((bf16[3,4,16,256]{3,2,1,0:T(8,128)(2,1)S(1)}, bf16[3,4,16,256]{3,2,1,0:T(8,128)(2,1)S(1)}, u32[]{:S(2)}, u32[]{:S(2)}) %collective-permute-start.9) | collective-permute-done | bytes 98336 | tf_op jit(solution)/shard_map/ppermute | solution.py:40
  68.1 6.0 %conv_one_back.1.after = bf16[4,12,16,256]{3,2,1,0:T(8,128)(2,1)} custom-call(bf16[4,12,16,256]{3,2,1,0:T(8,128)(2,1)S(1)} %copy-done.1, bf16[4,12,16,256]{3,2,1,0:T(8,128)(2,1)} %bitcast.21, bf16[3,4,16,256]{3,2,1,0:T(8,128)(2,1)S(1)} %collective-permute-done.9.row, bf16[4,16,256]{2,1,0:T(8,128)(2,1)S(1)} %collective-permute-done.5.left, ...), custom_call_target="tpu_custom_call" | custom-call | tf_op jit(solution)/shard_map/conv_one_back/pallas_call | solution.py:50
  77.3 2.8 %collective-permute-start.14 = (bf16[7,64,128]{2,1,0:T(8,128)(2,1)S(1)}, bf16[7,64,128]{2,1,0:T(8,128)(2,1)S(1)}, u32[]{:S(2)}, u32[]{:S(2)}) collective-permute-start(bf16[7,64,128]{2,1,0:T(8,128)(2,1)S(1)} %get-tuple-element.66), channel_id=1, source_target_pairs={{0,16},{1,17},{2,18},{3,19},{4,20},{5,21},{6,22},{7,23},{8,24},{9,... | collective-permute-start | bytes 344072 | tf_op jit(solution)/shard_map/ppermute | solution.py:40
  81.5 2.5 %grad_one_y.1 = (bf16[7,64,128]{2,1,0:T(8,128)(2,1)S(1)}, bf16[7,64,128]{2,1,0:T(8,128)(2,1)S(1)}, bf16[7,64,128]{2,1,0:T(8,128)(2,1)S(1)}, f32[7,64,128]{2,1,0:T(8,128)S(1)}) custom-call(bf16[4,27,64,128]{3,2,1,0:T(8,128)(2,1)} %all-to-all-done.got, f32[27,64,128]{2,1,0:T(8,128)} %get-tuple-element.68.own, bf16[4,12,16,256]{3,2,1,0:T(8,128)(2,1)} %conv_one_back.1.after), custom_call_target="tpu_custom_call" | custom-call | tf_op jit(solution)/shard_map/grad_one_y/pallas_call | solution.py:50
  85.7 1.9 %collective-permute-start.17 = (bf16[7,64,128]{2,1,0:T(8,128)(2,1)S(1)}, bf16[7,64,128]{2,1,0:T(8,128)(2,1)S(1)}, u32[]{:S(2)}, u32[]{:S(2)}) collective-permute-start(bf16[7,64,128]{2,1,0:T(8,128)(2,1)S(1)} %get-tuple-element.71), channel_id=1, source_target_pairs={{0,2},{1,3},{2,0},{3,1},{4,6},{5,7},{6,4},{7,5},{8,10},{9,11},{10,... | collective-permute-start | bytes 344072 | tf_op jit(solution)/shard_map/ppermute | solution.py:40
  87.6 2.3 %collective-permute-start.18 = (bf16[7,64,128]{2,1,0:T(8,128)(2,1)S(1)}, bf16[7,64,128]{2,1,0:T(8,128)(2,1)S(1)}, u32[]{:S(2)}, u32[]{:S(2)}) collective-permute-start(bf16[7,64,128]{2,1,0:T(8,128)(2,1)S(1)} %get-tuple-element.72), channel_id=1, source_target_pairs={{0,6},{1,7},{2,4},{3,5},{4,0},{5,1},{6,2},{7,3},{8,14},{9,15},{10,... | collective-permute-start | bytes 344072 | tf_op jit(solution)/shard_map/ppermute | solution.py:40
  90.0 2.6 %collective-permute-done.17.b2 = bf16[7,64,128]{2,1,0:T(8,128)(2,1)S(1)} collective-permute-done((bf16[7,64,128]{2,1,0:T(8,128)(2,1)S(1)}, bf16[7,64,128]{2,1,0:T(8,128)(2,1)S(1)}, u32[]{:S(2)}, u32[]{:S(2)}) %collective-permute-start.17) | collective-permute-done | bytes 114720 | tf_op jit(solution)/shard_map/ppermute | solution.py:40
  93.9 2.0 %collective-permute-start.19 = (bf16[112,128]{1,0:T(8,128)(2,1)S(1)}, bf16[112,128]{1,0:T(8,128)(2,1)S(1)}, u32[]{:S(2)}, u32[]{:S(2)}) collective-permute-start(bf16[112,128]{1,0:T(8,128)(2,1)S(1)} %get-tuple-element.74), channel_id=1, source_target_pairs={{0,32},{1,33},{2,34},{3,35},{4,36},{5,37},{6,38},{7,39},{8,40},{9,... | collective-permute-start | bytes 86024 | tf_op jit(solution)/shard_map/ppermute | solution.py:40
  95.9 3.3 %collective-permute-start.20 = (bf16[112,128]{1,0:T(8,128)(2,1)S(1)}, bf16[112,128]{1,0:T(8,128)(2,1)S(1)}, u32[]{:S(2)}, u32[]{:S(2)}) collective-permute-start(bf16[112,128]{1,0:T(8,128)(2,1)S(1)} %get-tuple-element.75), channel_id=1, source_target_pairs={{0,64},{1,65},{2,66},{3,67},{4,68},{5,69},{6,70},{7,71},{8,72},{9,... | collective-permute-start | bytes 86024 | tf_op jit(solution)/shard_map/ppermute | solution.py:40
  99.2 4.0 %collective-permute-start.21 = (bf16[112,128]{1,0:T(8,128)(2,1)S(1)}, bf16[112,128]{1,0:T(8,128)(2,1)S(1)}, u32[]{:S(2)}, u32[]{:S(2)}) collective-permute-start(bf16[112,128]{1,0:T(8,128)(2,1)S(1)} %get-tuple-element.76), channel_id=1, source_target_pairs={{0,96},{1,97},{2,98},{3,99},{4,100},{5,101},{6,102},{7,103},{8,104... | collective-permute-start | bytes 86024 | tf_op jit(solution)/shard_map/ppermute | solution.py:40
  103.8 4.9 %collective-permute-start.23 = (bf16[112,128]{1,0:T(8,128)(2,1)S(1)}, bf16[112,128]{1,0:T(8,128)(2,1)S(1)}, u32[]{:S(2)}, u32[]{:S(2)}) collective-permute-start(bf16[112,128]{1,0:T(8,128)(2,1)S(1)} %get-tuple-element.78), channel_id=1, source_target_pairs={{0,160},{1,161},{2,162},{3,163},{4,164},{5,165},{6,166},{7,167},{8... | collective-permute-start | bytes 86024 | tf_op jit(solution)/shard_map/ppermute | solution.py:40
  108.7 2.7 %collective-permute-start.24 = (bf16[112,128]{1,0:T(8,128)(2,1)S(1)}, bf16[112,128]{1,0:T(8,128)(2,1)S(1)}, u32[]{:S(2)}, u32[]{:S(2)}) collective-permute-start(bf16[112,128]{1,0:T(8,128)(2,1)S(1)} %get-tuple-element.79), channel_id=1, source_target_pairs={{0,192},{1,193},{2,194},{3,195},{4,196},{5,197},{6,198},{7,199},{8... | collective-permute-start | bytes 86024 | tf_op jit(solution)/shard_map/ppermute | solution.py:40
  (56 shorter events, 23.2 us)
Async XLA Ops:
  1.9 10.4 %collective-permute-start = (bf16[2,4,16,256]{3,2,1,0:T(8,128)(2,1)S(1)}, bf16[2,4,16,256]{3,2,1,0:T(8,128)(2,1)S(1)}, u32[]{:S(2)}, u32[]{:S(2)}) collective-permute-start(bf16[2,4,16,256]{3,2,1,0:T(8,128)(2,1)S(1)} %get-tuple-element.45), channel_id=1, source_target_pairs={{0,4},{1,5},{2,6},{3,7},{4,0},{5,1},{6,2},{7,3},{8,12},{9,13},{10,... | collective-permute-start | bytes 196616 | tf_op jit(solution)/shard_map/ppermute | solution.py:40
  4.3 8.0 %collective-permute-start.1 = (bf16[2,4,16,256]{3,2,1,0:T(8,128)(2,1)S(1)}, bf16[2,4,16,256]{3,2,1,0:T(8,128)(2,1)S(1)}, u32[]{:S(2)}, u32[]{:S(2)}) collective-permute-start(bf16[2,4,16,256]{3,2,1,0:T(8,128)(2,1)S(1)} %get-tuple-element.46), channel_id=1, source_target_pairs={{0,1},{1,2},{2,3},{3,0},{4,5},{5,6},{6,7},{7,4},{8,9},{9,10},{10,1... | collective-permute-start | bytes 196616 | tf_op jit(solution)/shard_map/ppermute | solution.py:40
  4.3 8.0 %collective-permute-start.2 = (bf16[2,4,16,256]{3,2,1,0:T(8,128)(2,1)S(1)}, bf16[2,4,16,256]{3,2,1,0:T(8,128)(2,1)S(1)}, u32[]{:S(2)}, u32[]{:S(2)}) collective-permute-start(bf16[2,4,16,256]{3,2,1,0:T(8,128)(2,1)S(1)} %get-tuple-element.47), channel_id=1, source_target_pairs={{0,3},{1,0},{2,1},{3,2},{4,7},{5,4},{6,5},{7,6},{8,11},{9,8},{10,9... | collective-permute-start | bytes 196616 | tf_op jit(solution)/shard_map/ppermute | solution.py:40
  7.6 4.8 %collective-permute-start.4 = (bf16[2,4,16,256]{3,2,1,0:T(8,128)(2,1)S(1)}, bf16[2,4,16,256]{3,2,1,0:T(8,128)(2,1)S(1)}, u32[]{:S(2)}, u32[]{:S(2)}) collective-permute-start(bf16[2,4,16,256]{3,2,1,0:T(8,128)(2,1)S(1)} %get-tuple-element.49), channel_id=1, source_target_pairs={{0,7},{1,4},{2,5},{3,6},{4,3},{5,0},{6,1},{7,2},{8,15},{9,12},{10,... | collective-permute-start | bytes 196616 | tf_op jit(solution)/shard_map/ppermute | solution.py:40
  18.8 6.3 %collective-permute-start.8 = (f32[4,27,64,128]{3,2,1,0:T(8,128)S(1)}, f32[4,27,64,128]{3,2,1,0:T(8,128)S(1)}, u32[]{:S(2)}, u32[]{:S(2)}) collective-permute-start(f32[4,27,64,128]{3,2,1,0:T(8,128)S(1)} %get-tuple-element.55.after), channel_id=1, source_target_pairs={{0,1},{1,0},{2,3},{3,2},{4,5},{5,4},{6,7},{7,6},{8,9},{9,8},{10,11... | collective-permute-start | bytes 10616840 | tf_op jit(solution)/shard_map/ppermute | solution.py:40
  20.4 11.2 %collective-permute-start.7 = (f32[9,128,768]{2,1,0:T(8,128)S(1)}, f32[9,128,768]{2,1,0:T(8,128)}, u32[]{:S(2)}, u32[]{:S(2)}) collective-permute-start(f32[9,128,768]{2,1,0:T(8,128)S(1)} %grad_two_pair.1.after), channel_id=1, source_target_pairs={{0,1},{1,0},{2,3},{3,2},{4,5},{5,4},{6,7},{7,6},{8,9},{9,8},{10,11... | collective-permute-start | bytes 10616840 | tf_op jit(solution)/shard_map/ppermute | solution.py:40
  27.0 54.5 %all-to-all-start = ((bf16[4,27,64,128]{3,2,1,0:T(8,128)(2,1)}), bf16[4,27,64,128]{3,2,1,0:T(8,128)(2,1)}, u32[]{:S(2)}, u32[]{:S(2)}) async-start(bf16[4,27,64,128]{3,2,1,0:T(8,128)(2,1)} %get-tuple-element.59.after), calls=%async_computation | async-start | bytes 3538944 | tf_op jit(solution)/shard_map/all_to_all | solution.py:443
  39.0 35.1 %collective-permute-start.10 = (bf16[9,32,768]{2,1,0:T(8,128)(2,1)S(1)}, bf16[9,32,768]{2,1,0:T(8,128)(2,1)S(1)}, u32[]{:S(2)}, u32[]{:S(2)}) collective-permute-start(bf16[9,32,768]{2,1,0:T(8,128)(2,1)S(1)} %get-tuple-element.60.after), channel_id=1, source_target_pairs={{0,4},{1,5},{2,6},{3,7},{4,2},{5,3},{6,0},{7,1},{8,12},{9,13},{10,... | collective-permute-start | bytes 1327112 | tf_op jit(solution)/shard_map/ppermute | solution.py:40
  39.5 34.6 %collective-permute-start.11 = (bf16[9,32,768]{2,1,0:T(8,128)(2,1)S(1)}, bf16[9,32,768]{2,1,0:T(8,128)(2,1)S(1)}, u32[]{:S(2)}, u32[]{:S(2)}) collective-permute-start(bf16[9,32,768]{2,1,0:T(8,128)(2,1)S(1)} %get-tuple-element.61), channel_id=1, source_target_pairs={{0,2},{1,3},{2,0},{3,1},{4,6},{5,7},{6,4},{7,5},{8,10},{9,11},{10,... | collective-permute-start | bytes 1327112 | tf_op jit(solution)/shard_map/ppermute | solution.py:40
  42.6 31.5 %collective-permute-start.12 = (bf16[9,32,768]{2,1,0:T(8,128)(2,1)S(1)}, bf16[9,32,768]{2,1,0:T(8,128)(2,1)S(1)}, u32[]{:S(2)}, u32[]{:S(2)}) collective-permute-start(bf16[9,32,768]{2,1,0:T(8,128)(2,1)S(1)} %get-tuple-element.62), channel_id=1, source_target_pairs={{0,6},{1,7},{2,4},{3,5},{4,0},{5,1},{6,2},{7,3},{8,14},{9,15},{10,... | collective-permute-start | bytes 1327112 | tf_op jit(solution)/shard_map/ppermute | solution.py:40
  43.6 18.9 %collective-permute-start.5 = (bf16[4,16,256]{2,1,0:T(8,128)(2,1)S(1)}, bf16[4,16,256]{2,1,0:T(8,128)(2,1)S(1)}, u32[]{:S(2)}, u32[]{:S(2)}) collective-permute-start(bf16[4,16,256]{2,1,0:T(8,128)(2,1)S(1)} %get-tuple-element.56), channel_id=1, source_target_pairs={{0,1},{1,2},{2,3},{3,0},{4,5},{5,6},{6,7},{7,4},{8,9},{9,10},{10,1... | collective-permute-start | bytes 98312 | tf_op jit(solution)/shard_map/ppermute | solution.py:40
  43.7 18.8 %collective-permute-start.6 = (bf16[4,16,256]{2,1,0:T(8,128)(2,1)S(1)}, bf16[4,16,256]{2,1,0:T(8,128)(2,1)S(1)}, u32[]{:S(2)}, u32[]{:S(2)}) collective-permute-start(bf16[4,16,256]{2,1,0:T(8,128)(2,1)S(1)} %get-tuple-element.57), channel_id=1, source_target_pairs={{0,3},{1,0},{2,1},{3,2},{4,7},{5,4},{6,5},{7,6},{8,11},{9,8},{10,9... | collective-permute-start | bytes 98312 | tf_op jit(solution)/shard_map/ppermute | solution.py:40
  62.6 5.5 %collective-permute-start.9 = (bf16[3,4,16,256]{3,2,1,0:T(8,128)(2,1)S(1)}, bf16[3,4,16,256]{3,2,1,0:T(8,128)(2,1)S(1)}, u32[]{:S(2)}, u32[]{:S(2)}) collective-permute-start(bf16[3,4,16,256]{3,2,1,0:T(8,128)(2,1)S(1)} %pack_rows.1), channel_id=1, source_target_pairs={{0,4},{1,5},{2,6},{3,7},{4,0},{5,1},{6,2},{7,3},{8,12},{9,13},{10,... | collective-permute-start | bytes 294920 | tf_op jit(solution)/shard_map/ppermute | solution.py:40
  75.7 11.9 %collective-permute-start.13 = (bf16[7,64,128]{2,1,0:T(8,128)(2,1)S(1)}, bf16[7,64,128]{2,1,0:T(8,128)(2,1)S(1)}, u32[]{:S(2)}, u32[]{:S(2)}) collective-permute-start(bf16[7,64,128]{2,1,0:T(8,128)(2,1)S(1)} %get-tuple-element.65), channel_id=1, source_target_pairs={{0,8},{1,9},{2,10},{3,11},{4,12},{5,13},{6,14},{7,15},{8,16},{9,17... | collective-permute-start | bytes 344072 | tf_op jit(solution)/shard_map/ppermute | solution.py:40
  77.3 12.7 %collective-permute-start.14 = (bf16[7,64,128]{2,1,0:T(8,128)(2,1)S(1)}, bf16[7,64,128]{2,1,0:T(8,128)(2,1)S(1)}, u32[]{:S(2)}, u32[]{:S(2)}) collective-permute-start(bf16[7,64,128]{2,1,0:T(8,128)(2,1)S(1)} %get-tuple-element.66), channel_id=1, source_target_pairs={{0,16},{1,17},{2,18},{3,19},{4,20},{5,21},{6,22},{7,23},{8,24},{9,... | collective-permute-start | bytes 344072 | tf_op jit(solution)/shard_map/ppermute | solution.py:40
  80.1 9.9 %collective-permute-start.15 = (bf16[7,64,128]{2,1,0:T(8,128)(2,1)S(1)}, bf16[7,64,128]{2,1,0:T(8,128)(2,1)S(1)}, u32[]{:S(2)}, u32[]{:S(2)}) collective-permute-start(bf16[7,64,128]{2,1,0:T(8,128)(2,1)S(1)} %get-tuple-element.67), channel_id=1, source_target_pairs={{0,24},{1,25},{2,26},{3,27},{4,28},{5,29},{6,30},{7,31},{8,0},{9,1... | collective-permute-start | bytes 344072 | tf_op jit(solution)/shard_map/ppermute | solution.py:40
  84.0 6.0 %collective-permute-start.16 = (bf16[7,64,128]{2,1,0:T(8,128)(2,1)S(1)}, bf16[7,64,128]{2,1,0:T(8,128)(2,1)S(1)}, u32[]{:S(2)}, u32[]{:S(2)}) collective-permute-start(bf16[7,64,128]{2,1,0:T(8,128)(2,1)S(1)} %get-tuple-element.70), channel_id=1, source_target_pairs={{0,4},{1,5},{2,6},{3,7},{4,2},{5,3},{6,0},{7,1},{8,12},{9,13},{10,... | collective-permute-start | bytes 344072 | tf_op jit(solution)/shard_map/ppermute | solution.py:40
  85.7 6.9 %collective-permute-start.17 = (bf16[7,64,128]{2,1,0:T(8,128)(2,1)S(1)}, bf16[7,64,128]{2,1,0:T(8,128)(2,1)S(1)}, u32[]{:S(2)}, u32[]{:S(2)}) collective-permute-start(bf16[7,64,128]{2,1,0:T(8,128)(2,1)S(1)} %get-tuple-element.71), channel_id=1, source_target_pairs={{0,2},{1,3},{2,0},{3,1},{4,6},{5,7},{6,4},{7,5},{8,10},{9,11},{10,... | collective-permute-start | bytes 344072 | tf_op jit(solution)/shard_map/ppermute | solution.py:40
  87.6 6.1 %collective-permute-start.18 = (bf16[7,64,128]{2,1,0:T(8,128)(2,1)S(1)}, bf16[7,64,128]{2,1,0:T(8,128)(2,1)S(1)}, u32[]{:S(2)}, u32[]{:S(2)}) collective-permute-start(bf16[7,64,128]{2,1,0:T(8,128)(2,1)S(1)} %get-tuple-element.72), channel_id=1, source_target_pairs={{0,6},{1,7},{2,4},{3,5},{4,0},{5,1},{6,2},{7,3},{8,14},{9,15},{10,... | collective-permute-start | bytes 344072 | tf_op jit(solution)/shard_map/ppermute | solution.py:40
  93.9 14.8 %collective-permute-start.19 = (bf16[112,128]{1,0:T(8,128)(2,1)S(1)}, bf16[112,128]{1,0:T(8,128)(2,1)S(1)}, u32[]{:S(2)}, u32[]{:S(2)}) collective-permute-start(bf16[112,128]{1,0:T(8,128)(2,1)S(1)} %get-tuple-element.74), channel_id=1, source_target_pairs={{0,32},{1,33},{2,34},{3,35},{4,36},{5,37},{6,38},{7,39},{8,40},{9,... | collective-permute-start | bytes 86024 | tf_op jit(solution)/shard_map/ppermute | solution.py:40
  95.9 15.5 %collective-permute-start.20 = (bf16[112,128]{1,0:T(8,128)(2,1)S(1)}, bf16[112,128]{1,0:T(8,128)(2,1)S(1)}, u32[]{:S(2)}, u32[]{:S(2)}) collective-permute-start(bf16[112,128]{1,0:T(8,128)(2,1)S(1)} %get-tuple-element.75), channel_id=1, source_target_pairs={{0,64},{1,65},{2,66},{3,67},{4,68},{5,69},{6,70},{7,71},{8,72},{9,... | collective-permute-start | bytes 86024 | tf_op jit(solution)/shard_map/ppermute | solution.py:40
  99.2 13.2 %collective-permute-start.21 = (bf16[112,128]{1,0:T(8,128)(2,1)S(1)}, bf16[112,128]{1,0:T(8,128)(2,1)S(1)}, u32[]{:S(2)}, u32[]{:S(2)}) collective-permute-start(bf16[112,128]{1,0:T(8,128)(2,1)S(1)} %get-tuple-element.76), channel_id=1, source_target_pairs={{0,96},{1,97},{2,98},{3,99},{4,100},{5,101},{6,102},{7,103},{8,104... | collective-permute-start | bytes 86024 | tf_op jit(solution)/shard_map/ppermute | solution.py:40
  103.2 9.1 %collective-permute-start.22 = (bf16[112,128]{1,0:T(8,128)(2,1)S(1)}, bf16[112,128]{1,0:T(8,128)(2,1)S(1)}, u32[]{:S(2)}, u32[]{:S(2)}) collective-permute-start(bf16[112,128]{1,0:T(8,128)(2,1)S(1)} %get-tuple-element.77), channel_id=1, source_target_pairs={{0,128},{1,129},{2,130},{3,131},{4,132},{5,133},{6,134},{7,135},{8... | collective-permute-start | bytes 86024 | tf_op jit(solution)/shard_map/ppermute | solution.py:40
  103.8 8.6 %collective-permute-start.23 = (bf16[112,128]{1,0:T(8,128)(2,1)S(1)}, bf16[112,128]{1,0:T(8,128)(2,1)S(1)}, u32[]{:S(2)}, u32[]{:S(2)}) collective-permute-start(bf16[112,128]{1,0:T(8,128)(2,1)S(1)} %get-tuple-element.78), channel_id=1, source_target_pairs={{0,160},{1,161},{2,162},{3,163},{4,164},{5,165},{6,166},{7,167},{8... | collective-permute-start | bytes 86024 | tf_op jit(solution)/shard_map/ppermute | solution.py:40
  (9 other events, 42.8 us)

commit v5 on v4

--- a/solution.py
+++ b/solution.py
@@ -27,11 +27,11 @@
     return [(i, i // 8 * 8 + (i // 4 % 2 ^ dh) * 4 + (i + dw) % 4) for i in range(256)]
 
 
-def ring_pairs(dx=0, dy=0, dz=0):
+def ring_pairs(dx=0, dy=0):
     pairs = []
     for i in range(256):
         core, xh, ha, y, z = i % 2, i // 2 % 2, i // 4 % 2, i // 8 % 4, i // 32
-        x, y, z = (xh * 2 + ha + dx) % 4, (y + dy) % 4, (z + dz) % 8
+        x, y = (xh * 2 + ha + dx) % 4, (y + dy) % 4
         pairs.append((i, ((z * 4 + y) * 2 + x % 2) * 4 + x // 2 * 2 + core))
     return pairs
 
@@ -95,8 +95,7 @@
                     corner[n, f, :, lanes] = jnp.broadcast_to(cell, (16, 128)).astype(BF)
 
 
-def pack_columns_kernel(block, after, hi, lo, wide):
-    del after
+def pack_columns_kernel(block, hi, lo, wide):
     spread(wide, block)
     for f in range(4):
         for j, out in ((15, hi), (0, lo)):
@@ -173,7 +172,7 @@
 
 def channel_order():
     lane = lax.broadcasted_iota(jnp.int32, (256, 256), 1)
-    goal, kept = (lane >> 5) & 3, lax.axis_index("core") ^ (lane >> 7)
+    goal, kept = (x_place() + (lane >> 5)) & 3, lax.axis_index("core") ^ (lane >> 7)
     source = ((goal & 1) << 7) + ((goal >> 1) << 6) + (kept << 5) + (lane & 31)
     return (lax.broadcasted_iota(jnp.int32, (256, 256), 0) == source).astype(BF)
 
@@ -212,29 +211,20 @@
 
 
 def first_kernel(
-    block, inp, slope, row, left, right, corner_left, corner_right, taps,
-    wide_in, wide, hid_out, total, side,
+    block, slope, row, left, right, corner_left, corner_right, taps, wide, hid_out, total,
 ):
     sides = (row, left, right, corner_left, corner_right)
     build_shifted(
         put_back(wide), lambda f, r: block[f, r], *[lambda f, s=s: s[0, f] for s in sides]
     )
-    order = channel_order()
-    for n, ref in enumerate(sides):
-        cells = jnp.dot(ref[1].reshape(64, 256), order, preferred_element_type=F32)
-        side[n] = cells.reshape(4, 16, 256)
-
-    def put(f, r, which, cells):
-        at = which * 128
-        wide_in[f, r, :, at : at + 128] = cells[:, 0:128]
-        wide_in[f, r, :, at + 384 : at + 512] = cells[:, 128:256]
-
-    build_shifted(put, lambda f, r: inp[f, r], *[lambda f, n=n: side[n, f] for n in range(5)])
     conv_sum(wide, taps, total)
     hid_out[...] = (total[...] * slope[...]).astype(BF).reshape(4, 12, 16, 256)
 
 
-def input_conv_kernel(hid, block, row, left, right, weight, out, held, total, sem, wide):
+def input_conv_kernel(
+    hid, block, row, left, right, after, weight, out, held, total, sem, wide
+):
+    del after
     copies = weight_copies(weight, held, sem)
     for copy in copies:
         copy.start()
@@ -268,19 +258,16 @@
             pair[a * 3 + b] = second_part(wide, act, 1, a, b)
 
 
-def second_own_kernel(wide, act, got, after, one, two, three, keep, held):
-    del after
-    x = x_place()
+def second_own_kernel(wide, act, got, after, also, keep, one, two, three):
+    del after, also
     for a in range(3):
         for b in range(3):
-            ab = a * 3 + b
-            held[...] = second_part(wide, act, 0, a, b) + got[ab]
+            total = second_part(wide, act, 0, a, b) + got[a * 3 + b]
             for d, out in enumerate((keep, one, two, three)):
-                rows = pl.ds(pl.multiple_of(((x + d) & 3) * 32, 32), 32)
-                out[ab] = held[rows, :].astype(out.dtype)
-
-
-def second_x_kernel(got1, got2, got3, own, after, one, two, three, keep, held):
+                out[a * 3 + b] = total[d * 32 : d * 32 + 32].astype(out.dtype)
+
+
+def second_x_kernel(got1, got2, got3, own, after, keep, one, two, three, held):
     del after
     y = lax.axis_index("y")
 
@@ -298,7 +285,21 @@
             out[g] = held[:, (y + d) & 3].reshape(64, 128).astype(out.dtype)
 
 
-def first_grad_kernel(hid, wide, own, pair):
+def first_grad_kernel(
+    hid, inp, row, left, right, corner_left, corner_right, after, own, pair, wide, side,
+):
+    del after
+    order = channel_order()
+    for n, ref in enumerate((row, left, right, corner_left, corner_right)):
+        cells = jnp.dot(ref[1].reshape(64, 256), order, preferred_element_type=F32)
+        side[n] = cells.reshape(4, 16, 256)
+
+    def put(f, r, which, cells):
+        at = which * 128
+        wide[f, r, :, at : at + 128] = cells[:, 0:128]
+        wide[f, r, :, at + 384 : at + 512] = cells[:, 128:256]
+
+    build_shifted(put, lambda f, r: inp[f, r], *[lambda f, n=n: side[n, f] for n in range(5)])
     for a in range(3):
         rows = (a + 2) * 192
         left = hid[2 - a : 4].reshape(rows, 256)
@@ -314,49 +315,50 @@
                     pair[q, t] = piece[:, e * 128 + 384 : e * 128 + 512]
 
 
-def first_pair_kernel(own, pair, out, keep):
+def first_sum_kernel(own, pair, after, keep, one, two, three):
+    del after
     y = lax.axis_index("y")
-    for q in range(4):
-        out[q] = (own[q] + pair[q]).astype(BF)
-    keep[...] = own[y] + pair[y]
-
-
-def first_y_kernel(got, own, after, one, two, three, keep, held):
-    del after
-    x, y = x_place(), lax.axis_index("y")
+    for d, out in enumerate((keep, one, two, three)):
+        q = (y + d) & 3
+        out[...] = (own[q] + pair[q]).astype(out.dtype)
+
+
+def first_y_kernel(got1, got2, got3, own, after, keep, one, two, three):
+    del after
 
     def tap(t):
         total = own[t]
-        for d in range(1, 4):
-            total = total + got[(y + d) & 3, t].astype(F32)
+        for got in (got1, got2, got3):
+            total = total + got[t].astype(F32)
         return total
 
     for g in range(7):
         taps = [tap(t) if t < 27 else jnp.zeros((64, 128), F32) for t in range(4 * g, 4 * g + 4)]
-        for q in range(4):
-            held[q] = jnp.concatenate([v[:, q * 32 : q * 32 + 32] for v in taps], axis=1)
         for d, out in enumerate((keep, one, two, three)):
-            out[g] = held[(x + d) & 3].astype(out.dtype)
-
-
-def last_kernel(own_two, a1, a2, a3, own_one, b1, b2, b3, *rest):
-    outs, held = rest[:8], rest[8]
+            piece = jnp.concatenate([v[:, d * 32 : d * 32 + 32] for v in taps], axis=1)
+            out[g] = piece.astype(out.dtype)
+
+
+def last_kernel(own_two, a1, a2, a3, own_one, b1, b2, b3, out, keep, held):
     for n, (own, got) in enumerate(((own_two, (a1, a2, a3)), (own_one, (b1, b2, b3)))):
         total = own[...]
         for ref in got:
             total = total + ref[...].astype(F32)
         held[n] = total.reshape(7, 8, 8, 128)
+
+    def plane(z):
+        return jnp.concatenate([held[n, :, z].reshape(56, 128) for n in range(2)], axis=0)
+
+    for q in range(8):
+        out[q] = plane(q).astype(BF)
+    keep[...] = plane(lax.axis_index("z"))
+
+
+def final_kernel(factor, got, own, one, two):
     z = lax.axis_index("z")
-    for d, out in enumerate(outs):
-        plane = [held[n, :, (z + d) & 7].reshape(56, 128) for n in range(2)]
-        out[...] = jnp.concatenate(plane, axis=0).astype(out.dtype)
-
-
-def final_kernel(factor, own, *rest):
-    got, (one, two) = rest[:7], rest[7:]
     total = own[...]
-    for ref in got:
-        total = total + ref[...].astype(F32)
+    for d in range(1, 8):
+        total = total + got[(z + d) & 7].astype(F32)
     total = (total * factor).reshape(2, 7, 8, 128)
     for out, which in ((two, 0), (one, 1)):
         for t in range(27):
@@ -368,10 +370,10 @@
     taps_one = conv_one.transpose(1, 2, 3, 0, 4).reshape(27, 256, 256)
     taps_two = conv_two.transpose(1, 2, 3, 0, 4).reshape(27, 256, 256)
     wide = near((4, 14, 16, 768), BF)
-    quads = [near((7, 64, 128), BF)] * 3 + [near((7, 64, 128), F32)]
+    quads = [near((7, 64, 128), F32)] + [near((7, 64, 128), BF)] * 3
 
     def ring(parts, axis):
-        return [send(p, ring_pairs(**{axis: d + 1})) for d, p in enumerate(parts)]
+        return [send(parts[d - 1], ring_pairs(**{axis: d})) for d in (2, 1, 3)]
 
     packed = call(
         pack_kernel,
@@ -402,68 +404,68 @@
             pltpu.SemaphoreType.DMA((3,)),
         ],
     )
-    wide_in, wide_cot, grad_hidden = call(
+    wide_cot, grad_hidden = call(
         first_kernel,
         "conv_two_back",
-        (block, inp, slope, *sides, held_two),
-        "pvv" + "v" * 5 + "v",
-        [wide, wide, near((4, 12, 16, 256), BF)],
-        [pltpu.VMEM((768, 256), F32), pltpu.VMEM((5, 4, 16, 256), F32)],
-    )
-
-    split = near((4, 27, 64, 128), F32)
-    own_one, pair_one = call(
-        first_grad_kernel, "grad_one", (grad_hidden, wide_in), "vv", [split, split]
-    )
-    got_pair_one = send(pair_one, core_pairs())
-    (pair_two,) = call(
-        second_pair_kernel,
-        "grad_two_pair",
-        (wide_cot, act, pair_one),
-        "vvv",
-        [near((9, 128, 768), F32)],
-    )
-    got_pair_two = send(pair_two, core_pairs())
+        (block, slope, *sides, held_two),
+        "pv" + "v" * 5 + "v",
+        [wide, near((4, 12, 16, 256), BF)],
+        [pltpu.VMEM((768, 256), F32)],
+    )
+
     hi, lo = call(
         pack_columns_kernel,
         "pack_columns",
-        (grad_hidden, pair_two),
-        "vv",
+        (grad_hidden,),
+        "v",
         [near((4, 16, 256), BF)] * 2,
         [pltpu.VMEM((2, 768, 128), F32)],
     )
     left, right = send(hi, block_pairs(0, 1)), send(lo, block_pairs(0, -1))
-    out_one, own_one = call(
-        first_pair_kernel,
-        "grad_one_sum",
-        (own_one, got_pair_one),
-        "vv",
-        [far((4, 27, 64, 128), BF), far((27, 64, 128), F32)],
-    )
-    got_one = lax.all_to_all(out_one, "y", 0, 0, tiled=True)
-    *parts, own_two = call(
-        second_own_kernel,
-        "grad_two_own",
-        (wide_cot, act, got_pair_two, out_one),
-        "vvvh",
-        [near((9, 32, 768), BF)] * 3 + [far((9, 32, 768), F32)],
-        [pltpu.VMEM((128, 768), F32)],
-    )
-    got_two = ring(parts, "dx")
-
+    (pair_two,) = call(
+        second_pair_kernel, "grad_two_pair", (wide_cot, act, hi), "vvv", [near((9, 128, 768), F32)]
+    )
+    got_pair_two = send(pair_two, core_pairs())
     (row,) = call(
         pack_rows_kernel,
         "pack_rows",
-        (grad_hidden, left, right, parts[0]),
+        (grad_hidden, left, right, pair_two),
         "vvvv",
         [near((3, 4, 16, 256), BF)],
     )
-    row = send(row, block_pairs(1, 0))
+    got_row = send(row, block_pairs(1, 0))
+    split = near((4, 27, 64, 128), F32)
+    own_one, pair_one = call(
+        first_grad_kernel,
+        "grad_one",
+        (grad_hidden, inp, *sides, row),
+        "vv" + "v" * 5 + "v",
+        [split, split],
+        [pltpu.VMEM((4, 14, 16, 768), BF), pltpu.VMEM((5, 4, 16, 256), F32)],
+    )
+    got_pair_one = send(pair_one, core_pairs())
+    own_two, *parts = call(
+        second_own_kernel,
+        "grad_two_own",
+        (wide_cot, act, got_pair_two, got_row, pair_one),
+        "vvvvv",
+        [near((9, 32, 768), F32)] + [near((9, 32, 768), BF)] * 3,
+    )
+    got_two = ring(parts, "dx")
+    own_one, *parts_one = call(
+        first_sum_kernel,
+        "grad_one_sum",
+        (own_one, got_pair_one, parts[0]),
+        "vvv",
+        [near((27, 64, 128), F32)] + [near((27, 64, 128), BF)] * 3,
+    )
+    got_one = ring(parts_one, "dy")
+
     (grad_input,) = call(
         input_conv_kernel,
         "conv_one_back",
-        (grad_hidden, block, row, left, right, taps_one),
-        "vpvvvh",
+        (grad_hidden, block, got_row, left, right, parts_one[0], taps_one),
+        "vpvvvvh",
         [(jax.ShapeDtypeStruct((4, 12, 16, 256), BF), "v")],
         [
             pltpu.VMEM((27, 256, 256), BF),
@@ -473,42 +475,33 @@
         ],
     )
 
-    *parts, own_one = call(
-        first_y_kernel,
-        "grad_one_y",
-        (got_one, own_one, grad_input),
-        "vph",
-        quads,
-        [pltpu.VMEM((4, 64, 128), F32)],
-    )
-    got_one = ring(parts, "dx")
-    *parts, own_two = call(
+    own_two, *parts = call(
         second_x_kernel,
         "grad_two_x",
         (*got_two, own_two, grad_input),
-        "vvvph",
+        "vvvvh",
         quads,
         [pltpu.VMEM((8, 4, 8, 128), F32)],
     )
     got_two = ring(parts, "dy")
-
-    own, *parts = call(
+    own_one, *parts_one = call(
+        first_y_kernel, "grad_one_y", (*got_one, own_one, parts[0]), "vvvvv", quads
+    )
+    got_one = ring(parts_one, "dx")
+
+    out, own = call(
         last_kernel,
         "last_stage",
         (own_two, *got_two, own_one, *got_one),
         "v" * 8,
-        [near((112, 128), F32)] + [near((112, 128), BF)] * 7,
+        [far((8, 112, 128), BF), near((112, 128), F32)],
         [pltpu.VMEM((2, 7, 8, 8, 128), F32)],
     )
-    planes = ring(parts, "dz")
+    planes = lax.all_to_all(out, "z", 0, 0, tiled=True)
     factor = float(256 * 768) ** (-0.5)
     result = jax.ShapeDtypeStruct((27, 8, 32), F32), "v"
     grad_one, grad_two = call(
-        functools.partial(final_kernel, factor),
-        "final_sum",
-        (own, *planes),
-        "v" * 8,
-        [result, result],
+        functools.partial(final_kernel, factor), "final_sum", (planes, own), "vv", [result, result]
     )
     shape = lambda g: g.transpose(2, 0, 1).reshape(32, 3, 3, 3, 8)
     return grad_input[None], shape(grad_one), shape(grad_two)

time: 117 us -> 92.9 us (0.79)
  the two profiles are of different devices: /device:TPU:2 before, /device:TPU:24 now
where the time goes in v5:
time: 92.9 us; the launch traced here: 92.1 us
  starting transfers between devices  27.1 us (29%)
  waiting for transfers between devices  22.9 us (25%)
  Pallas kernels  21.7 us (23%)
  blocking collectives  19 us (20%)
  between operations  1.41 us (2%)
    ppermute x22, starting transfers between devices, send(): return lax.ppermute(value, AX, pairs)  27.1 us
    ppermute x22, waiting for transfers between devices, send(): return lax.ppermute(value, AX, pairs)  22.9 us
    pallas_call x14, Pallas kernels, call(): pl.pallas_call(kernel, out_shape=tuple((o for o, _ in outs)), in_specs=[s...  21.7 us
    all_to_all x1, blocking collectives, shards(): planes = lax.all_to_all(out, 'z', 0, 0, tiled=True)  19 us
  transfers between devices with their start and end apart: 22, of which 8 were waited for; matrix products, arithmetic and copies ran while one was open for 0% of the time, Pallas kernels for 15%

profile of v5, /device:TPU:24, one launch (start us, length us, event | category | flops | bytes accessed | tf_op | source)
XLA Modules:
  0.0 92.1 jit_solution(11296564570267202223)
XLA Ops:
  0.6 1.3 %pack_first.1 = (bf16[2,4,16,256]{3,2,1,0:T(8,128)(2,1)S(1)}, bf16[2,4,16,256]{3,2,1,0:T(8,128)(2,1)S(1)}, bf16[2,4,16,256]{3,2,1,0:T(8,128)(2,1)S(1)}, bf16[2,4...) custom-call(bf16[4,12,16,256]{3,2,1,0:T(8,128)(2,1)} %bitcast.18, bf16[4,12,16,256]{3,2,1,0:T(8,128)(2,1)} %bitcast.21), custom_call_target="tpu_custom_call" | custom-call | tf_op jit(solution)/shard_map/pack_first/pallas_call | solution.py:50
  1.9 1.6 %collective-permute-start = (bf16[2,4,16,256]{3,2,1,0:T(8,128)(2,1)S(1)}, bf16[2,4,16,256]{3,2,1,0:T(8,128)(2,1)S(1)}, u32[]{:S(2)}, u32[]{:S(2)}) collective-permute-start(bf16[2,4,16,256]{3,2,1,0:T(8,128)(2,1)S(1)} %get-tuple-element.39), channel_id=1, source_target_pairs={{0,4},{1,5},{2,6},{3,7},{4,0},{5,1},{6,2},{7,3},{8,12},{9,13},{10,... | collective-permute-start | bytes 196616 | tf_op jit(solution)/shard_map/ppermute | solution.py:40
  3.5 3.2 %collective-permute-start.2 = (bf16[2,4,16,256]{3,2,1,0:T(8,128)(2,1)S(1)}, bf16[2,4,16,256]{3,2,1,0:T(8,128)(2,1)S(1)}, u32[]{:S(2)}, u32[]{:S(2)}) collective-permute-start(bf16[2,4,16,256]{3,2,1,0:T(8,128)(2,1)S(1)} %get-tuple-element.41), channel_id=1, source_target_pairs={{0,3},{1,0},{2,1},{3,2},{4,7},{5,4},{6,5},{7,6},{8,11},{9,8},{10,9... | collective-permute-start | bytes 196616 | tf_op jit(solution)/shard_map/ppermute | solution.py:40
  6.8 3.0 %collective-permute-start.4 = (bf16[2,4,16,256]{3,2,1,0:T(8,128)(2,1)S(1)}, bf16[2,4,16,256]{3,2,1,0:T(8,128)(2,1)S(1)}, u32[]{:S(2)}, u32[]{:S(2)}) collective-permute-start(bf16[2,4,16,256]{3,2,1,0:T(8,128)(2,1)S(1)} %get-tuple-element.43), channel_id=1, source_target_pairs={{0,7},{1,4},{2,5},{3,6},{4,3},{5,0},{6,1},{7,2},{8,15},{9,12},{10,... | collective-permute-start | bytes 196616 | tf_op jit(solution)/shard_map/ppermute | solution.py:40
  10.4 2.3 %film.1 = (bf16[768,256]{1,0:T(8,128)(2,1)S(1)}, bf16[4,12,16,256]{3,2,1,0:T(8,128)(2,1)S(1)}, f32[768,256]{1,0:T(8,128)S(1)}, bf16[27,256,256]{2,1,0:T(8,128)(2,1)S(1)}) custom-call(s32[1]{0:T(128)S(6)} %copy.10.step, bf16[4,12,16,256]{3,2,1,0:T(8,128)(2,1)} %bitcast.22, bf16[4,12,16,256]{3,2,1,0:T(8,128)(2,1)} %bitcast.24, f32[1000,512]{1,0:T(8,128)} %table.1, ...), custom_call_target="tpu_custom_call" | custom-call | tf_op jit(solution)/shard_map/film/pallas_call | solution.py:50
  12.8 3.3 %conv_two_back.1 = (bf16[4,14,16,768]{3,2,1,0:T(8,128)(2,1)S(1)}, bf16[4,12,16,256]{3,2,1,0:T(8,128)(2,1)S(1)}) custom-call(bf16[4,12,16,256]{3,2,1,0:T(8,128)(2,1)} %bitcast.19, f32[768,256]{1,0:T(8,128)S(1)} %get-tuple-element.38.slope, bf16[2,4,16,256]{3,2,1,0:T(8,128)(2,1)S(1)} %collective-permute-done.row, ...), custom_call_target="tpu_custom_call" | custom-call | tf_op jit(solution)/shard_map/conv_two_back/pallas_call | solution.py:50
  16.2 1.4 %grad_two_pair.1.after = f32[9,128,768]{2,1,0:T(8,128)S(1)} custom-call(bf16[4,14,16,768]{3,2,1,0:T(8,128)(2,1)S(1)} %get-tuple-element.48.wide, bf16[768,256]{1,0:T(8,128)(2,1)S(1)} %get-tuple-element.49.act, bf16[4,16,256]{2,1,0:T(8,128)(2,1)S(1)} %get-tuple-element.46.after), custom_call_target="tpu_custom_call" | custom-call | tf_op jit(solution)/shard_map/grad_two_pair/pallas_call | solution.py:50
  17.6 1.2 %collective-permute-start.9 = (f32[9,128,768]{2,1,0:T(8,128)S(1)}, f32[9,128,768]{2,1,0:T(8,128)S(1)}, u32[]{:S(2)}, u32[]{:S(2)}) collective-permute-start(f32[9,128,768]{2,1,0:T(8,128)S(1)} %grad_two_pair.1.after), channel_id=1, source_target_pairs={{0,1},{1,0},{2,3},{3,2},{4,5},{5,4},{6,7},{7,6},{8,9},{9,8},{10,11... | collective-permute-start | bytes 10616840 | tf_op jit(solution)/shard_map/ppermute | solution.py:40
  19.3 5.2 %collective-permute-done.6.right = bf16[4,16,256]{2,1,0:T(8,128)(2,1)S(1)} collective-permute-done((bf16[4,16,256]{2,1,0:T(8,128)(2,1)S(1)}, bf16[4,16,256]{2,1,0:T(8,128)(2,1)S(1)}, u32[]{:S(2)}, u32[]{:S(2)}) %collective-permute-start.6) | collective-permute-done | bytes 32800 | tf_op jit(solution)/shard_map/ppermute | solution.py:40
  24.7 3.0 %grad_one.1 = (f32[4,27,64,128]{3,2,1,0:T(8,128)S(1)}, f32[4,27,64,128]{3,2,1,0:T(8,128)S(1)}) custom-call(bf16[4,12,16,256]{3,2,1,0:T(8,128)(2,1)S(1)} %get-tuple-element.45.block.hid, bf16[4,12,16,256]{3,2,1,0:T(8,128)(2,1)S(1)} %get-tuple-element.50.inp, bf16[2,4,16,256]{3,2,1,0:T(8,128)(2,1)S(1)} %collective-permute-done.row, ...), custom_call_target="tpu_custom_call" | custom-call | tf_op jit(solution)/shard_map/grad_one/pallas_call | solution.py:50
  28.8 4.2 %collective-permute-done.7.after.row = bf16[3,4,16,256]{3,2,1,0:T(8,128)(2,1)S(1)} collective-permute-done((bf16[3,4,16,256]{3,2,1,0:T(8,128)(2,1)S(1)}, bf16[3,4,16,256]{3,2,1,0:T(8,128)(2,1)S(1)}, u32[]{:S(2)}, u32[]{:S(2)}) %collective-permute-start.7) | collective-permute-done | bytes 98336 | tf_op jit(solution)/shard_map/ppermute | solution.py:40
  32.9 1.4 %grad_two_own.1 = (f32[9,32,768]{2,1,0:T(8,128)S(1)}, bf16[9,32,768]{2,1,0:T(8,128)(2,1)S(1)}, bf16[9,32,768]{2,1,0:T(8,128)(2,1)S(1)}, bf16[9,32,768]{2,1,0:T(8,128)(2,1)S(1)}) custom-call(bf16[4,14,16,768]{3,2,1,0:T(8,128)(2,1)S(1)} %get-tuple-element.48.wide, bf16[768,256]{1,0:T(8,128)(2,1)S(1)} %get-tuple-element.49.act, ...), custom_call_target="tpu_custom_call" | custom-call | tf_op jit(solution)/shard_map/grad_two_own/pallas_call | solution.py:50
  34.4 2.3 %collective-permute-start.10 = (bf16[9,32,768]{2,1,0:T(8,128)(2,1)S(1)}, bf16[9,32,768]{2,1,0:T(8,128)(2,1)S(1)}, u32[]{:S(2)}, u32[]{:S(2)}) collective-permute-start(bf16[9,32,768]{2,1,0:T(8,128)(2,1)S(1)} %get-tuple-element.55), channel_id=1, source_target_pairs={{0,2},{1,3},{2,0},{3,1},{4,6},{5,7},{6,4},{7,5},{8,10},{9,11},{10,... | collective-permute-start | bytes 1327112 | tf_op jit(solution)/shard_map/ppermute | solution.py:40
  36.7 1.4 %collective-permute-start.12 = (bf16[9,32,768]{2,1,0:T(8,128)(2,1)S(1)}, bf16[9,32,768]{2,1,0:T(8,128)(2,1)S(1)}, u32[]{:S(2)}, u32[]{:S(2)}) collective-permute-start(bf16[9,32,768]{2,1,0:T(8,128)(2,1)S(1)} %get-tuple-element.56), channel_id=1, source_target_pairs={{0,6},{1,7},{2,4},{3,5},{4,0},{5,1},{6,2},{7,3},{8,14},{9,15},{10,... | collective-permute-start | bytes 1327112 | tf_op jit(solution)/shard_map/ppermute | solution.py:40
  39.0 1.3 %collective-permute-start.16 = (bf16[27,64,128]{2,1,0:T(8,128)(2,1)S(1)}, bf16[27,64,128]{2,1,0:T(8,128)(2,1)S(1)}, u32[]{:S(2)}, u32[]{:S(2)}) collective-permute-start(bf16[27,64,128]{2,1,0:T(8,128)(2,1)S(1)} %get-tuple-element.62), channel_id=1, source_target_pairs={{0,16},{1,17},{2,18},{3,19},{4,20},{5,21},{6,22},{7,23},{8,24},{9,... | collective-permute-start | bytes 1327112 | tf_op jit(solution)/shard_map/ppermute | solution.py:40
  40.3 8.8 %collective-permute-done.10.got1 = bf16[9,32,768]{2,1,0:T(8,128)(2,1)S(1)} collective-permute-done((bf16[9,32,768]{2,1,0:T(8,128)(2,1)S(1)}, bf16[9,32,768]{2,1,0:T(8,128)(2,1)S(1)}, u32[]{:S(2)}, u32[]{:S(2)}) %collective-permute-start.10) | collective-permute-done | bytes 442400 | tf_op jit(solution)/shard_map/ppermute | solution.py:40
  49.3 6.0 %conv_one_back.1.after = bf16[4,12,16,256]{3,2,1,0:T(8,128)(2,1)} custom-call(bf16[4,12,16,256]{3,2,1,0:T(8,128)(2,1)S(1)} %get-tuple-element.45.block.hid, bf16[4,12,16,256]{3,2,1,0:T(8,128)(2,1)} %bitcast.20, bf16[3,4,16,256]{3,2,1,0:T(8,128)(2,1)S(1)} %collective-permute-done.7.after.row, bf16[4,16,256]{2,1,0:T(8,128)(2,1)S(1)} %collective-permute-done.5.left, ...), custom_call_target="tpu_custom_call" | custom-call | tf_op jit(solution)/shard_map/conv_one_back/pallas_call | solution.py:50
  57.3 1.5 %collective-permute-start.13 = (bf16[7,64,128]{2,1,0:T(8,128)(2,1)S(1)}, bf16[7,64,128]{2,1,0:T(8,128)(2,1)S(1)}, u32[]{:S(2)}, u32[]{:S(2)}) collective-permute-start(bf16[7,64,128]{2,1,0:T(8,128)(2,1)S(1)} %get-tuple-element.59), channel_id=1, source_target_pairs={{0,16},{1,17},{2,18},{3,19},{4,20},{5,21},{6,22},{7,23},{8,24},{9,... | collective-permute-start | bytes 344072 | tf_op jit(solution)/shard_map/ppermute | solution.py:40
  58.8 3.2 %collective-permute-start.14 = (bf16[7,64,128]{2,1,0:T(8,128)(2,1)S(1)}, bf16[7,64,128]{2,1,0:T(8,128)(2,1)S(1)}, u32[]{:S(2)}, u32[]{:S(2)}) collective-permute-start(bf16[7,64,128]{2,1,0:T(8,128)(2,1)S(1)} %get-tuple-element.60.after), channel_id=1, source_target_pairs={{0,8},{1,9},{2,10},{3,11},{4,12},{5,13},{6,14},{7,15},{8,16},{9,17... | collective-permute-start | bytes 344072 | tf_op jit(solution)/shard_map/ppermute | solution.py:40
  62.5 2.6 %collective-permute-start.19 = (bf16[7,64,128]{2,1,0:T(8,128)(2,1)S(1)}, bf16[7,64,128]{2,1,0:T(8,128)(2,1)S(1)}, u32[]{:S(2)}, u32[]{:S(2)}) collective-permute-start(bf16[7,64,128]{2,1,0:T(8,128)(2,1)S(1)} %get-tuple-element.66), channel_id=1, source_target_pairs={{0,2},{1,3},{2,0},{3,1},{4,6},{5,7},{6,4},{7,5},{8,10},{9,11},{10,... | collective-permute-start | bytes 344072 | tf_op jit(solution)/shard_map/ppermute | solution.py:40
  65.2 3.2 %collective-permute-start.21 = (bf16[7,64,128]{2,1,0:T(8,128)(2,1)S(1)}, bf16[7,64,128]{2,1,0:T(8,128)(2,1)S(1)}, u32[]{:S(2)}, u32[]{:S(2)}) collective-permute-start(bf16[7,64,128]{2,1,0:T(8,128)(2,1)S(1)} %get-tuple-element.68), channel_id=1, source_target_pairs={{0,6},{1,7},{2,4},{3,5},{4,0},{5,1},{6,2},{7,3},{8,14},{9,15},{10,... | collective-permute-start | bytes 344072 | tf_op jit(solution)/shard_map/ppermute | solution.py:40
  68.4 1.3 %collective-permute-done.19.b1 = bf16[7,64,128]{2,1,0:T(8,128)(2,1)S(1)} collective-permute-done((bf16[7,64,128]{2,1,0:T(8,128)(2,1)S(1)}, bf16[7,64,128]{2,1,0:T(8,128)(2,1)S(1)}, u32[]{:S(2)}, u32[]{:S(2)}) %collective-permute-start.19) | collective-permute-done | bytes 114720 | tf_op jit(solution)/shard_map/ppermute | solution.py:40
  69.7 1.8 %collective-permute-done.20.b2 = bf16[7,64,128]{2,1,0:T(8,128)(2,1)S(1)} collective-permute-done((bf16[7,64,128]{2,1,0:T(8,128)(2,1)S(1)}, bf16[7,64,128]{2,1,0:T(8,128)(2,1)S(1)}, u32[]{:S(2)}, u32[]{:S(2)}) %collective-permute-start.20) | collective-permute-done | bytes 114720 | tf_op jit(solution)/shard_map/ppermute | solution.py:40
  72.3 19.0 %all_to_all.5.got = bf16[8,112,128]{2,1,0:T(8,128)(2,1)S(1)} all-to-all(bf16[8,112,128]{2,1,0:T(8,128)(2,1)} %get-tuple-element.69), channel_id=1, replica_groups=mesh['z'=8,'y'=4,'ha'=2,'xh'=2,'core'=2] {'z'}, dimensions={0} | all-to-all | bytes 458752 | tf_op jit(solution)/shard_map/all_to_all | solution.py:500
  (35 shorter events, 7.2 us)
Async XLA Ops:
  1.9 10.8 %collective-permute-start = (bf16[2,4,16,256]{3,2,1,0:T(8,128)(2,1)S(1)}, bf16[2,4,16,256]{3,2,1,0:T(8,128)(2,1)S(1)}, u32[]{:S(2)}, u32[]{:S(2)}) collective-permute-start(bf16[2,4,16,256]{3,2,1,0:T(8,128)(2,1)S(1)} %get-tuple-element.39), channel_id=1, source_target_pairs={{0,4},{1,5},{2,6},{3,7},{4,0},{5,1},{6,2},{7,3},{8,12},{9,13},{10,... | collective-permute-start | bytes 196616 | tf_op jit(solution)/shard_map/ppermute | solution.py:40
  3.5 9.2 %collective-permute-start.1 = (bf16[2,4,16,256]{3,2,1,0:T(8,128)(2,1)S(1)}, bf16[2,4,16,256]{3,2,1,0:T(8,128)(2,1)S(1)}, u32[]{:S(2)}, u32[]{:S(2)}) collective-permute-start(bf16[2,4,16,256]{3,2,1,0:T(8,128)(2,1)S(1)} %get-tuple-element.40), channel_id=1, source_target_pairs={{0,1},{1,2},{2,3},{3,0},{4,5},{5,6},{6,7},{7,4},{8,9},{9,10},{10,1... | collective-permute-start | bytes 196616 | tf_op jit(solution)/shard_map/ppermute | solution.py:40
  3.5 9.2 %collective-permute-start.2 = (bf16[2,4,16,256]{3,2,1,0:T(8,128)(2,1)S(1)}, bf16[2,4,16,256]{3,2,1,0:T(8,128)(2,1)S(1)}, u32[]{:S(2)}, u32[]{:S(2)}) collective-permute-start(bf16[2,4,16,256]{3,2,1,0:T(8,128)(2,1)S(1)} %get-tuple-element.41), channel_id=1, source_target_pairs={{0,3},{1,0},{2,1},{3,2},{4,7},{5,4},{6,5},{7,6},{8,11},{9,8},{10,9... | collective-permute-start | bytes 196616 | tf_op jit(solution)/shard_map/ppermute | solution.py:40
  6.8 6.0 %collective-permute-start.3 = (bf16[2,4,16,256]{3,2,1,0:T(8,128)(2,1)S(1)}, bf16[2,4,16,256]{3,2,1,0:T(8,128)(2,1)S(1)}, u32[]{:S(2)}, u32[]{:S(2)}) collective-permute-start(bf16[2,4,16,256]{3,2,1,0:T(8,128)(2,1)S(1)} %get-tuple-element.42), channel_id=1, source_target_pairs={{0,5},{1,6},{2,7},{3,4},{4,1},{5,2},{6,3},{7,0},{8,13},{9,14},{10,... | collective-permute-start | bytes 196616 | tf_op jit(solution)/shard_map/ppermute | solution.py:40
  6.8 6.0 %collective-permute-start.4 = (bf16[2,4,16,256]{3,2,1,0:T(8,128)(2,1)S(1)}, bf16[2,4,16,256]{3,2,1,0:T(8,128)(2,1)S(1)}, u32[]{:S(2)}, u32[]{:S(2)}) collective-permute-start(bf16[2,4,16,256]{3,2,1,0:T(8,128)(2,1)S(1)} %get-tuple-element.43), channel_id=1, source_target_pairs={{0,7},{1,4},{2,5},{3,6},{4,3},{5,0},{6,1},{7,2},{8,15},{9,12},{10,... | collective-permute-start | bytes 196616 | tf_op jit(solution)/shard_map/ppermute | solution.py:40
  17.6 15.4 %collective-permute-start.9 = (f32[9,128,768]{2,1,0:T(8,128)S(1)}, f32[9,128,768]{2,1,0:T(8,128)S(1)}, u32[]{:S(2)}, u32[]{:S(2)}) collective-permute-start(f32[9,128,768]{2,1,0:T(8,128)S(1)} %grad_two_pair.1.after), channel_id=1, source_target_pairs={{0,1},{1,0},{2,3},{3,2},{4,5},{5,4},{6,7},{7,6},{8,9},{9,8},{10,11... | collective-permute-start | bytes 10616840 | tf_op jit(solution)/shard_map/ppermute | solution.py:40
  18.8 5.8 %collective-permute-start.6 = (bf16[4,16,256]{2,1,0:T(8,128)(2,1)S(1)}, bf16[4,16,256]{2,1,0:T(8,128)(2,1)S(1)}, u32[]{:S(2)}, u32[]{:S(2)}) collective-permute-start(bf16[4,16,256]{2,1,0:T(8,128)(2,1)S(1)} %get-tuple-element.47), channel_id=1, source_target_pairs={{0,3},{1,0},{2,1},{3,2},{4,7},{5,4},{6,5},{7,6},{8,11},{9,8},{10,9... | collective-permute-start | bytes 98312 | tf_op jit(solution)/shard_map/ppermute | solution.py:40
  19.3 5.4 %collective-permute-start.5 = (bf16[4,16,256]{2,1,0:T(8,128)(2,1)S(1)}, bf16[4,16,256]{2,1,0:T(8,128)(2,1)S(1)}, u32[]{:S(2)}, u32[]{:S(2)}) collective-permute-start(bf16[4,16,256]{2,1,0:T(8,128)(2,1)S(1)} %get-tuple-element.46.after), channel_id=1, source_target_pairs={{0,1},{1,2},{2,3},{3,0},{4,5},{5,6},{6,7},{7,4},{8,9},{9,10},{10,1... | collective-permute-start | bytes 98312 | tf_op jit(solution)/shard_map/ppermute | solution.py:40
  27.6 11.0 %collective-permute-start.8 = (f32[4,27,64,128]{3,2,1,0:T(8,128)S(1)}, f32[4,27,64,128]{3,2,1,0:T(8,128)S(1)}, u32[]{:S(2)}, u32[]{:S(2)}) collective-permute-start(f32[4,27,64,128]{3,2,1,0:T(8,128)S(1)} %get-tuple-element.52.also), channel_id=1, source_target_pairs={{0,1},{1,0},{2,3},{3,2},{4,5},{5,4},{6,7},{7,6},{8,9},{9,8},{10,11... | collective-permute-start | bytes 10616840 | tf_op jit(solution)/shard_map/ppermute | solution.py:40
  28.1 4.8 %collective-permute-start.7 = (bf16[3,4,16,256]{3,2,1,0:T(8,128)(2,1)S(1)}, bf16[3,4,16,256]{3,2,1,0:T(8,128)(2,1)S(1)}, u32[]{:S(2)}, u32[]{:S(2)}) collective-permute-start(bf16[3,4,16,256]{3,2,1,0:T(8,128)(2,1)S(1)} %pack_rows.1.after), channel_id=1, source_target_pairs={{0,4},{1,5},{2,6},{3,7},{4,0},{5,1},{6,2},{7,3},{8,12},{9,13},{10,... | collective-permute-start | bytes 294920 | tf_op jit(solution)/shard_map/ppermute | solution.py:40
  34.4 14.7 %collective-permute-start.10 = (bf16[9,32,768]{2,1,0:T(8,128)(2,1)S(1)}, bf16[9,32,768]{2,1,0:T(8,128)(2,1)S(1)}, u32[]{:S(2)}, u32[]{:S(2)}) collective-permute-start(bf16[9,32,768]{2,1,0:T(8,128)(2,1)S(1)} %get-tuple-element.55), channel_id=1, source_target_pairs={{0,2},{1,3},{2,0},{3,1},{4,6},{5,7},{6,4},{7,5},{8,10},{9,11},{10,... | collective-permute-start | bytes 1327112 | tf_op jit(solution)/shard_map/ppermute | solution.py:40
  36.7 19.2 %collective-permute-start.12 = (bf16[9,32,768]{2,1,0:T(8,128)(2,1)S(1)}, bf16[9,32,768]{2,1,0:T(8,128)(2,1)S(1)}, u32[]{:S(2)}, u32[]{:S(2)}) collective-permute-start(bf16[9,32,768]{2,1,0:T(8,128)(2,1)S(1)} %get-tuple-element.56), channel_id=1, source_target_pairs={{0,6},{1,7},{2,4},{3,5},{4,0},{5,1},{6,2},{7,3},{8,14},{9,15},{10,... | collective-permute-start | bytes 1327112 | tf_op jit(solution)/shard_map/ppermute | solution.py:40
  38.1 18.7 %collective-permute-start.11 = (bf16[9,32,768]{2,1,0:T(8,128)(2,1)S(1)}, bf16[9,32,768]{2,1,0:T(8,128)(2,1)S(1)}, u32[]{:S(2)}, u32[]{:S(2)}) collective-permute-start(bf16[9,32,768]{2,1,0:T(8,128)(2,1)S(1)} %get-tuple-element.53.after), channel_id=1, source_target_pairs={{0,4},{1,5},{2,6},{3,7},{4,2},{5,3},{6,0},{7,1},{8,12},{9,13},{10,... | collective-permute-start | bytes 1327112 | tf_op jit(solution)/shard_map/ppermute | solution.py:40
  39.0 19.8 %collective-permute-start.16 = (bf16[27,64,128]{2,1,0:T(8,128)(2,1)S(1)}, bf16[27,64,128]{2,1,0:T(8,128)(2,1)S(1)}, u32[]{:S(2)}, u32[]{:S(2)}) collective-permute-start(bf16[27,64,128]{2,1,0:T(8,128)(2,1)S(1)} %get-tuple-element.62), channel_id=1, source_target_pairs={{0,16},{1,17},{2,18},{3,19},{4,20},{5,21},{6,22},{7,23},{8,24},{9,... | collective-permute-start | bytes 1327112 | tf_op jit(solution)/shard_map/ppermute | solution.py:40
  40.3 21.7 %collective-permute-start.18 = (bf16[27,64,128]{2,1,0:T(8,128)(2,1)S(1)}, bf16[27,64,128]{2,1,0:T(8,128)(2,1)S(1)}, u32[]{:S(2)}, u32[]{:S(2)}) collective-permute-start(bf16[27,64,128]{2,1,0:T(8,128)(2,1)S(1)} %get-tuple-element.63), channel_id=1, source_target_pairs={{0,24},{1,25},{2,26},{3,27},{4,28},{5,29},{6,30},{7,31},{8,0},{9,1... | collective-permute-start | bytes 1327112 | tf_op jit(solution)/shard_map/ppermute | solution.py:40
  49.1 12.9 %collective-permute-start.17 = (bf16[27,64,128]{2,1,0:T(8,128)(2,1)S(1)}, bf16[27,64,128]{2,1,0:T(8,128)(2,1)S(1)}, u32[]{:S(2)}, u32[]{:S(2)}) collective-permute-start(bf16[27,64,128]{2,1,0:T(8,128)(2,1)S(1)} %get-tuple-element.54.after), channel_id=1, source_target_pairs={{0,8},{1,9},{2,10},{3,11},{4,12},{5,13},{6,14},{7,15},{8,16},{9,17... | collective-permute-start | bytes 1327112 | tf_op jit(solution)/shard_map/ppermute | solution.py:40
  57.3 8.0 %collective-permute-start.13 = (bf16[7,64,128]{2,1,0:T(8,128)(2,1)S(1)}, bf16[7,64,128]{2,1,0:T(8,128)(2,1)S(1)}, u32[]{:S(2)}, u32[]{:S(2)}) collective-permute-start(bf16[7,64,128]{2,1,0:T(8,128)(2,1)S(1)} %get-tuple-element.59), channel_id=1, source_target_pairs={{0,16},{1,17},{2,18},{3,19},{4,20},{5,21},{6,22},{7,23},{8,24},{9,... | collective-permute-start | bytes 344072 | tf_op jit(solution)/shard_map/ppermute | solution.py:40
  58.8 9.6 %collective-permute-start.15 = (bf16[7,64,128]{2,1,0:T(8,128)(2,1)S(1)}, bf16[7,64,128]{2,1,0:T(8,128)(2,1)S(1)}, u32[]{:S(2)}, u32[]{:S(2)}) collective-permute-start(bf16[7,64,128]{2,1,0:T(8,128)(2,1)S(1)} %get-tuple-element.61), channel_id=1, source_target_pairs={{0,24},{1,25},{2,26},{3,27},{4,28},{5,29},{6,30},{7,31},{8,0},{9,1... | collective-permute-start | bytes 344072 | tf_op jit(solution)/shard_map/ppermute | solution.py:40
  58.8 9.6 %collective-permute-start.14 = (bf16[7,64,128]{2,1,0:T(8,128)(2,1)S(1)}, bf16[7,64,128]{2,1,0:T(8,128)(2,1)S(1)}, u32[]{:S(2)}, u32[]{:S(2)}) collective-permute-start(bf16[7,64,128]{2,1,0:T(8,128)(2,1)S(1)} %get-tuple-element.60.after), channel_id=1, source_target_pairs={{0,8},{1,9},{2,10},{3,11},{4,12},{5,13},{6,14},{7,15},{8,16},{9,17... | collective-permute-start | bytes 344072 | tf_op jit(solution)/shard_map/ppermute | solution.py:40
  62.5 7.2 %collective-permute-start.19 = (bf16[7,64,128]{2,1,0:T(8,128)(2,1)S(1)}, bf16[7,64,128]{2,1,0:T(8,128)(2,1)S(1)}, u32[]{:S(2)}, u32[]{:S(2)}) collective-permute-start(bf16[7,64,128]{2,1,0:T(8,128)(2,1)S(1)} %get-tuple-element.66), channel_id=1, source_target_pairs={{0,2},{1,3},{2,0},{3,1},{4,6},{5,7},{6,4},{7,5},{8,10},{9,11},{10,... | collective-permute-start | bytes 344072 | tf_op jit(solution)/shard_map/ppermute | solution.py:40
  65.2 6.3 %collective-permute-start.20 = (bf16[7,64,128]{2,1,0:T(8,128)(2,1)S(1)}, bf16[7,64,128]{2,1,0:T(8,128)(2,1)S(1)}, u32[]{:S(2)}, u32[]{:S(2)}) collective-permute-start(bf16[7,64,128]{2,1,0:T(8,128)(2,1)S(1)} %get-tuple-element.67), channel_id=1, source_target_pairs={{0,4},{1,5},{2,6},{3,7},{4,2},{5,3},{6,0},{7,1},{8,12},{9,13},{10,... | collective-permute-start | bytes 344072 | tf_op jit(solution)/shard_map/ppermute | solution.py:40
  65.2 6.3 %collective-permute-start.21 = (bf16[7,64,128]{2,1,0:T(8,128)(2,1)S(1)}, bf16[7,64,128]{2,1,0:T(8,128)(2,1)S(1)}, u32[]{:S(2)}, u32[]{:S(2)}) collective-permute-start(bf16[7,64,128]{2,1,0:T(8,128)(2,1)S(1)} %get-tuple-element.68), channel_id=1, source_target_pairs={{0,6},{1,7},{2,4},{3,5},{4,0},{5,1},{6,2},{7,3},{8,14},{9,15},{10,... | collective-permute-start | bytes 344072 | tf_op jit(solution)/shard_map/ppermute | solution.py:40

commit v6 on v5

--- a/solution.py
+++ b/solution.py
@@ -95,7 +95,8 @@
                     corner[n, f, :, lanes] = jnp.broadcast_to(cell, (16, 128)).astype(BF)
 
 
-def pack_columns_kernel(block, hi, lo, wide):
+def pack_columns_kernel(block, after, hi, lo, wide):
+    del after
     spread(wide, block)
     for f in range(4):
         for j, out in ((15, hi), (0, lo)):
@@ -251,8 +252,7 @@
     return lax.dot_general(left, window, TN, preferred_element_type=F32)
 
 
-def second_pair_kernel(wide, act, after, pair):
-    del after
+def second_pair_kernel(wide, act, pair):
     for a in range(3):
         for b in range(3):
             pair[a * 3 + b] = second_part(wide, act, 1, a, b)
@@ -354,7 +354,8 @@
     keep[...] = plane(lax.axis_index("z"))
 
 
-def final_kernel(factor, got, own, one, two):
+def final_kernel(factor, got, own, after, one, two):
+    del after
     z = lax.axis_index("z")
     total = own[...]
     for d in range(1, 8):
@@ -413,41 +414,33 @@
         [pltpu.VMEM((768, 256), F32)],
     )
 
-    hi, lo = call(
-        pack_columns_kernel,
-        "pack_columns",
-        (grad_hidden,),
-        "v",
-        [near((4, 16, 256), BF)] * 2,
-        [pltpu.VMEM((2, 768, 128), F32)],
-    )
-    left, right = send(hi, block_pairs(0, 1)), send(lo, block_pairs(0, -1))
     (pair_two,) = call(
-        second_pair_kernel, "grad_two_pair", (wide_cot, act, hi), "vvv", [near((9, 128, 768), F32)]
+        second_pair_kernel, "grad_two_pair", (wide_cot, act), "vv", [near((9, 128, 768), F32)]
     )
     got_pair_two = send(pair_two, core_pairs())
-    (row,) = call(
-        pack_rows_kernel,
-        "pack_rows",
-        (grad_hidden, left, right, pair_two),
-        "vvvv",
-        [near((3, 4, 16, 256), BF)],
-    )
-    got_row = send(row, block_pairs(1, 0))
     split = near((4, 27, 64, 128), F32)
     own_one, pair_one = call(
         first_grad_kernel,
         "grad_one",
-        (grad_hidden, inp, *sides, row),
+        (grad_hidden, inp, *sides, pair_two),
         "vv" + "v" * 5 + "v",
         [split, split],
         [pltpu.VMEM((4, 14, 16, 768), BF), pltpu.VMEM((5, 4, 16, 256), F32)],
     )
     got_pair_one = send(pair_one, core_pairs())
+    hi, lo = call(
+        pack_columns_kernel,
+        "pack_columns",
+        (grad_hidden, pair_one),
+        "vv",
+        [near((4, 16, 256), BF)] * 2,
+        [pltpu.VMEM((2, 768, 128), F32)],
+    )
+    left, right = send(hi, block_pairs(0, 1)), send(lo, block_pairs(0, -1))
     own_two, *parts = call(
         second_own_kernel,
         "grad_two_own",
-        (wide_cot, act, got_pair_two, got_row, pair_one),
+        (wide_cot, act, got_pair_two, left, right),
         "vvvvv",
         [near((9, 32, 768), F32)] + [near((9, 32, 768), BF)] * 3,
     )
@@ -461,10 +454,43 @@
     )
     got_one = ring(parts_one, "dy")
 
+    (row,) = call(
+        pack_rows_kernel,
+        "pack_rows",
+        (grad_hidden, left, right, parts_one[0]),
+        "vvvv",
+        [near((3, 4, 16, 256), BF)],
+    )
+    row = send(row, block_pairs(1, 0))
+
+    own_two, *parts = call(
+        second_x_kernel,
+        "grad_two_x",
+        (*got_two, own_two, row),
+        "vvvvv",
+        quads,
+        [pltpu.VMEM((8, 4, 8, 128), F32)],
+    )
+    got_two = ring(parts, "dy")
+    own_one, *parts_one = call(
+        first_y_kernel, "grad_one_y", (*got_one, own_one, parts[0]), "vvvvv", quads
+    )
+    got_one = ring(parts_one, "dx")
+
+    out, own = call(
+        last_kernel,
+        "last_stage",
+        (own_two, *got_two, own_one, *got_one),
+        "v" * 8,
+        [far((8, 112, 128), BF), near((112, 128), F32)],
+        [pltpu.VMEM((2, 7, 8, 8, 128), F32)],
+    )
+    planes = lax.all_to_all(out, "z", 0, 0, tiled=True)
+
     (grad_input,) = call(
         input_conv_kernel,
         "conv_one_back",
-        (grad_hidden, block, got_row, left, right, parts_one[0], taps_one),
+        (grad_hidden, block, row, left, right, own, taps_one),
         "vpvvvvh",
         [(jax.ShapeDtypeStruct((4, 12, 16, 256), BF), "v")],
         [
@@ -475,33 +501,10 @@
         ],
     )
 
-    own_two, *parts = call(
-        second_x_kernel,
-        "grad_two_x",
-        (*got_two, own_two, grad_input),
-        "vvvvh",
-        quads,
-        [pltpu.VMEM((8, 4, 8, 128), F32)],
-    )
-    got_two = ring(parts, "dy")
-    own_one, *parts_one = call(
-        first_y_kernel, "grad_one_y", (*got_one, own_one, parts[0]), "vvvvv", quads
-    )
-    got_one = ring(parts_one, "dx")
-
-    out, own = call(
-        last_kernel,
-        "last_stage",
-        (own_two, *got_two, own_one, *got_one),
-        "v" * 8,
-        [far((8, 112, 128), BF), near((112, 128), F32)],
-        [pltpu.VMEM((2, 7, 8, 8, 128), F32)],
-    )
-    planes = lax.all_to_all(out, "z", 0, 0, tiled=True)
     factor = float(256 * 768) ** (-0.5)
     result = jax.ShapeDtypeStruct((27, 8, 32), F32), "v"
     grad_one, grad_two = call(
-        functools.partial(final_kernel, factor), "final_sum", (planes, own), "vv", [result, result]
+        functools.partial(final_kernel, factor), "final_sum", (planes, own, grad_input), "vvh", [result, result]
     )
     shape = lambda g: g.transpose(2, 0, 1).reshape(32, 3, 3, 3, 8)
     return grad_input[None], shape(grad_one), shape(grad_two)

time: 92.9 us -> 101 us (1.087)
  blocking collectives: 19 us -> 0 us
  waiting for transfers between devices: 22.9 us -> 40.3 us
  starting transfers between devices: 27.1 us -> 36.8 us
    all_to_all x1 -> x0, blocking collectives: 19 us -> none  [shards(): planes = lax.all_to_all(out, 'z', 0, 0, tiled=True)]
    ppermute x22, waiting for transfers between devices: 22.9 us -> 36.2 us  [send(): return lax.ppermute(value, AX, pairs)]
    all_to_all x0 -> x1, starting transfers between devices: none -> 8.29 us  [shards(): planes = lax.all_to_all(out, 'z', 0, 0, tiled=True)]
    all_to_all x0 -> x1, waiting for transfers between devices: none -> 4.1 us  [shards(): planes = lax.all_to_all(out, 'z', 0, 0, tiled=True)]
    ppermute x22, starting transfers between devices: 27.1 us -> 28.6 us  [send(): return lax.ppermute(value, AX, pairs)]
  transfers between devices with their start and end apart: 22 -> 23, of which waited for: 8 -> 7; matrix products, arithmetic and copies ran while one was open for 0% -> 0% of each run, Pallas kernels for 15% -> 14%
where the time goes in v6:
time: 101 us; the launch traced here: 100 us
  waiting for transfers between devices  40.3 us (40%)
  starting transfers between devices  36.8 us (36%)
  Pallas kernels  21.7 us (21%)
  between operations  1.41 us (1%)
    ppermute x22, waiting for transfers between devices, send(): return lax.ppermute(value, AX, pairs)  36.2 us
    ppermute x22, starting transfers between devices, send(): return lax.ppermute(value, AX, pairs)  28.6 us
    pallas_call x14, Pallas kernels, call(): pl.pallas_call(kernel, out_shape=tuple((o for o, _ in outs)), in_specs=[s...  21.7 us
    all_to_all x1, starting transfers between devices, shards(): planes = lax.all_to_all(out, 'z', 0, 0, tiled=True)  8.29 us
    all_to_all x1, waiting for transfers between devices, shards(): planes = lax.all_to_all(out, 'z', 0, 0, tiled=True)  4.1 us
  transfers between devices with their start and end apart: 23, of which 7 were waited for; matrix products, arithmetic and copies ran while one was open for 0% of the time, Pallas kernels for 14%

profile of v6, /device:TPU:24, one launch (start us, length us, event | category | flops | bytes accessed | tf_op | source)
XLA Modules:
  0.0 100.3 jit_solution(38737441971566748)
XLA Ops:
  1.9 1.6 %collective-permute-start = (bf16[2,4,16,256]{3,2,1,0:T(8,128)(2,1)S(1)}, bf16[2,4,16,256]{3,2,1,0:T(8,128)(2,1)S(1)}, u32[]{:S(2)}, u32[]{:S(2)}) collective-permute-start(bf16[2,4,16,256]{3,2,1,0:T(8,128)(2,1)S(1)} %get-tuple-element.39), channel_id=1, source_target_pairs={{0,4},{1,5},{2,6},{3,7},{4,0},{5,1},{6,2},{7,3},{8,12},{9,13},{10,... | collective-permute-start | bytes 196616 | tf_op jit(solution)/shard_map/ppermute | solution.py:40
  3.5 3.2 %collective-permute-start.2 = (bf16[2,4,16,256]{3,2,1,0:T(8,128)(2,1)S(1)}, bf16[2,4,16,256]{3,2,1,0:T(8,128)(2,1)S(1)}, u32[]{:S(2)}, u32[]{:S(2)}) collective-permute-start(bf16[2,4,16,256]{3,2,1,0:T(8,128)(2,1)S(1)} %get-tuple-element.41), channel_id=1, source_target_pairs={{0,3},{1,0},{2,1},{3,2},{4,7},{5,4},{6,5},{7,6},{8,11},{9,8},{10,9... | collective-permute-start | bytes 196616 | tf_op jit(solution)/shard_map/ppermute | solution.py:40
  6.8 3.0 %collective-permute-start.4 = (bf16[2,4,16,256]{3,2,1,0:T(8,128)(2,1)S(1)}, bf16[2,4,16,256]{3,2,1,0:T(8,128)(2,1)S(1)}, u32[]{:S(2)}, u32[]{:S(2)}) collective-permute-start(bf16[2,4,16,256]{3,2,1,0:T(8,128)(2,1)S(1)} %get-tuple-element.43), channel_id=1, source_target_pairs={{0,7},{1,4},{2,5},{3,6},{4,3},{5,0},{6,1},{7,2},{8,15},{9,12},{10,... | collective-permute-start | bytes 196616 | tf_op jit(solution)/shard_map/ppermute | solution.py:40
  10.4 2.3 %film.1 = (bf16[768,256]{1,0:T(8,128)(2,1)S(1)}, bf16[4,12,16,256]{3,2,1,0:T(8,128)(2,1)S(1)}, f32[768,256]{1,0:T(8,128)S(1)}, bf16[27,256,256]{2,1,0:T(8,128)(2,1)S(1)}) custom-call(s32[1]{0:T(128)S(6)} %copy.10.step, bf16[4,12,16,256]{3,2,1,0:T(8,128)(2,1)} %bitcast.22, bf16[4,12,16,256]{3,2,1,0:T(8,128)(2,1)} %bitcast.24, f32[1000,512]{1,0:T(8,128)} %table.1, ...), custom_call_target="tpu_custom_call" | custom-call | tf_op jit(solution)/shard_map/film/pallas_call | solution.py:50
  12.8 3.3 %conv_two_back.1 = (bf16[4,14,16,768]{3,2,1,0:T(8,128)(2,1)S(1)}, bf16[4,12,16,256]{3,2,1,0:T(8,128)(2,1)S(1)}) custom-call(bf16[4,12,16,256]{3,2,1,0:T(8,128)(2,1)} %bitcast.17, f32[768,256]{1,0:T(8,128)S(1)} %get-tuple-element.38.slope, bf16[2,4,16,256]{3,2,1,0:T(8,128)(2,1)S(1)} %collective-permute-done.row, ...), custom_call_target="tpu_custom_call" | custom-call | tf_op jit(solution)/shard_map/conv_two_back/pallas_call | solution.py:50
  16.1 1.4 %grad_two_pair.1.after = f32[9,128,768]{2,1,0:T(8,128)S(1)} custom-call(bf16[4,14,16,768]{3,2,1,0:T(8,128)(2,1)S(1)} %get-tuple-element.47.wide, bf16[768,256]{1,0:T(8,128)(2,1)S(1)} %get-tuple-element.48.act), custom_call_target="tpu_custom_call" | custom-call | tf_op jit(solution)/shard_map/grad_two_pair/pallas_call | solution.py:50
  18.7 3.0 %grad_one.1 = (f32[4,27,64,128]{3,2,1,0:T(8,128)S(1)}, f32[4,27,64,128]{3,2,1,0:T(8,128)S(1)}) custom-call(bf16[4,12,16,256]{3,2,1,0:T(8,128)(2,1)S(1)} %get-tuple-element.45.hid.block, bf16[4,12,16,256]{3,2,1,0:T(8,128)(2,1)S(1)} %get-tuple-element.46.inp, bf16[2,4,16,256]{3,2,1,0:T(8,128)(2,1)S(1)} %collective-permute-done.row, ...), custom_call_target="tpu_custom_call" | custom-call | tf_op jit(solution)/shard_map/grad_one/pallas_call | solution.py:50
  22.4 2.8 %collective-permute-start.6 = (bf16[4,16,256]{2,1,0:T(8,128)(2,1)S(1)}, bf16[4,16,256]{2,1,0:T(8,128)(2,1)S(1)}, u32[]{:S(2)}, u32[]{:S(2)}) collective-permute-start(bf16[4,16,256]{2,1,0:T(8,128)(2,1)S(1)} %get-tuple-element.51), channel_id=1, source_target_pairs={{0,3},{1,0},{2,1},{3,2},{4,7},{5,4},{6,5},{7,6},{8,11},{9,8},{10,9... | collective-permute-start | bytes 98312 | tf_op jit(solution)/shard_map/ppermute | solution.py:40
  25.2 4.5 %collective-permute-done.5.after.left = bf16[4,16,256]{2,1,0:T(8,128)(2,1)S(1)} collective-permute-done((bf16[4,16,256]{2,1,0:T(8,128)(2,1)S(1)}, bf16[4,16,256]{2,1,0:T(8,128)(2,1)S(1)}, u32[]{:S(2)}, u32[]{:S(2)}) %collective-permute-start.5) | collective-permute-done | bytes 32800 | tf_op jit(solution)/shard_map/ppermute | solution.py:40
  29.6 1.4 %grad_two_own.1 = (f32[9,32,768]{2,1,0:T(8,128)S(1)}, bf16[9,32,768]{2,1,0:T(8,128)(2,1)S(1)}, bf16[9,32,768]{2,1,0:T(8,128)(2,1)S(1)}, bf16[9,32,768]{2,1,0:T(8,128)(2,1)S(1)}) custom-call(bf16[4,14,16,768]{3,2,1,0:T(8,128)(2,1)S(1)} %get-tuple-element.47.wide, bf16[768,256]{1,0:T(8,128)(2,1)S(1)} %get-tuple-element.48.act, ...), custom_call_target="tpu_custom_call" | custom-call | tf_op jit(solution)/shard_map/grad_two_own/pallas_call | solution.py:50
  32.0 1.4 %collective-permute-start.11 = (bf16[9,32,768]{2,1,0:T(8,128)(2,1)S(1)}, bf16[9,32,768]{2,1,0:T(8,128)(2,1)S(1)}, u32[]{:S(2)}, u32[]{:S(2)}) collective-permute-start(bf16[9,32,768]{2,1,0:T(8,128)(2,1)S(1)} %get-tuple-element.53.after), channel_id=1, source_target_pairs={{0,4},{1,5},{2,6},{3,7},{4,2},{5,3},{6,0},{7,1},{8,12},{9,13},{10,... | collective-permute-start | bytes 1327112 | tf_op jit(solution)/shard_map/ppermute | solution.py:40
  33.4 1.8 %collective-permute-start.12 = (bf16[9,32,768]{2,1,0:T(8,128)(2,1)S(1)}, bf16[9,32,768]{2,1,0:T(8,128)(2,1)S(1)}, u32[]{:S(2)}, u32[]{:S(2)}) collective-permute-start(bf16[9,32,768]{2,1,0:T(8,128)(2,1)S(1)} %get-tuple-element.56), channel_id=1, source_target_pairs={{0,6},{1,7},{2,4},{3,5},{4,0},{5,1},{6,2},{7,3},{8,14},{9,15},{10,... | collective-permute-start | bytes 1327112 | tf_op jit(solution)/shard_map/ppermute | solution.py:40
  37.1 18.1 %collective-permute-done.9.after.row = bf16[3,4,16,256]{3,2,1,0:T(8,128)(2,1)S(1)} collective-permute-done((bf16[3,4,16,256]{3,2,1,0:T(8,128)(2,1)S(1)}, bf16[3,4,16,256]{3,2,1,0:T(8,128)(2,1)S(1)}, u32[]{:S(2)}, u32[]{:S(2)}) %collective-permute-start.9) | collective-permute-done | bytes 98336 | tf_op jit(solution)/shard_map/ppermute | solution.py:40
  55.8 1.5 %collective-permute-start.18 = (bf16[27,64,128]{2,1,0:T(8,128)(2,1)S(1)}, bf16[27,64,128]{2,1,0:T(8,128)(2,1)S(1)}, u32[]{:S(2)}, u32[]{:S(2)}) collective-permute-start(bf16[27,64,128]{2,1,0:T(8,128)(2,1)S(1)} %get-tuple-element.63), channel_id=1, source_target_pairs={{0,24},{1,25},{2,26},{3,27},{4,28},{5,29},{6,30},{7,31},{8,0},{9,1... | collective-permute-start | bytes 1327112 | tf_op jit(solution)/shard_map/ppermute | solution.py:40
  59.0 2.2 %collective-permute-start.14 = (bf16[7,64,128]{2,1,0:T(8,128)(2,1)S(1)}, bf16[7,64,128]{2,1,0:T(8,128)(2,1)S(1)}, u32[]{:S(2)}, u32[]{:S(2)}) collective-permute-start(bf16[7,64,128]{2,1,0:T(8,128)(2,1)S(1)} %get-tuple-element.60.after), channel_id=1, source_target_pairs={{0,8},{1,9},{2,10},{3,11},{4,12},{5,13},{6,14},{7,15},{8,16},{9,17... | collective-permute-start | bytes 344072 | tf_op jit(solution)/shard_map/ppermute | solution.py:40
  61.2 7.1 %collective-permute-done.17.got2 = bf16[27,64,128]{2,1,0:T(8,128)(2,1)S(1)} collective-permute-done((bf16[27,64,128]{2,1,0:T(8,128)(2,1)S(1)}, bf16[27,64,128]{2,1,0:T(8,128)(2,1)S(1)}, u32[]{:S(2)}, u32[]{:S(2)}) %collective-permute-start.17) | collective-permute-done | bytes 442400 | tf_op jit(solution)/shard_map/ppermute | solution.py:40
  68.3 3.7 %collective-permute-done.18.got3 = bf16[27,64,128]{2,1,0:T(8,128)(2,1)S(1)} collective-permute-done((bf16[27,64,128]{2,1,0:T(8,128)(2,1)S(1)}, bf16[27,64,128]{2,1,0:T(8,128)(2,1)S(1)}, u32[]{:S(2)}, u32[]{:S(2)}) %collective-permute-start.18) | collective-permute-done | bytes 442400 | tf_op jit(solution)/shard_map/ppermute | solution.py:40
  72.5 1.7 %collective-permute-start.19 = (bf16[7,64,128]{2,1,0:T(8,128)(2,1)S(1)}, bf16[7,64,128]{2,1,0:T(8,128)(2,1)S(1)}, u32[]{:S(2)}, u32[]{:S(2)}) collective-permute-start(bf16[7,64,128]{2,1,0:T(8,128)(2,1)S(1)} %get-tuple-element.66), channel_id=1, source_target_pairs={{0,2},{1,3},{2,0},{3,1},{4,6},{5,7},{6,4},{7,5},{8,10},{9,11},{10,... | collective-permute-start | bytes 344072 | tf_op jit(solution)/shard_map/ppermute | solution.py:40
  75.3 2.2 %collective-permute-start.21 = (bf16[7,64,128]{2,1,0:T(8,128)(2,1)S(1)}, bf16[7,64,128]{2,1,0:T(8,128)(2,1)S(1)}, u32[]{:S(2)}, u32[]{:S(2)}) collective-permute-start(bf16[7,64,128]{2,1,0:T(8,128)(2,1)S(1)} %get-tuple-element.68), channel_id=1, source_target_pairs={{0,6},{1,7},{2,4},{3,5},{4,0},{5,1},{6,2},{7,3},{8,14},{9,15},{10,... | collective-permute-start | bytes 344072 | tf_op jit(solution)/shard_map/ppermute | solution.py:40
  77.5 1.4 %collective-permute-done.19.b1 = bf16[7,64,128]{2,1,0:T(8,128)(2,1)S(1)} collective-permute-done((bf16[7,64,128]{2,1,0:T(8,128)(2,1)S(1)}, bf16[7,64,128]{2,1,0:T(8,128)(2,1)S(1)}, u32[]{:S(2)}, u32[]{:S(2)}) %collective-permute-start.19) | collective-permute-done | bytes 114720 | tf_op jit(solution)/shard_map/ppermute | solution.py:40
  78.9 1.4 %collective-permute-done.20.b2 = bf16[7,64,128]{2,1,0:T(8,128)(2,1)S(1)} collective-permute-done((bf16[7,64,128]{2,1,0:T(8,128)(2,1)S(1)}, bf16[7,64,128]{2,1,0:T(8,128)(2,1)S(1)}, u32[]{:S(2)}, u32[]{:S(2)}) %collective-permute-start.20) | collective-permute-done | bytes 114720 | tf_op jit(solution)/shard_map/ppermute | solution.py:40
  81.1 8.3 %all-to-all-start = ((bf16[8,112,128]{2,1,0:T(8,128)(2,1)}), bf16[8,112,128]{2,1,0:T(8,128)(2,1)S(1)}, u32[]{:S(2)}, u32[]{:S(2)}) async-start(bf16[8,112,128]{2,1,0:T(8,128)(2,1)} %get-tuple-element.70), calls=%async_computation | async-start | bytes 458752 | tf_op jit(solution)/shard_map/all_to_all | solution.py:488
  89.4 6.0 %conv_one_back.1.after = bf16[4,12,16,256]{3,2,1,0:T(8,128)(2,1)} custom-call(bf16[4,12,16,256]{3,2,1,0:T(8,128)(2,1)S(1)} %get-tuple-element.45.hid.block, bf16[4,12,16,256]{3,2,1,0:T(8,128)(2,1)} %bitcast.18, bf16[3,4,16,256]{3,2,1,0:T(8,128)(2,1)S(1)} %collective-permute-done.9.after.row, bf16[4,16,256]{2,1,0:T(8,128)(2,1)S(1)} %collective-permute-done.5.after.left, ...), custom_call_target="tpu_custom_call" | custom-call | tf_op jit(solution)/shard_map/conv_one_back/pallas_call | solution.py:50
  95.4 4.1 %all-to-all-done.got = bf16[8,112,128]{2,1,0:T(8,128)(2,1)S(1)} async-done(((bf16[8,112,128]{2,1,0:T(8,128)(2,1)}), bf16[8,112,128]{2,1,0:T(8,128)(2,1)S(1)}, u32[]{:S(2)}, u32[]{:S(2)}) %all-to-all-start) | async-done | bytes 229408 | tf_op jit(solution)/shard_map/all_to_all | solution.py:488
  (36 shorter events, 11.5 us)
Async XLA Ops:
  1.9 10.8 %collective-permute-start = (bf16[2,4,16,256]{3,2,1,0:T(8,128)(2,1)S(1)}, bf16[2,4,16,256]{3,2,1,0:T(8,128)(2,1)S(1)}, u32[]{:S(2)}, u32[]{:S(2)}) collective-permute-start(bf16[2,4,16,256]{3,2,1,0:T(8,128)(2,1)S(1)} %get-tuple-element.39), channel_id=1, source_target_pairs={{0,4},{1,5},{2,6},{3,7},{4,0},{5,1},{6,2},{7,3},{8,12},{9,13},{10,... | collective-permute-start | bytes 196616 | tf_op jit(solution)/shard_map/ppermute | solution.py:40
  3.5 9.2 %collective-permute-start.1 = (bf16[2,4,16,256]{3,2,1,0:T(8,128)(2,1)S(1)}, bf16[2,4,16,256]{3,2,1,0:T(8,128)(2,1)S(1)}, u32[]{:S(2)}, u32[]{:S(2)}) collective-permute-start(bf16[2,4,16,256]{3,2,1,0:T(8,128)(2,1)S(1)} %get-tuple-element.40), channel_id=1, source_target_pairs={{0,1},{1,2},{2,3},{3,0},{4,5},{5,6},{6,7},{7,4},{8,9},{9,10},{10,1... | collective-permute-start | bytes 196616 | tf_op jit(solution)/shard_map/ppermute | solution.py:40
  3.5 9.2 %collective-permute-start.2 = (bf16[2,4,16,256]{3,2,1,0:T(8,128)(2,1)S(1)}, bf16[2,4,16,256]{3,2,1,0:T(8,128)(2,1)S(1)}, u32[]{:S(2)}, u32[]{:S(2)}) collective-permute-start(bf16[2,4,16,256]{3,2,1,0:T(8,128)(2,1)S(1)} %get-tuple-element.41), channel_id=1, source_target_pairs={{0,3},{1,0},{2,1},{3,2},{4,7},{5,4},{6,5},{7,6},{8,11},{9,8},{10,9... | collective-permute-start | bytes 196616 | tf_op jit(solution)/shard_map/ppermute | solution.py:40
  6.8 6.0 %collective-permute-start.3 = (bf16[2,4,16,256]{3,2,1,0:T(8,128)(2,1)S(1)}, bf16[2,4,16,256]{3,2,1,0:T(8,128)(2,1)S(1)}, u32[]{:S(2)}, u32[]{:S(2)}) collective-permute-start(bf16[2,4,16,256]{3,2,1,0:T(8,128)(2,1)S(1)} %get-tuple-element.42), channel_id=1, source_target_pairs={{0,5},{1,6},{2,7},{3,4},{4,1},{5,2},{6,3},{7,0},{8,13},{9,14},{10,... | collective-permute-start | bytes 196616 | tf_op jit(solution)/shard_map/ppermute | solution.py:40
  6.8 6.0 %collective-permute-start.4 = (bf16[2,4,16,256]{3,2,1,0:T(8,128)(2,1)S(1)}, bf16[2,4,16,256]{3,2,1,0:T(8,128)(2,1)S(1)}, u32[]{:S(2)}, u32[]{:S(2)}) collective-permute-start(bf16[2,4,16,256]{3,2,1,0:T(8,128)(2,1)S(1)} %get-tuple-element.43), channel_id=1, source_target_pairs={{0,7},{1,4},{2,5},{3,6},{4,3},{5,0},{6,1},{7,2},{8,15},{9,12},{10,... | collective-permute-start | bytes 196616 | tf_op jit(solution)/shard_map/ppermute | solution.py:40
  17.5 12.1 %collective-permute-start.8 = (f32[9,128,768]{2,1,0:T(8,128)S(1)}, f32[9,128,768]{2,1,0:T(8,128)S(1)}, u32[]{:S(2)}, u32[]{:S(2)}) collective-permute-start(f32[9,128,768]{2,1,0:T(8,128)S(1)} %grad_two_pair.1.after), channel_id=1, source_target_pairs={{0,1},{1,0},{2,3},{3,2},{4,5},{5,4},{6,7},{7,6},{8,9},{9,8},{10,11... | collective-permute-start | bytes 10616840 | tf_op jit(solution)/shard_map/ppermute | solution.py:40
  21.6 13.6 %collective-permute-start.7 = (f32[4,27,64,128]{3,2,1,0:T(8,128)S(1)}, f32[4,27,64,128]{3,2,1,0:T(8,128)S(1)}, u32[]{:S(2)}, u32[]{:S(2)}) collective-permute-start(f32[4,27,64,128]{3,2,1,0:T(8,128)S(1)} %get-tuple-element.49.after), channel_id=1, source_target_pairs={{0,1},{1,0},{2,3},{3,2},{4,5},{5,4},{6,7},{7,6},{8,9},{9,8},{10,11... | collective-permute-start | bytes 10616840 | tf_op jit(solution)/shard_map/ppermute | solution.py:40
  21.8 7.8 %collective-permute-start.5 = (bf16[4,16,256]{2,1,0:T(8,128)(2,1)S(1)}, bf16[4,16,256]{2,1,0:T(8,128)(2,1)S(1)}, u32[]{:S(2)}, u32[]{:S(2)}) collective-permute-start(bf16[4,16,256]{2,1,0:T(8,128)(2,1)S(1)} %get-tuple-element.50), channel_id=1, source_target_pairs={{0,1},{1,2},{2,3},{3,0},{4,5},{5,6},{6,7},{7,4},{8,9},{9,10},{10,1... | collective-permute-start | bytes 98312 | tf_op jit(solution)/shard_map/ppermute | solution.py:40
  22.4 7.2 %collective-permute-start.6 = (bf16[4,16,256]{2,1,0:T(8,128)(2,1)S(1)}, bf16[4,16,256]{2,1,0:T(8,128)(2,1)S(1)}, u32[]{:S(2)}, u32[]{:S(2)}) collective-permute-start(bf16[4,16,256]{2,1,0:T(8,128)(2,1)S(1)} %get-tuple-element.51), channel_id=1, source_target_pairs={{0,3},{1,0},{2,1},{3,2},{4,7},{5,4},{6,5},{7,6},{8,11},{9,8},{10,9... | collective-permute-start | bytes 98312 | tf_op jit(solution)/shard_map/ppermute | solution.py:40
  31.1 24.7 %collective-permute-start.10 = (bf16[9,32,768]{2,1,0:T(8,128)(2,1)S(1)}, bf16[9,32,768]{2,1,0:T(8,128)(2,1)S(1)}, u32[]{:S(2)}, u32[]{:S(2)}) collective-permute-start(bf16[9,32,768]{2,1,0:T(8,128)(2,1)S(1)} %get-tuple-element.55), channel_id=1, source_target_pairs={{0,2},{1,3},{2,0},{3,1},{4,6},{5,7},{6,4},{7,5},{8,10},{9,11},{10,... | collective-permute-start | bytes 1327112 | tf_op jit(solution)/shard_map/ppermute | solution.py:40
  32.0 25.3 %collective-permute-start.11 = (bf16[9,32,768]{2,1,0:T(8,128)(2,1)S(1)}, bf16[9,32,768]{2,1,0:T(8,128)(2,1)S(1)}, u32[]{:S(2)}, u32[]{:S(2)}) collective-permute-start(bf16[9,32,768]{2,1,0:T(8,128)(2,1)S(1)} %get-tuple-element.53.after), channel_id=1, source_target_pairs={{0,4},{1,5},{2,6},{3,7},{4,2},{5,3},{6,0},{7,1},{8,12},{9,13},{10,... | collective-permute-start | bytes 1327112 | tf_op jit(solution)/shard_map/ppermute | solution.py:40
  33.4 23.9 %collective-permute-start.12 = (bf16[9,32,768]{2,1,0:T(8,128)(2,1)S(1)}, bf16[9,32,768]{2,1,0:T(8,128)(2,1)S(1)}, u32[]{:S(2)}, u32[]{:S(2)}) collective-permute-start(bf16[9,32,768]{2,1,0:T(8,128)(2,1)S(1)} %get-tuple-element.56), channel_id=1, source_target_pairs={{0,6},{1,7},{2,4},{3,5},{4,0},{5,1},{6,2},{7,3},{8,14},{9,15},{10,... | collective-permute-start | bytes 1327112 | tf_op jit(solution)/shard_map/ppermute | solution.py:40
  35.5 19.7 %collective-permute-start.9 = (bf16[3,4,16,256]{3,2,1,0:T(8,128)(2,1)S(1)}, bf16[3,4,16,256]{3,2,1,0:T(8,128)(2,1)S(1)}, u32[]{:S(2)}, u32[]{:S(2)}) collective-permute-start(bf16[3,4,16,256]{3,2,1,0:T(8,128)(2,1)S(1)} %pack_rows.1), channel_id=1, source_target_pairs={{0,4},{1,5},{2,6},{3,7},{4,0},{5,1},{6,2},{7,3},{8,12},{9,13},{10,... | collective-permute-start | bytes 294920 | tf_op jit(solution)/shard_map/ppermute | solution.py:40
  35.9 25.3 %collective-permute-start.16 = (bf16[27,64,128]{2,1,0:T(8,128)(2,1)S(1)}, bf16[27,64,128]{2,1,0:T(8,128)(2,1)S(1)}, u32[]{:S(2)}, u32[]{:S(2)}) collective-permute-start(bf16[27,64,128]{2,1,0:T(8,128)(2,1)S(1)} %get-tuple-element.62), channel_id=1, source_target_pairs={{0,16},{1,17},{2,18},{3,19},{4,20},{5,21},{6,22},{7,23},{8,24},{9,... | collective-permute-start | bytes 1327112 | tf_op jit(solution)/shard_map/ppermute | solution.py:40
  55.2 13.1 %collective-permute-start.17 = (bf16[27,64,128]{2,1,0:T(8,128)(2,1)S(1)}, bf16[27,64,128]{2,1,0:T(8,128)(2,1)S(1)}, u32[]{:S(2)}, u32[]{:S(2)}) collective-permute-start(bf16[27,64,128]{2,1,0:T(8,128)(2,1)S(1)} %get-tuple-element.54.after), channel_id=1, source_target_pairs={{0,8},{1,9},{2,10},{3,11},{4,12},{5,13},{6,14},{7,15},{8,16},{9,17... | collective-permute-start | bytes 1327112 | tf_op jit(solution)/shard_map/ppermute | solution.py:40
  55.8 16.2 %collective-permute-start.18 = (bf16[27,64,128]{2,1,0:T(8,128)(2,1)S(1)}, bf16[27,64,128]{2,1,0:T(8,128)(2,1)S(1)}, u32[]{:S(2)}, u32[]{:S(2)}) collective-permute-start(bf16[27,64,128]{2,1,0:T(8,128)(2,1)S(1)} %get-tuple-element.63), channel_id=1, source_target_pairs={{0,24},{1,25},{2,26},{3,27},{4,28},{5,29},{6,30},{7,31},{8,0},{9,1... | collective-permute-start | bytes 1327112 | tf_op jit(solution)/shard_map/ppermute | solution.py:40
  57.7 17.6 %collective-permute-start.13 = (bf16[7,64,128]{2,1,0:T(8,128)(2,1)S(1)}, bf16[7,64,128]{2,1,0:T(8,128)(2,1)S(1)}, u32[]{:S(2)}, u32[]{:S(2)}) collective-permute-start(bf16[7,64,128]{2,1,0:T(8,128)(2,1)S(1)} %get-tuple-element.59), channel_id=1, source_target_pairs={{0,16},{1,17},{2,18},{3,19},{4,20},{5,21},{6,22},{7,23},{8,24},{9,... | collective-permute-start | bytes 344072 | tf_op jit(solution)/shard_map/ppermute | solution.py:40
  59.0 18.5 %collective-permute-start.14 = (bf16[7,64,128]{2,1,0:T(8,128)(2,1)S(1)}, bf16[7,64,128]{2,1,0:T(8,128)(2,1)S(1)}, u32[]{:S(2)}, u32[]{:S(2)}) collective-permute-start(bf16[7,64,128]{2,1,0:T(8,128)(2,1)S(1)} %get-tuple-element.60.after), channel_id=1, source_target_pairs={{0,8},{1,9},{2,10},{3,11},{4,12},{5,13},{6,14},{7,15},{8,16},{9,17... | collective-permute-start | bytes 344072 | tf_op jit(solution)/shard_map/ppermute | solution.py:40
  61.2 16.3 %collective-permute-start.15 = (bf16[7,64,128]{2,1,0:T(8,128)(2,1)S(1)}, bf16[7,64,128]{2,1,0:T(8,128)(2,1)S(1)}, u32[]{:S(2)}, u32[]{:S(2)}) collective-permute-start(bf16[7,64,128]{2,1,0:T(8,128)(2,1)S(1)} %get-tuple-element.61), channel_id=1, source_target_pairs={{0,24},{1,25},{2,26},{3,27},{4,28},{5,29},{6,30},{7,31},{8,0},{9,1... | collective-permute-start | bytes 344072 | tf_op jit(solution)/shard_map/ppermute | solution.py:40
  72.5 6.4 %collective-permute-start.19 = (bf16[7,64,128]{2,1,0:T(8,128)(2,1)S(1)}, bf16[7,64,128]{2,1,0:T(8,128)(2,1)S(1)}, u32[]{:S(2)}, u32[]{:S(2)}) collective-permute-start(bf16[7,64,128]{2,1,0:T(8,128)(2,1)S(1)} %get-tuple-element.66), channel_id=1, source_target_pairs={{0,2},{1,3},{2,0},{3,1},{4,6},{5,7},{6,4},{7,5},{8,10},{9,11},{10,... | collective-permute-start | bytes 344072 | tf_op jit(solution)/shard_map/ppermute | solution.py:40
  74.3 6.0 %collective-permute-start.20 = (bf16[7,64,128]{2,1,0:T(8,128)(2,1)S(1)}, bf16[7,64,128]{2,1,0:T(8,128)(2,1)S(1)}, u32[]{:S(2)}, u32[]{:S(2)}) collective-permute-start(bf16[7,64,128]{2,1,0:T(8,128)(2,1)S(1)} %get-tuple-element.67), channel_id=1, source_target_pairs={{0,4},{1,5},{2,6},{3,7},{4,2},{5,3},{6,0},{7,1},{8,12},{9,13},{10,... | collective-permute-start | bytes 344072 | tf_op jit(solution)/shard_map/ppermute | solution.py:40
  75.3 5.0 %collective-permute-start.21 = (bf16[7,64,128]{2,1,0:T(8,128)(2,1)S(1)}, bf16[7,64,128]{2,1,0:T(8,128)(2,1)S(1)}, u32[]{:S(2)}, u32[]{:S(2)}) collective-permute-start(bf16[7,64,128]{2,1,0:T(8,128)(2,1)S(1)} %get-tuple-element.68), channel_id=1, source_target_pairs={{0,6},{1,7},{2,4},{3,5},{4,0},{5,1},{6,2},{7,3},{8,14},{9,15},{10,... | collective-permute-start | bytes 344072 | tf_op jit(solution)/shard_map/ppermute | solution.py:40
  81.1 18.4 %all-to-all-start = ((bf16[8,112,128]{2,1,0:T(8,128)(2,1)}), bf16[8,112,128]{2,1,0:T(8,128)(2,1)S(1)}, u32[]{:S(2)}, u32[]{:S(2)}) async-start(bf16[8,112,128]{2,1,0:T(8,128)(2,1)} %get-tuple-element.70), calls=%async_computation | async-start | bytes 458752 | tf_op jit(solution)/shard_map/all_to_all | solution.py:488

commit v7 on v6

--- a/solution.py
+++ b/solution.py
@@ -72,7 +72,7 @@
 
 def column(wide, lanes_half, f, j):
     cells = wide[lanes_half, pl.ds(f * 192 + j, 12, stride=16), :]
-    return jnp.concatenate([cells, jnp.zeros((4, 128), F32)], axis=0).astype(BF)
+    return jnp.concatenate([cells, jnp.zeros((4, 128), F32)], axis=0)
 
 
 def spread(wide, block):
@@ -90,29 +90,9 @@
             for j, out, corner in ((15, hi, corner_hi), (0, lo, corner_lo)):
                 for h in range(2):
                     lanes = slice(h * 128, h * 128 + 128)
-                    out[n, f, :, lanes] = column(wide, h, f, j)
+                    out[n, f, :, lanes] = column(wide, h, f, j).astype(BF)
                     cell = wide[h, pl.ds(f * 192 + edge * 16 + j, 1), :]
                     corner[n, f, :, lanes] = jnp.broadcast_to(cell, (16, 128)).astype(BF)
-
-
-def pack_columns_kernel(block, after, hi, lo, wide):
-    del after
-    spread(wide, block)
-    for f in range(4):
-        for j, out in ((15, hi), (0, lo)):
-            for h in range(2):
-                out[f, :, h * 128 : h * 128 + 128] = column(wide, h, f, j)
-
-
-def pack_rows_kernel(block, left, right, after, row):
-    del after
-    edge = 11 * (1 - lax.axis_index("ha"))
-    for f in range(4):
-        row[0, f] = block[f, edge]
-        for n, side in ((1, left), (2, right)):
-            cells = side[f].astype(F32)
-            cell = jnp.where(edge == 0, cells[0:1], cells[11:12])
-            row[n, f] = jnp.broadcast_to(cell, (16, 256)).astype(BF)
 
 
 def build_shifted(put, cell_row, row, left, right, corner_left, corner_right):
@@ -222,21 +202,25 @@
     hid_out[...] = (total[...] * slope[...]).astype(BF).reshape(4, 12, 16, 256)
 
 
-def input_conv_kernel(
-    hid, block, row, left, right, after, weight, out, held, total, sem, wide
-):
+def input_conv_kernel(hid, block, border, face, after, weight, out, held, total, sem, wide):
     del after
     copies = weight_copies(weight, held, sem)
     for copy in copies:
         copy.start()
+    is_one = lax.axis_index("core") == 1
+
+    def pick(when_one, when_zero):
+        return jnp.where(is_one, when_one.astype(F32), when_zero.astype(F32))
+
+    faces, outers = border[8].astype(F32), border[9].astype(F32)[4:8]
     build_shifted(
         put_back(wide),
         lambda f, r: hid[f, r],
-        lambda f: row[0, f],
-        lambda f: left[f],
-        lambda f: right[f],
-        lambda f: row[1, f],
-        lambda f: row[2, f],
+        lambda f: border[f],
+        lambda f: pick(face[f], border[4 + f]),
+        lambda f: pick(border[4 + f], face[f]),
+        lambda f: pick(faces[f : f + 1], outers[f : f + 1]),
+        lambda f: pick(outers[f : f + 1], faces[f : f + 1]),
     )
     for copy in copies:
         copy.wait()
@@ -252,14 +236,44 @@
     return lax.dot_general(left, window, TN, preferred_element_type=F32)
 
 
-def second_pair_kernel(wide, act, pair):
+def tile(n):
+    return slice(n // 3 * 16, n // 3 * 16 + 16), slice(n % 3 * 256, n % 3 * 256 + 256)
+
+
+def second_pair_kernel(wide, act, hid, pair, flat):
+    spread(flat, hid)
+    pair[9] = jnp.zeros((128, 768), F32)
+    for f in range(4):
+        for n, j in ((f, 15), (4 + f, 0)):
+            rows, lanes = tile(n)
+            for h in range(2):
+                at = slice(lanes.start + h * 128, lanes.start + h * 128 + 128)
+                pair[9, rows, at] = column(flat, h, f, j)
     for a in range(3):
         for b in range(3):
             pair[a * 3 + b] = second_part(wide, act, 1, a, b)
 
 
-def second_own_kernel(wide, act, got, after, also, keep, one, two, three):
-    del after, also
+def second_own_kernel(wide, act, hid, got, after, keep, one, two, three, face_out):
+    del after
+    is_one = lax.axis_index("core") == 1
+    edge = 11 * (1 - lax.axis_index("ha"))
+    faces, outers = [], []
+    for f in range(4):
+        hi, lo = got[(9, *tile(f))], got[(9, *tile(4 + f))]
+        face, outer = jnp.where(is_one, hi, lo), jnp.where(is_one, lo, hi)
+        face_out[f] = face.astype(BF)
+        two[(9, *tile(f))] = outer.astype(BF)
+        for out in (one, three):
+            out[(9, *tile(f))] = hid[f, edge]
+        faces.append(jnp.where(edge == 0, face[0:1], face[11:12]))
+        outers.append(jnp.where(edge == 0, outer[0:1], outer[11:12]))
+    corners = jnp.concatenate(faces + outers + [jnp.zeros((8, 256), F32)], axis=0).astype(BF)
+    for out in (one, three):
+        out[(9, *tile(4))] = corners
+        out[(9, *tile(5))] = jnp.zeros((16, 256), BF)
+    for n in (4, 5):
+        two[(9, *tile(n))] = jnp.zeros((16, 256), BF)
     for a in range(3):
         for b in range(3):
             total = second_part(wide, act, 0, a, b) + got[a * 3 + b]
@@ -267,9 +281,16 @@
                 out[a * 3 + b] = total[d * 32 : d * 32 + 32].astype(out.dtype)
 
 
-def second_x_kernel(got1, got2, got3, own, after, keep, one, two, three, held):
-    del after
-    y = lax.axis_index("y")
+def second_x_kernel(got2, got1, got3, own, keep, one, two, three, border, held):
+    y, low = lax.axis_index("y"), lax.axis_index("ha") == 0
+    for n in range(5):
+        first, last = got1[(9, *tile(n))].astype(F32), got3[(9, *tile(n))].astype(F32)
+        across, along = jnp.where(low, last, first), jnp.where(low, first, last)
+        if n < 4:
+            border[n] = across.astype(BF)
+            border[4 + n] = got2[(9, *tile(n))]
+        else:
+            border[8], border[9] = across.astype(BF), along.astype(BF)
 
     def tap(t):
         ab, lanes = t // 3, slice(t % 3 * 256, t % 3 * 256 + 256)
@@ -415,7 +436,12 @@
     )
 
     (pair_two,) = call(
-        second_pair_kernel, "grad_two_pair", (wide_cot, act), "vv", [near((9, 128, 768), F32)]
+        second_pair_kernel,
+        "grad_two_pair",
+        (wide_cot, act, grad_hidden),
+        "vvv",
+        [near((10, 128, 768), F32)],
+        [pltpu.VMEM((2, 768, 128), F32)],
     )
     got_pair_two = send(pair_two, core_pairs())
     split = near((4, 27, 64, 128), F32)
@@ -428,21 +454,12 @@
         [pltpu.VMEM((4, 14, 16, 768), BF), pltpu.VMEM((5, 4, 16, 256), F32)],
     )
     got_pair_one = send(pair_one, core_pairs())
-    hi, lo = call(
-        pack_columns_kernel,
-        "pack_columns",
-        (grad_hidden, pair_one),
-        "vv",
-        [near((4, 16, 256), BF)] * 2,
-        [pltpu.VMEM((2, 768, 128), F32)],
-    )
-    left, right = send(hi, block_pairs(0, 1)), send(lo, block_pairs(0, -1))
-    own_two, *parts = call(
+    own_two, *parts, face = call(
         second_own_kernel,
         "grad_two_own",
-        (wide_cot, act, got_pair_two, left, right),
+        (wide_cot, act, grad_hidden, got_pair_two, pair_one),
         "vvvvv",
-        [near((9, 32, 768), F32)] + [near((9, 32, 768), BF)] * 3,
+        [near((9, 32, 768), F32)] + [near((10, 32, 768), BF)] * 3 + [near((4, 16, 256), BF)],
     )
     got_two = ring(parts, "dx")
     own_one, *parts_one = call(
@@ -454,21 +471,12 @@
     )
     got_one = ring(parts_one, "dy")
 
-    (row,) = call(
-        pack_rows_kernel,
-        "pack_rows",
-        (grad_hidden, left, right, parts_one[0]),
-        "vvvv",
-        [near((3, 4, 16, 256), BF)],
-    )
-    row = send(row, block_pairs(1, 0))
-
-    own_two, *parts = call(
+    own_two, *parts, border = call(
         second_x_kernel,
         "grad_two_x",
-        (*got_two, own_two, row),
-        "vvvvv",
-        quads,
+        (*got_two, own_two),
+        "vvvv",
+        quads + [near((10, 16, 256), BF)],
         [pltpu.VMEM((8, 4, 8, 128), F32)],
     )
     got_two = ring(parts, "dy")
@@ -490,8 +498,8 @@
     (grad_input,) = call(
         input_conv_kernel,
         "conv_one_back",
-        (grad_hidden, block, row, left, right, own, taps_one),
-        "vpvvvvh",
+        (grad_hidden, block, border, face, own, taps_one),
+        "vpvvvh",
         [(jax.ShapeDtypeStruct((4, 12, 16, 256), BF), "v")],
         [
             pltpu.VMEM((27, 256, 256), BF),

time: 101 us -> 87 us (0.86)
  waiting for transfers between devices: 40.3 us -> 30.8 us
  starting transfers between devices: 36.8 us -> 32.9 us
    ppermute x22 -> x19, waiting for transfers between devices: 36.2 us -> 26.1 us  [send(): return lax.ppermute(value, AX, pairs)]
    ppermute x22 -> x19, starting transfers between devices: 28.6 us -> 24.4 us  [send(): return lax.ppermute(value, AX, pairs)]
    pallas_call x14 -> x12, Pallas kernels: 21.7 us -> 21.7 us  [call(): pl.pallas_call(kernel, out_shape=tuple((o for o, _ in outs)), in_specs=[s...]
  transfers between devices with their start and end apart: 23 -> 20, of which waited for: 7 -> 10; matrix products, arithmetic and copies ran while one was open for 0% -> 0% of each run, Pallas kernels for 14% -> 16%
where the time goes in v7:
time: 87 us; the launch traced here: 86.7 us
  starting transfers between devices  32.9 us (38%)
  waiting for transfers between devices  30.8 us (35%)
  Pallas kernels  21.7 us (25%)
  between operations  1.39 us (2%)
    ppermute x19, waiting for transfers between devices, send(): return lax.ppermute(value, AX, pairs)  26.1 us
    ppermute x19, starting transfers between devices, send(): return lax.ppermute(value, AX, pairs)  24.4 us
    pallas_call x12, Pallas kernels, call(): pl.pallas_call(kernel, out_shape=tuple((o for o, _ in outs)), in_specs=[s...  21.7 us
    all_to_all x1, starting transfers between devices, shards(): planes = lax.all_to_all(out, 'z', 0, 0, tiled=True)  8.46 us
    all_to_all x1, waiting for transfers between devices, shards(): planes = lax.all_to_all(out, 'z', 0, 0, tiled=True)  4.61 us
  transfers between devices with their start and end apart: 20, of which 10 were waited for; matrix products, arithmetic and copies ran while one was open for 0% of the time, Pallas kernels for 16%

profile of v7, /device:TPU:24, one launch (start us, length us, event | category | flops | bytes accessed | tf_op | source)
XLA Modules:
  0.0 86.7 jit_solution(3924877700098592118)
XLA Ops:
  0.6 1.3 %pack_first.1 = (bf16[2,4,16,256]{3,2,1,0:T(8,128)(2,1)S(1)}, bf16[2,4,16,256]{3,2,1,0:T(8,128)(2,1)S(1)}, bf16[2,4,16,256]{3,2,1,0:T(8,128)(2,1)S(1)}, bf16[2,4...) custom-call(bf16[4,12,16,256]{3,2,1,0:T(8,128)(2,1)} %bitcast.16, bf16[4,12,16,256]{3,2,1,0:T(8,128)(2,1)} %bitcast.21), custom_call_target="tpu_custom_call" | custom-call | tf_op jit(solution)/shard_map/pack_first/pallas_call | solution.py:50
  1.9 1.6 %collective-permute-start = (bf16[2,4,16,256]{3,2,1,0:T(8,128)(2,1)S(1)}, bf16[2,4,16,256]{3,2,1,0:T(8,128)(2,1)S(1)}, u32[]{:S(2)}, u32[]{:S(2)}) collective-permute-start(bf16[2,4,16,256]{3,2,1,0:T(8,128)(2,1)S(1)} %get-tuple-element.39), channel_id=1, source_target_pairs={{0,4},{1,5},{2,6},{3,7},{4,0},{5,1},{6,2},{7,3},{8,12},{9,13},{10,... | collective-permute-start | bytes 196616 | tf_op jit(solution)/shard_map/ppermute | solution.py:40
  3.5 3.2 %collective-permute-start.2 = (bf16[2,4,16,256]{3,2,1,0:T(8,128)(2,1)S(1)}, bf16[2,4,16,256]{3,2,1,0:T(8,128)(2,1)S(1)}, u32[]{:S(2)}, u32[]{:S(2)}) collective-permute-start(bf16[2,4,16,256]{3,2,1,0:T(8,128)(2,1)S(1)} %get-tuple-element.41), channel_id=1, source_target_pairs={{0,3},{1,0},{2,1},{3,2},{4,7},{5,4},{6,5},{7,6},{8,11},{9,8},{10,9... | collective-permute-start | bytes 196616 | tf_op jit(solution)/shard_map/ppermute | solution.py:40
  6.8 3.0 %collective-permute-start.4 = (bf16[2,4,16,256]{3,2,1,0:T(8,128)(2,1)S(1)}, bf16[2,4,16,256]{3,2,1,0:T(8,128)(2,1)S(1)}, u32[]{:S(2)}, u32[]{:S(2)}) collective-permute-start(bf16[2,4,16,256]{3,2,1,0:T(8,128)(2,1)S(1)} %get-tuple-element.43), channel_id=1, source_target_pairs={{0,7},{1,4},{2,5},{3,6},{4,3},{5,0},{6,1},{7,2},{8,15},{9,12},{10,... | collective-permute-start | bytes 196616 | tf_op jit(solution)/shard_map/ppermute | solution.py:40
  10.4 2.3 %film.1 = (bf16[768,256]{1,0:T(8,128)(2,1)S(1)}, bf16[4,12,16,256]{3,2,1,0:T(8,128)(2,1)S(1)}, f32[768,256]{1,0:T(8,128)S(1)}, bf16[27,256,256]{2,1,0:T(8,128)(2,1)S(1)}) custom-call(s32[1]{0:T(128)S(6)} %copy.10.step, bf16[4,12,16,256]{3,2,1,0:T(8,128)(2,1)} %bitcast.22, bf16[4,12,16,256]{3,2,1,0:T(8,128)(2,1)} %bitcast.24, f32[1000,512]{1,0:T(8,128)} %table.1, ...), custom_call_target="tpu_custom_call" | custom-call | tf_op jit(solution)/shard_map/film/pallas_call | solution.py:50
  12.8 3.3 %conv_two_back.1 = (bf16[4,14,16,768]{3,2,1,0:T(8,128)(2,1)S(1)}, bf16[4,12,16,256]{3,2,1,0:T(8,128)(2,1)S(1)}) custom-call(bf16[4,12,16,256]{3,2,1,0:T(8,128)(2,1)} %bitcast.17, f32[768,256]{1,0:T(8,128)S(1)} %get-tuple-element.38.slope, bf16[2,4,16,256]{3,2,1,0:T(8,128)(2,1)S(1)} %collective-permute-done.row, ...), custom_call_target="tpu_custom_call" | custom-call | tf_op jit(solution)/shard_map/conv_two_back/pallas_call | solution.py:50
  16.1 1.5 %grad_two_pair.1.after = f32[10,128,768]{2,1,0:T(8,128)S(1)} custom-call(bf16[4,14,16,768]{3,2,1,0:T(8,128)(2,1)S(1)} %get-tuple-element.46.wide, bf16[768,256]{1,0:T(8,128)(2,1)S(1)} %get-tuple-element.47.act, bf16[4,12,16,256]{3,2,1,0:T(8,128)(2,1)S(1)} %get-tuple-element.45.hid), custom_call_target="tpu_custom_call" | custom-call | tf_op jit(solution)/shard_map/grad_two_pair/pallas_call | solution.py:50
  18.7 3.0 %grad_one.1 = (f32[4,27,64,128]{3,2,1,0:T(8,128)S(1)}, f32[4,27,64,128]{3,2,1,0:T(8,128)S(1)}) custom-call(bf16[4,12,16,256]{3,2,1,0:T(8,128)(2,1)S(1)} %get-tuple-element.45.hid, bf16[4,12,16,256]{3,2,1,0:T(8,128)(2,1)S(1)} %get-tuple-element.48.inp, bf16[2,4,16,256]{3,2,1,0:T(8,128)(2,1)S(1)} %collective-permute-done.row, ...), custom_call_target="tpu_custom_call" | custom-call | tf_op jit(solution)/shard_map/grad_one/pallas_call | solution.py:50
  22.0 3.2 %collective-permute-done.5.got = f32[10,128,768]{2,1,0:T(8,128)S(1)} collective-permute-done((f32[10,128,768]{2,1,0:T(8,128)S(1)}, f32[10,128,768]{2,1,0:T(8,128)S(1)}, u32[]{:S(2)}, u32[]{:S(2)}) %collective-permute-start.5) | collective-permute-done | bytes 3932192 | tf_op jit(solution)/shard_map/ppermute | solution.py:40
  25.1 1.4 %grad_two_own.1 = (f32[9,32,768]{2,1,0:T(8,128)S(1)}, bf16[10,32,768]{2,1,0:T(8,128)(2,1)S(1)}, bf16[10,32,768]{2,1,0:T(8,128)(2,1)S(1)}, bf16[10,32,768]{2,1,0:T(8,128)(2,1)S(1)}, bf16[4,16,256]{2,1,0:T(8,128)(2,1)S(1)}) custom-call(bf16[4,14,16,768]{3,2,1,0:T(8,128)(2,1)S(1)} %get-tuple-element.46.wide, bf16[768,256]{1,0:T(8,128)(2,1)S(1)} %get-tuple-element.47.act, ...), custom_call_target="tpu_custom_call" | custom-call | tf_op jit(solution)/shard_map/grad_two_own/pallas_call | solution.py:50
  27.5 1.3 %collective-permute-start.8 = (bf16[10,32,768]{2,1,0:T(8,128)(2,1)S(1)}, bf16[10,32,768]{2,1,0:T(8,128)(2,1)S(1)}, u32[]{:S(2)}, u32[]{:S(2)}) collective-permute-start(bf16[10,32,768]{2,1,0:T(8,128)(2,1)S(1)} %get-tuple-element.52), channel_id=1, source_target_pairs={{0,6},{1,7},{2,4},{3,5},{4,0},{5,1},{6,2},{7,3},{8,14},{9,15},{10,... | collective-permute-start | bytes 1474568 | tf_op jit(solution)/shard_map/ppermute | solution.py:40
  30.5 1.3 %collective-permute-start.13 = (bf16[27,64,128]{2,1,0:T(8,128)(2,1)S(1)}, bf16[27,64,128]{2,1,0:T(8,128)(2,1)S(1)}, u32[]{:S(2)}, u32[]{:S(2)}) collective-permute-start(bf16[27,64,128]{2,1,0:T(8,128)(2,1)S(1)} %get-tuple-element.61), channel_id=1, source_target_pairs={{0,16},{1,17},{2,18},{3,19},{4,20},{5,21},{6,22},{7,23},{8,24},{9,... | collective-permute-start | bytes 1327112 | tf_op jit(solution)/shard_map/ppermute | solution.py:40
  31.8 2.2 %collective-permute-start.14 = (bf16[27,64,128]{2,1,0:T(8,128)(2,1)S(1)}, bf16[27,64,128]{2,1,0:T(8,128)(2,1)S(1)}, u32[]{:S(2)}, u32[]{:S(2)}) collective-permute-start(bf16[27,64,128]{2,1,0:T(8,128)(2,1)S(1)} %get-tuple-element.62), channel_id=1, source_target_pairs={{0,8},{1,9},{2,10},{3,11},{4,12},{5,13},{6,14},{7,15},{8,16},{9,17... | collective-permute-start | bytes 1327112 | tf_op jit(solution)/shard_map/ppermute | solution.py:40
  34.0 8.2 %collective-permute-done.6.got2 = bf16[10,32,768]{2,1,0:T(8,128)(2,1)S(1)} collective-permute-done((bf16[10,32,768]{2,1,0:T(8,128)(2,1)S(1)}, bf16[10,32,768]{2,1,0:T(8,128)(2,1)S(1)}, u32[]{:S(2)}, u32[]{:S(2)}) %collective-permute-start.6) | collective-permute-done | bytes 491552 | tf_op jit(solution)/shard_map/ppermute | solution.py:40
  43.0 7.7 %collective-permute-done.8.got3 = bf16[10,32,768]{2,1,0:T(8,128)(2,1)S(1)} collective-permute-done((bf16[10,32,768]{2,1,0:T(8,128)(2,1)S(1)}, bf16[10,32,768]{2,1,0:T(8,128)(2,1)S(1)}, u32[]{:S(2)}, u32[]{:S(2)}) %collective-permute-start.8) | collective-permute-done | bytes 491552 | tf_op jit(solution)/shard_map/ppermute | solution.py:40
  50.7 1.5 %collective-permute-done.7.got1 = bf16[10,32,768]{2,1,0:T(8,128)(2,1)S(1)} collective-permute-done((bf16[10,32,768]{2,1,0:T(8,128)(2,1)S(1)}, bf16[10,32,768]{2,1,0:T(8,128)(2,1)S(1)}, u32[]{:S(2)}, u32[]{:S(2)}) %collective-permute-start.7) | collective-permute-done | bytes 491552 | tf_op jit(solution)/shard_map/ppermute | solution.py:40
  52.6 1.3 %collective-permute-start.9 = (bf16[7,64,128]{2,1,0:T(8,128)(2,1)S(1)}, bf16[7,64,128]{2,1,0:T(8,128)(2,1)S(1)}, u32[]{:S(2)}, u32[]{:S(2)}) collective-permute-start(bf16[7,64,128]{2,1,0:T(8,128)(2,1)S(1)} %get-tuple-element.57), channel_id=1, source_target_pairs={{0,16},{1,17},{2,18},{3,19},{4,20},{5,21},{6,22},{7,23},{8,24},{9,... | collective-permute-start | bytes 344072 | tf_op jit(solution)/shard_map/ppermute | solution.py:40
  53.9 3.2 %collective-permute-start.10 = (bf16[7,64,128]{2,1,0:T(8,128)(2,1)S(1)}, bf16[7,64,128]{2,1,0:T(8,128)(2,1)S(1)}, u32[]{:S(2)}, u32[]{:S(2)}) collective-permute-start(bf16[7,64,128]{2,1,0:T(8,128)(2,1)S(1)} %get-tuple-element.58.after), channel_id=1, source_target_pairs={{0,8},{1,9},{2,10},{3,11},{4,12},{5,13},{6,14},{7,15},{8,16},{9,17... | collective-permute-start | bytes 344072 | tf_op jit(solution)/shard_map/ppermute | solution.py:40
  58.3 1.4 %collective-permute-start.17 = (bf16[7,64,128]{2,1,0:T(8,128)(2,1)S(1)}, bf16[7,64,128]{2,1,0:T(8,128)(2,1)S(1)}, u32[]{:S(2)}, u32[]{:S(2)}) collective-permute-start(bf16[7,64,128]{2,1,0:T(8,128)(2,1)S(1)} %get-tuple-element.67), channel_id=1, source_target_pairs={{0,4},{1,5},{2,6},{3,7},{4,2},{5,3},{6,0},{7,1},{8,12},{9,13},{10,... | collective-permute-start | bytes 344072 | tf_op jit(solution)/shard_map/ppermute | solution.py:40
  60.2 1.4 %collective-permute-start.18 = (bf16[7,64,128]{2,1,0:T(8,128)(2,1)S(1)}, bf16[7,64,128]{2,1,0:T(8,128)(2,1)S(1)}, u32[]{:S(2)}, u32[]{:S(2)}) collective-permute-start(bf16[7,64,128]{2,1,0:T(8,128)(2,1)S(1)} %get-tuple-element.68), channel_id=1, source_target_pairs={{0,6},{1,7},{2,4},{3,5},{4,0},{5,1},{6,2},{7,3},{8,14},{9,15},{10,... | collective-permute-start | bytes 344072 | tf_op jit(solution)/shard_map/ppermute | solution.py:40
  61.8 3.1 %collective-permute-done.16.b1 = bf16[7,64,128]{2,1,0:T(8,128)(2,1)S(1)} collective-permute-done((bf16[7,64,128]{2,1,0:T(8,128)(2,1)S(1)}, bf16[7,64,128]{2,1,0:T(8,128)(2,1)S(1)}, u32[]{:S(2)}, u32[]{:S(2)}) %collective-permute-start.16) | collective-permute-done | bytes 114720 | tf_op jit(solution)/shard_map/ppermute | solution.py:40
  66.8 8.5 %all-to-all-start = ((bf16[8,112,128]{2,1,0:T(8,128)(2,1)}), bf16[8,112,128]{2,1,0:T(8,128)(2,1)S(1)}, u32[]{:S(2)}, u32[]{:S(2)}) async-start(bf16[8,112,128]{2,1,0:T(8,128)(2,1)} %get-tuple-element.70), calls=%async_computation | async-start | bytes 458752 | tf_op jit(solution)/shard_map/all_to_all | solution.py:496
  75.3 6.0 %conv_one_back.1.after = bf16[4,12,16,256]{3,2,1,0:T(8,128)(2,1)} custom-call(bf16[4,12,16,256]{3,2,1,0:T(8,128)(2,1)S(1)} %get-tuple-element.45.hid, bf16[4,12,16,256]{3,2,1,0:T(8,128)(2,1)} %bitcast.18, bf16[10,16,256]{2,1,0:T(8,128)(2,1)S(1)} %get-tuple-element.54.border, bf16[4,16,256]{2,1,0:T(8,128)(2,1)S(1)} %get-tuple-element.55.face, ...), custom_call_target="tpu_custom_call" | custom-call | tf_op jit(solution)/shard_map/conv_one_back/pallas_call | solution.py:50
  81.3 4.6 %all-to-all-done.got = bf16[8,112,128]{2,1,0:T(8,128)(2,1)S(1)} async-done(((bf16[8,112,128]{2,1,0:T(8,128)(2,1)}), bf16[8,112,128]{2,1,0:T(8,128)(2,1)S(1)}, u32[]{:S(2)}, u32[]{:S(2)}) %all-to-all-start) | async-done | bytes 229408 | tf_op jit(solution)/shard_map/all_to_all | solution.py:496
  (28 shorter events, 9.9 us)
Async XLA Ops:
  1.9 10.8 %collective-permute-start = (bf16[2,4,16,256]{3,2,1,0:T(8,128)(2,1)S(1)}, bf16[2,4,16,256]{3,2,1,0:T(8,128)(2,1)S(1)}, u32[]{:S(2)}, u32[]{:S(2)}) collective-permute-start(bf16[2,4,16,256]{3,2,1,0:T(8,128)(2,1)S(1)} %get-tuple-element.39), channel_id=1, source_target_pairs={{0,4},{1,5},{2,6},{3,7},{4,0},{5,1},{6,2},{7,3},{8,12},{9,13},{10,... | collective-permute-start | bytes 196616 | tf_op jit(solution)/shard_map/ppermute | solution.py:40
  3.5 9.2 %collective-permute-start.1 = (bf16[2,4,16,256]{3,2,1,0:T(8,128)(2,1)S(1)}, bf16[2,4,16,256]{3,2,1,0:T(8,128)(2,1)S(1)}, u32[]{:S(2)}, u32[]{:S(2)}) collective-permute-start(bf16[2,4,16,256]{3,2,1,0:T(8,128)(2,1)S(1)} %get-tuple-element.40), channel_id=1, source_target_pairs={{0,1},{1,2},{2,3},{3,0},{4,5},{5,6},{6,7},{7,4},{8,9},{9,10},{10,1... | collective-permute-start | bytes 196616 | tf_op jit(solution)/shard_map/ppermute | solution.py:40
  3.5 9.2 %collective-permute-start.2 = (bf16[2,4,16,256]{3,2,1,0:T(8,128)(2,1)S(1)}, bf16[2,4,16,256]{3,2,1,0:T(8,128)(2,1)S(1)}, u32[]{:S(2)}, u32[]{:S(2)}) collective-permute-start(bf16[2,4,16,256]{3,2,1,0:T(8,128)(2,1)S(1)} %get-tuple-element.41), channel_id=1, source_target_pairs={{0,3},{1,0},{2,1},{3,2},{4,7},{5,4},{6,5},{7,6},{8,11},{9,8},{10,9... | collective-permute-start | bytes 196616 | tf_op jit(solution)/shard_map/ppermute | solution.py:40
  6.8 6.0 %collective-permute-start.3 = (bf16[2,4,16,256]{3,2,1,0:T(8,128)(2,1)S(1)}, bf16[2,4,16,256]{3,2,1,0:T(8,128)(2,1)S(1)}, u32[]{:S(2)}, u32[]{:S(2)}) collective-permute-start(bf16[2,4,16,256]{3,2,1,0:T(8,128)(2,1)S(1)} %get-tuple-element.42), channel_id=1, source_target_pairs={{0,5},{1,6},{2,7},{3,4},{4,1},{5,2},{6,3},{7,0},{8,13},{9,14},{10,... | collective-permute-start | bytes 196616 | tf_op jit(solution)/shard_map/ppermute | solution.py:40
  6.8 6.0 %collective-permute-start.4 = (bf16[2,4,16,256]{3,2,1,0:T(8,128)(2,1)S(1)}, bf16[2,4,16,256]{3,2,1,0:T(8,128)(2,1)S(1)}, u32[]{:S(2)}, u32[]{:S(2)}) collective-permute-start(bf16[2,4,16,256]{3,2,1,0:T(8,128)(2,1)S(1)} %get-tuple-element.43), channel_id=1, source_target_pairs={{0,7},{1,4},{2,5},{3,6},{4,3},{5,0},{6,1},{7,2},{8,15},{9,12},{10,... | collective-permute-start | bytes 196616 | tf_op jit(solution)/shard_map/ppermute | solution.py:40
  17.5 7.6 %collective-permute-start.5 = (f32[10,128,768]{2,1,0:T(8,128)S(1)}, f32[10,128,768]{2,1,0:T(8,128)S(1)}, u32[]{:S(2)}, u32[]{:S(2)}) collective-permute-start(f32[10,128,768]{2,1,0:T(8,128)S(1)} %grad_two_pair.1.after), channel_id=1, source_target_pairs={{0,1},{1,0},{2,3},{3,2},{4,5},{5,4},{6,7},{7,6},{8,9},{9,8},{10,11... | collective-permute-start | bytes 11796488 | tf_op jit(solution)/shard_map/ppermute | solution.py:40
  21.7 8.5 %collective-permute-start.12 = (f32[4,27,64,128]{3,2,1,0:T(8,128)S(1)}, f32[4,27,64,128]{3,2,1,0:T(8,128)S(1)}, u32[]{:S(2)}, u32[]{:S(2)}) collective-permute-start(f32[4,27,64,128]{3,2,1,0:T(8,128)S(1)} %get-tuple-element.49.after), channel_id=1, source_target_pairs={{0,1},{1,0},{2,3},{3,2},{4,5},{5,4},{6,7},{7,6},{8,9},{9,8},{10,11... | collective-permute-start | bytes 10616840 | tf_op jit(solution)/shard_map/ppermute | solution.py:40
  26.6 15.7 %collective-permute-start.6 = (bf16[10,32,768]{2,1,0:T(8,128)(2,1)S(1)}, bf16[10,32,768]{2,1,0:T(8,128)(2,1)S(1)}, u32[]{:S(2)}, u32[]{:S(2)}) collective-permute-start(bf16[10,32,768]{2,1,0:T(8,128)(2,1)S(1)} %get-tuple-element.50), channel_id=1, source_target_pairs={{0,2},{1,3},{2,0},{3,1},{4,6},{5,7},{6,4},{7,5},{8,10},{9,11},{10,... | collective-permute-start | bytes 1474568 | tf_op jit(solution)/shard_map/ppermute | solution.py:40
  27.5 23.2 %collective-permute-start.8 = (bf16[10,32,768]{2,1,0:T(8,128)(2,1)S(1)}, bf16[10,32,768]{2,1,0:T(8,128)(2,1)S(1)}, u32[]{:S(2)}, u32[]{:S(2)}) collective-permute-start(bf16[10,32,768]{2,1,0:T(8,128)(2,1)S(1)} %get-tuple-element.52), channel_id=1, source_target_pairs={{0,6},{1,7},{2,4},{3,5},{4,0},{5,1},{6,2},{7,3},{8,14},{9,15},{10,... | collective-permute-start | bytes 1474568 | tf_op jit(solution)/shard_map/ppermute | solution.py:40
  28.7 23.5 %collective-permute-start.7 = (bf16[10,32,768]{2,1,0:T(8,128)(2,1)S(1)}, bf16[10,32,768]{2,1,0:T(8,128)(2,1)S(1)}, u32[]{:S(2)}, u32[]{:S(2)}) collective-permute-start(bf16[10,32,768]{2,1,0:T(8,128)(2,1)S(1)} %get-tuple-element.51.after), channel_id=1, source_target_pairs={{0,4},{1,5},{2,6},{3,7},{4,2},{5,3},{6,0},{7,1},{8,12},{9,13},{10,... | collective-permute-start | bytes 1474568 | tf_op jit(solution)/shard_map/ppermute | solution.py:40
  30.5 23.4 %collective-permute-start.13 = (bf16[27,64,128]{2,1,0:T(8,128)(2,1)S(1)}, bf16[27,64,128]{2,1,0:T(8,128)(2,1)S(1)}, u32[]{:S(2)}, u32[]{:S(2)}) collective-permute-start(bf16[27,64,128]{2,1,0:T(8,128)(2,1)S(1)} %get-tuple-element.61), channel_id=1, source_target_pairs={{0,16},{1,17},{2,18},{3,19},{4,20},{5,21},{6,22},{7,23},{8,24},{9,... | collective-permute-start | bytes 1327112 | tf_op jit(solution)/shard_map/ppermute | solution.py:40
  31.8 25.3 %collective-permute-start.14 = (bf16[27,64,128]{2,1,0:T(8,128)(2,1)S(1)}, bf16[27,64,128]{2,1,0:T(8,128)(2,1)S(1)}, u32[]{:S(2)}, u32[]{:S(2)}) collective-permute-start(bf16[27,64,128]{2,1,0:T(8,128)(2,1)S(1)} %get-tuple-element.62), channel_id=1, source_target_pairs={{0,8},{1,9},{2,10},{3,11},{4,12},{5,13},{6,14},{7,15},{8,16},{9,17... | collective-permute-start | bytes 1327112 | tf_op jit(solution)/shard_map/ppermute | solution.py:40
  42.3 14.9 %collective-permute-start.15 = (bf16[27,64,128]{2,1,0:T(8,128)(2,1)S(1)}, bf16[27,64,128]{2,1,0:T(8,128)(2,1)S(1)}, u32[]{:S(2)}, u32[]{:S(2)}) collective-permute-start(bf16[27,64,128]{2,1,0:T(8,128)(2,1)S(1)} %get-tuple-element.63), channel_id=1, source_target_pairs={{0,24},{1,25},{2,26},{3,27},{4,28},{5,29},{6,30},{7,31},{8,0},{9,1... | collective-permute-start | bytes 1327112 | tf_op jit(solution)/shard_map/ppermute | solution.py:40
  52.6 7.6 %collective-permute-start.9 = (bf16[7,64,128]{2,1,0:T(8,128)(2,1)S(1)}, bf16[7,64,128]{2,1,0:T(8,128)(2,1)S(1)}, u32[]{:S(2)}, u32[]{:S(2)}) collective-permute-start(bf16[7,64,128]{2,1,0:T(8,128)(2,1)S(1)} %get-tuple-element.57), channel_id=1, source_target_pairs={{0,16},{1,17},{2,18},{3,19},{4,20},{5,21},{6,22},{7,23},{8,24},{9,... | collective-permute-start | bytes 344072 | tf_op jit(solution)/shard_map/ppermute | solution.py:40
  53.9 7.8 %collective-permute-start.11 = (bf16[7,64,128]{2,1,0:T(8,128)(2,1)S(1)}, bf16[7,64,128]{2,1,0:T(8,128)(2,1)S(1)}, u32[]{:S(2)}, u32[]{:S(2)}) collective-permute-start(bf16[7,64,128]{2,1,0:T(8,128)(2,1)S(1)} %get-tuple-element.59), channel_id=1, source_target_pairs={{0,24},{1,25},{2,26},{3,27},{4,28},{5,29},{6,30},{7,31},{8,0},{9,1... | collective-permute-start | bytes 344072 | tf_op jit(solution)/shard_map/ppermute | solution.py:40
  53.9 7.8 %collective-permute-start.10 = (bf16[7,64,128]{2,1,0:T(8,128)(2,1)S(1)}, bf16[7,64,128]{2,1,0:T(8,128)(2,1)S(1)}, u32[]{:S(2)}, u32[]{:S(2)}) collective-permute-start(bf16[7,64,128]{2,1,0:T(8,128)(2,1)S(1)} %get-tuple-element.58.after), channel_id=1, source_target_pairs={{0,8},{1,9},{2,10},{3,11},{4,12},{5,13},{6,14},{7,15},{8,16},{9,17... | collective-permute-start | bytes 344072 | tf_op jit(solution)/shard_map/ppermute | solution.py:40
  57.7 7.1 %collective-permute-start.16 = (bf16[7,64,128]{2,1,0:T(8,128)(2,1)S(1)}, bf16[7,64,128]{2,1,0:T(8,128)(2,1)S(1)}, u32[]{:S(2)}, u32[]{:S(2)}) collective-permute-start(bf16[7,64,128]{2,1,0:T(8,128)(2,1)S(1)} %get-tuple-element.66), channel_id=1, source_target_pairs={{0,2},{1,3},{2,0},{3,1},{4,6},{5,7},{6,4},{7,5},{8,10},{9,11},{10,... | collective-permute-start | bytes 344072 | tf_op jit(solution)/shard_map/ppermute | solution.py:40
  58.3 7.6 %collective-permute-start.17 = (bf16[7,64,128]{2,1,0:T(8,128)(2,1)S(1)}, bf16[7,64,128]{2,1,0:T(8,128)(2,1)S(1)}, u32[]{:S(2)}, u32[]{:S(2)}) collective-permute-start(bf16[7,64,128]{2,1,0:T(8,128)(2,1)S(1)} %get-tuple-element.67), channel_id=1, source_target_pairs={{0,4},{1,5},{2,6},{3,7},{4,2},{5,3},{6,0},{7,1},{8,12},{9,13},{10,... | collective-permute-start | bytes 344072 | tf_op jit(solution)/shard_map/ppermute | solution.py:40
  60.2 5.7 %collective-permute-start.18 = (bf16[7,64,128]{2,1,0:T(8,128)(2,1)S(1)}, bf16[7,64,128]{2,1,0:T(8,128)(2,1)S(1)}, u32[]{:S(2)}, u32[]{:S(2)}) collective-permute-start(bf16[7,64,128]{2,1,0:T(8,128)(2,1)S(1)} %get-tuple-element.68), channel_id=1, source_target_pairs={{0,6},{1,7},{2,4},{3,5},{4,0},{5,1},{6,2},{7,3},{8,14},{9,15},{10,... | collective-permute-start | bytes 344072 | tf_op jit(solution)/shard_map/ppermute | solution.py:40
  66.8 19.1 %all-to-all-start = ((bf16[8,112,128]{2,1,0:T(8,128)(2,1)}), bf16[8,112,128]{2,1,0:T(8,128)(2,1)S(1)}, u32[]{:S(2)}, u32[]{:S(2)}) async-start(bf16[8,112,128]{2,1,0:T(8,128)(2,1)} %get-tuple-element.70), calls=%async_computation | async-start | bytes 458752 | tf_op jit(solution)/shard_map/all_to_all | solution.py:496

commit v8 on v7

--- a/solution.py
+++ b/solution.py
@@ -95,26 +95,41 @@
                     corner[n, f, :, lanes] = jnp.broadcast_to(cell, (16, 128)).astype(BF)
 
 
-def build_shifted(put, cell_row, row, left, right, corner_left, corner_right):
+def pad_block(put, block, row, left, right, corner_left, corner_right):
     ha, wa = lax.axis_index("ha"), lax.axis_index("xh") * 2 + lax.axis_index("core")
-    col = lax.broadcasted_iota(jnp.int32, (16, 256), 0)
     is_top, is_low = (ha == 1).astype(F32), (ha == 0).astype(F32)
-    has_left, has_right = (wa > 0).astype(F32), (wa < 3).astype(F32)
+    rest = jnp.zeros((2, 256), F32)
     for f in range(4):
         edge = row(f).astype(F32)
-        lefts, rights = left(f).astype(F32) * has_left, right(f).astype(F32) * has_right
-        cl = corner_left(f).astype(F32)[0:1] * has_left
-        cr = corner_right(f).astype(F32)[0:1] * has_right
+        put(f, 0, edge * is_top)
+        put(f, 13, edge * is_low)
+        for r in range(12):
+            put(f, r + 1, block(f, r))
+        for n, side, corner, has in (
+            (14, left, corner_left, (wa > 0).astype(F32)),
+            (15, right, corner_right, (wa < 3).astype(F32)),
+        ):
+            cells, end = side(f).astype(F32)[0:12], corner(f).astype(F32)[0:1]
+            cells = jnp.concatenate([end * is_top, cells, end * is_low, rest], axis=0)
+            put(f, n, cells * has)
+
+
+def build_shifted(put, padded):
+    col = lax.broadcasted_iota(jnp.int32, (16, 256), 0)
+    for f in range(4):
+        lefts, rights = padded[f, 14].astype(F32), padded[f, 15].astype(F32)
         for r in range(14):
-            if r in (0, 13):
-                keep = is_top if r == 0 else is_low
-                cells, lo, hi = edge * keep, cl * keep, cr * keep
-            else:
-                cells = cell_row(f, r - 1).astype(F32)
-                lo, hi = lefts[r - 1 : r], rights[r - 1 : r]
-            put(f, r, 1, cells.astype(BF))
+            cells, lo, hi = padded[f, r].astype(F32), lefts[r : r + 1], rights[r : r + 1]
+            put(f, r, 1, padded[f, r])
             put(f, r, 0, jnp.where(col == 0, lo, pltpu.roll(cells, 1, 0)).astype(BF))
             put(f, r, 2, jnp.where(col == 15, hi, pltpu.roll(cells, 15, 0)).astype(BF))
+
+
+def keep_in(padded):
+    def put(f, n, cells):
+        padded[f, n] = cells.astype(BF)
+
+    return put
 
 
 def put_back(wide):
@@ -191,18 +206,24 @@
         copy.wait()
 
 
-def first_kernel(
-    block, slope, row, left, right, corner_left, corner_right, taps, wide, hid_out, total,
-):
+def pad_kernel(block, row, left, right, corner_left, corner_right, act, out):
     sides = (row, left, right, corner_left, corner_right)
-    build_shifted(
-        put_back(wide), lambda f, r: block[f, r], *[lambda f, s=s: s[0, f] for s in sides]
-    )
+    pad_block(keep_in(out), lambda f, r: block[f, r], *[lambda f, s=s: s[0, f] for s in sides])
+    for f in range(4):
+        for n in range(12):
+            cells = act[f * 192 + n * 16 : f * 192 + n * 16 + 16, 128:256]
+            out[f, 16 + n % 6, :, n // 6 * 128 : n // 6 * 128 + 128] = cells
+
+
+def first_kernel(padded, slope, taps, wide, hid_out, total):
+    build_shifted(put_back(wide), padded)
     conv_sum(wide, taps, total)
     hid_out[...] = (total[...] * slope[...]).astype(BF).reshape(4, 12, 16, 256)
 
 
-def input_conv_kernel(hid, block, border, face, after, weight, out, held, total, sem, wide):
+def input_conv_kernel(
+    hid, block, border, cols, after, weight, out, held, total, sem, wide, padded
+):
     del after
     copies = weight_copies(weight, held, sem)
     for copy in copies:
@@ -213,15 +234,16 @@
         return jnp.where(is_one, when_one.astype(F32), when_zero.astype(F32))
 
     faces, outers = border[8].astype(F32), border[9].astype(F32)[4:8]
-    build_shifted(
-        put_back(wide),
+    pad_block(
+        keep_in(padded),
         lambda f, r: hid[f, r],
         lambda f: border[f],
-        lambda f: pick(face[f], border[4 + f]),
-        lambda f: pick(border[4 + f], face[f]),
+        lambda f: pick(cols[0, f], border[4 + f]),
+        lambda f: pick(border[4 + f], cols[1, f]),
         lambda f: pick(faces[f : f + 1], outers[f : f + 1]),
         lambda f: pick(outers[f : f + 1], faces[f : f + 1]),
     )
+    build_shifted(put_back(wide), padded)
     for copy in copies:
         copy.wait()
     conv_sum(wide, held, total)
@@ -229,68 +251,27 @@
     out[...] = grad.astype(BF).reshape(4, 12, 16, 256)
 
 
-def second_part(wide, act, half, a, b):
-    rows = (a + 2) * 192
-    window = wide[2 - a : 4, 2 - b : 14 - b].reshape(rows, 768)
-    left = act[0:rows, half * 128 : half * 128 + 128]
-    return lax.dot_general(left, window, TN, preferred_element_type=F32)
-
-
-def tile(n):
-    return slice(n // 3 * 16, n // 3 * 16 + 16), slice(n % 3 * 256, n % 3 * 256 + 256)
-
-
-def second_pair_kernel(wide, act, hid, pair, flat):
-    spread(flat, hid)
-    pair[9] = jnp.zeros((128, 768), F32)
+def second_own_kernel(wide, act, got, after, keep, one, two, three, pair_wide, pair_act):
+    del after
+    build_shifted(put_back(pair_wide), got)
     for f in range(4):
-        for n, j in ((f, 15), (4 + f, 0)):
-            rows, lanes = tile(n)
-            for h in range(2):
-                at = slice(lanes.start + h * 128, lanes.start + h * 128 + 128)
-                pair[9, rows, at] = column(flat, h, f, j)
+        for n in range(12):
+            cells = got[f, 16 + n % 6, :, n // 6 * 128 : n // 6 * 128 + 128]
+            pair_act[f * 192 + n * 16 : f * 192 + n * 16 + 16, :] = cells
     for a in range(3):
+        rows = (a + 2) * 192
         for b in range(3):
-            pair[a * 3 + b] = second_part(wide, act, 1, a, b)
-
-
-def second_own_kernel(wide, act, hid, got, after, keep, one, two, three, face_out):
-    del after
-    is_one = lax.axis_index("core") == 1
-    edge = 11 * (1 - lax.axis_index("ha"))
-    faces, outers = [], []
-    for f in range(4):
-        hi, lo = got[(9, *tile(f))], got[(9, *tile(4 + f))]
-        face, outer = jnp.where(is_one, hi, lo), jnp.where(is_one, lo, hi)
-        face_out[f] = face.astype(BF)
-        two[(9, *tile(f))] = outer.astype(BF)
-        for out in (one, three):
-            out[(9, *tile(f))] = hid[f, edge]
-        faces.append(jnp.where(edge == 0, face[0:1], face[11:12]))
-        outers.append(jnp.where(edge == 0, outer[0:1], outer[11:12]))
-    corners = jnp.concatenate(faces + outers + [jnp.zeros((8, 256), F32)], axis=0).astype(BF)
-    for out in (one, three):
-        out[(9, *tile(4))] = corners
-        out[(9, *tile(5))] = jnp.zeros((16, 256), BF)
-    for n in (4, 5):
-        two[(9, *tile(n))] = jnp.zeros((16, 256), BF)
-    for a in range(3):
-        for b in range(3):
-            total = second_part(wide, act, 0, a, b) + got[a * 3 + b]
+            total = None
+            for left, right in ((act[0:rows, 0:128], wide), (pair_act[0:rows], pair_wide)):
+                window = right[2 - a : 4, 2 - b : 14 - b].reshape(rows, 768)
+                part = lax.dot_general(left, window, TN, preferred_element_type=F32)
+                total = part if total is None else total + part
             for d, out in enumerate((keep, one, two, three)):
                 out[a * 3 + b] = total[d * 32 : d * 32 + 32].astype(out.dtype)
 
 
-def second_x_kernel(got2, got1, got3, own, keep, one, two, three, border, held):
-    y, low = lax.axis_index("y"), lax.axis_index("ha") == 0
-    for n in range(5):
-        first, last = got1[(9, *tile(n))].astype(F32), got3[(9, *tile(n))].astype(F32)
-        across, along = jnp.where(low, last, first), jnp.where(low, first, last)
-        if n < 4:
-            border[n] = across.astype(BF)
-            border[4 + n] = got2[(9, *tile(n))]
-        else:
-            border[8], border[9] = across.astype(BF), along.astype(BF)
+def second_x_kernel(got1, got2, got3, own, keep, one, two, three, held):
+    y = lax.axis_index("y")
 
     def tap(t):
         ab, lanes = t // 3, slice(t % 3 * 256, t % 3 * 256 + 256)
@@ -306,8 +287,14 @@
             out[g] = held[:, (y + d) & 3].reshape(64, 128).astype(out.dtype)
 
 
+def border_at(base, n, h):
+    slot = n * 2 + h
+    return base + slot // 4, slice(slot % 4 * 16, slot % 4 * 16 + 16)
+
+
 def first_grad_kernel(
-    hid, inp, row, left, right, corner_left, corner_right, after, own, pair, wide, side,
+    hid, inp, row, left, right, corner_left, corner_right, after,
+    own, pair, wide, padded, side, flat,
 ):
     del after
     order = channel_order()
@@ -320,7 +307,16 @@
         wide[f, r, :, at : at + 128] = cells[:, 0:128]
         wide[f, r, :, at + 384 : at + 512] = cells[:, 128:256]
 
-    build_shifted(put, lambda f, r: inp[f, r], *[lambda f, n=n: side[n, f] for n in range(5)])
+    pad_block(
+        keep_in(padded), lambda f, r: inp[f, r], *[lambda f, n=n: side[n, f] for n in range(5)]
+    )
+    build_shifted(put, padded)
+    spread(flat, hid)
+    for f in range(4):
+        for n, j in ((f, 15), (4 + f, 0)):
+            for h in range(2):
+                q, rows = border_at(0, n, h)
+                pair[q, 27, rows] = column(flat, h, f, j)
     for a in range(3):
         rows = (a + 2) * 192
         left = hid[2 - a : 4].reshape(rows, 256)
@@ -336,15 +332,19 @@
                     pair[q, t] = piece[:, e * 128 + 384 : e * 128 + 512]
 
 
-def first_sum_kernel(own, pair, after, keep, one, two, three):
+def first_sum_kernel(own, pair, after, keep, one, two, three, cols):
     del after
     y = lax.axis_index("y")
     for d, out in enumerate((keep, one, two, three)):
         q = (y + d) & 3
-        out[...] = (own[q] + pair[q]).astype(out.dtype)
-
-
-def first_y_kernel(got1, got2, got3, own, after, keep, one, two, three):
+        out[...] = (own[q] + pair[q, 0:27]).astype(out.dtype)
+    for n in range(8):
+        for h in range(2):
+            q, rows = border_at(0, n, h)
+            cols[n // 4, n % 4, :, h * 128 : h * 128 + 128] = pair[q, 27, rows].astype(BF)
+
+
+def first_y_kernel(got1, got2, got3, own, hid, cols, after, keep, one, two, three):
     del after
 
     def tap(t):
@@ -359,12 +359,41 @@
             piece = jnp.concatenate([v[:, d * 32 : d * 32 + 32] for v in taps], axis=1)
             out[g] = piece.astype(out.dtype)
 
-
-def last_kernel(own_two, a1, a2, a3, own_one, b1, b2, b3, out, keep, held):
+    is_one = lax.axis_index("core") == 1
+    edge = 11 * (1 - lax.axis_index("ha"))
+    along, across, faces, outers = [], [], [], []
+    for f in range(4):
+        hi, lo = cols[0, f].astype(F32), cols[1, f].astype(F32)
+        face, outer = jnp.where(is_one, hi, lo), jnp.where(is_one, lo, hi)
+        along.append(hid[f, edge])
+        across.append(outer.astype(BF))
+        faces.append(jnp.where(edge == 0, face[0:1], face[11:12]))
+        outers.append(jnp.where(edge == 0, outer[0:1], outer[11:12]))
+    corners = jnp.concatenate(faces + outers + [jnp.zeros((8, 256), F32)], axis=0).astype(BF)
+    rest = [jnp.zeros((16, 256), BF)] * 2
+    along, across = along + [corners, rest[0]], across + rest
+    for out, tiles in ((one, along), (two, across), (three, along)):
+        for n, cells in enumerate(tiles):
+            for h in range(2):
+                out[border_at(7, n, h)] = cells[:, h * 128 : h * 128 + 128]
+
+
+def last_kernel(own_two, a2, a1, a3, own_one, b2, b1, b3, out, keep, border, held):
+    low = lax.axis_index("ha") == 0
+    for h in range(2):
+        lanes = slice(h * 128, h * 128 + 128)
+        for n in range(5):
+            first, last = b1[border_at(7, n, h)].astype(F32), b3[border_at(7, n, h)].astype(F32)
+            across, along = jnp.where(low, last, first), jnp.where(low, first, last)
+            if n < 4:
+                border[n, :, lanes] = across.astype(BF)
+                border[4 + n, :, lanes] = b2[border_at(7, n, h)]
+            else:
+                border[8, :, lanes], border[9, :, lanes] = across.astype(BF), along.astype(BF)
     for n, (own, got) in enumerate(((own_two, (a1, a2, a3)), (own_one, (b1, b2, b3)))):
         total = own[...]
         for ref in got:
-            total = total + ref[...].astype(F32)
+            total = total + ref[0:7].astype(F32)
         held[n] = total.reshape(7, 8, 8, 128)
 
     def plane(z):
@@ -426,71 +455,81 @@
             pltpu.SemaphoreType.DMA((3,)),
         ],
     )
+    (padded,) = call(
+        pad_kernel,
+        "pad_cotangent",
+        (block, *sides, act),
+        "pvvvvvv",
+        [near((4, 22, 16, 256), BF)],
+    )
+    pair_padded = send(padded, core_pairs())
     wide_cot, grad_hidden = call(
         first_kernel,
         "conv_two_back",
-        (block, slope, *sides, held_two),
-        "pv" + "v" * 5 + "v",
+        (padded, slope, held_two),
+        "vvv",
         [wide, near((4, 12, 16, 256), BF)],
         [pltpu.VMEM((768, 256), F32)],
     )
 
-    (pair_two,) = call(
-        second_pair_kernel,
-        "grad_two_pair",
-        (wide_cot, act, grad_hidden),
-        "vvv",
-        [near((10, 128, 768), F32)],
-        [pltpu.VMEM((2, 768, 128), F32)],
-    )
-    got_pair_two = send(pair_two, core_pairs())
-    split = near((4, 27, 64, 128), F32)
     own_one, pair_one = call(
         first_grad_kernel,
         "grad_one",
-        (grad_hidden, inp, *sides, pair_two),
-        "vv" + "v" * 5 + "v",
-        [split, split],
-        [pltpu.VMEM((4, 14, 16, 768), BF), pltpu.VMEM((5, 4, 16, 256), F32)],
+        (grad_hidden, inp, *sides, pair_padded),
+        "vv" + "v" * 6,
+        [near((4, 27, 64, 128), F32), near((4, 28, 64, 128), F32)],
+        [
+            pltpu.VMEM((4, 14, 16, 768), BF),
+            pltpu.VMEM((4, 16, 16, 256), BF),
+            pltpu.VMEM((5, 4, 16, 256), F32),
+            pltpu.VMEM((2, 768, 128), F32),
+        ],
     )
     got_pair_one = send(pair_one, core_pairs())
-    own_two, *parts, face = call(
+    own_two, *parts = call(
         second_own_kernel,
-        "grad_two_own",
-        (wide_cot, act, grad_hidden, got_pair_two, pair_one),
-        "vvvvv",
-        [near((9, 32, 768), F32)] + [near((10, 32, 768), BF)] * 3 + [near((4, 16, 256), BF)],
+        "grad_two",
+        (wide_cot, act, pair_padded, pair_one),
+        "vvvv",
+        [near((9, 32, 768), F32)] + [near((9, 32, 768), BF)] * 3,
+        [pltpu.VMEM((4, 14, 16, 768), BF), pltpu.VMEM((768, 128), BF)],
     )
     got_two = ring(parts, "dx")
-    own_one, *parts_one = call(
+    own_one, *parts_one, cols = call(
         first_sum_kernel,
         "grad_one_sum",
         (own_one, got_pair_one, parts[0]),
         "vvv",
-        [near((27, 64, 128), F32)] + [near((27, 64, 128), BF)] * 3,
+        [near((27, 64, 128), F32)]
+        + [near((27, 64, 128), BF)] * 3
+        + [near((2, 4, 16, 256), BF)],
     )
     got_one = ring(parts_one, "dy")
 
-    own_two, *parts, border = call(
+    own_two, *parts = call(
         second_x_kernel,
         "grad_two_x",
         (*got_two, own_two),
         "vvvv",
-        quads + [near((10, 16, 256), BF)],
+        quads,
         [pltpu.VMEM((8, 4, 8, 128), F32)],
     )
     got_two = ring(parts, "dy")
     own_one, *parts_one = call(
-        first_y_kernel, "grad_one_y", (*got_one, own_one, parts[0]), "vvvvv", quads
+        first_y_kernel,
+        "grad_one_y",
+        (*got_one, own_one, grad_hidden, cols, parts[0]),
+        "v" * 7,
+        [near((7, 64, 128), F32)] + [near((10, 64, 128), BF)] * 3,
     )
     got_one = ring(parts_one, "dx")
 
-    out, own = call(
+    out, own, border = call(
         last_kernel,
         "last_stage",
         (own_two, *got_two, own_one, *got_one),
         "v" * 8,
-        [far((8, 112, 128), BF), near((112, 128), F32)],
+        [far((8, 112, 128), BF), near((112, 128), F32), near((10, 16, 256), BF)],
         [pltpu.VMEM((2, 7, 8, 8, 128), F32)],
     )
     planes = lax.all_to_all(out, "z", 0, 0, tiled=True)
@@ -498,7 +537,7 @@
     (grad_input,) = call(
         input_conv_kernel,
         "conv_one_back",
-        (grad_hidden, block, border, face, own, taps_one),
+        (grad_hidden, block, border, cols, own, taps_one),
         "vpvvvh",
         [(jax.ShapeDtypeStruct((4, 12, 16, 256), BF), "v")],
         [
@@ -506,6 +545,7 @@
             pltpu.VMEM((768, 256), F32),
             pltpu.SemaphoreType.DMA((3,)),
             pltpu.VMEM((4, 14, 16, 768), BF),
+            pltpu.VMEM((4, 16, 16, 256), BF),
         ],
     )
 

time: 87 us -> 85.7 us (0.985)
  the two profiles are of different devices: /device:TPU:24 before, /device:TPU:6 now
where the time goes in v8:
time: 85.7 us; the launch traced here: 85.3 us
  starting transfers between devices  39.2 us (46%)
  waiting for transfers between devices  23.1 us (27%)
  Pallas kernels  21.6 us (25%)
  between operations  1.41 us (2%)
    ppermute x19, starting transfers between devices, send(): return lax.ppermute(value, AX, pairs)  30.8 us
    pallas_call x12, Pallas kernels, call(): pl.pallas_call(kernel, out_shape=tuple((o for o, _ in outs)), in_specs=[s...  21.6 us
    ppermute x19, waiting for transfers between devices, send(): return lax.ppermute(value, AX, pairs)  19 us
    all_to_all x1, starting transfers between devices, shards(): planes = lax.all_to_all(out, 'z', 0, 0, tiled=True)  8.47 us
    all_to_all x1, waiting for transfers between devices, shards(): planes = lax.all_to_all(out, 'z', 0, 0, tiled=True)  4.11 us
  transfers between devices with their start and end apart: 20, of which 6 were waited for; matrix products, arithmetic and copies ran while one was open for 0% of the time, Pallas kernels for 17%

profile of v8, /device:TPU:6, one launch (start us, length us, event | category | flops | bytes accessed | tf_op | source)
XLA Modules:
  0.0 85.3 jit_solution(6593473934885659540)
XLA Ops:
  0.6 1.3 %pack_first.1 = (bf16[2,4,16,256]{3,2,1,0:T(8,128)(2,1)S(1)}, bf16[2,4,16,256]{3,2,1,0:T(8,128)(2,1)S(1)}, bf16[2,4,16,256]{3,2,1,0:T(8,128)(2,1)S(1)}, bf16[2,4...) custom-call(bf16[4,12,16,256]{3,2,1,0:T(8,128)(2,1)} %bitcast.16, bf16[4,12,16,256]{3,2,1,0:T(8,128)(2,1)} %bitcast.21), custom_call_target="tpu_custom_call" | custom-call | tf_op jit(solution)/shard_map/pack_first/pallas_call | solution.py:50
  2.9 3.2 %collective-permute-start.2 = (bf16[2,4,16,256]{3,2,1,0:T(8,128)(2,1)S(1)}, bf16[2,4,16,256]{3,2,1,0:T(8,128)(2,1)S(1)}, u32[]{:S(2)}, u32[]{:S(2)}) collective-permute-start(bf16[2,4,16,256]{3,2,1,0:T(8,128)(2,1)S(1)} %get-tuple-element.40), channel_id=1, source_target_pairs={{0,3},{1,0},{2,1},{3,2},{4,7},{5,4},{6,5},{7,6},{8,11},{9,8},{10,9... | collective-permute-start | bytes 196616 | tf_op jit(solution)/shard_map/ppermute | solution.py:40
  6.1 3.0 %collective-permute-start.4 = (bf16[2,4,16,256]{3,2,1,0:T(8,128)(2,1)S(1)}, bf16[2,4,16,256]{3,2,1,0:T(8,128)(2,1)S(1)}, u32[]{:S(2)}, u32[]{:S(2)}) collective-permute-start(bf16[2,4,16,256]{3,2,1,0:T(8,128)(2,1)S(1)} %get-tuple-element.42), channel_id=1, source_target_pairs={{0,7},{1,4},{2,5},{3,6},{4,3},{5,0},{6,1},{7,2},{8,15},{9,12},{10,... | collective-permute-start | bytes 196616 | tf_op jit(solution)/shard_map/ppermute | solution.py:40
  9.7 2.3 %film.1 = (bf16[768,256]{1,0:T(8,128)(2,1)S(1)}, bf16[4,12,16,256]{3,2,1,0:T(8,128)(2,1)S(1)}, f32[768,256]{1,0:T(8,128)S(1)}, bf16[27,256,256]{2,1,0:T(8,128)(2,1)S(1)}) custom-call(s32[1]{0:T(128)S(6)} %copy.10.step, bf16[4,12,16,256]{3,2,1,0:T(8,128)(2,1)} %bitcast.22, bf16[4,12,16,256]{3,2,1,0:T(8,128)(2,1)} %bitcast.24, f32[1000,512]{1,0:T(8,128)} %table.1, ...), custom_call_target="tpu_custom_call" | custom-call | tf_op jit(solution)/shard_map/film/pallas_call | solution.py:50
  12.1 1.1 %pad_cotangent.1.padded = bf16[4,22,16,256]{3,2,1,0:T(8,128)(2,1)S(1)} custom-call(bf16[4,12,16,256]{3,2,1,0:T(8,128)(2,1)} %bitcast.17, bf16[2,4,16,256]{3,2,1,0:T(8,128)(2,1)S(1)} %collective-permute-done.row, bf16[2,4,16,256]{3,2,1,0:T(8,128)(2,1)S(1)} %collective-permute-done.1.left, bf16[2,4,16,256]{3,2,1,0:T(8,128)(2,1)S(1)} %collective-permute-done.2.right, ...), custom_call_target="tpu_custom_call" | custom-call | tf_op jit(solution)/shard_map/pad_cotangent/pallas_call | solution.py:50
  13.8 2.3 %conv_two_back.1 = (bf16[4,14,16,768]{3,2,1,0:T(8,128)(2,1)S(1)}, bf16[4,12,16,256]{3,2,1,0:T(8,128)(2,1)S(1)}) custom-call(bf16[4,22,16,256]{3,2,1,0:T(8,128)(2,1)S(1)} %pad_cotangent.1.padded, f32[768,256]{1,0:T(8,128)S(1)} %get-tuple-element.44.slope, bf16[27,256,256]{2,1,0:T(8,128)(2,1)S(1)} %get-tuple-element.45.taps), custom_call_target="tpu_custom_call" | custom-call | tf_op jit(solution)/shard_map/conv_two_back/pallas_call | solution.py:50
  16.0 3.0 %grad_one.1 = (f32[4,27,64,128]{3,2,1,0:T(8,128)S(1)}, f32[4,28,64,128]{3,2,1,0:T(8,128)S(1)}) custom-call(bf16[4,12,16,256]{3,2,1,0:T(8,128)(2,1)S(1)} %get-tuple-element.46.hid, bf16[4,12,16,256]{3,2,1,0:T(8,128)(2,1)S(1)} %get-tuple-element.48.inp, bf16[2,4,16,256]{3,2,1,0:T(8,128)(2,1)S(1)} %collective-permute-done.row, ...), custom_call_target="tpu_custom_call" | custom-call | tf_op jit(solution)/shard_map/grad_one/pallas_call | solution.py:50
  19.3 2.7 %grad_two.1 = (f32[9,32,768]{2,1,0:T(8,128)S(1)}, bf16[9,32,768]{2,1,0:T(8,128)(2,1)S(1)}, bf16[9,32,768]{2,1,0:T(8,128)(2,1)S(1)}, bf16[9,32,768]{2,1,0:T(8,128)(2,1)S(1)}) custom-call(bf16[4,14,16,768]{3,2,1,0:T(8,128)(2,1)S(1)} %get-tuple-element.47.wide, bf16[768,256]{1,0:T(8,128)(2,1)S(1)} %get-tuple-element.43.act, ...), custom_call_target="tpu_custom_call" | custom-call | tf_op jit(solution)/shard_map/grad_two/pallas_call | solution.py:50
  22.0 1.7 %collective-permute-start.6 = (bf16[9,32,768]{2,1,0:T(8,128)(2,1)S(1)}, bf16[9,32,768]{2,1,0:T(8,128)(2,1)S(1)}, u32[]{:S(2)}, u32[]{:S(2)}) collective-permute-start(bf16[9,32,768]{2,1,0:T(8,128)(2,1)S(1)} %get-tuple-element.50), channel_id=1, source_target_pairs={{0,2},{1,3},{2,0},{3,1},{4,6},{5,7},{6,4},{7,5},{8,10},{9,11},{10,... | collective-permute-start | bytes 1327112 | tf_op jit(solution)/shard_map/ppermute | solution.py:40
  23.8 1.0 %collective-permute-start.8 = (bf16[9,32,768]{2,1,0:T(8,128)(2,1)S(1)}, bf16[9,32,768]{2,1,0:T(8,128)(2,1)S(1)}, u32[]{:S(2)}, u32[]{:S(2)}) collective-permute-start(bf16[9,32,768]{2,1,0:T(8,128)(2,1)S(1)} %get-tuple-element.52), channel_id=1, source_target_pairs={{0,6},{1,7},{2,4},{3,5},{4,0},{5,1},{6,2},{7,3},{8,14},{9,15},{10,... | collective-permute-start | bytes 1327112 | tf_op jit(solution)/shard_map/ppermute | solution.py:40
  24.7 2.3 %collective-permute-start.7 = (bf16[9,32,768]{2,1,0:T(8,128)(2,1)S(1)}, bf16[9,32,768]{2,1,0:T(8,128)(2,1)S(1)}, u32[]{:S(2)}, u32[]{:S(2)}) collective-permute-start(bf16[9,32,768]{2,1,0:T(8,128)(2,1)S(1)} %get-tuple-element.51.after), channel_id=1, source_target_pairs={{0,4},{1,5},{2,6},{3,7},{4,2},{5,3},{6,0},{7,1},{8,12},{9,13},{10,... | collective-permute-start | bytes 1327112 | tf_op jit(solution)/shard_map/ppermute | solution.py:40
  27.3 2.2 %collective-permute-start.13 = (bf16[27,64,128]{2,1,0:T(8,128)(2,1)S(1)}, bf16[27,64,128]{2,1,0:T(8,128)(2,1)S(1)}, u32[]{:S(2)}, u32[]{:S(2)}) collective-permute-start(bf16[27,64,128]{2,1,0:T(8,128)(2,1)S(1)} %get-tuple-element.59), channel_id=1, source_target_pairs={{0,16},{1,17},{2,18},{3,19},{4,20},{5,21},{6,22},{7,23},{8,24},{9,... | collective-permute-start | bytes 1327112 | tf_op jit(solution)/shard_map/ppermute | solution.py:40
  30.2 6.4 %collective-permute-done.6.got1 = bf16[9,32,768]{2,1,0:T(8,128)(2,1)S(1)} collective-permute-done((bf16[9,32,768]{2,1,0:T(8,128)(2,1)S(1)}, bf16[9,32,768]{2,1,0:T(8,128)(2,1)S(1)}, u32[]{:S(2)}, u32[]{:S(2)}) %collective-permute-start.6) | collective-permute-done | bytes 442400 | tf_op jit(solution)/shard_map/ppermute | solution.py:40
  36.6 3.1 %collective-permute-start.15 = (bf16[27,64,128]{2,1,0:T(8,128)(2,1)S(1)}, bf16[27,64,128]{2,1,0:T(8,128)(2,1)S(1)}, u32[]{:S(2)}, u32[]{:S(2)}) collective-permute-start(bf16[27,64,128]{2,1,0:T(8,128)(2,1)S(1)} %get-tuple-element.61), channel_id=1, source_target_pairs={{0,24},{1,25},{2,26},{3,27},{4,28},{5,29},{6,30},{7,31},{8,0},{9,1... | collective-permute-start | bytes 1327112 | tf_op jit(solution)/shard_map/ppermute | solution.py:40
  39.7 6.0 %collective-permute-done.8.got3 = bf16[9,32,768]{2,1,0:T(8,128)(2,1)S(1)} collective-permute-done((bf16[9,32,768]{2,1,0:T(8,128)(2,1)S(1)}, bf16[9,32,768]{2,1,0:T(8,128)(2,1)S(1)}, u32[]{:S(2)}, u32[]{:S(2)}) %collective-permute-start.8) | collective-permute-done | bytes 442400 | tf_op jit(solution)/shard_map/ppermute | solution.py:40
  46.1 2.9 %collective-permute-start.9 = (bf16[7,64,128]{2,1,0:T(8,128)(2,1)S(1)}, bf16[7,64,128]{2,1,0:T(8,128)(2,1)S(1)}, u32[]{:S(2)}, u32[]{:S(2)}) collective-permute-start(bf16[7,64,128]{2,1,0:T(8,128)(2,1)S(1)} %get-tuple-element.55), channel_id=1, source_target_pairs={{0,16},{1,17},{2,18},{3,19},{4,20},{5,21},{6,22},{7,23},{8,24},{9,... | collective-permute-start | bytes 344072 | tf_op jit(solution)/shard_map/ppermute | solution.py:40
  50.2 1.3 %collective-permute-start.16 = (bf16[10,64,128]{2,1,0:T(8,128)(2,1)S(1)}, bf16[10,64,128]{2,1,0:T(8,128)(2,1)S(1)}, u32[]{:S(2)}, u32[]{:S(2)}) collective-permute-start(bf16[10,64,128]{2,1,0:T(8,128)(2,1)S(1)} %get-tuple-element.65), channel_id=1, source_target_pairs={{0,2},{1,3},{2,0},{3,1},{4,6},{5,7},{6,4},{7,5},{8,10},{9,11},{10,... | collective-permute-start | bytes 491528 | tf_op jit(solution)/shard_map/ppermute | solution.py:40
  51.5 2.0 %collective-permute-start.17 = (bf16[10,64,128]{2,1,0:T(8,128)(2,1)S(1)}, bf16[10,64,128]{2,1,0:T(8,128)(2,1)S(1)}, u32[]{:S(2)}, u32[]{:S(2)}) collective-permute-start(bf16[10,64,128]{2,1,0:T(8,128)(2,1)S(1)} %get-tuple-element.66), channel_id=1, source_target_pairs={{0,4},{1,5},{2,6},{3,7},{4,2},{5,3},{6,0},{7,1},{8,12},{9,13},{10,... | collective-permute-start | bytes 491528 | tf_op jit(solution)/shard_map/ppermute | solution.py:40
  53.5 5.6 %collective-permute-start.11 = (bf16[7,64,128]{2,1,0:T(8,128)(2,1)S(1)}, bf16[7,64,128]{2,1,0:T(8,128)(2,1)S(1)}, u32[]{:S(2)}, u32[]{:S(2)}) collective-permute-start(bf16[7,64,128]{2,1,0:T(8,128)(2,1)S(1)} %get-tuple-element.57), channel_id=1, source_target_pairs={{0,24},{1,25},{2,26},{3,27},{4,28},{5,29},{6,30},{7,31},{8,0},{9,1... | collective-permute-start | bytes 344072 | tf_op jit(solution)/shard_map/ppermute | solution.py:40
  59.1 2.4 %collective-permute-done.11.a3 = bf16[7,64,128]{2,1,0:T(8,128)(2,1)S(1)} collective-permute-done((bf16[7,64,128]{2,1,0:T(8,128)(2,1)S(1)}, bf16[7,64,128]{2,1,0:T(8,128)(2,1)S(1)}, u32[]{:S(2)}, u32[]{:S(2)}) %collective-permute-start.11) | collective-permute-done | bytes 114720 | tf_op jit(solution)/shard_map/ppermute | solution.py:40
  61.5 3.6 %collective-permute-done.10.a1 = bf16[7,64,128]{2,1,0:T(8,128)(2,1)S(1)} collective-permute-done((bf16[7,64,128]{2,1,0:T(8,128)(2,1)S(1)}, bf16[7,64,128]{2,1,0:T(8,128)(2,1)S(1)}, u32[]{:S(2)}, u32[]{:S(2)}) %collective-permute-start.10) | collective-permute-done | bytes 114720 | tf_op jit(solution)/shard_map/ppermute | solution.py:40
  66.0 8.5 %all-to-all-start = ((bf16[8,112,128]{2,1,0:T(8,128)(2,1)}), bf16[8,112,128]{2,1,0:T(8,128)(2,1)S(1)}, u32[]{:S(2)}, u32[]{:S(2)}) async-start(bf16[8,112,128]{2,1,0:T(8,128)(2,1)} %get-tuple-element.70), calls=%async_computation | async-start | bytes 458752 | tf_op jit(solution)/shard_map/all_to_all | solution.py:535
  74.4 6.0 %conv_one_back.1.after = bf16[4,12,16,256]{3,2,1,0:T(8,128)(2,1)} custom-call(bf16[4,12,16,256]{3,2,1,0:T(8,128)(2,1)S(1)} %get-tuple-element.46.hid, bf16[4,12,16,256]{3,2,1,0:T(8,128)(2,1)} %bitcast.18, bf16[10,16,256]{2,1,0:T(8,128)(2,1)S(1)} %get-tuple-element.68.border, bf16[2,4,16,256]{3,2,1,0:T(8,128)(2,1)S(1)} %get-tuple-element.63.cols, ...), custom_call_target="tpu_custom_call" | custom-call | tf_op jit(solution)/shard_map/conv_one_back/pallas_call | solution.py:50
  80.5 4.1 %all-to-all-done.got = bf16[8,112,128]{2,1,0:T(8,128)(2,1)S(1)} async-done(((bf16[8,112,128]{2,1,0:T(8,128)(2,1)}), bf16[8,112,128]{2,1,0:T(8,128)(2,1)S(1)}, u32[]{:S(2)}, u32[]{:S(2)}) %all-to-all-start) | async-done | bytes 229408 | tf_op jit(solution)/shard_map/all_to_all | solution.py:535
  (28 shorter events, 6.0 us)
Async XLA Ops:
  1.9 10.1 %collective-permute-start = (bf16[2,4,16,256]{3,2,1,0:T(8,128)(2,1)S(1)}, bf16[2,4,16,256]{3,2,1,0:T(8,128)(2,1)S(1)}, u32[]{:S(2)}, u32[]{:S(2)}) collective-permute-start(bf16[2,4,16,256]{3,2,1,0:T(8,128)(2,1)S(1)} %get-tuple-element.38), channel_id=1, source_target_pairs={{0,4},{1,5},{2,6},{3,7},{4,0},{5,1},{6,2},{7,3},{8,12},{9,13},{10,... | collective-permute-start | bytes 196616 | tf_op jit(solution)/shard_map/ppermute | solution.py:40
  2.9 9.2 %collective-permute-start.1 = (bf16[2,4,16,256]{3,2,1,0:T(8,128)(2,1)S(1)}, bf16[2,4,16,256]{3,2,1,0:T(8,128)(2,1)S(1)}, u32[]{:S(2)}, u32[]{:S(2)}) collective-permute-start(bf16[2,4,16,256]{3,2,1,0:T(8,128)(2,1)S(1)} %get-tuple-element.39), channel_id=1, source_target_pairs={{0,1},{1,2},{2,3},{3,0},{4,5},{5,6},{6,7},{7,4},{8,9},{9,10},{10,1... | collective-permute-start | bytes 196616 | tf_op jit(solution)/shard_map/ppermute | solution.py:40
  2.9 9.2 %collective-permute-start.2 = (bf16[2,4,16,256]{3,2,1,0:T(8,128)(2,1)S(1)}, bf16[2,4,16,256]{3,2,1,0:T(8,128)(2,1)S(1)}, u32[]{:S(2)}, u32[]{:S(2)}) collective-permute-start(bf16[2,4,16,256]{3,2,1,0:T(8,128)(2,1)S(1)} %get-tuple-element.40), channel_id=1, source_target_pairs={{0,3},{1,0},{2,1},{3,2},{4,7},{5,4},{6,5},{7,6},{8,11},{9,8},{10,9... | collective-permute-start | bytes 196616 | tf_op jit(solution)/shard_map/ppermute | solution.py:40
  6.1 6.0 %collective-permute-start.3 = (bf16[2,4,16,256]{3,2,1,0:T(8,128)(2,1)S(1)}, bf16[2,4,16,256]{3,2,1,0:T(8,128)(2,1)S(1)}, u32[]{:S(2)}, u32[]{:S(2)}) collective-permute-start(bf16[2,4,16,256]{3,2,1,0:T(8,128)(2,1)S(1)} %get-tuple-element.41), channel_id=1, source_target_pairs={{0,5},{1,6},{2,7},{3,4},{4,1},{5,2},{6,3},{7,0},{8,13},{9,14},{10,... | collective-permute-start | bytes 196616 | tf_op jit(solution)/shard_map/ppermute | solution.py:40
  6.1 6.0 %collective-permute-start.4 = (bf16[2,4,16,256]{3,2,1,0:T(8,128)(2,1)S(1)}, bf16[2,4,16,256]{3,2,1,0:T(8,128)(2,1)S(1)}, u32[]{:S(2)}, u32[]{:S(2)}) collective-permute-start(bf16[2,4,16,256]{3,2,1,0:T(8,128)(2,1)S(1)} %get-tuple-element.42), channel_id=1, source_target_pairs={{0,7},{1,4},{2,5},{3,6},{4,3},{5,0},{6,1},{7,2},{8,15},{9,12},{10,... | collective-permute-start | bytes 196616 | tf_op jit(solution)/shard_map/ppermute | solution.py:40
  13.2 2.8 %collective-permute-start.5 = (bf16[4,22,16,256]{3,2,1,0:T(8,128)(2,1)S(1)}, bf16[4,22,16,256]{3,2,1,0:T(8,128)(2,1)S(1)}, u32[]{:S(2)}, u32[]{:S(2)}) collective-permute-start(bf16[4,22,16,256]{3,2,1,0:T(8,128)(2,1)S(1)} %pad_cotangent.1.padded), channel_id=1, source_target_pairs={{0,1},{1,0},{2,3},{3,2},{4,5},{5,4},{6,7},{7,6},{8,9},{9,8},{10,11... | collective-permute-start | bytes 2162696 | tf_op jit(solution)/shard_map/ppermute | solution.py:40
  19.0 8.0 %collective-permute-start.12 = (f32[4,28,64,128]{3,2,1,0:T(8,128)S(1)}, f32[4,28,64,128]{3,2,1,0:T(8,128)S(1)}, u32[]{:S(2)}, u32[]{:S(2)}) collective-permute-start(f32[4,28,64,128]{3,2,1,0:T(8,128)S(1)} %get-tuple-element.49.after), channel_id=1, source_target_pairs={{0,1},{1,0},{2,3},{3,2},{4,5},{5,4},{6,7},{7,6},{8,9},{9,8},{10,11... | collective-permute-start | bytes 11010056 | tf_op jit(solution)/shard_map/ppermute | solution.py:40
  22.0 14.6 %collective-permute-start.6 = (bf16[9,32,768]{2,1,0:T(8,128)(2,1)S(1)}, bf16[9,32,768]{2,1,0:T(8,128)(2,1)S(1)}, u32[]{:S(2)}, u32[]{:S(2)}) collective-permute-start(bf16[9,32,768]{2,1,0:T(8,128)(2,1)S(1)} %get-tuple-element.50), channel_id=1, source_target_pairs={{0,2},{1,3},{2,0},{3,1},{4,6},{5,7},{6,4},{7,5},{8,10},{9,11},{10,... | collective-permute-start | bytes 1327112 | tf_op jit(solution)/shard_map/ppermute | solution.py:40
  23.8 21.9 %collective-permute-start.8 = (bf16[9,32,768]{2,1,0:T(8,128)(2,1)S(1)}, bf16[9,32,768]{2,1,0:T(8,128)(2,1)S(1)}, u32[]{:S(2)}, u32[]{:S(2)}) collective-permute-start(bf16[9,32,768]{2,1,0:T(8,128)(2,1)S(1)} %get-tuple-element.52), channel_id=1, source_target_pairs={{0,6},{1,7},{2,4},{3,5},{4,0},{5,1},{6,2},{7,3},{8,14},{9,15},{10,... | collective-permute-start | bytes 1327112 | tf_op jit(solution)/shard_map/ppermute | solution.py:40
  24.7 20.9 %collective-permute-start.7 = (bf16[9,32,768]{2,1,0:T(8,128)(2,1)S(1)}, bf16[9,32,768]{2,1,0:T(8,128)(2,1)S(1)}, u32[]{:S(2)}, u32[]{:S(2)}) collective-permute-start(bf16[9,32,768]{2,1,0:T(8,128)(2,1)S(1)} %get-tuple-element.51.after), channel_id=1, source_target_pairs={{0,4},{1,5},{2,6},{3,7},{4,2},{5,3},{6,0},{7,1},{8,12},{9,13},{10,... | collective-permute-start | bytes 1327112 | tf_op jit(solution)/shard_map/ppermute | solution.py:40
  27.3 21.7 %collective-permute-start.13 = (bf16[27,64,128]{2,1,0:T(8,128)(2,1)S(1)}, bf16[27,64,128]{2,1,0:T(8,128)(2,1)S(1)}, u32[]{:S(2)}, u32[]{:S(2)}) collective-permute-start(bf16[27,64,128]{2,1,0:T(8,128)(2,1)S(1)} %get-tuple-element.59), channel_id=1, source_target_pairs={{0,16},{1,17},{2,18},{3,19},{4,20},{5,21},{6,22},{7,23},{8,24},{9,... | collective-permute-start | bytes 1327112 | tf_op jit(solution)/shard_map/ppermute | solution.py:40
  29.5 20.1 %collective-permute-start.14 = (bf16[27,64,128]{2,1,0:T(8,128)(2,1)S(1)}, bf16[27,64,128]{2,1,0:T(8,128)(2,1)S(1)}, u32[]{:S(2)}, u32[]{:S(2)}) collective-permute-start(bf16[27,64,128]{2,1,0:T(8,128)(2,1)S(1)} %get-tuple-element.60), channel_id=1, source_target_pairs={{0,8},{1,9},{2,10},{3,11},{4,12},{5,13},{6,14},{7,15},{8,16},{9,17... | collective-permute-start | bytes 1327112 | tf_op jit(solution)/shard_map/ppermute | solution.py:40
  36.6 13.0 %collective-permute-start.15 = (bf16[27,64,128]{2,1,0:T(8,128)(2,1)S(1)}, bf16[27,64,128]{2,1,0:T(8,128)(2,1)S(1)}, u32[]{:S(2)}, u32[]{:S(2)}) collective-permute-start(bf16[27,64,128]{2,1,0:T(8,128)(2,1)S(1)} %get-tuple-element.61), channel_id=1, source_target_pairs={{0,24},{1,25},{2,26},{3,27},{4,28},{5,29},{6,30},{7,31},{8,0},{9,1... | collective-permute-start | bytes 1327112 | tf_op jit(solution)/shard_map/ppermute | solution.py:40
  46.1 13.0 %collective-permute-start.9 = (bf16[7,64,128]{2,1,0:T(8,128)(2,1)S(1)}, bf16[7,64,128]{2,1,0:T(8,128)(2,1)S(1)}, u32[]{:S(2)}, u32[]{:S(2)}) collective-permute-start(bf16[7,64,128]{2,1,0:T(8,128)(2,1)S(1)} %get-tuple-element.55), channel_id=1, source_target_pairs={{0,16},{1,17},{2,18},{3,19},{4,20},{5,21},{6,22},{7,23},{8,24},{9,... | collective-permute-start | bytes 344072 | tf_op jit(solution)/shard_map/ppermute | solution.py:40
  50.2 14.9 %collective-permute-start.16 = (bf16[10,64,128]{2,1,0:T(8,128)(2,1)S(1)}, bf16[10,64,128]{2,1,0:T(8,128)(2,1)S(1)}, u32[]{:S(2)}, u32[]{:S(2)}) collective-permute-start(bf16[10,64,128]{2,1,0:T(8,128)(2,1)S(1)} %get-tuple-element.65), channel_id=1, source_target_pairs={{0,2},{1,3},{2,0},{3,1},{4,6},{5,7},{6,4},{7,5},{8,10},{9,11},{10,... | collective-permute-start | bytes 491528 | tf_op jit(solution)/shard_map/ppermute | solution.py:40
  51.5 13.6 %collective-permute-start.17 = (bf16[10,64,128]{2,1,0:T(8,128)(2,1)S(1)}, bf16[10,64,128]{2,1,0:T(8,128)(2,1)S(1)}, u32[]{:S(2)}, u32[]{:S(2)}) collective-permute-start(bf16[10,64,128]{2,1,0:T(8,128)(2,1)S(1)} %get-tuple-element.66), channel_id=1, source_target_pairs={{0,4},{1,5},{2,6},{3,7},{4,2},{5,3},{6,0},{7,1},{8,12},{9,13},{10,... | collective-permute-start | bytes 491528 | tf_op jit(solution)/shard_map/ppermute | solution.py:40
  53.5 11.6 %collective-permute-start.18 = (bf16[10,64,128]{2,1,0:T(8,128)(2,1)S(1)}, bf16[10,64,128]{2,1,0:T(8,128)(2,1)S(1)}, u32[]{:S(2)}, u32[]{:S(2)}) collective-permute-start(bf16[10,64,128]{2,1,0:T(8,128)(2,1)S(1)} %get-tuple-element.67), channel_id=1, source_target_pairs={{0,6},{1,7},{2,4},{3,5},{4,0},{5,1},{6,2},{7,3},{8,14},{9,15},{10,... | collective-permute-start | bytes 491528 | tf_op jit(solution)/shard_map/ppermute | solution.py:40
  53.5 8.0 %collective-permute-start.11 = (bf16[7,64,128]{2,1,0:T(8,128)(2,1)S(1)}, bf16[7,64,128]{2,1,0:T(8,128)(2,1)S(1)}, u32[]{:S(2)}, u32[]{:S(2)}) collective-permute-start(bf16[7,64,128]{2,1,0:T(8,128)(2,1)S(1)} %get-tuple-element.57), channel_id=1, source_target_pairs={{0,24},{1,25},{2,26},{3,27},{4,28},{5,29},{6,30},{7,31},{8,0},{9,1... | collective-permute-start | bytes 344072 | tf_op jit(solution)/shard_map/ppermute | solution.py:40
  59.1 6.0 %collective-permute-start.10 = (bf16[7,64,128]{2,1,0:T(8,128)(2,1)S(1)}, bf16[7,64,128]{2,1,0:T(8,128)(2,1)S(1)}, u32[]{:S(2)}, u32[]{:S(2)}) collective-permute-start(bf16[7,64,128]{2,1,0:T(8,128)(2,1)S(1)} %get-tuple-element.56.after), channel_id=1, source_target_pairs={{0,8},{1,9},{2,10},{3,11},{4,12},{5,13},{6,14},{7,15},{8,16},{9,17... | collective-permute-start | bytes 344072 | tf_op jit(solution)/shard_map/ppermute | solution.py:40
  66.0 18.6 %all-to-all-start = ((bf16[8,112,128]{2,1,0:T(8,128)(2,1)}), bf16[8,112,128]{2,1,0:T(8,128)(2,1)S(1)}, u32[]{:S(2)}, u32[]{:S(2)}) async-start(bf16[8,112,128]{2,1,0:T(8,128)(2,1)} %get-tuple-element.70), calls=%async_computation | async-start | bytes 458752 | tf_op jit(solution)/shard_map/all_to_all | solution.py:535

commit v9 on v8

--- a/solution.py
+++ b/solution.py
@@ -81,18 +81,26 @@
     wide[1] = flat[:, 128:256]
 
 
-def pack_kernel(one, two, row, hi, lo, corner_hi, corner_lo, wide):
-    edge = 11 * (1 - lax.axis_index("ha"))
+def pack_columns_kernel(one, two, hi, lo, wide):
     for n, block in enumerate((one, two)):
         spread(wide, block)
         for f in range(4):
+            for j, out in ((15, hi), (0, lo)):
+                for h in range(2):
+                    out[n, f, :, h * 128 : h * 128 + 128] = column(wide, h, f, j).astype(BF)
+
+
+def pack_rows_kernel(one, two, left, right, after, row):
+    del after
+    edge = 11 * (1 - lax.axis_index("ha"))
+    for n, block in enumerate((one, two)):
+        for f in range(4):
             row[n, f] = block[f, edge]
-            for j, out, corner in ((15, hi, corner_hi), (0, lo, corner_lo)):
-                for h in range(2):
-                    lanes = slice(h * 128, h * 128 + 128)
-                    out[n, f, :, lanes] = column(wide, h, f, j).astype(BF)
-                    cell = wide[h, pl.ds(f * 192 + edge * 16 + j, 1), :]
-                    corner[n, f, :, lanes] = jnp.broadcast_to(cell, (16, 128)).astype(BF)
+        for at, side in ((0, left), (4, right)):
+            cells = [side[n, f].astype(F32) for f in range(4)]
+            cells = [jnp.where(edge == 0, c[0:1], c[11:12]) for c in cells]
+            cells = jnp.concatenate(cells + [jnp.zeros((4, 256), F32)], axis=0)
+            row[n, 4 + at // 4] = jnp.concatenate([cells, cells], axis=0).astype(BF)
 
 
 def pad_block(put, block, row, left, right, corner_left, corner_right):
@@ -173,42 +181,49 @@
     return (lax.broadcasted_iota(jnp.int32, (256, 256), 0) == source).astype(BF)
 
 
-def film_kernel(
-    step, inputs, hidden, table, weight, act_out, inp_out, slope, taps,
-    film, blocks, sem, block_sem, tap_sem,
-):
+def sort_kernel(inputs, weight, inp_out, taps, block, sem, tap_sem):
+    block_copy = pltpu.make_async_copy(inputs, block, sem)
+    block_copy.start()
+    copies = weight_copies(weight, taps, tap_sem)
+    for copy in copies:
+        copy.start()
+    order = channel_order()
+    block_copy.wait()
+    cells = jnp.dot(block[...].reshape(768, 256), order, preferred_element_type=F32)
+    inp_out[...] = cells.astype(BF).reshape(4, 12, 16, 256)
+    for copy in copies:
+        copy.wait()
+
+
+def film_kernel(step, hidden, table, act_out, slope, film, block, sem, block_sem):
     start = step[0]
     whole = pl.multiple_of(start // 8 * 8, 8)
     film_copy = pltpu.make_async_copy(table.at[pl.ds(whole, 8)], film, sem)
     film_copy.start()
-    block_copies = [
-        pltpu.make_async_copy(ref, blocks.at[n], block_sem.at[n])
-        for n, ref in enumerate((inputs, hidden))
-    ]
-    for copy in block_copies:
-        copy.start()
-    copies = weight_copies(weight, taps, tap_sem)
-    for copy in copies:
-        copy.start()
+    block_copy = pltpu.make_async_copy(hidden, block, block_sem)
+    block_copy.start()
     order = channel_order()
-    sort = lambda v: jnp.dot(v, order, preferred_element_type=F32).astype(BF)
-    for copy in block_copies:
-        copy.wait()
+    block_copy.wait()
     film_copy.wait()
-    inp_out[...] = sort(blocks[0].reshape(768, 256)).reshape(4, 12, 16, 256)
     line = film[pl.ds(start - whole, 1), :]
     scale, shift = 1.0 + line[:, 0:256], line[:, 256:512]
-    shifted = blocks[1].reshape(768, 256).astype(F32) * scale + shift
+    shifted = block[...].reshape(768, 256).astype(F32) * scale + shift
     sigma = jax.nn.sigmoid(shifted)
-    act_out[...] = sort((shifted * sigma).astype(BF))
+    activated = (shifted * sigma).astype(BF)
+    act_out[...] = jnp.dot(activated, order, preferred_element_type=F32).astype(BF)
     slope[...] = scale * sigma * (1.0 + shifted * (1.0 - sigma))
-    for copy in copies:
-        copy.wait()
-
-
-def pad_kernel(block, row, left, right, corner_left, corner_right, act, out):
-    sides = (row, left, right, corner_left, corner_right)
-    pad_block(keep_in(out), lambda f, r: block[f, r], *[lambda f, s=s: s[0, f] for s in sides])
+
+
+def pad_kernel(block, row, left, right, act, out):
+    pad_block(
+        keep_in(out),
+        lambda f, r: block[f, r],
+        lambda f: row[0, f],
+        lambda f: left[0, f],
+        lambda f: right[0, f],
+        lambda f: row[0, 4].astype(F32)[f : f + 1],
+        lambda f: row[0, 5].astype(F32)[f : f + 1],
+    )
     for f in range(4):
         for n in range(12):
             cells = act[f * 192 + n * 16 : f * 192 + n * 16 + 16, 128:256]
@@ -270,7 +285,7 @@
                 out[a * 3 + b] = total[d * 32 : d * 32 + 32].astype(out.dtype)
 
 
-def second_x_kernel(got1, got2, got3, own, keep, one, two, three, held):
+def second_x_kernel(got1, got2, got3, own, out, keep, held):
     y = lax.axis_index("y")
 
     def tap(t):
@@ -283,8 +298,9 @@
     for g in range(7):
         parts = [tap(t) if t < 27 else jnp.zeros((32, 256), F32) for t in range(4 * g, 4 * g + 4)]
         held[...] = jnp.concatenate(parts, axis=0).T.reshape(8, 4, 8, 128)
-        for d, out in enumerate((keep, one, two, three)):
-            out[g] = held[:, (y + d) & 3].reshape(64, 128).astype(out.dtype)
+        for q in range(4):
+            out[q, g] = held[:, q].reshape(64, 128).astype(BF)
+        keep[g] = held[:, y].reshape(64, 128)
 
 
 def border_at(base, n, h):
@@ -293,14 +309,13 @@
 
 
 def first_grad_kernel(
-    hid, inp, row, left, right, corner_left, corner_right, after,
-    own, pair, wide, padded, side, flat,
+    hid, inp, row, left, right, after, own, pair, wide, padded, side, flat,
 ):
     del after
     order = channel_order()
-    for n, ref in enumerate((row, left, right, corner_left, corner_right)):
-        cells = jnp.dot(ref[1].reshape(64, 256), order, preferred_element_type=F32)
-        side[n] = cells.reshape(4, 16, 256)
+    for at, ref, size in ((0, row, 6), (6, left, 4), (10, right, 4)):
+        cells = jnp.dot(ref[1].reshape(size * 16, 256), order, preferred_element_type=F32)
+        side[at : at + size] = cells.reshape(size, 16, 256)
 
     def put(f, r, which, cells):
         at = which * 128
@@ -308,7 +323,13 @@
         wide[f, r, :, at + 384 : at + 512] = cells[:, 128:256]
 
     pad_block(
-        keep_in(padded), lambda f, r: inp[f, r], *[lambda f, n=n: side[n, f] for n in range(5)]
+        keep_in(padded),
+        lambda f, r: inp[f, r],
+        lambda f: side[f],
+        lambda f: side[6 + f],
+        lambda f: side[10 + f],
+        lambda f: side[4, f : f + 1],
+        lambda f: side[5, f : f + 1],
     )
     build_shifted(put, padded)
     spread(flat, hid)
@@ -378,7 +399,7 @@
                 out[border_at(7, n, h)] = cells[:, h * 128 : h * 128 + 128]
 
 
-def last_kernel(own_two, a2, a1, a3, own_one, b2, b1, b3, out, keep, border, held):
+def last_kernel(own_two, got_two, own_one, b2, b1, b3, out, keep, border, held):
     low = lax.axis_index("ha") == 0
     for h in range(2):
         lanes = slice(h * 128, h * 128 + 128)
@@ -390,10 +411,13 @@
                 border[4 + n, :, lanes] = b2[border_at(7, n, h)]
             else:
                 border[8, :, lanes], border[9, :, lanes] = across.astype(BF), along.astype(BF)
-    for n, (own, got) in enumerate(((own_two, (a1, a2, a3)), (own_one, (b1, b2, b3)))):
+    y = lax.axis_index("y")
+    parts_two = [got_two[(y + d) & 3] for d in range(1, 4)]
+    parts_one = [ref[0:7] for ref in (b1, b2, b3)]
+    for n, (own, parts) in enumerate(((own_two, parts_two), (own_one, parts_one))):
         total = own[...]
-        for ref in got:
-            total = total + ref[0:7].astype(F32)
+        for part in parts:
+            total = total + part.astype(F32)
         held[n] = total.reshape(7, 8, 8, 128)
 
     def plane(z):
@@ -421,45 +445,56 @@
     taps_one = conv_one.transpose(1, 2, 3, 0, 4).reshape(27, 256, 256)
     taps_two = conv_two.transpose(1, 2, 3, 0, 4).reshape(27, 256, 256)
     wide = near((4, 14, 16, 768), BF)
-    quads = [near((7, 64, 128), F32)] + [near((7, 64, 128), BF)] * 3
-
     def ring(parts, axis):
         return [send(parts[d - 1], ring_pairs(**{axis: d})) for d in (2, 1, 3)]
 
-    packed = call(
-        pack_kernel,
-        "pack_first",
+    hi, lo = call(
+        pack_columns_kernel,
+        "pack_columns",
         (block, inputs),
         "pp",
-        [near((2, 4, 16, 256), BF)] * 5,
+        [near((2, 4, 16, 256), BF)] * 2,
         [pltpu.VMEM((2, 768, 128), F32)],
     )
-    ways = ((1, 0), (0, 1), (0, -1), (1, 1), (1, -1))
-    sides = [send(p, block_pairs(*way)) for p, way in zip(packed, ways)]
-    act, inp, slope, held_two = call(
+    left, right = send(hi, block_pairs(0, 1)), send(lo, block_pairs(0, -1))
+    inp, held_two = call(
+        sort_kernel,
+        "sort_input",
+        (inputs, taps_two),
+        "hh",
+        [near((4, 12, 16, 256), BF), near((27, 256, 256), BF)],
+        [
+            pltpu.VMEM((4, 12, 16, 256), BF),
+            pltpu.SemaphoreType.DMA,
+            pltpu.SemaphoreType.DMA((3,)),
+        ],
+    )
+    (row,) = call(
+        pack_rows_kernel,
+        "pack_rows",
+        (block, inputs, left, right, inp),
+        "ppvvv",
+        [near((2, 6, 16, 256), BF)],
+    )
+    row = send(row, block_pairs(1, 0))
+    act, slope = call(
         film_kernel,
         "film",
-        (timesteps, inputs, hidden, film_table, taps_two),
-        "shhhh",
-        [
-            near((768, 256), BF),
-            near((4, 12, 16, 256), BF),
-            near((768, 256), F32),
-            near((27, 256, 256), BF),
-        ],
+        (timesteps, hidden, film_table),
+        "shh",
+        [near((768, 256), BF), near((768, 256), F32)],
         [
             pltpu.VMEM((8, 512), F32),
-            pltpu.VMEM((2, 4, 12, 16, 256), BF),
+            pltpu.VMEM((4, 12, 16, 256), BF),
             pltpu.SemaphoreType.DMA,
-            pltpu.SemaphoreType.DMA((2,)),
-            pltpu.SemaphoreType.DMA((3,)),
+            pltpu.SemaphoreType.DMA,
         ],
     )
     (padded,) = call(
         pad_kernel,
         "pad_cotangent",
-        (block, *sides, act),
-        "pvvvvvv",
+        (block, row, left, right, act),
+        "pvvvv",
         [near((4, 22, 16, 256), BF)],
     )
     pair_padded = send(padded, core_pairs())
@@ -475,13 +510,13 @@
     own_one, pair_one = call(
         first_grad_kernel,
         "grad_one",
-        (grad_hidden, inp, *sides, pair_padded),
-        "vv" + "v" * 6,
+        (grad_hidden, inp, row, left, right, pair_padded),
+        "v" * 6,
         [near((4, 27, 64, 128), F32), near((4, 28, 64, 128), F32)],
         [
             pltpu.VMEM((4, 14, 16, 768), BF),
             pltpu.VMEM((4, 16, 16, 256), BF),
-            pltpu.VMEM((5, 4, 16, 256), F32),
+            pltpu.VMEM((14, 16, 256), F32),
             pltpu.VMEM((2, 768, 128), F32),
         ],
     )
@@ -506,19 +541,19 @@
     )
     got_one = ring(parts_one, "dy")
 
-    own_two, *parts = call(
+    out_two, own_two = call(
         second_x_kernel,
         "grad_two_x",
         (*got_two, own_two),
         "vvvv",
-        quads,
+        [far((4, 7, 64, 128), BF), near((7, 64, 128), F32)],
         [pltpu.VMEM((8, 4, 8, 128), F32)],
     )
-    got_two = ring(parts, "dy")
+    got_two = lax.all_to_all(out_two, "y", 0, 0, tiled=True)
     own_one, *parts_one = call(
         first_y_kernel,
         "grad_one_y",
-        (*got_one, own_one, grad_hidden, cols, parts[0]),
+        (*got_one, own_one, grad_hidden, cols, own_two),
         "v" * 7,
         [near((7, 64, 128), F32)] + [near((10, 64, 128), BF)] * 3,
     )
@@ -527,8 +562,8 @@
     out, own, border = call(
         last_kernel,
         "last_stage",
-        (own_two, *got_two, own_one, *got_one),
-        "v" * 8,
+        (own_two, got_two, own_one, *got_one),
+        "v" * 6,
         [far((8, 112, 128), BF), near((112, 128), F32), near((10, 16, 256), BF)],
         [pltpu.VMEM((2, 7, 8, 8, 128), F32)],
     )

time: 85.7 us -> 88.7 us (1.035)
  the two profiles are of different devices: /device:TPU:6 before, /device:TPU:24 now
where the time goes in v9:
time: 88.7 us; the launch traced here: 88.1 us
  starting transfers between devices  34 us (38%)
  Pallas kernels  26.3 us (30%)
  waiting for transfers between devices  24.8 us (28%)
  local copies, waits for them, and re-layouts  1.63 us (2%)
  between operations  1.38 us (2%)
    pallas_call x14, Pallas kernels, call(): pl.pallas_call(kernel, out_shape=tuple((o for o, _ in outs)), in_specs=[s...  26.3 us
    ppermute x14, starting transfers between devices, send(): return lax.ppermute(value, AX, pairs)  21.1 us
    ppermute x14, waiting for transfers between devices, send(): return lax.ppermute(value, AX, pairs)  20.1 us
    all_to_all x1, starting transfers between devices, shards(): planes = lax.all_to_all(out, 'z', 0, 0, tiled=True)  8.3 us
    all_to_all x1, starting transfers between devices, shards(): got_two = lax.all_to_all(out_two, 'y', 0, 0, tiled=True)  4.68 us
    all_to_all x1, waiting for transfers between devices, shards(): planes = lax.all_to_all(out, 'z', 0, 0, tiled=True)  4.66 us
  transfers between devices with their start and end apart: 16, of which 7 were waited for; matrix products, arithmetic and copies ran while one was open for 0% of the time, Pallas kernels for 21%

profile of v9, /device:TPU:24, one launch (start us, length us, event | category | flops | bytes accessed | tf_op | source)
XLA Modules:
  0.0 88.1 jit_solution(10719708306889274472)
XLA Ops:
  0.6 1.3 %pack_columns.1 = (bf16[2,4,16,256]{3,2,1,0:T(8,128)(2,1)S(1)}, bf16[2,4,16,256]{3,2,1,0:T(8,128)(2,1)S(1)}) custom-call(bf16[4,12,16,256]{3,2,1,0:T(8,128)(2,1)} %bitcast.16, bf16[4,12,16,256]{3,2,1,0:T(8,128)(2,1)} %bitcast.22), custom_call_target="tpu_custom_call" | custom-call | tf_op jit(solution)/shard_map/pack_columns/pallas_call | solution.py:50
  2.0 3.2 %collective-permute-start.1 = (bf16[2,4,16,256]{3,2,1,0:T(8,128)(2,1)S(1)}, bf16[2,4,16,256]{3,2,1,0:T(8,128)(2,1)S(1)}, u32[]{:S(2)}, u32[]{:S(2)}) collective-permute-start(bf16[2,4,16,256]{3,2,1,0:T(8,128)(2,1)S(1)} %get-tuple-element.34), channel_id=1, source_target_pairs={{0,3},{1,0},{2,1},{3,2},{4,7},{5,4},{6,5},{7,6},{8,11},{9,8},{10,9... | collective-permute-start | bytes 196616 | tf_op jit(solution)/shard_map/ppermute | solution.py:40
  5.2 2.1 %sort_input.1 = (bf16[4,12,16,256]{3,2,1,0:T(8,128)(2,1)S(1)}, bf16[27,256,256]{2,1,0:T(8,128)(2,1)S(1)}) custom-call(bf16[4,12,16,256]{3,2,1,0:T(8,128)(2,1)} %bitcast.23, bf16[27,256,256]{2,1,0:T(8,128)(2,1)} %bitcast.21), custom_call_target="tpu_custom_call" | custom-call | tf_op jit(solution)/shard_map/sort_input/pallas_call | solution.py:50
  8.5 1.6 %collective-permute-start.2 = (bf16[2,6,16,256]{3,2,1,0:T(8,128)(2,1)S(1)}, bf16[2,6,16,256]{3,2,1,0:T(8,128)(2,1)S(1)}, u32[]{:S(2)}, u32[]{:S(2)}) collective-permute-start(bf16[2,6,16,256]{3,2,1,0:T(8,128)(2,1)S(1)} %pack_rows.1), channel_id=1, source_target_pairs={{0,4},{1,5},{2,6},{3,7},{4,0},{5,1},{6,2},{7,3},{8,12},{9,13},{10,... | collective-permute-start | bytes 294920 | tf_op jit(solution)/shard_map/ppermute | solution.py:40
  10.8 1.5 %film.1 = (bf16[768,256]{1,0:T(8,128)(2,1)S(1)}, f32[768,256]{1,0:T(8,128)S(1)}) custom-call(s32[1]{0:T(128)S(6)} %copy.10.step, bf16[4,12,16,256]{3,2,1,0:T(8,128)(2,1)} %bitcast.26, f32[1000,512]{1,0:T(8,128)} %table.1), custom_call_target="tpu_custom_call" | custom-call | tf_op jit(solution)/shard_map/film/pallas_call | solution.py:50
  14.3 1.9 %collective-permute-start.3 = (bf16[4,22,16,256]{3,2,1,0:T(8,128)(2,1)S(1)}, bf16[4,22,16,256]{3,2,1,0:T(8,128)(2,1)S(1)}, u32[]{:S(2)}, u32[]{:S(2)}) collective-permute-start(bf16[4,22,16,256]{3,2,1,0:T(8,128)(2,1)S(1)} %pad_cotangent.1.padded), channel_id=1, source_target_pairs={{0,1},{1,0},{2,3},{3,2},{4,5},{5,4},{6,7},{7,6},{8,9},{9,8},{10,11... | collective-permute-start | bytes 2162696 | tf_op jit(solution)/shard_map/ppermute | solution.py:40
  16.2 2.3 %conv_two_back.1 = (bf16[4,14,16,768]{3,2,1,0:T(8,128)(2,1)S(1)}, bf16[4,12,16,256]{3,2,1,0:T(8,128)(2,1)S(1)}) custom-call(bf16[4,22,16,256]{3,2,1,0:T(8,128)(2,1)S(1)} %pad_cotangent.1.padded, f32[768,256]{1,0:T(8,128)S(1)} %get-tuple-element.37.slope, bf16[27,256,256]{2,1,0:T(8,128)(2,1)S(1)} %get-tuple-element.38.taps), custom_call_target="tpu_custom_call" | custom-call | tf_op jit(solution)/shard_map/conv_two_back/pallas_call | solution.py:50
  18.4 2.9 %grad_one.1 = (f32[4,27,64,128]{3,2,1,0:T(8,128)S(1)}, f32[4,28,64,128]{3,2,1,0:T(8,128)S(1)}) custom-call(bf16[4,12,16,256]{3,2,1,0:T(8,128)(2,1)S(1)} %get-tuple-element.39.hid, bf16[4,12,16,256]{3,2,1,0:T(8,128)(2,1)S(1)} %get-tuple-element.35.after.inp, bf16[2,6,16,256]{3,2,1,0:T(8,128)(2,1)S(1)} %collective-permute-done.2.row, ...), custom_call_target="tpu_custom_call" | custom-call | tf_op jit(solution)/shard_map/grad_one/pallas_call | solution.py:50
  21.5 2.7 %grad_two.1 = (f32[9,32,768]{2,1,0:T(8,128)S(1)}, bf16[9,32,768]{2,1,0:T(8,128)(2,1)S(1)}, bf16[9,32,768]{2,1,0:T(8,128)(2,1)S(1)}, bf16[9,32,768]{2,1,0:T(8,128)(2,1)S(1)}) custom-call(bf16[4,14,16,768]{3,2,1,0:T(8,128)(2,1)S(1)} %get-tuple-element.40.wide, bf16[768,256]{1,0:T(8,128)(2,1)S(1)} %get-tuple-element.36.act, ...), custom_call_target="tpu_custom_call" | custom-call | tf_op jit(solution)/shard_map/grad_two/pallas_call | solution.py:50
  24.2 2.7 %collective-permute-start.4 = (bf16[9,32,768]{2,1,0:T(8,128)(2,1)S(1)}, bf16[9,32,768]{2,1,0:T(8,128)(2,1)S(1)}, u32[]{:S(2)}, u32[]{:S(2)}) collective-permute-start(bf16[9,32,768]{2,1,0:T(8,128)(2,1)S(1)} %get-tuple-element.42), channel_id=1, source_target_pairs={{0,2},{1,3},{2,0},{3,1},{4,6},{5,7},{6,4},{7,5},{8,10},{9,11},{10,... | collective-permute-start | bytes 1327112 | tf_op jit(solution)/shard_map/ppermute | solution.py:40
  27.5 1.3 %collective-permute-start.5 = (bf16[9,32,768]{2,1,0:T(8,128)(2,1)S(1)}, bf16[9,32,768]{2,1,0:T(8,128)(2,1)S(1)}, u32[]{:S(2)}, u32[]{:S(2)}) collective-permute-start(bf16[9,32,768]{2,1,0:T(8,128)(2,1)S(1)} %get-tuple-element.43.after), channel_id=1, source_target_pairs={{0,4},{1,5},{2,6},{3,7},{4,2},{5,3},{6,0},{7,1},{8,12},{9,13},{10,... | collective-permute-start | bytes 1327112 | tf_op jit(solution)/shard_map/ppermute | solution.py:40
  28.9 1.3 %grad_one_sum.1 = (f32[27,64,128]{2,1,0:T(8,128)S(1)}, bf16[27,64,128]{2,1,0:T(8,128)(2,1)}, bf16[27,64,128]{2,1,0:T(8,128)(2,1)}, bf16[27,64,128]{2,1,0:T(8,128)(2,1)}, bf16[2,4,16,256]{3,2,1,0:T(8,128)(2,1)S(1)}) custom-call(f32[4,27,64,128]{3,2,1,0:T(8,128)S(1)} %get-tuple-element.48.own, f32[4,28,64,128]{3,2,1,0:T(8,128)S(1)} %collective-permute-done.7.pair, ...), custom_call_target="tpu_custom_call" | custom-call | tf_op jit(solution)/shard_map/grad_one_sum/pallas_call | solution.py:50
  30.2 1.2 %collective-permute-start.8 = (bf16[27,64,128]{2,1,0:T(8,128)(2,1)}, bf16[27,64,128]{2,1,0:T(8,128)(2,1)S(1)}, u32[]{:S(2)}, u32[]{:S(2)}) collective-permute-start(bf16[27,64,128]{2,1,0:T(8,128)(2,1)} %get-tuple-element.49), channel_id=1, source_target_pairs={{0,16},{1,17},{2,18},{3,19},{4,20},{5,21},{6,22},{7,23},{8,24},{9,... | collective-permute-start | bytes 1327112 | tf_op jit(solution)/shard_map/ppermute | solution.py:40
  31.4 2.2 %collective-permute-start.9 = (bf16[27,64,128]{2,1,0:T(8,128)(2,1)}, bf16[27,64,128]{2,1,0:T(8,128)(2,1)S(1)}, u32[]{:S(2)}, u32[]{:S(2)}) collective-permute-start(bf16[27,64,128]{2,1,0:T(8,128)(2,1)} %get-tuple-element.50), channel_id=1, source_target_pairs={{0,8},{1,9},{2,10},{3,11},{4,12},{5,13},{6,14},{7,15},{8,16},{9,17... | collective-permute-start | bytes 1327112 | tf_op jit(solution)/shard_map/ppermute | solution.py:40
  33.6 5.2 %collective-permute-done.4.got1 = bf16[9,32,768]{2,1,0:T(8,128)(2,1)S(1)} collective-permute-done((bf16[9,32,768]{2,1,0:T(8,128)(2,1)S(1)}, bf16[9,32,768]{2,1,0:T(8,128)(2,1)S(1)}, u32[]{:S(2)}, u32[]{:S(2)}) %collective-permute-start.4) | collective-permute-done | bytes 442400 | tf_op jit(solution)/shard_map/ppermute | solution.py:40
  39.5 7.5 %collective-permute-done.6.got3 = bf16[9,32,768]{2,1,0:T(8,128)(2,1)S(1)} collective-permute-done((bf16[9,32,768]{2,1,0:T(8,128)(2,1)S(1)}, bf16[9,32,768]{2,1,0:T(8,128)(2,1)S(1)}, u32[]{:S(2)}, u32[]{:S(2)}) %collective-permute-start.6) | collective-permute-done | bytes 442400 | tf_op jit(solution)/shard_map/ppermute | solution.py:40
  48.9 4.7 %all-to-all-start = ((bf16[4,7,64,128]{3,2,1,0:T(8,128)(2,1)}), bf16[4,7,64,128]{3,2,1,0:T(8,128)(2,1)S(1)}, u32[]{:S(2)}, u32[]{:S(2)}) async-start(bf16[4,7,64,128]{3,2,1,0:T(8,128)(2,1)} %get-tuple-element.47), calls=%async_computation | async-start | bytes 917504 | tf_op jit(solution)/shard_map/all_to_all | solution.py:552
  55.5 2.1 %collective-permute-start.11 = (bf16[10,64,128]{2,1,0:T(8,128)(2,1)}, bf16[10,64,128]{2,1,0:T(8,128)(2,1)S(1)}, u32[]{:S(2)}, u32[]{:S(2)}) collective-permute-start(bf16[10,64,128]{2,1,0:T(8,128)(2,1)} %get-tuple-element.55), channel_id=1, source_target_pairs={{0,2},{1,3},{2,0},{3,1},{4,6},{5,7},{6,4},{7,5},{8,10},{9,11},{10,... | collective-permute-start | bytes 491528 | tf_op jit(solution)/shard_map/ppermute | solution.py:40
  58.2 2.6 %collective-permute-start.13 = (bf16[10,64,128]{2,1,0:T(8,128)(2,1)S(1)}, bf16[10,64,128]{2,1,0:T(8,128)(2,1)S(1)}, u32[]{:S(2)}, u32[]{:S(2)}) collective-permute-start(bf16[10,64,128]{2,1,0:T(8,128)(2,1)S(1)} %get-tuple-element.57), channel_id=1, source_target_pairs={{0,6},{1,7},{2,4},{3,5},{4,0},{5,1},{6,2},{7,3},{8,14},{9,15},{10,... | collective-permute-start | bytes 491528 | tf_op jit(solution)/shard_map/ppermute | solution.py:40
  60.9 3.5 %collective-permute-done.11.b2 = bf16[10,64,128]{2,1,0:T(8,128)(2,1)S(1)} collective-permute-done((bf16[10,64,128]{2,1,0:T(8,128)(2,1)}, bf16[10,64,128]{2,1,0:T(8,128)(2,1)S(1)}, u32[]{:S(2)}, u32[]{:S(2)}) %collective-permute-start.11) | collective-permute-done | bytes 163872 | tf_op jit(solution)/shard_map/ppermute | solution.py:40
  64.3 2.1 %collective-permute-done.12.b1 = bf16[10,64,128]{2,1,0:T(8,128)(2,1)S(1)} collective-permute-done((bf16[10,64,128]{2,1,0:T(8,128)(2,1)}, bf16[10,64,128]{2,1,0:T(8,128)(2,1)S(1)}, u32[]{:S(2)}, u32[]{:S(2)}) %collective-permute-start.12) | collective-permute-done | bytes 163872 | tf_op jit(solution)/shard_map/ppermute | solution.py:40
  68.3 8.3 %all-to-all-start.1 = ((bf16[8,112,128]{2,1,0:T(8,128)(2,1)}), bf16[8,112,128]{2,1,0:T(8,128)(2,1)S(1)}, u32[]{:S(2)}, u32[]{:S(2)}) async-start(bf16[8,112,128]{2,1,0:T(8,128)(2,1)} %get-tuple-element.60), calls=%async_computation.1 | async-start | bytes 458752 | tf_op jit(solution)/shard_map/all_to_all | solution.py:570
  76.6 6.0 %conv_one_back.1.after = bf16[4,12,16,256]{3,2,1,0:T(8,128)(2,1)} custom-call(bf16[4,12,16,256]{3,2,1,0:T(8,128)(2,1)S(1)} %get-tuple-element.39.hid, bf16[4,12,16,256]{3,2,1,0:T(8,128)(2,1)} %bitcast.19, bf16[10,16,256]{2,1,0:T(8,128)(2,1)S(1)} %get-tuple-element.58.border, bf16[2,4,16,256]{3,2,1,0:T(8,128)(2,1)S(1)} %get-tuple-element.53.cols, ...), custom_call_target="tpu_custom_call" | custom-call | tf_op jit(solution)/shard_map/conv_one_back/pallas_call | solution.py:50
  82.6 4.7 %all-to-all-done.1.got = bf16[8,112,128]{2,1,0:T(8,128)(2,1)S(1)} async-done(((bf16[8,112,128]{2,1,0:T(8,128)(2,1)}), bf16[8,112,128]{2,1,0:T(8,128)(2,1)S(1)}, u32[]{:S(2)}, u32[]{:S(2)}) %all-to-all-start.1) | async-done | bytes 229408 | tf_op jit(solution)/shard_map/all_to_all | solution.py:570
  (26 shorter events, 11.8 us)
Async XLA Ops:
  1.9 5.5 %collective-permute-start = (bf16[2,4,16,256]{3,2,1,0:T(8,128)(2,1)S(1)}, bf16[2,4,16,256]{3,2,1,0:T(8,128)(2,1)S(1)}, u32[]{:S(2)}, u32[]{:S(2)}) collective-permute-start(bf16[2,4,16,256]{3,2,1,0:T(8,128)(2,1)S(1)} %get-tuple-element.33), channel_id=1, source_target_pairs={{0,1},{1,2},{2,3},{3,0},{4,5},{5,6},{6,7},{7,4},{8,9},{9,10},{10,1... | collective-permute-start | bytes 196616 | tf_op jit(solution)/shard_map/ppermute | solution.py:40
  2.0 5.4 %collective-permute-start.1 = (bf16[2,4,16,256]{3,2,1,0:T(8,128)(2,1)S(1)}, bf16[2,4,16,256]{3,2,1,0:T(8,128)(2,1)S(1)}, u32[]{:S(2)}, u32[]{:S(2)}) collective-permute-start(bf16[2,4,16,256]{3,2,1,0:T(8,128)(2,1)S(1)} %get-tuple-element.34), channel_id=1, source_target_pairs={{0,3},{1,0},{2,1},{3,2},{4,7},{5,4},{6,5},{7,6},{8,11},{9,8},{10,9... | collective-permute-start | bytes 196616 | tf_op jit(solution)/shard_map/ppermute | solution.py:40
  8.5 4.7 %collective-permute-start.2 = (bf16[2,6,16,256]{3,2,1,0:T(8,128)(2,1)S(1)}, bf16[2,6,16,256]{3,2,1,0:T(8,128)(2,1)S(1)}, u32[]{:S(2)}, u32[]{:S(2)}) collective-permute-start(bf16[2,6,16,256]{3,2,1,0:T(8,128)(2,1)S(1)} %pack_rows.1), channel_id=1, source_target_pairs={{0,4},{1,5},{2,6},{3,7},{4,0},{5,1},{6,2},{7,3},{8,12},{9,13},{10,... | collective-permute-start | bytes 294920 | tf_op jit(solution)/shard_map/ppermute | solution.py:40
  14.3 4.1 %collective-permute-start.3 = (bf16[4,22,16,256]{3,2,1,0:T(8,128)(2,1)S(1)}, bf16[4,22,16,256]{3,2,1,0:T(8,128)(2,1)S(1)}, u32[]{:S(2)}, u32[]{:S(2)}) collective-permute-start(bf16[4,22,16,256]{3,2,1,0:T(8,128)(2,1)S(1)} %pad_cotangent.1.padded), channel_id=1, source_target_pairs={{0,1},{1,0},{2,3},{3,2},{4,5},{5,4},{6,7},{7,6},{8,9},{9,8},{10,11... | collective-permute-start | bytes 2162696 | tf_op jit(solution)/shard_map/ppermute | solution.py:40
  21.4 7.5 %collective-permute-start.7 = (f32[4,28,64,128]{3,2,1,0:T(8,128)S(1)}, f32[4,28,64,128]{3,2,1,0:T(8,128)S(1)}, u32[]{:S(2)}, u32[]{:S(2)}) collective-permute-start(f32[4,28,64,128]{3,2,1,0:T(8,128)S(1)} %get-tuple-element.41.after), channel_id=1, source_target_pairs={{0,1},{1,0},{2,3},{3,2},{4,5},{5,4},{6,7},{7,6},{8,9},{9,8},{10,11... | collective-permute-start | bytes 11010056 | tf_op jit(solution)/shard_map/ppermute | solution.py:40
  24.2 14.6 %collective-permute-start.4 = (bf16[9,32,768]{2,1,0:T(8,128)(2,1)S(1)}, bf16[9,32,768]{2,1,0:T(8,128)(2,1)S(1)}, u32[]{:S(2)}, u32[]{:S(2)}) collective-permute-start(bf16[9,32,768]{2,1,0:T(8,128)(2,1)S(1)} %get-tuple-element.42), channel_id=1, source_target_pairs={{0,2},{1,3},{2,0},{3,1},{4,6},{5,7},{6,4},{7,5},{8,10},{9,11},{10,... | collective-permute-start | bytes 1327112 | tf_op jit(solution)/shard_map/ppermute | solution.py:40
  26.9 20.2 %collective-permute-start.6 = (bf16[9,32,768]{2,1,0:T(8,128)(2,1)S(1)}, bf16[9,32,768]{2,1,0:T(8,128)(2,1)S(1)}, u32[]{:S(2)}, u32[]{:S(2)}) collective-permute-start(bf16[9,32,768]{2,1,0:T(8,128)(2,1)S(1)} %get-tuple-element.44), channel_id=1, source_target_pairs={{0,6},{1,7},{2,4},{3,5},{4,0},{5,1},{6,2},{7,3},{8,14},{9,15},{10,... | collective-permute-start | bytes 1327112 | tf_op jit(solution)/shard_map/ppermute | solution.py:40
  27.5 20.3 %collective-permute-start.5 = (bf16[9,32,768]{2,1,0:T(8,128)(2,1)S(1)}, bf16[9,32,768]{2,1,0:T(8,128)(2,1)S(1)}, u32[]{:S(2)}, u32[]{:S(2)}) collective-permute-start(bf16[9,32,768]{2,1,0:T(8,128)(2,1)S(1)} %get-tuple-element.43.after), channel_id=1, source_target_pairs={{0,4},{1,5},{2,6},{3,7},{4,2},{5,3},{6,0},{7,1},{8,12},{9,13},{10,... | collective-permute-start | bytes 1327112 | tf_op jit(solution)/shard_map/ppermute | solution.py:40
  30.2 23.4 %collective-permute-start.8 = (bf16[27,64,128]{2,1,0:T(8,128)(2,1)}, bf16[27,64,128]{2,1,0:T(8,128)(2,1)S(1)}, u32[]{:S(2)}, u32[]{:S(2)}) collective-permute-start(bf16[27,64,128]{2,1,0:T(8,128)(2,1)} %get-tuple-element.49), channel_id=1, source_target_pairs={{0,16},{1,17},{2,18},{3,19},{4,20},{5,21},{6,22},{7,23},{8,24},{9,... | collective-permute-start | bytes 1327112 | tf_op jit(solution)/shard_map/ppermute | solution.py:40
  31.4 22.2 %collective-permute-start.9 = (bf16[27,64,128]{2,1,0:T(8,128)(2,1)}, bf16[27,64,128]{2,1,0:T(8,128)(2,1)S(1)}, u32[]{:S(2)}, u32[]{:S(2)}) collective-permute-start(bf16[27,64,128]{2,1,0:T(8,128)(2,1)} %get-tuple-element.50), channel_id=1, source_target_pairs={{0,8},{1,9},{2,10},{3,11},{4,12},{5,13},{6,14},{7,15},{8,16},{9,17... | collective-permute-start | bytes 1327112 | tf_op jit(solution)/shard_map/ppermute | solution.py:40
  38.8 14.8 %collective-permute-start.10 = (bf16[27,64,128]{2,1,0:T(8,128)(2,1)}, bf16[27,64,128]{2,1,0:T(8,128)(2,1)S(1)}, u32[]{:S(2)}, u32[]{:S(2)}) collective-permute-start(bf16[27,64,128]{2,1,0:T(8,128)(2,1)} %get-tuple-element.51), channel_id=1, source_target_pairs={{0,24},{1,25},{2,26},{3,27},{4,28},{5,29},{6,30},{7,31},{8,0},{9,1... | collective-permute-start | bytes 1327112 | tf_op jit(solution)/shard_map/ppermute | solution.py:40
  48.9 12.0 %all-to-all-start = ((bf16[4,7,64,128]{3,2,1,0:T(8,128)(2,1)}), bf16[4,7,64,128]{3,2,1,0:T(8,128)(2,1)S(1)}, u32[]{:S(2)}, u32[]{:S(2)}) async-start(bf16[4,7,64,128]{3,2,1,0:T(8,128)(2,1)} %get-tuple-element.47), calls=%async_computation | async-start | bytes 917504 | tf_op jit(solution)/shard_map/all_to_all | solution.py:552
  54.8 0.7 copy-start
  55.5 8.8 %collective-permute-start.11 = (bf16[10,64,128]{2,1,0:T(8,128)(2,1)}, bf16[10,64,128]{2,1,0:T(8,128)(2,1)S(1)}, u32[]{:S(2)}, u32[]{:S(2)}) collective-permute-start(bf16[10,64,128]{2,1,0:T(8,128)(2,1)} %get-tuple-element.55), channel_id=1, source_target_pairs={{0,2},{1,3},{2,0},{3,1},{4,6},{5,7},{6,4},{7,5},{8,10},{9,11},{10,... | collective-permute-start | bytes 491528 | tf_op jit(solution)/shard_map/ppermute | solution.py:40
  57.6 8.8 %collective-permute-start.12 = (bf16[10,64,128]{2,1,0:T(8,128)(2,1)}, bf16[10,64,128]{2,1,0:T(8,128)(2,1)S(1)}, u32[]{:S(2)}, u32[]{:S(2)}) collective-permute-start(bf16[10,64,128]{2,1,0:T(8,128)(2,1)} %get-tuple-element.56), channel_id=1, source_target_pairs={{0,4},{1,5},{2,6},{3,7},{4,2},{5,3},{6,0},{7,1},{8,12},{9,13},{10,... | collective-permute-start | bytes 491528 | tf_op jit(solution)/shard_map/ppermute | solution.py:40
  58.2 8.2 %collective-permute-start.13 = (bf16[10,64,128]{2,1,0:T(8,128)(2,1)S(1)}, bf16[10,64,128]{2,1,0:T(8,128)(2,1)S(1)}, u32[]{:S(2)}, u32[]{:S(2)}) collective-permute-start(bf16[10,64,128]{2,1,0:T(8,128)(2,1)S(1)} %get-tuple-element.57), channel_id=1, source_target_pairs={{0,6},{1,7},{2,4},{3,5},{4,0},{5,1},{6,2},{7,3},{8,14},{9,15},{10,... | collective-permute-start | bytes 491528 | tf_op jit(solution)/shard_map/ppermute | solution.py:40
  66.5 0.9 %copy-start.1 = (f32[7,64,128]{2,1,0:T(8,128)S(1)}, f32[7,64,128]{2,1,0:T(8,128)}, u32[]{:S(2)}) copy-start(f32[7,64,128]{2,1,0:T(8,128)} %copy-done) | copy-start | bytes 688132
  68.3 19.0 %all-to-all-start.1 = ((bf16[8,112,128]{2,1,0:T(8,128)(2,1)}), bf16[8,112,128]{2,1,0:T(8,128)(2,1)S(1)}, u32[]{:S(2)}, u32[]{:S(2)}) async-start(bf16[8,112,128]{2,1,0:T(8,128)(2,1)} %get-tuple-element.60), calls=%async_computation.1 | async-start | bytes 458752 | tf_op jit(solution)/shard_map/all_to_all | solution.py:570

commit v10 on v8

--- a/solution.py
+++ b/solution.py
@@ -81,7 +81,8 @@
     wide[1] = flat[:, 128:256]
 
 
-def pack_kernel(one, two, row, hi, lo, corner_hi, corner_lo, wide):
+def pack_kernel(one, two, row, hi, lo, corner_hi, corner_lo, same, wide):
+    same[...] = one[...]
     edge = 11 * (1 - lax.axis_index("ha"))
     for n, block in enumerate((one, two)):
         spread(wide, block)
@@ -222,10 +223,11 @@
 
 
 def input_conv_kernel(
-    hid, block, border, cols, after, weight, out, held, total, sem, wide, padded
+    hid, block, border, cols, after, weight, out, held, total, sem, wide, padded, near_block
 ):
     del after
     copies = weight_copies(weight, held, sem)
+    copies.append(pltpu.make_async_copy(block, near_block, sem.at[3]))
     for copy in copies:
         copy.start()
     is_one = lax.axis_index("core") == 1
@@ -247,7 +249,7 @@
     for copy in copies:
         copy.wait()
     conv_sum(wide, held, total)
-    grad = block[...].reshape(768, 256).astype(F32) + total[...]
+    grad = near_block[...].reshape(768, 256).astype(F32) + total[...]
     out[...] = grad.astype(BF).reshape(4, 12, 16, 256)
 
 
@@ -285,6 +287,8 @@
         held[...] = jnp.concatenate(parts, axis=0).T.reshape(8, 4, 8, 128)
         for d, out in enumerate((keep, one, two, three)):
             out[g] = held[:, (y + d) & 3].reshape(64, 128).astype(out.dtype)
+    for out in (one, two, three):
+        out[7:10] = jnp.zeros((3, 64, 128), BF)
 
 
 def border_at(base, n, h):
@@ -421,17 +425,17 @@
     taps_one = conv_one.transpose(1, 2, 3, 0, 4).reshape(27, 256, 256)
     taps_two = conv_two.transpose(1, 2, 3, 0, 4).reshape(27, 256, 256)
     wide = near((4, 14, 16, 768), BF)
-    quads = [near((7, 64, 128), F32)] + [near((7, 64, 128), BF)] * 3
+    quads = [near((7, 64, 128), F32)] + [near((10, 64, 128), BF)] * 3
 
     def ring(parts, axis):
         return [send(parts[d - 1], ring_pairs(**{axis: d})) for d in (2, 1, 3)]
 
-    packed = call(
+    *packed, held_block = call(
         pack_kernel,
         "pack_first",
         (block, inputs),
         "pp",
-        [near((2, 4, 16, 256), BF)] * 5,
+        [near((2, 4, 16, 256), BF)] * 5 + [near((4, 12, 16, 256), BF)],
         [pltpu.VMEM((2, 768, 128), F32)],
     )
     ways = ((1, 0), (0, 1), (0, -1), (1, 1), (1, -1))
@@ -458,8 +462,8 @@
     (padded,) = call(
         pad_kernel,
         "pad_cotangent",
-        (block, *sides, act),
-        "pvvvvvv",
+        (held_block, *sides, act),
+        "vvvvvvv",
         [near((4, 22, 16, 256), BF)],
     )
     pair_padded = send(padded, core_pairs())
@@ -520,7 +524,7 @@
         "grad_one_y",
         (*got_one, own_one, grad_hidden, cols, parts[0]),
         "v" * 7,
-        [near((7, 64, 128), F32)] + [near((10, 64, 128), BF)] * 3,
+        quads,
     )
     got_one = ring(parts_one, "dx")
 
@@ -538,14 +542,15 @@
         input_conv_kernel,
         "conv_one_back",
         (grad_hidden, block, border, cols, own, taps_one),
-        "vpvvvh",
+        "vhvvvh",
         [(jax.ShapeDtypeStruct((4, 12, 16, 256), BF), "v")],
         [
             pltpu.VMEM((27, 256, 256), BF),
             pltpu.VMEM((768, 256), F32),
-            pltpu.SemaphoreType.DMA((3,)),
+            pltpu.SemaphoreType.DMA((4,)),
             pltpu.VMEM((4, 14, 16, 768), BF),
             pltpu.VMEM((4, 16, 16, 256), BF),
+            pltpu.VMEM((4, 12, 16, 256), BF),
         ],
     )
 

time: 85.7 us -> 83.3 us (0.972)
  the two profiles are of different devices: /device:TPU:6 before, /device:TPU:24 now
where the time goes in v10:
time: 83.3 us; the launch traced here: 82.5 us
  starting transfers between devices  32.8 us (39%)
  waiting for transfers between devices  28.7 us (34%)
  Pallas kernels  19.7 us (24%)
  between operations  1.41 us (2%)
    ppermute x19, starting transfers between devices, send(): return lax.ppermute(value, AX, pairs)  24.3 us
    ppermute x19, waiting for transfers between devices, send(): return lax.ppermute(value, AX, pairs)  23.1 us
    pallas_call x12, Pallas kernels, call(): pl.pallas_call(kernel, out_shape=tuple((o for o, _ in outs)), in_specs=[s...  19.7 us
    all_to_all x1, starting transfers between devices, shards(): planes = lax.all_to_all(out, 'z', 0, 0, tiled=True)  8.47 us
    all_to_all x1, waiting for transfers between devices, shards(): planes = lax.all_to_all(out, 'z', 0, 0, tiled=True)  5.58 us
  transfers between devices with their start and end apart: 20, of which 9 were waited for; matrix products, arithmetic and copies ran while one was open for 0% of the time, Pallas kernels for 17%

profile of v10, /device:TPU:24, one launch (start us, length us, event | category | flops | bytes accessed | tf_op | source)
XLA Modules:
  0.0 82.5 jit_solution(3499563369695856046)
XLA Ops:
  0.6 1.3 %pack_first.1 = (bf16[2,4,16,256]{3,2,1,0:T(8,128)(2,1)S(1)}, bf16[2,4,16,256]{3,2,1,0:T(8,128)(2,1)S(1)}, bf16[2,4,16,256]{3,2,1,0:T(8,128)(2,1)S(1)}, bf16[2,4...) custom-call(bf16[4,12,16,256]{3,2,1,0:T(8,128)(2,1)} %bitcast.20, ...), custom_call_target="tpu_custom_call" | custom-call | tf_op jit(solution)/shard_map/pack_first/pallas_call | solution.py:50
  2.0 1.6 %collective-permute-start = (bf16[2,4,16,256]{3,2,1,0:T(8,128)(2,1)S(1)}, bf16[2,4,16,256]{3,2,1,0:T(8,128)(2,1)S(1)}, u32[]{:S(2)}, u32[]{:S(2)}) collective-permute-start(bf16[2,4,16,256]{3,2,1,0:T(8,128)(2,1)S(1)} %get-tuple-element.40), channel_id=1, source_target_pairs={{0,4},{1,5},{2,6},{3,7},{4,0},{5,1},{6,2},{7,3},{8,12},{9,13},{10,... | collective-permute-start | bytes 196616 | tf_op jit(solution)/shard_map/ppermute | solution.py:40
  3.5 3.2 %collective-permute-start.2 = (bf16[2,4,16,256]{3,2,1,0:T(8,128)(2,1)S(1)}, bf16[2,4,16,256]{3,2,1,0:T(8,128)(2,1)S(1)}, u32[]{:S(2)}, u32[]{:S(2)}) collective-permute-start(bf16[2,4,16,256]{3,2,1,0:T(8,128)(2,1)S(1)} %get-tuple-element.42), channel_id=1, source_target_pairs={{0,3},{1,0},{2,1},{3,2},{4,7},{5,4},{6,5},{7,6},{8,11},{9,8},{10,9... | collective-permute-start | bytes 196616 | tf_op jit(solution)/shard_map/ppermute | solution.py:40
  6.8 3.0 %collective-permute-start.4 = (bf16[2,4,16,256]{3,2,1,0:T(8,128)(2,1)S(1)}, bf16[2,4,16,256]{3,2,1,0:T(8,128)(2,1)S(1)}, u32[]{:S(2)}, u32[]{:S(2)}) collective-permute-start(bf16[2,4,16,256]{3,2,1,0:T(8,128)(2,1)S(1)} %get-tuple-element.44), channel_id=1, source_target_pairs={{0,7},{1,4},{2,5},{3,6},{4,3},{5,0},{6,1},{7,2},{8,15},{9,12},{10,... | collective-permute-start | bytes 196616 | tf_op jit(solution)/shard_map/ppermute | solution.py:40
  10.4 2.3 %film.1 = (bf16[768,256]{1,0:T(8,128)(2,1)S(1)}, bf16[4,12,16,256]{3,2,1,0:T(8,128)(2,1)S(1)}, f32[768,256]{1,0:T(8,128)S(1)}, bf16[27,256,256]{2,1,0:T(8,128)(2,1)S(1)}) custom-call(s32[1]{0:T(128)S(6)} %copy.10.step, bf16[4,12,16,256]{3,2,1,0:T(8,128)(2,1)} %bitcast.19, bf16[4,12,16,256]{3,2,1,0:T(8,128)(2,1)} %bitcast.23, f32[1000,512]{1,0:T(8,128)} %table.1, ...), custom_call_target="tpu_custom_call" | custom-call | tf_op jit(solution)/shard_map/film/pallas_call | solution.py:50
  12.9 1.2 %collective-permute-start.5 = (bf16[4,22,16,256]{3,2,1,0:T(8,128)(2,1)S(1)}, bf16[4,22,16,256]{3,2,1,0:T(8,128)(2,1)S(1)}, u32[]{:S(2)}, u32[]{:S(2)}) collective-permute-start(bf16[4,22,16,256]{3,2,1,0:T(8,128)(2,1)S(1)} %pad_cotangent.1.padded), channel_id=1, source_target_pairs={{0,1},{1,0},{2,3},{3,2},{4,5},{5,4},{6,7},{7,6},{8,9},{9,8},{10,11... | collective-permute-start | bytes 2162696 | tf_op jit(solution)/shard_map/ppermute | solution.py:40
  14.1 2.3 %conv_two_back.1 = (bf16[4,14,16,768]{3,2,1,0:T(8,128)(2,1)S(1)}, bf16[4,12,16,256]{3,2,1,0:T(8,128)(2,1)S(1)}) custom-call(bf16[4,22,16,256]{3,2,1,0:T(8,128)(2,1)S(1)} %pad_cotangent.1.padded, f32[768,256]{1,0:T(8,128)S(1)} %get-tuple-element.46.slope, bf16[27,256,256]{2,1,0:T(8,128)(2,1)S(1)} %get-tuple-element.47.taps), custom_call_target="tpu_custom_call" | custom-call | tf_op jit(solution)/shard_map/conv_two_back/pallas_call | solution.py:50
  16.4 3.0 %grad_one.1 = (f32[4,27,64,128]{3,2,1,0:T(8,128)S(1)}, f32[4,28,64,128]{3,2,1,0:T(8,128)S(1)}) custom-call(bf16[4,12,16,256]{3,2,1,0:T(8,128)(2,1)S(1)} %get-tuple-element.48.hid, bf16[4,12,16,256]{3,2,1,0:T(8,128)(2,1)S(1)} %get-tuple-element.50.inp, bf16[2,4,16,256]{3,2,1,0:T(8,128)(2,1)S(1)} %collective-permute-done.row, ...), custom_call_target="tpu_custom_call" | custom-call | tf_op jit(solution)/shard_map/grad_one/pallas_call | solution.py:50
  19.6 2.7 %grad_two.1 = (f32[9,32,768]{2,1,0:T(8,128)S(1)}, bf16[9,32,768]{2,1,0:T(8,128)(2,1)S(1)}, bf16[9,32,768]{2,1,0:T(8,128)(2,1)S(1)}, bf16[9,32,768]{2,1,0:T(8,128)(2,1)S(1)}) custom-call(bf16[4,14,16,768]{3,2,1,0:T(8,128)(2,1)S(1)} %get-tuple-element.49.wide, bf16[768,256]{1,0:T(8,128)(2,1)S(1)} %get-tuple-element.45.act, ...), custom_call_target="tpu_custom_call" | custom-call | tf_op jit(solution)/shard_map/grad_two/pallas_call | solution.py:50
  26.4 1.3 %collective-permute-start.13 = (bf16[27,64,128]{2,1,0:T(8,128)(2,1)S(1)}, bf16[27,64,128]{2,1,0:T(8,128)(2,1)S(1)}, u32[]{:S(2)}, u32[]{:S(2)}) collective-permute-start(bf16[27,64,128]{2,1,0:T(8,128)(2,1)S(1)} %get-tuple-element.61), channel_id=1, source_target_pairs={{0,16},{1,17},{2,18},{3,19},{4,20},{5,21},{6,22},{7,23},{8,24},{9,... | collective-permute-start | bytes 1327112 | tf_op jit(solution)/shard_map/ppermute | solution.py:40
  27.7 2.2 %collective-permute-start.14 = (bf16[27,64,128]{2,1,0:T(8,128)(2,1)S(1)}, bf16[27,64,128]{2,1,0:T(8,128)(2,1)S(1)}, u32[]{:S(2)}, u32[]{:S(2)}) collective-permute-start(bf16[27,64,128]{2,1,0:T(8,128)(2,1)S(1)} %get-tuple-element.62), channel_id=1, source_target_pairs={{0,8},{1,9},{2,10},{3,11},{4,12},{5,13},{6,14},{7,15},{8,16},{9,17... | collective-permute-start | bytes 1327112 | tf_op jit(solution)/shard_map/ppermute | solution.py:40
  29.9 7.1 %collective-permute-done.6.got1 = bf16[9,32,768]{2,1,0:T(8,128)(2,1)S(1)} collective-permute-done((bf16[9,32,768]{2,1,0:T(8,128)(2,1)S(1)}, bf16[9,32,768]{2,1,0:T(8,128)(2,1)S(1)}, u32[]{:S(2)}, u32[]{:S(2)}) %collective-permute-start.6) | collective-permute-done | bytes 442400 | tf_op jit(solution)/shard_map/ppermute | solution.py:40
  37.7 6.8 %collective-permute-done.8.got3 = bf16[9,32,768]{2,1,0:T(8,128)(2,1)S(1)} collective-permute-done((bf16[9,32,768]{2,1,0:T(8,128)(2,1)S(1)}, bf16[9,32,768]{2,1,0:T(8,128)(2,1)S(1)}, u32[]{:S(2)}, u32[]{:S(2)}) %collective-permute-start.8) | collective-permute-done | bytes 442400 | tf_op jit(solution)/shard_map/ppermute | solution.py:40
  44.5 1.5 %collective-permute-done.7.got2 = bf16[9,32,768]{2,1,0:T(8,128)(2,1)S(1)} collective-permute-done((bf16[9,32,768]{2,1,0:T(8,128)(2,1)S(1)}, bf16[9,32,768]{2,1,0:T(8,128)(2,1)S(1)}, u32[]{:S(2)}, u32[]{:S(2)}) %collective-permute-start.7) | collective-permute-done | bytes 442400 | tf_op jit(solution)/shard_map/ppermute | solution.py:40
  46.4 1.3 %collective-permute-start.9 = (bf16[10,64,128]{2,1,0:T(8,128)(2,1)S(1)}, bf16[10,64,128]{2,1,0:T(8,128)(2,1)S(1)}, u32[]{:S(2)}, u32[]{:S(2)}) collective-permute-start(bf16[10,64,128]{2,1,0:T(8,128)(2,1)S(1)} %get-tuple-element.57), channel_id=1, source_target_pairs={{0,16},{1,17},{2,18},{3,19},{4,20},{5,21},{6,22},{7,23},{8,24},{9,... | collective-permute-start | bytes 491528 | tf_op jit(solution)/shard_map/ppermute | solution.py:40
  47.7 3.2 %collective-permute-start.10 = (bf16[10,64,128]{2,1,0:T(8,128)(2,1)S(1)}, bf16[10,64,128]{2,1,0:T(8,128)(2,1)S(1)}, u32[]{:S(2)}, u32[]{:S(2)}) collective-permute-start(bf16[10,64,128]{2,1,0:T(8,128)(2,1)S(1)} %get-tuple-element.58.after), channel_id=1, source_target_pairs={{0,8},{1,9},{2,10},{3,11},{4,12},{5,13},{6,14},{7,15},{8,16},{9,17... | collective-permute-start | bytes 491528 | tf_op jit(solution)/shard_map/ppermute | solution.py:40
  52.0 1.6 %collective-permute-start.17 = (bf16[10,64,128]{2,1,0:T(8,128)(2,1)S(1)}, bf16[10,64,128]{2,1,0:T(8,128)(2,1)S(1)}, u32[]{:S(2)}, u32[]{:S(2)}) collective-permute-start(bf16[10,64,128]{2,1,0:T(8,128)(2,1)S(1)} %get-tuple-element.68), channel_id=1, source_target_pairs={{0,4},{1,5},{2,6},{3,7},{4,2},{5,3},{6,0},{7,1},{8,12},{9,13},{10,... | collective-permute-start | bytes 491528 | tf_op jit(solution)/shard_map/ppermute | solution.py:40
  53.6 1.5 %collective-permute-done.9.a2 = bf16[10,64,128]{2,1,0:T(8,128)(2,1)S(1)} collective-permute-done((bf16[10,64,128]{2,1,0:T(8,128)(2,1)S(1)}, bf16[10,64,128]{2,1,0:T(8,128)(2,1)S(1)}, u32[]{:S(2)}, u32[]{:S(2)}) %collective-permute-start.9) | collective-permute-done | bytes 163872 | tf_op jit(solution)/shard_map/ppermute | solution.py:40
  56.2 1.4 %collective-permute-done.11.a3 = bf16[10,64,128]{2,1,0:T(8,128)(2,1)S(1)} collective-permute-done((bf16[10,64,128]{2,1,0:T(8,128)(2,1)S(1)}, bf16[10,64,128]{2,1,0:T(8,128)(2,1)S(1)}, u32[]{:S(2)}, u32[]{:S(2)}) %collective-permute-start.11) | collective-permute-done | bytes 163872 | tf_op jit(solution)/shard_map/ppermute | solution.py:40
  57.6 2.5 %collective-permute-done.16.b2 = bf16[10,64,128]{2,1,0:T(8,128)(2,1)S(1)} collective-permute-done((bf16[10,64,128]{2,1,0:T(8,128)(2,1)S(1)}, bf16[10,64,128]{2,1,0:T(8,128)(2,1)S(1)}, u32[]{:S(2)}, u32[]{:S(2)}) %collective-permute-start.16) | collective-permute-done | bytes 163872 | tf_op jit(solution)/shard_map/ppermute | solution.py:40
  60.1 1.6 %collective-permute-done.17.b1 = bf16[10,64,128]{2,1,0:T(8,128)(2,1)S(1)} collective-permute-done((bf16[10,64,128]{2,1,0:T(8,128)(2,1)S(1)}, bf16[10,64,128]{2,1,0:T(8,128)(2,1)S(1)}, u32[]{:S(2)}, u32[]{:S(2)}) %collective-permute-start.17) | collective-permute-done | bytes 163872 | tf_op jit(solution)/shard_map/ppermute | solution.py:40
  62.6 8.5 %all-to-all-start = ((bf16[8,112,128]{2,1,0:T(8,128)(2,1)}), bf16[8,112,128]{2,1,0:T(8,128)(2,1)S(1)}, u32[]{:S(2)}, u32[]{:S(2)}) async-start(bf16[8,112,128]{2,1,0:T(8,128)(2,1)} %get-tuple-element.72), calls=%async_computation | async-start | bytes 458752 | tf_op jit(solution)/shard_map/all_to_all | solution.py:539
  71.0 5.1 %conv_one_back.1.after = bf16[4,12,16,256]{3,2,1,0:T(8,128)(2,1)} custom-call(bf16[4,12,16,256]{3,2,1,0:T(8,128)(2,1)S(1)} %get-tuple-element.48.hid, bf16[4,12,16,256]{3,2,1,0:T(8,128)(2,1)} %bitcast.21, bf16[10,16,256]{2,1,0:T(8,128)(2,1)S(1)} %get-tuple-element.70.border, bf16[2,4,16,256]{3,2,1,0:T(8,128)(2,1)S(1)} %get-tuple-element.65.cols, ...), custom_call_target="tpu_custom_call" | custom-call | tf_op jit(solution)/shard_map/conv_one_back/pallas_call | solution.py:50
  76.2 5.6 %all-to-all-done.got = bf16[8,112,128]{2,1,0:T(8,128)(2,1)S(1)} async-done(((bf16[8,112,128]{2,1,0:T(8,128)(2,1)}), bf16[8,112,128]{2,1,0:T(8,128)(2,1)S(1)}, u32[]{:S(2)}, u32[]{:S(2)}) %all-to-all-start) | async-done | bytes 229408 | tf_op jit(solution)/shard_map/all_to_all | solution.py:539
  (28 shorter events, 9.4 us)
Async XLA Ops:
  2.0 10.8 %collective-permute-start = (bf16[2,4,16,256]{3,2,1,0:T(8,128)(2,1)S(1)}, bf16[2,4,16,256]{3,2,1,0:T(8,128)(2,1)S(1)}, u32[]{:S(2)}, u32[]{:S(2)}) collective-permute-start(bf16[2,4,16,256]{3,2,1,0:T(8,128)(2,1)S(1)} %get-tuple-element.40), channel_id=1, source_target_pairs={{0,4},{1,5},{2,6},{3,7},{4,0},{5,1},{6,2},{7,3},{8,12},{9,13},{10,... | collective-permute-start | bytes 196616 | tf_op jit(solution)/shard_map/ppermute | solution.py:40
  3.5 9.2 %collective-permute-start.1 = (bf16[2,4,16,256]{3,2,1,0:T(8,128)(2,1)S(1)}, bf16[2,4,16,256]{3,2,1,0:T(8,128)(2,1)S(1)}, u32[]{:S(2)}, u32[]{:S(2)}) collective-permute-start(bf16[2,4,16,256]{3,2,1,0:T(8,128)(2,1)S(1)} %get-tuple-element.41), channel_id=1, source_target_pairs={{0,1},{1,2},{2,3},{3,0},{4,5},{5,6},{6,7},{7,4},{8,9},{9,10},{10,1... | collective-permute-start | bytes 196616 | tf_op jit(solution)/shard_map/ppermute | solution.py:40
  3.5 9.2 %collective-permute-start.2 = (bf16[2,4,16,256]{3,2,1,0:T(8,128)(2,1)S(1)}, bf16[2,4,16,256]{3,2,1,0:T(8,128)(2,1)S(1)}, u32[]{:S(2)}, u32[]{:S(2)}) collective-permute-start(bf16[2,4,16,256]{3,2,1,0:T(8,128)(2,1)S(1)} %get-tuple-element.42), channel_id=1, source_target_pairs={{0,3},{1,0},{2,1},{3,2},{4,7},{5,4},{6,5},{7,6},{8,11},{9,8},{10,9... | collective-permute-start | bytes 196616 | tf_op jit(solution)/shard_map/ppermute | solution.py:40
  6.8 6.0 %collective-permute-start.3 = (bf16[2,4,16,256]{3,2,1,0:T(8,128)(2,1)S(1)}, bf16[2,4,16,256]{3,2,1,0:T(8,128)(2,1)S(1)}, u32[]{:S(2)}, u32[]{:S(2)}) collective-permute-start(bf16[2,4,16,256]{3,2,1,0:T(8,128)(2,1)S(1)} %get-tuple-element.43), channel_id=1, source_target_pairs={{0,5},{1,6},{2,7},{3,4},{4,1},{5,2},{6,3},{7,0},{8,13},{9,14},{10,... | collective-permute-start | bytes 196616 | tf_op jit(solution)/shard_map/ppermute | solution.py:40
  6.8 6.0 %collective-permute-start.4 = (bf16[2,4,16,256]{3,2,1,0:T(8,128)(2,1)S(1)}, bf16[2,4,16,256]{3,2,1,0:T(8,128)(2,1)S(1)}, u32[]{:S(2)}, u32[]{:S(2)}) collective-permute-start(bf16[2,4,16,256]{3,2,1,0:T(8,128)(2,1)S(1)} %get-tuple-element.44), channel_id=1, source_target_pairs={{0,7},{1,4},{2,5},{3,6},{4,3},{5,0},{6,1},{7,2},{8,15},{9,12},{10,... | collective-permute-start | bytes 196616 | tf_op jit(solution)/shard_map/ppermute | solution.py:40
  12.9 3.5 %collective-permute-start.5 = (bf16[4,22,16,256]{3,2,1,0:T(8,128)(2,1)S(1)}, bf16[4,22,16,256]{3,2,1,0:T(8,128)(2,1)S(1)}, u32[]{:S(2)}, u32[]{:S(2)}) collective-permute-start(bf16[4,22,16,256]{3,2,1,0:T(8,128)(2,1)S(1)} %pad_cotangent.1.padded), channel_id=1, source_target_pairs={{0,1},{1,0},{2,3},{3,2},{4,5},{5,4},{6,7},{7,6},{8,9},{9,8},{10,11... | collective-permute-start | bytes 2162696 | tf_op jit(solution)/shard_map/ppermute | solution.py:40
  19.4 6.7 %collective-permute-start.12 = (f32[4,28,64,128]{3,2,1,0:T(8,128)S(1)}, f32[4,28,64,128]{3,2,1,0:T(8,128)S(1)}, u32[]{:S(2)}, u32[]{:S(2)}) collective-permute-start(f32[4,28,64,128]{3,2,1,0:T(8,128)S(1)} %get-tuple-element.51.after), channel_id=1, source_target_pairs={{0,1},{1,0},{2,3},{3,2},{4,5},{5,4},{6,7},{7,6},{8,9},{9,8},{10,11... | collective-permute-start | bytes 11010056 | tf_op jit(solution)/shard_map/ppermute | solution.py:40
  22.3 14.6 %collective-permute-start.6 = (bf16[9,32,768]{2,1,0:T(8,128)(2,1)S(1)}, bf16[9,32,768]{2,1,0:T(8,128)(2,1)S(1)}, u32[]{:S(2)}, u32[]{:S(2)}) collective-permute-start(bf16[9,32,768]{2,1,0:T(8,128)(2,1)S(1)} %get-tuple-element.52), channel_id=1, source_target_pairs={{0,2},{1,3},{2,0},{3,1},{4,6},{5,7},{6,4},{7,5},{8,10},{9,11},{10,... | collective-permute-start | bytes 1327112 | tf_op jit(solution)/shard_map/ppermute | solution.py:40
  23.3 21.1 %collective-permute-start.8 = (bf16[9,32,768]{2,1,0:T(8,128)(2,1)S(1)}, bf16[9,32,768]{2,1,0:T(8,128)(2,1)S(1)}, u32[]{:S(2)}, u32[]{:S(2)}) collective-permute-start(bf16[9,32,768]{2,1,0:T(8,128)(2,1)S(1)} %get-tuple-element.54), channel_id=1, source_target_pairs={{0,6},{1,7},{2,4},{3,5},{4,0},{5,1},{6,2},{7,3},{8,14},{9,15},{10,... | collective-permute-start | bytes 1327112 | tf_op jit(solution)/shard_map/ppermute | solution.py:40
  24.5 21.5 %collective-permute-start.7 = (bf16[9,32,768]{2,1,0:T(8,128)(2,1)S(1)}, bf16[9,32,768]{2,1,0:T(8,128)(2,1)S(1)}, u32[]{:S(2)}, u32[]{:S(2)}) collective-permute-start(bf16[9,32,768]{2,1,0:T(8,128)(2,1)S(1)} %get-tuple-element.53.after), channel_id=1, source_target_pairs={{0,4},{1,5},{2,6},{3,7},{4,2},{5,3},{6,0},{7,1},{8,12},{9,13},{10,... | collective-permute-start | bytes 1327112 | tf_op jit(solution)/shard_map/ppermute | solution.py:40
  26.4 21.4 %collective-permute-start.13 = (bf16[27,64,128]{2,1,0:T(8,128)(2,1)S(1)}, bf16[27,64,128]{2,1,0:T(8,128)(2,1)S(1)}, u32[]{:S(2)}, u32[]{:S(2)}) collective-permute-start(bf16[27,64,128]{2,1,0:T(8,128)(2,1)S(1)} %get-tuple-element.61), channel_id=1, source_target_pairs={{0,16},{1,17},{2,18},{3,19},{4,20},{5,21},{6,22},{7,23},{8,24},{9,... | collective-permute-start | bytes 1327112 | tf_op jit(solution)/shard_map/ppermute | solution.py:40
  27.7 23.3 %collective-permute-start.14 = (bf16[27,64,128]{2,1,0:T(8,128)(2,1)S(1)}, bf16[27,64,128]{2,1,0:T(8,128)(2,1)S(1)}, u32[]{:S(2)}, u32[]{:S(2)}) collective-permute-start(bf16[27,64,128]{2,1,0:T(8,128)(2,1)S(1)} %get-tuple-element.62), channel_id=1, source_target_pairs={{0,8},{1,9},{2,10},{3,11},{4,12},{5,13},{6,14},{7,15},{8,16},{9,17... | collective-permute-start | bytes 1327112 | tf_op jit(solution)/shard_map/ppermute | solution.py:40
  36.9 14.0 %collective-permute-start.15 = (bf16[27,64,128]{2,1,0:T(8,128)(2,1)S(1)}, bf16[27,64,128]{2,1,0:T(8,128)(2,1)S(1)}, u32[]{:S(2)}, u32[]{:S(2)}) collective-permute-start(bf16[27,64,128]{2,1,0:T(8,128)(2,1)S(1)} %get-tuple-element.63), channel_id=1, source_target_pairs={{0,24},{1,25},{2,26},{3,27},{4,28},{5,29},{6,30},{7,31},{8,0},{9,1... | collective-permute-start | bytes 1327112 | tf_op jit(solution)/shard_map/ppermute | solution.py:40
  46.4 8.7 %collective-permute-start.9 = (bf16[10,64,128]{2,1,0:T(8,128)(2,1)S(1)}, bf16[10,64,128]{2,1,0:T(8,128)(2,1)S(1)}, u32[]{:S(2)}, u32[]{:S(2)}) collective-permute-start(bf16[10,64,128]{2,1,0:T(8,128)(2,1)S(1)} %get-tuple-element.57), channel_id=1, source_target_pairs={{0,16},{1,17},{2,18},{3,19},{4,20},{5,21},{6,22},{7,23},{8,24},{9,... | collective-permute-start | bytes 491528 | tf_op jit(solution)/shard_map/ppermute | solution.py:40
  47.7 9.9 %collective-permute-start.11 = (bf16[10,64,128]{2,1,0:T(8,128)(2,1)S(1)}, bf16[10,64,128]{2,1,0:T(8,128)(2,1)S(1)}, u32[]{:S(2)}, u32[]{:S(2)}) collective-permute-start(bf16[10,64,128]{2,1,0:T(8,128)(2,1)S(1)} %get-tuple-element.59), channel_id=1, source_target_pairs={{0,24},{1,25},{2,26},{3,27},{4,28},{5,29},{6,30},{7,31},{8,0},{9,1... | collective-permute-start | bytes 491528 | tf_op jit(solution)/shard_map/ppermute | solution.py:40
  47.7 9.9 %collective-permute-start.10 = (bf16[10,64,128]{2,1,0:T(8,128)(2,1)S(1)}, bf16[10,64,128]{2,1,0:T(8,128)(2,1)S(1)}, u32[]{:S(2)}, u32[]{:S(2)}) collective-permute-start(bf16[10,64,128]{2,1,0:T(8,128)(2,1)S(1)} %get-tuple-element.58.after), channel_id=1, source_target_pairs={{0,8},{1,9},{2,10},{3,11},{4,12},{5,13},{6,14},{7,15},{8,16},{9,17... | collective-permute-start | bytes 491528 | tf_op jit(solution)/shard_map/ppermute | solution.py:40
  51.5 8.7 %collective-permute-start.16 = (bf16[10,64,128]{2,1,0:T(8,128)(2,1)S(1)}, bf16[10,64,128]{2,1,0:T(8,128)(2,1)S(1)}, u32[]{:S(2)}, u32[]{:S(2)}) collective-permute-start(bf16[10,64,128]{2,1,0:T(8,128)(2,1)S(1)} %get-tuple-element.67), channel_id=1, source_target_pairs={{0,2},{1,3},{2,0},{3,1},{4,6},{5,7},{6,4},{7,5},{8,10},{9,11},{10,... | collective-permute-start | bytes 491528 | tf_op jit(solution)/shard_map/ppermute | solution.py:40
  52.0 9.7 %collective-permute-start.17 = (bf16[10,64,128]{2,1,0:T(8,128)(2,1)S(1)}, bf16[10,64,128]{2,1,0:T(8,128)(2,1)S(1)}, u32[]{:S(2)}, u32[]{:S(2)}) collective-permute-start(bf16[10,64,128]{2,1,0:T(8,128)(2,1)S(1)} %get-tuple-element.68), channel_id=1, source_target_pairs={{0,4},{1,5},{2,6},{3,7},{4,2},{5,3},{6,0},{7,1},{8,12},{9,13},{10,... | collective-permute-start | bytes 491528 | tf_op jit(solution)/shard_map/ppermute | solution.py:40
  55.1 6.6 %collective-permute-start.18 = (bf16[10,64,128]{2,1,0:T(8,128)(2,1)S(1)}, bf16[10,64,128]{2,1,0:T(8,128)(2,1)S(1)}, u32[]{:S(2)}, u32[]{:S(2)}) collective-permute-start(bf16[10,64,128]{2,1,0:T(8,128)(2,1)S(1)} %get-tuple-element.69), channel_id=1, source_target_pairs={{0,6},{1,7},{2,4},{3,5},{4,0},{5,1},{6,2},{7,3},{8,14},{9,15},{10,... | collective-permute-start | bytes 491528 | tf_op jit(solution)/shard_map/ppermute | solution.py:40
  62.6 19.2 %all-to-all-start = ((bf16[8,112,128]{2,1,0:T(8,128)(2,1)}), bf16[8,112,128]{2,1,0:T(8,128)(2,1)S(1)}, u32[]{:S(2)}, u32[]{:S(2)}) async-start(bf16[8,112,128]{2,1,0:T(8,128)(2,1)} %get-tuple-element.72), calls=%async_computation | async-start | bytes 458752 | tf_op jit(solution)/shard_map/all_to_all | solution.py:539

commit v11 on v10

--- a/solution.py
+++ b/solution.py
@@ -70,30 +70,28 @@
     return lax.axis_index("xh") * 2 + lax.axis_index("ha")
 
 
-def column(wide, lanes_half, f, j):
-    cells = wide[lanes_half, pl.ds(f * 192 + j, 12, stride=16), :]
-    return jnp.concatenate([cells, jnp.zeros((4, 128), F32)], axis=0)
-
-
-def spread(wide, block):
-    flat = block[...].reshape(768, 256).astype(F32)
-    wide[0] = flat[:, 0:128]
-    wide[1] = flat[:, 128:256]
-
-
-def pack_kernel(one, two, row, hi, lo, corner_hi, corner_lo, same, wide):
+def border_cells(block, rows):
+    edge = 11 * (1 - lax.axis_index("ha"))
+    row = lax.broadcasted_iota(jnp.int32, (rows, 1), 0)
+    column = jnp.where(row < 64, 15, 0) + (row >> 4 & 3) * 192 + (row & 15) * 16
+    column = jnp.where((row & 15) < 12, column, -1)
+    corner = jnp.where(row < 144, 15, 0) + (row & 15) * 192 + edge * 16
+    corner = jnp.where((row & 15) < 4, corner, -1)
+    source = jnp.where(row < 128, column, corner)
+    chosen = (lax.broadcasted_iota(jnp.int32, (rows, 768), 1) == source).astype(BF)
+    return jnp.dot(chosen, block.reshape(768, 256), preferred_element_type=F32)
+
+
+def pack_kernel(one, two, row, hi, lo, corner_hi, corner_lo, same):
     same[...] = one[...]
     edge = 11 * (1 - lax.axis_index("ha"))
     for n, block in enumerate((one, two)):
-        spread(wide, block)
+        cells = border_cells(block[...], 160).astype(BF)
+        hi[n] = cells[0:64].reshape(4, 16, 256)
+        lo[n] = cells[64:128].reshape(4, 16, 256)
+        corner_hi[n], corner_lo[n] = cells[128:144], cells[144:160]
         for f in range(4):
             row[n, f] = block[f, edge]
-            for j, out, corner in ((15, hi, corner_hi), (0, lo, corner_lo)):
-                for h in range(2):
-                    lanes = slice(h * 128, h * 128 + 128)
-                    out[n, f, :, lanes] = column(wide, h, f, j).astype(BF)
-                    cell = wide[h, pl.ds(f * 192 + edge * 16 + j, 1), :]
-                    corner[n, f, :, lanes] = jnp.broadcast_to(cell, (16, 128)).astype(BF)
 
 
 def pad_block(put, block, row, left, right, corner_left, corner_right):
@@ -195,8 +193,8 @@
     sort = lambda v: jnp.dot(v, order, preferred_element_type=F32).astype(BF)
     for copy in block_copies:
         copy.wait()
+    inp_out[...] = sort(blocks[0].reshape(768, 256)).reshape(4, 12, 16, 256)
     film_copy.wait()
-    inp_out[...] = sort(blocks[0].reshape(768, 256)).reshape(4, 12, 16, 256)
     line = film[pl.ds(start - whole, 1), :]
     scale, shift = 1.0 + line[:, 0:256], line[:, 256:512]
     shifted = blocks[1].reshape(768, 256).astype(F32) * scale + shift
@@ -208,8 +206,12 @@
 
 
 def pad_kernel(block, row, left, right, corner_left, corner_right, act, out):
-    sides = (row, left, right, corner_left, corner_right)
-    pad_block(keep_in(out), lambda f, r: block[f, r], *[lambda f, s=s: s[0, f] for s in sides])
+    pad_block(
+        keep_in(out),
+        lambda f, r: block[f, r],
+        *[lambda f, s=s: s[0, f] for s in (row, left, right)],
+        *[lambda f, s=s: s[0].astype(F32)[f : f + 1] for s in (corner_left, corner_right)],
+    )
     for f in range(4):
         for n in range(12):
             cells = act[f * 192 + n * 16 : f * 192 + n * 16 + 16, 128:256]
@@ -298,13 +300,14 @@
 
 def first_grad_kernel(
     hid, inp, row, left, right, corner_left, corner_right, after,
-    own, pair, wide, padded, side, flat,
+    own, pair, wide, padded, side,
 ):
     del after
     order = channel_order()
-    for n, ref in enumerate((row, left, right, corner_left, corner_right)):
-        cells = jnp.dot(ref[1].reshape(64, 256), order, preferred_element_type=F32)
-        side[n] = cells.reshape(4, 16, 256)
+    for at, ref in ((0, row), (4, left), (8, right), (12, corner_left), (13, corner_right)):
+        size = 4 if at < 12 else 1
+        cells = jnp.dot(ref[1].reshape(size * 16, 256), order, preferred_element_type=F32)
+        side[at : at + size] = cells.reshape(size, 16, 256)
 
     def put(f, r, which, cells):
         at = which * 128
@@ -312,15 +315,17 @@
         wide[f, r, :, at + 384 : at + 512] = cells[:, 128:256]
 
     pad_block(
-        keep_in(padded), lambda f, r: inp[f, r], *[lambda f, n=n: side[n, f] for n in range(5)]
+        keep_in(padded),
+        lambda f, r: inp[f, r],
+        *[lambda f, n=n: side[n + f] for n in (0, 4, 8)],
+        *[lambda f, n=n: side[n, f : f + 1] for n in (12, 13)],
     )
     build_shifted(put, padded)
-    spread(flat, hid)
-    for f in range(4):
-        for n, j in ((f, 15), (4 + f, 0)):
-            for h in range(2):
-                q, rows = border_at(0, n, h)
-                pair[q, 27, rows] = column(flat, h, f, j)
+    cells = border_cells(hid[...], 128)
+    for n in range(8):
+        for h in range(2):
+            q, rows = border_at(0, n, h)
+            pair[q, 27, rows] = cells[n * 16 : n * 16 + 16, h * 128 : h * 128 + 128]
     for a in range(3):
         rows = (a + 2) * 192
         left = hid[2 - a : 4].reshape(rows, 256)
@@ -435,8 +440,9 @@
         "pack_first",
         (block, inputs),
         "pp",
-        [near((2, 4, 16, 256), BF)] * 5 + [near((4, 12, 16, 256), BF)],
-        [pltpu.VMEM((2, 768, 128), F32)],
+        [near((2, 4, 16, 256), BF)] * 3
+        + [near((2, 16, 256), BF)] * 2
+        + [near((4, 12, 16, 256), BF)],
     )
     ways = ((1, 0), (0, 1), (0, -1), (1, 1), (1, -1))
     sides = [send(p, block_pairs(*way)) for p, way in zip(packed, ways)]
@@ -485,8 +491,7 @@
         [
             pltpu.VMEM((4, 14, 16, 768), BF),
             pltpu.VMEM((4, 16, 16, 256), BF),
-            pltpu.VMEM((5, 4, 16, 256), F32),
-            pltpu.VMEM((2, 768, 128), F32),
+            pltpu.VMEM((14, 16, 256), F32),
         ],
     )
     got_pair_one = send(pair_one, core_pairs())

time: 83.3 us -> 82.6 us (level)
  waiting for transfers between devices: 28.7 us -> 26.4 us
  starting transfers between devices: 32.8 us -> 34.1 us
    ppermute x19, waiting for transfers between devices: 23.1 us -> 21.1 us  [send(): return lax.ppermute(value, AX, pairs)]
    ppermute x19, starting transfers between devices: 24.3 us -> 25.6 us  [send(): return lax.ppermute(value, AX, pairs)]
  transfers between devices with their start and end apart: 20 -> 20, of which waited for: 9 -> 8; matrix products, arithmetic and copies ran while one was open for 0% -> 0% of each run, Pallas kernels for 17% -> 17%
where the time goes in v11:
time: 82.6 us; the launch traced here: 82 us
  starting transfers between devices  34.1 us (41%)
  waiting for transfers between devices  26.4 us (32%)
  Pallas kernels  20.2 us (24%)
  between operations  1.41 us (2%)
    ppermute x19, starting transfers between devices, send(): return lax.ppermute(value, AX, pairs)  25.6 us
    ppermute x19, waiting for transfers between devices, send(): return lax.ppermute(value, AX, pairs)  21.1 us
    pallas_call x12, Pallas kernels, call(): pl.pallas_call(kernel, out_shape=tuple((o for o, _ in outs)), in_specs=[s...  20.2 us
    all_to_all x1, starting transfers between devices, shards(): planes = lax.all_to_all(out, 'z', 0, 0, tiled=True)  8.47 us
    all_to_all x1, waiting for transfers between devices, shards(): planes = lax.all_to_all(out, 'z', 0, 0, tiled=True)  5.32 us
  transfers between devices with their start and end apart: 20, of which 8 were waited for; matrix products, arithmetic and copies ran while one was open for 0% of the time, Pallas kernels for 17%

profile of v11, /device:TPU:24, one launch (start us, length us, event | category | flops | bytes accessed | tf_op | source)
XLA Modules:
  0.0 82.0 jit_solution(6812817742908190636)
XLA Ops:
  0.6 1.4 %pack_first.1 = (bf16[2,4,16,256]{3,2,1,0:T(8,128)(2,1)S(1)}, bf16[2,4,16,256]{3,2,1,0:T(8,128)(2,1)S(1)}, bf16[2,4,16,256]{3,2,1,0:T(8,128)(2,1)S(1)}, bf16[2,1...) custom-call(bf16[4,12,16,256]{3,2,1,0:T(8,128)(2,1)} %bitcast.20, ...), custom_call_target="tpu_custom_call" | custom-call | tf_op jit(solution)/shard_map/pack_first/pallas_call | solution.py:50
  2.1 1.6 %collective-permute-start = (bf16[2,4,16,256]{3,2,1,0:T(8,128)(2,1)S(1)}, bf16[2,4,16,256]{3,2,1,0:T(8,128)(2,1)S(1)}, u32[]{:S(2)}, u32[]{:S(2)}) collective-permute-start(bf16[2,4,16,256]{3,2,1,0:T(8,128)(2,1)S(1)} %get-tuple-element.40), channel_id=1, source_target_pairs={{0,4},{1,5},{2,6},{3,7},{4,0},{5,1},{6,2},{7,3},{8,12},{9,13},{10,... | collective-permute-start | bytes 196616 | tf_op jit(solution)/shard_map/ppermute | solution.py:40
  3.6 3.2 %collective-permute-start.2 = (bf16[2,4,16,256]{3,2,1,0:T(8,128)(2,1)S(1)}, bf16[2,4,16,256]{3,2,1,0:T(8,128)(2,1)S(1)}, u32[]{:S(2)}, u32[]{:S(2)}) collective-permute-start(bf16[2,4,16,256]{3,2,1,0:T(8,128)(2,1)S(1)} %get-tuple-element.42), channel_id=1, source_target_pairs={{0,3},{1,0},{2,1},{3,2},{4,7},{5,4},{6,5},{7,6},{8,11},{9,8},{10,9... | collective-permute-start | bytes 196616 | tf_op jit(solution)/shard_map/ppermute | solution.py:40
  6.9 3.0 %collective-permute-start.4 = (bf16[2,16,256]{2,1,0:T(8,128)(2,1)S(1)}, bf16[2,16,256]{2,1,0:T(8,128)(2,1)S(1)}, u32[]{:S(2)}, u32[]{:S(2)}) collective-permute-start(bf16[2,16,256]{2,1,0:T(8,128)(2,1)S(1)} %get-tuple-element.44), channel_id=1, source_target_pairs={{0,7},{1,4},{2,5},{3,6},{4,3},{5,0},{6,1},{7,2},{8,15},{9,12},{10,... | collective-permute-start | bytes 49160 | tf_op jit(solution)/shard_map/ppermute | solution.py:40
  10.5 2.7 %film.1 = (bf16[768,256]{1,0:T(8,128)(2,1)S(1)}, bf16[4,12,16,256]{3,2,1,0:T(8,128)(2,1)S(1)}, f32[768,256]{1,0:T(8,128)S(1)}, bf16[27,256,256]{2,1,0:T(8,128)(2,1)S(1)}) custom-call(s32[1]{0:T(128)S(6)} %copy.10.step, bf16[4,12,16,256]{3,2,1,0:T(8,128)(2,1)} %bitcast.19, bf16[4,12,16,256]{3,2,1,0:T(8,128)(2,1)} %bitcast.23, f32[1000,512]{1,0:T(8,128)} %table.1, ...), custom_call_target="tpu_custom_call" | custom-call | tf_op jit(solution)/shard_map/film/pallas_call | solution.py:50
  13.7 2.3 %conv_two_back.1 = (bf16[4,14,16,768]{3,2,1,0:T(8,128)(2,1)S(1)}, bf16[4,12,16,256]{3,2,1,0:T(8,128)(2,1)S(1)}) custom-call(bf16[4,22,16,256]{3,2,1,0:T(8,128)(2,1)S(1)} %pad_cotangent.1.padded, f32[768,256]{1,0:T(8,128)S(1)} %get-tuple-element.46.slope, bf16[27,256,256]{2,1,0:T(8,128)(2,1)S(1)} %get-tuple-element.47.taps), custom_call_target="tpu_custom_call" | custom-call | tf_op jit(solution)/shard_map/conv_two_back/pallas_call | solution.py:50
  15.9 3.1 %grad_one.1 = (f32[4,27,64,128]{3,2,1,0:T(8,128)S(1)}, f32[4,28,64,128]{3,2,1,0:T(8,128)S(1)}) custom-call(bf16[4,12,16,256]{3,2,1,0:T(8,128)(2,1)S(1)} %get-tuple-element.48.hid, bf16[4,12,16,256]{3,2,1,0:T(8,128)(2,1)S(1)} %get-tuple-element.50.inp, bf16[2,4,16,256]{3,2,1,0:T(8,128)(2,1)S(1)} %collective-permute-done.row, ...), custom_call_target="tpu_custom_call" | custom-call | tf_op jit(solution)/shard_map/grad_one/pallas_call | solution.py:50
  19.5 2.7 %grad_two.1 = (f32[9,32,768]{2,1,0:T(8,128)S(1)}, bf16[9,32,768]{2,1,0:T(8,128)(2,1)S(1)}, bf16[9,32,768]{2,1,0:T(8,128)(2,1)S(1)}, bf16[9,32,768]{2,1,0:T(8,128)(2,1)S(1)}) custom-call(bf16[4,14,16,768]{3,2,1,0:T(8,128)(2,1)S(1)} %get-tuple-element.49.wide, bf16[768,256]{1,0:T(8,128)(2,1)S(1)} %get-tuple-element.45.act, ...), custom_call_target="tpu_custom_call" | custom-call | tf_op jit(solution)/shard_map/grad_two/pallas_call | solution.py:50
  22.2 1.6 %collective-permute-start.6 = (bf16[9,32,768]{2,1,0:T(8,128)(2,1)S(1)}, bf16[9,32,768]{2,1,0:T(8,128)(2,1)S(1)}, u32[]{:S(2)}, u32[]{:S(2)}) collective-permute-start(bf16[9,32,768]{2,1,0:T(8,128)(2,1)S(1)} %get-tuple-element.52), channel_id=1, source_target_pairs={{0,2},{1,3},{2,0},{3,1},{4,6},{5,7},{6,4},{7,5},{8,10},{9,11},{10,... | collective-permute-start | bytes 1327112 | tf_op jit(solution)/shard_map/ppermute | solution.py:40
  24.5 1.4 %collective-permute-start.7 = (bf16[9,32,768]{2,1,0:T(8,128)(2,1)S(1)}, bf16[9,32,768]{2,1,0:T(8,128)(2,1)S(1)}, u32[]{:S(2)}, u32[]{:S(2)}) collective-permute-start(bf16[9,32,768]{2,1,0:T(8,128)(2,1)S(1)} %get-tuple-element.53.after), channel_id=1, source_target_pairs={{0,4},{1,5},{2,6},{3,7},{4,2},{5,3},{6,0},{7,1},{8,12},{9,13},{10,... | collective-permute-start | bytes 1327112 | tf_op jit(solution)/shard_map/ppermute | solution.py:40
  26.2 1.3 %collective-permute-start.13 = (bf16[27,64,128]{2,1,0:T(8,128)(2,1)S(1)}, bf16[27,64,128]{2,1,0:T(8,128)(2,1)S(1)}, u32[]{:S(2)}, u32[]{:S(2)}) collective-permute-start(bf16[27,64,128]{2,1,0:T(8,128)(2,1)S(1)} %get-tuple-element.61), channel_id=1, source_target_pairs={{0,16},{1,17},{2,18},{3,19},{4,20},{5,21},{6,22},{7,23},{8,24},{9,... | collective-permute-start | bytes 1327112 | tf_op jit(solution)/shard_map/ppermute | solution.py:40
  27.5 2.2 %collective-permute-start.14 = (bf16[27,64,128]{2,1,0:T(8,128)(2,1)S(1)}, bf16[27,64,128]{2,1,0:T(8,128)(2,1)S(1)}, u32[]{:S(2)}, u32[]{:S(2)}) collective-permute-start(bf16[27,64,128]{2,1,0:T(8,128)(2,1)S(1)} %get-tuple-element.62), channel_id=1, source_target_pairs={{0,8},{1,9},{2,10},{3,11},{4,12},{5,13},{6,14},{7,15},{8,16},{9,17... | collective-permute-start | bytes 1327112 | tf_op jit(solution)/shard_map/ppermute | solution.py:40
  29.7 7.2 %collective-permute-done.6.got1 = bf16[9,32,768]{2,1,0:T(8,128)(2,1)S(1)} collective-permute-done((bf16[9,32,768]{2,1,0:T(8,128)(2,1)S(1)}, bf16[9,32,768]{2,1,0:T(8,128)(2,1)S(1)}, u32[]{:S(2)}, u32[]{:S(2)}) %collective-permute-start.6) | collective-permute-done | bytes 442400 | tf_op jit(solution)/shard_map/ppermute | solution.py:40
  37.6 7.3 %collective-permute-done.8.got3 = bf16[9,32,768]{2,1,0:T(8,128)(2,1)S(1)} collective-permute-done((bf16[9,32,768]{2,1,0:T(8,128)(2,1)S(1)}, bf16[9,32,768]{2,1,0:T(8,128)(2,1)S(1)}, u32[]{:S(2)}, u32[]{:S(2)}) %collective-permute-start.8) | collective-permute-done | bytes 442400 | tf_op jit(solution)/shard_map/ppermute | solution.py:40
  46.1 1.3 %collective-permute-start.9 = (bf16[10,64,128]{2,1,0:T(8,128)(2,1)S(1)}, bf16[10,64,128]{2,1,0:T(8,128)(2,1)S(1)}, u32[]{:S(2)}, u32[]{:S(2)}) collective-permute-start(bf16[10,64,128]{2,1,0:T(8,128)(2,1)S(1)} %get-tuple-element.57), channel_id=1, source_target_pairs={{0,16},{1,17},{2,18},{3,19},{4,20},{5,21},{6,22},{7,23},{8,24},{9,... | collective-permute-start | bytes 491528 | tf_op jit(solution)/shard_map/ppermute | solution.py:40
  47.4 3.2 %collective-permute-start.10 = (bf16[10,64,128]{2,1,0:T(8,128)(2,1)S(1)}, bf16[10,64,128]{2,1,0:T(8,128)(2,1)S(1)}, u32[]{:S(2)}, u32[]{:S(2)}) collective-permute-start(bf16[10,64,128]{2,1,0:T(8,128)(2,1)S(1)} %get-tuple-element.58.after), channel_id=1, source_target_pairs={{0,8},{1,9},{2,10},{3,11},{4,12},{5,13},{6,14},{7,15},{8,16},{9,17... | collective-permute-start | bytes 491528 | tf_op jit(solution)/shard_map/ppermute | solution.py:40
  51.1 1.3 %collective-permute-start.16 = (bf16[10,64,128]{2,1,0:T(8,128)(2,1)S(1)}, bf16[10,64,128]{2,1,0:T(8,128)(2,1)S(1)}, u32[]{:S(2)}, u32[]{:S(2)}) collective-permute-start(bf16[10,64,128]{2,1,0:T(8,128)(2,1)S(1)} %get-tuple-element.67), channel_id=1, source_target_pairs={{0,2},{1,3},{2,0},{3,1},{4,6},{5,7},{6,4},{7,5},{8,10},{9,11},{10,... | collective-permute-start | bytes 491528 | tf_op jit(solution)/shard_map/ppermute | solution.py:40
  52.5 1.4 %collective-permute-start.17 = (bf16[10,64,128]{2,1,0:T(8,128)(2,1)S(1)}, bf16[10,64,128]{2,1,0:T(8,128)(2,1)S(1)}, u32[]{:S(2)}, u32[]{:S(2)}) collective-permute-start(bf16[10,64,128]{2,1,0:T(8,128)(2,1)S(1)} %get-tuple-element.68), channel_id=1, source_target_pairs={{0,4},{1,5},{2,6},{3,7},{4,2},{5,3},{6,0},{7,1},{8,12},{9,13},{10,... | collective-permute-start | bytes 491528 | tf_op jit(solution)/shard_map/ppermute | solution.py:40
  54.8 1.7 %collective-permute-start.18 = (bf16[10,64,128]{2,1,0:T(8,128)(2,1)S(1)}, bf16[10,64,128]{2,1,0:T(8,128)(2,1)S(1)}, u32[]{:S(2)}, u32[]{:S(2)}) collective-permute-start(bf16[10,64,128]{2,1,0:T(8,128)(2,1)S(1)} %get-tuple-element.69), channel_id=1, source_target_pairs={{0,6},{1,7},{2,4},{3,5},{4,0},{5,1},{6,2},{7,3},{8,14},{9,15},{10,... | collective-permute-start | bytes 491528 | tf_op jit(solution)/shard_map/ppermute | solution.py:40
  57.3 2.5 %collective-permute-done.16.b2 = bf16[10,64,128]{2,1,0:T(8,128)(2,1)S(1)} collective-permute-done((bf16[10,64,128]{2,1,0:T(8,128)(2,1)S(1)}, bf16[10,64,128]{2,1,0:T(8,128)(2,1)S(1)}, u32[]{:S(2)}, u32[]{:S(2)}) %collective-permute-start.16) | collective-permute-done | bytes 163872 | tf_op jit(solution)/shard_map/ppermute | solution.py:40
  59.8 1.7 %collective-permute-done.17.b1 = bf16[10,64,128]{2,1,0:T(8,128)(2,1)S(1)} collective-permute-done((bf16[10,64,128]{2,1,0:T(8,128)(2,1)S(1)}, bf16[10,64,128]{2,1,0:T(8,128)(2,1)S(1)}, u32[]{:S(2)}, u32[]{:S(2)}) %collective-permute-start.17) | collective-permute-done | bytes 163872 | tf_op jit(solution)/shard_map/ppermute | solution.py:40
  62.3 8.5 %all-to-all-start = ((bf16[8,112,128]{2,1,0:T(8,128)(2,1)}), bf16[8,112,128]{2,1,0:T(8,128)(2,1)S(1)}, u32[]{:S(2)}, u32[]{:S(2)}) async-start(bf16[8,112,128]{2,1,0:T(8,128)(2,1)} %get-tuple-element.72), calls=%async_computation | async-start | bytes 458752 | tf_op jit(solution)/shard_map/all_to_all | solution.py:544
  70.8 5.1 %conv_one_back.1.after = bf16[4,12,16,256]{3,2,1,0:T(8,128)(2,1)} custom-call(bf16[4,12,16,256]{3,2,1,0:T(8,128)(2,1)S(1)} %get-tuple-element.48.hid, bf16[4,12,16,256]{3,2,1,0:T(8,128)(2,1)} %bitcast.21, bf16[10,16,256]{2,1,0:T(8,128)(2,1)S(1)} %get-tuple-element.70.border, bf16[2,4,16,256]{3,2,1,0:T(8,128)(2,1)S(1)} %get-tuple-element.65.cols, ...), custom_call_target="tpu_custom_call" | custom-call | tf_op jit(solution)/shard_map/conv_one_back/pallas_call | solution.py:50
  75.9 5.3 %all-to-all-done.got = bf16[8,112,128]{2,1,0:T(8,128)(2,1)S(1)} async-done(((bf16[8,112,128]{2,1,0:T(8,128)(2,1)}), bf16[8,112,128]{2,1,0:T(8,128)(2,1)S(1)}, u32[]{:S(2)}, u32[]{:S(2)}) %all-to-all-start) | async-done | bytes 229408 | tf_op jit(solution)/shard_map/all_to_all | solution.py:544
  (28 shorter events, 7.7 us)
Async XLA Ops:
  2.1 11.1 %collective-permute-start = (bf16[2,4,16,256]{3,2,1,0:T(8,128)(2,1)S(1)}, bf16[2,4,16,256]{3,2,1,0:T(8,128)(2,1)S(1)}, u32[]{:S(2)}, u32[]{:S(2)}) collective-permute-start(bf16[2,4,16,256]{3,2,1,0:T(8,128)(2,1)S(1)} %get-tuple-element.40), channel_id=1, source_target_pairs={{0,4},{1,5},{2,6},{3,7},{4,0},{5,1},{6,2},{7,3},{8,12},{9,13},{10,... | collective-permute-start | bytes 196616 | tf_op jit(solution)/shard_map/ppermute | solution.py:40
  3.6 9.6 %collective-permute-start.1 = (bf16[2,4,16,256]{3,2,1,0:T(8,128)(2,1)S(1)}, bf16[2,4,16,256]{3,2,1,0:T(8,128)(2,1)S(1)}, u32[]{:S(2)}, u32[]{:S(2)}) collective-permute-start(bf16[2,4,16,256]{3,2,1,0:T(8,128)(2,1)S(1)} %get-tuple-element.41), channel_id=1, source_target_pairs={{0,1},{1,2},{2,3},{3,0},{4,5},{5,6},{6,7},{7,4},{8,9},{9,10},{10,1... | collective-permute-start | bytes 196616 | tf_op jit(solution)/shard_map/ppermute | solution.py:40
  3.6 9.6 %collective-permute-start.2 = (bf16[2,4,16,256]{3,2,1,0:T(8,128)(2,1)S(1)}, bf16[2,4,16,256]{3,2,1,0:T(8,128)(2,1)S(1)}, u32[]{:S(2)}, u32[]{:S(2)}) collective-permute-start(bf16[2,4,16,256]{3,2,1,0:T(8,128)(2,1)S(1)} %get-tuple-element.42), channel_id=1, source_target_pairs={{0,3},{1,0},{2,1},{3,2},{4,7},{5,4},{6,5},{7,6},{8,11},{9,8},{10,9... | collective-permute-start | bytes 196616 | tf_op jit(solution)/shard_map/ppermute | solution.py:40
  6.9 6.3 %collective-permute-start.3 = (bf16[2,16,256]{2,1,0:T(8,128)(2,1)S(1)}, bf16[2,16,256]{2,1,0:T(8,128)(2,1)S(1)}, u32[]{:S(2)}, u32[]{:S(2)}) collective-permute-start(bf16[2,16,256]{2,1,0:T(8,128)(2,1)S(1)} %get-tuple-element.43), channel_id=1, source_target_pairs={{0,5},{1,6},{2,7},{3,4},{4,1},{5,2},{6,3},{7,0},{8,13},{9,14},{10,... | collective-permute-start | bytes 49160 | tf_op jit(solution)/shard_map/ppermute | solution.py:40
  6.9 6.3 %collective-permute-start.4 = (bf16[2,16,256]{2,1,0:T(8,128)(2,1)S(1)}, bf16[2,16,256]{2,1,0:T(8,128)(2,1)S(1)}, u32[]{:S(2)}, u32[]{:S(2)}) collective-permute-start(bf16[2,16,256]{2,1,0:T(8,128)(2,1)S(1)} %get-tuple-element.44), channel_id=1, source_target_pairs={{0,7},{1,4},{2,5},{3,6},{4,3},{5,0},{6,1},{7,2},{8,15},{9,12},{10,... | collective-permute-start | bytes 49160 | tf_op jit(solution)/shard_map/ppermute | solution.py:40
  13.3 2.6 %collective-permute-start.5 = (bf16[4,22,16,256]{3,2,1,0:T(8,128)(2,1)S(1)}, bf16[4,22,16,256]{3,2,1,0:T(8,128)(2,1)S(1)}, u32[]{:S(2)}, u32[]{:S(2)}) collective-permute-start(bf16[4,22,16,256]{3,2,1,0:T(8,128)(2,1)S(1)} %pad_cotangent.1.padded), channel_id=1, source_target_pairs={{0,1},{1,0},{2,3},{3,2},{4,5},{5,4},{6,7},{7,6},{8,9},{9,8},{10,11... | collective-permute-start | bytes 2162696 | tf_op jit(solution)/shard_map/ppermute | solution.py:40
  19.0 6.8 %collective-permute-start.12 = (f32[4,28,64,128]{3,2,1,0:T(8,128)S(1)}, f32[4,28,64,128]{3,2,1,0:T(8,128)S(1)}, u32[]{:S(2)}, u32[]{:S(2)}) collective-permute-start(f32[4,28,64,128]{3,2,1,0:T(8,128)S(1)} %get-tuple-element.51.after), channel_id=1, source_target_pairs={{0,1},{1,0},{2,3},{3,2},{4,5},{5,4},{6,7},{7,6},{8,9},{9,8},{10,11... | collective-permute-start | bytes 11010056 | tf_op jit(solution)/shard_map/ppermute | solution.py:40
  22.2 14.6 %collective-permute-start.6 = (bf16[9,32,768]{2,1,0:T(8,128)(2,1)S(1)}, bf16[9,32,768]{2,1,0:T(8,128)(2,1)S(1)}, u32[]{:S(2)}, u32[]{:S(2)}) collective-permute-start(bf16[9,32,768]{2,1,0:T(8,128)(2,1)S(1)} %get-tuple-element.52), channel_id=1, source_target_pairs={{0,2},{1,3},{2,0},{3,1},{4,6},{5,7},{6,4},{7,5},{8,10},{9,11},{10,... | collective-permute-start | bytes 1327112 | tf_op jit(solution)/shard_map/ppermute | solution.py:40
  23.8 21.0 %collective-permute-start.8 = (bf16[9,32,768]{2,1,0:T(8,128)(2,1)S(1)}, bf16[9,32,768]{2,1,0:T(8,128)(2,1)S(1)}, u32[]{:S(2)}, u32[]{:S(2)}) collective-permute-start(bf16[9,32,768]{2,1,0:T(8,128)(2,1)S(1)} %get-tuple-element.54), channel_id=1, source_target_pairs={{0,6},{1,7},{2,4},{3,5},{4,0},{5,1},{6,2},{7,3},{8,14},{9,15},{10,... | collective-permute-start | bytes 1327112 | tf_op jit(solution)/shard_map/ppermute | solution.py:40
  24.5 21.1 %collective-permute-start.7 = (bf16[9,32,768]{2,1,0:T(8,128)(2,1)S(1)}, bf16[9,32,768]{2,1,0:T(8,128)(2,1)S(1)}, u32[]{:S(2)}, u32[]{:S(2)}) collective-permute-start(bf16[9,32,768]{2,1,0:T(8,128)(2,1)S(1)} %get-tuple-element.53.after), channel_id=1, source_target_pairs={{0,4},{1,5},{2,6},{3,7},{4,2},{5,3},{6,0},{7,1},{8,12},{9,13},{10,... | collective-permute-start | bytes 1327112 | tf_op jit(solution)/shard_map/ppermute | solution.py:40
  26.2 21.2 %collective-permute-start.13 = (bf16[27,64,128]{2,1,0:T(8,128)(2,1)S(1)}, bf16[27,64,128]{2,1,0:T(8,128)(2,1)S(1)}, u32[]{:S(2)}, u32[]{:S(2)}) collective-permute-start(bf16[27,64,128]{2,1,0:T(8,128)(2,1)S(1)} %get-tuple-element.61), channel_id=1, source_target_pairs={{0,16},{1,17},{2,18},{3,19},{4,20},{5,21},{6,22},{7,23},{8,24},{9,... | collective-permute-start | bytes 1327112 | tf_op jit(solution)/shard_map/ppermute | solution.py:40
  27.5 23.1 %collective-permute-start.14 = (bf16[27,64,128]{2,1,0:T(8,128)(2,1)S(1)}, bf16[27,64,128]{2,1,0:T(8,128)(2,1)S(1)}, u32[]{:S(2)}, u32[]{:S(2)}) collective-permute-start(bf16[27,64,128]{2,1,0:T(8,128)(2,1)S(1)} %get-tuple-element.62), channel_id=1, source_target_pairs={{0,8},{1,9},{2,10},{3,11},{4,12},{5,13},{6,14},{7,15},{8,16},{9,17... | collective-permute-start | bytes 1327112 | tf_op jit(solution)/shard_map/ppermute | solution.py:40
  36.8 13.8 %collective-permute-start.15 = (bf16[27,64,128]{2,1,0:T(8,128)(2,1)S(1)}, bf16[27,64,128]{2,1,0:T(8,128)(2,1)S(1)}, u32[]{:S(2)}, u32[]{:S(2)}) collective-permute-start(bf16[27,64,128]{2,1,0:T(8,128)(2,1)S(1)} %get-tuple-element.63), channel_id=1, source_target_pairs={{0,24},{1,25},{2,26},{3,27},{4,28},{5,29},{6,30},{7,31},{8,0},{9,1... | collective-permute-start | bytes 1327112 | tf_op jit(solution)/shard_map/ppermute | solution.py:40
  46.1 8.7 %collective-permute-start.9 = (bf16[10,64,128]{2,1,0:T(8,128)(2,1)S(1)}, bf16[10,64,128]{2,1,0:T(8,128)(2,1)S(1)}, u32[]{:S(2)}, u32[]{:S(2)}) collective-permute-start(bf16[10,64,128]{2,1,0:T(8,128)(2,1)S(1)} %get-tuple-element.57), channel_id=1, source_target_pairs={{0,16},{1,17},{2,18},{3,19},{4,20},{5,21},{6,22},{7,23},{8,24},{9,... | collective-permute-start | bytes 491528 | tf_op jit(solution)/shard_map/ppermute | solution.py:40
  47.4 9.9 %collective-permute-start.11 = (bf16[10,64,128]{2,1,0:T(8,128)(2,1)S(1)}, bf16[10,64,128]{2,1,0:T(8,128)(2,1)S(1)}, u32[]{:S(2)}, u32[]{:S(2)}) collective-permute-start(bf16[10,64,128]{2,1,0:T(8,128)(2,1)S(1)} %get-tuple-element.59), channel_id=1, source_target_pairs={{0,24},{1,25},{2,26},{3,27},{4,28},{5,29},{6,30},{7,31},{8,0},{9,1... | collective-permute-start | bytes 491528 | tf_op jit(solution)/shard_map/ppermute | solution.py:40
  47.4 9.9 %collective-permute-start.10 = (bf16[10,64,128]{2,1,0:T(8,128)(2,1)S(1)}, bf16[10,64,128]{2,1,0:T(8,128)(2,1)S(1)}, u32[]{:S(2)}, u32[]{:S(2)}) collective-permute-start(bf16[10,64,128]{2,1,0:T(8,128)(2,1)S(1)} %get-tuple-element.58.after), channel_id=1, source_target_pairs={{0,8},{1,9},{2,10},{3,11},{4,12},{5,13},{6,14},{7,15},{8,16},{9,17... | collective-permute-start | bytes 491528 | tf_op jit(solution)/shard_map/ppermute | solution.py:40
  51.1 8.6 %collective-permute-start.16 = (bf16[10,64,128]{2,1,0:T(8,128)(2,1)S(1)}, bf16[10,64,128]{2,1,0:T(8,128)(2,1)S(1)}, u32[]{:S(2)}, u32[]{:S(2)}) collective-permute-start(bf16[10,64,128]{2,1,0:T(8,128)(2,1)S(1)} %get-tuple-element.67), channel_id=1, source_target_pairs={{0,2},{1,3},{2,0},{3,1},{4,6},{5,7},{6,4},{7,5},{8,10},{9,11},{10,... | collective-permute-start | bytes 491528 | tf_op jit(solution)/shard_map/ppermute | solution.py:40
  52.5 9.0 %collective-permute-start.17 = (bf16[10,64,128]{2,1,0:T(8,128)(2,1)S(1)}, bf16[10,64,128]{2,1,0:T(8,128)(2,1)S(1)}, u32[]{:S(2)}, u32[]{:S(2)}) collective-permute-start(bf16[10,64,128]{2,1,0:T(8,128)(2,1)S(1)} %get-tuple-element.68), channel_id=1, source_target_pairs={{0,4},{1,5},{2,6},{3,7},{4,2},{5,3},{6,0},{7,1},{8,12},{9,13},{10,... | collective-permute-start | bytes 491528 | tf_op jit(solution)/shard_map/ppermute | solution.py:40
  54.8 6.8 %collective-permute-start.18 = (bf16[10,64,128]{2,1,0:T(8,128)(2,1)S(1)}, bf16[10,64,128]{2,1,0:T(8,128)(2,1)S(1)}, u32[]{:S(2)}, u32[]{:S(2)}) collective-permute-start(bf16[10,64,128]{2,1,0:T(8,128)(2,1)S(1)} %get-tuple-element.69), channel_id=1, source_target_pairs={{0,6},{1,7},{2,4},{3,5},{4,0},{5,1},{6,2},{7,3},{8,14},{9,15},{10,... | collective-permute-start | bytes 491528 | tf_op jit(solution)/shard_map/ppermute | solution.py:40
  62.3 18.9 %all-to-all-start = ((bf16[8,112,128]{2,1,0:T(8,128)(2,1)}), bf16[8,112,128]{2,1,0:T(8,128)(2,1)S(1)}, u32[]{:S(2)}, u32[]{:S(2)}) async-start(bf16[8,112,128]{2,1,0:T(8,128)(2,1)} %get-tuple-element.72), calls=%async_computation | async-start | bytes 458752 | tf_op jit(solution)/shard_map/all_to_all | solution.py:544

commit v12 on v11

--- a/solution.py
+++ b/solution.py
@@ -24,14 +24,14 @@
 
 
 def block_pairs(dh, dw):
-    return [(i, i // 8 * 8 + (i // 4 % 2 ^ dh) * 4 + (i + dw) % 4) for i in range(256)]
+    return [(i, i ^ (dh * 4 + dw)) for i in range(256)]
 
 
 def ring_pairs(dx=0, dy=0):
     pairs = []
     for i in range(256):
         core, xh, ha, y, z = i % 2, i // 2 % 2, i // 4 % 2, i // 8 % 4, i // 32
-        x, y = (xh * 2 + ha + dx) % 4, (y + dy) % 4
+        x, y = (xh * 2 + ha) ^ dx, y ^ dy
         pairs.append((i, ((z * 4 + y) * 2 + x % 2) * 4 + x // 2 * 2 + core))
     return pairs
 
@@ -70,6 +70,10 @@
     return lax.axis_index("xh") * 2 + lax.axis_index("ha")
 
 
+def by_core(when_one, when_zero):
+    return jnp.where(lax.axis_index("core") == 1, when_one, when_zero)
+
+
 def border_cells(block, rows):
     edge = 11 * (1 - lax.axis_index("ha"))
     row = lax.broadcasted_iota(jnp.int32, (rows, 1), 0)
@@ -82,14 +86,15 @@
     return jnp.dot(chosen, block.reshape(768, 256), preferred_element_type=F32)
 
 
-def pack_kernel(one, two, row, hi, lo, corner_hi, corner_lo, same):
+def pack_kernel(one, two, row, face, outer, corner_face, corner_outer, same):
     same[...] = one[...]
     edge = 11 * (1 - lax.axis_index("ha"))
     for n, block in enumerate((one, two)):
-        cells = border_cells(block[...], 160).astype(BF)
-        hi[n] = cells[0:64].reshape(4, 16, 256)
-        lo[n] = cells[64:128].reshape(4, 16, 256)
-        corner_hi[n], corner_lo[n] = cells[128:144], cells[144:160]
+        cells = border_cells(block[...], 160)
+        hi, lo = cells[0:64].reshape(4, 16, 256), cells[64:128].reshape(4, 16, 256)
+        face[n], outer[n] = by_core(lo, hi).astype(BF), by_core(hi, lo).astype(BF)
+        hi, lo = cells[128:144], cells[144:160]
+        corner_face[n], corner_outer[n] = by_core(lo, hi).astype(BF), by_core(hi, lo).astype(BF)
         for f in range(4):
             row[n, f] = block[f, edge]
 
@@ -167,7 +172,7 @@
 
 def channel_order():
     lane = lax.broadcasted_iota(jnp.int32, (256, 256), 1)
-    goal, kept = (x_place() + (lane >> 5)) & 3, lax.axis_index("core") ^ (lane >> 7)
+    goal, kept = x_place() ^ ((lane >> 5) & 3), lax.axis_index("core") ^ (lane >> 7)
     source = ((goal & 1) << 7) + ((goal >> 1) << 6) + (kept << 5) + (lane & 31)
     return (lax.broadcasted_iota(jnp.int32, (256, 256), 0) == source).astype(BF)
 
@@ -205,12 +210,17 @@
         copy.wait()
 
 
-def pad_kernel(block, row, left, right, corner_left, corner_right, act, out):
+def pad_kernel(block, row, face, outer, corner_face, corner_outer, act, out):
+    near_cells, far_cells = face[0].astype(F32), outer[0].astype(F32)
+    near_ends, far_ends = corner_face[0].astype(F32), corner_outer[0].astype(F32)
     pad_block(
         keep_in(out),
         lambda f, r: block[f, r],
-        *[lambda f, s=s: s[0, f] for s in (row, left, right)],
-        *[lambda f, s=s: s[0].astype(F32)[f : f + 1] for s in (corner_left, corner_right)],
+        lambda f: row[0, f],
+        lambda f: by_core(near_cells[f], far_cells[f]),
+        lambda f: by_core(far_cells[f], near_cells[f]),
+        lambda f: by_core(near_ends[f : f + 1], far_ends[f : f + 1]),
+        lambda f: by_core(far_ends[f : f + 1], near_ends[f : f + 1]),
     )
     for f in range(4):
         for n in range(12):
@@ -232,20 +242,15 @@
     copies.append(pltpu.make_async_copy(block, near_block, sem.at[3]))
     for copy in copies:
         copy.start()
-    is_one = lax.axis_index("core") == 1
-
-    def pick(when_one, when_zero):
-        return jnp.where(is_one, when_one.astype(F32), when_zero.astype(F32))
-
-    faces, outers = border[8].astype(F32), border[9].astype(F32)[4:8]
+    faces, outers = border[8].astype(F32), border[9].astype(F32)
     pad_block(
         keep_in(padded),
         lambda f, r: hid[f, r],
         lambda f: border[f],
-        lambda f: pick(cols[0, f], border[4 + f]),
-        lambda f: pick(border[4 + f], cols[1, f]),
-        lambda f: pick(faces[f : f + 1], outers[f : f + 1]),
-        lambda f: pick(outers[f : f + 1], faces[f : f + 1]),
+        lambda f: by_core(cols[0, f].astype(F32), border[4 + f].astype(F32)),
+        lambda f: by_core(border[4 + f].astype(F32), cols[1, f].astype(F32)),
+        lambda f: by_core(faces[f : f + 1], outers[f : f + 1]),
+        lambda f: by_core(outers[f : f + 1], faces[f : f + 1]),
     )
     build_shifted(put_back(wide), padded)
     for copy in copies:
@@ -288,23 +293,27 @@
         parts = [tap(t) if t < 27 else jnp.zeros((32, 256), F32) for t in range(4 * g, 4 * g + 4)]
         held[...] = jnp.concatenate(parts, axis=0).T.reshape(8, 4, 8, 128)
         for d, out in enumerate((keep, one, two, three)):
-            out[g] = held[:, (y + d) & 3].reshape(64, 128).astype(out.dtype)
+            out[g * 64 : g * 64 + 64] = held[:, y ^ d].reshape(64, 128).astype(out.dtype)
     for out in (one, two, three):
-        out[7:10] = jnp.zeros((3, 64, 128), BF)
-
-
-def border_at(base, n, h):
+        out[448:592] = jnp.zeros((144, 128), BF)
+
+
+def border_at(n, h):
     slot = n * 2 + h
-    return base + slot // 4, slice(slot % 4 * 16, slot % 4 * 16 + 16)
+    return slot // 4, slice(slot % 4 * 16, slot % 4 * 16 + 16)
+
+
+def border_rows(n, h):
+    return slice(448 + (n * 2 + h) * 16, 464 + (n * 2 + h) * 16)
 
 
 def first_grad_kernel(
-    hid, inp, row, left, right, corner_left, corner_right, after,
+    hid, inp, row, face, outer, corner_face, corner_outer, after,
     own, pair, wide, padded, side,
 ):
     del after
     order = channel_order()
-    for at, ref in ((0, row), (4, left), (8, right), (12, corner_left), (13, corner_right)):
+    for at, ref in ((0, row), (4, face), (8, outer), (12, corner_face), (13, corner_outer)):
         size = 4 if at < 12 else 1
         cells = jnp.dot(ref[1].reshape(size * 16, 256), order, preferred_element_type=F32)
         side[at : at + size] = cells.reshape(size, 16, 256)
@@ -317,14 +326,17 @@
     pad_block(
         keep_in(padded),
         lambda f, r: inp[f, r],
-        *[lambda f, n=n: side[n + f] for n in (0, 4, 8)],
-        *[lambda f, n=n: side[n, f : f + 1] for n in (12, 13)],
+        lambda f: side[f],
+        lambda f: by_core(side[4 + f], side[8 + f]),
+        lambda f: by_core(side[8 + f], side[4 + f]),
+        lambda f: by_core(side[12, f : f + 1], side[13, f : f + 1]),
+        lambda f: by_core(side[13, f : f + 1], side[12, f : f + 1]),
     )
     build_shifted(put, padded)
     cells = border_cells(hid[...], 128)
     for n in range(8):
         for h in range(2):
-            q, rows = border_at(0, n, h)
+            q, rows = border_at(n, h)
             pair[q, 27, rows] = cells[n * 16 : n * 16 + 16, h * 128 : h * 128 + 128]
     for a in range(3):
         rows = (a + 2) * 192
@@ -345,11 +357,11 @@
     del after
     y = lax.axis_index("y")
     for d, out in enumerate((keep, one, two, three)):
-        q = (y + d) & 3
+        q = y ^ d
         out[...] = (own[q] + pair[q, 0:27]).astype(out.dtype)
     for n in range(8):
         for h in range(2):
-            q, rows = border_at(0, n, h)
+            q, rows = border_at(n, h)
             cols[n // 4, n % 4, :, h * 128 : h * 128 + 128] = pair[q, 27, rows].astype(BF)
 
 
@@ -366,43 +378,42 @@
         taps = [tap(t) if t < 27 else jnp.zeros((64, 128), F32) for t in range(4 * g, 4 * g + 4)]
         for d, out in enumerate((keep, one, two, three)):
             piece = jnp.concatenate([v[:, d * 32 : d * 32 + 32] for v in taps], axis=1)
-            out[g] = piece.astype(out.dtype)
-
-    is_one = lax.axis_index("core") == 1
+            out[g * 64 : g * 64 + 64] = piece.astype(out.dtype)
+
     edge = 11 * (1 - lax.axis_index("ha"))
-    along, across, faces, outers = [], [], [], []
+    faces, outers = [], []
     for f in range(4):
         hi, lo = cols[0, f].astype(F32), cols[1, f].astype(F32)
-        face, outer = jnp.where(is_one, hi, lo), jnp.where(is_one, lo, hi)
-        along.append(hid[f, edge])
-        across.append(outer.astype(BF))
+        face, outer = by_core(hi, lo), by_core(lo, hi)
+        row, across = hid[f, edge], outer.astype(BF)
+        for h in range(2):
+            lanes = slice(h * 128, h * 128 + 128)
+            one[border_rows(f, h)] = row[:, lanes]
+            two[border_rows(f, h)] = across[:, lanes]
         faces.append(jnp.where(edge == 0, face[0:1], face[11:12]))
         outers.append(jnp.where(edge == 0, outer[0:1], outer[11:12]))
-    corners = jnp.concatenate(faces + outers + [jnp.zeros((8, 256), F32)], axis=0).astype(BF)
-    rest = [jnp.zeros((16, 256), BF)] * 2
-    along, across = along + [corners, rest[0]], across + rest
-    for out, tiles in ((one, along), (two, across), (three, along)):
-        for n, cells in enumerate(tiles):
-            for h in range(2):
-                out[border_at(7, n, h)] = cells[:, h * 128 : h * 128 + 128]
+    rest = [jnp.zeros((8, 128), F32)]
+    for out, rows, cells in ((one, slice(576, 592), faces), (three, slice(448, 464), outers)):
+        halves = [c[:, 0:128] for c in cells] + [c[:, 128:256] for c in cells]
+        out[rows] = jnp.concatenate(halves + rest, axis=0).astype(BF)
 
 
 def last_kernel(own_two, a2, a1, a3, own_one, b2, b1, b3, out, keep, border, held):
-    low = lax.axis_index("ha") == 0
-    for h in range(2):
-        lanes = slice(h * 128, h * 128 + 128)
-        for n in range(5):
-            first, last = b1[border_at(7, n, h)].astype(F32), b3[border_at(7, n, h)].astype(F32)
-            across, along = jnp.where(low, last, first), jnp.where(low, first, last)
-            if n < 4:
-                border[n, :, lanes] = across.astype(BF)
-                border[4 + n, :, lanes] = b2[border_at(7, n, h)]
-            else:
-                border[8, :, lanes], border[9, :, lanes] = across.astype(BF), along.astype(BF)
+    for f in range(4):
+        for h in range(2):
+            lanes = slice(h * 128, h * 128 + 128)
+            border[f, :, lanes] = b1[border_rows(f, h)]
+            border[4 + f, :, lanes] = b2[border_rows(f, h)]
+    for n, corners in ((8, b1[576:592]), (9, b3[448:464])):
+        corners = corners.astype(F32)
+        for h in range(2):
+            cells = corners[h * 4 : h * 4 + 4]
+            cells = jnp.concatenate([cells, jnp.zeros((12, 128), F32)], axis=0)
+            border[n, :, h * 128 : h * 128 + 128] = cells.astype(BF)
     for n, (own, got) in enumerate(((own_two, (a1, a2, a3)), (own_one, (b1, b2, b3)))):
         total = own[...]
         for ref in got:
-            total = total + ref[0:7].astype(F32)
+            total = total + ref[0:448].astype(F32)
         held[n] = total.reshape(7, 8, 8, 128)
 
     def plane(z):
@@ -430,8 +441,6 @@
     taps_one = conv_one.transpose(1, 2, 3, 0, 4).reshape(27, 256, 256)
     taps_two = conv_two.transpose(1, 2, 3, 0, 4).reshape(27, 256, 256)
     wide = near((4, 14, 16, 768), BF)
-    quads = [near((7, 64, 128), F32)] + [near((10, 64, 128), BF)] * 3
-
     def ring(parts, axis):
         return [send(parts[d - 1], ring_pairs(**{axis: d})) for d in (2, 1, 3)]
 
@@ -444,7 +453,7 @@
         + [near((2, 16, 256), BF)] * 2
         + [near((4, 12, 16, 256), BF)],
     )
-    ways = ((1, 0), (0, 1), (0, -1), (1, 1), (1, -1))
+    ways = ((1, 0), (0, 1), (0, 3), (1, 1), (1, 3))
     sides = [send(p, block_pairs(*way)) for p, way in zip(packed, ways)]
     act, inp, slope, held_two = call(
         film_kernel,
@@ -520,7 +529,7 @@
         "grad_two_x",
         (*got_two, own_two),
         "vvvv",
-        quads,
+        [near((448, 128), F32)] + [near((592, 128), BF)] * 3,
         [pltpu.VMEM((8, 4, 8, 128), F32)],
     )
     got_two = ring(parts, "dy")
@@ -529,7 +538,7 @@
         "grad_one_y",
         (*got_one, own_one, grad_hidden, cols, parts[0]),
         "v" * 7,
-        quads,
+        [near((448, 128), F32), near((592, 128), BF), near((576, 128), BF), near((464, 128), BF)],
     )
     got_one = ring(parts_one, "dx")
 

time: 82.6 us -> 81.8 us (level)
  transfers between devices with their start and end apart: 20 -> 20, of which waited for: 8 -> 4; matrix products, arithmetic and copies ran while one was open for 0% -> 0% of each run, Pallas kernels for 17% -> 17%
where the time goes in v12:
time: 81.8 us; the launch traced here: 81.5 us
  starting transfers between devices  33.3 us (41%)
  waiting for transfers between devices  26.6 us (33%)
  Pallas kernels  20.2 us (25%)
  between operations  1.41 us (2%)
    ppermute x19, starting transfers between devices, send(): return lax.ppermute(value, AX, pairs)  24.9 us
    ppermute x19, waiting for transfers between devices, send(): return lax.ppermute(value, AX, pairs)  21.6 us
    pallas_call x12, Pallas kernels, call(): pl.pallas_call(kernel, out_shape=tuple((o for o, _ in outs)), in_specs=[s...  20.2 us
    all_to_all x1, starting transfers between devices, shards(): planes = lax.all_to_all(out, 'z', 0, 0, tiled=True)  8.47 us
    all_to_all x1, waiting for transfers between devices, shards(): planes = lax.all_to_all(out, 'z', 0, 0, tiled=True)  5.02 us
  transfers between devices with their start and end apart: 20, of which 4 were waited for; matrix products, arithmetic and copies ran while one was open for 0% of the time, Pallas kernels for 17%

profile of v12, /device:TPU:24, one launch (start us, length us, event | category | flops | bytes accessed | tf_op | source)
XLA Modules:
  0.0 81.5 jit_solution(7771773924552250277)
XLA Ops:
  0.6 1.4 %pack_first.1 = (bf16[2,4,16,256]{3,2,1,0:T(8,128)(2,1)S(1)}, bf16[2,4,16,256]{3,2,1,0:T(8,128)(2,1)S(1)}, bf16[2,4,16,256]{3,2,1,0:T(8,128)(2,1)S(1)}, bf16[2,1...) custom-call(bf16[4,12,16,256]{3,2,1,0:T(8,128)(2,1)} %bitcast.20, ...), custom_call_target="tpu_custom_call" | custom-call | tf_op jit(solution)/shard_map/pack_first/pallas_call | solution.py:50
  2.1 1.6 %collective-permute-start = (bf16[2,4,16,256]{3,2,1,0:T(8,128)(2,1)S(1)}, bf16[2,4,16,256]{3,2,1,0:T(8,128)(2,1)S(1)}, u32[]{:S(2)}, u32[]{:S(2)}) collective-permute-start(bf16[2,4,16,256]{3,2,1,0:T(8,128)(2,1)S(1)} %get-tuple-element.40), channel_id=1, source_target_pairs={{0,4},{1,5},{2,6},{3,7},{4,0},{5,1},{6,2},{7,3},{8,12},{9,13},{10,... | collective-permute-start | bytes 196616 | tf_op jit(solution)/shard_map/ppermute | solution.py:40
  3.6 2.8 %collective-permute-start.2 = (bf16[2,4,16,256]{3,2,1,0:T(8,128)(2,1)S(1)}, bf16[2,4,16,256]{3,2,1,0:T(8,128)(2,1)S(1)}, u32[]{:S(2)}, u32[]{:S(2)}) collective-permute-start(bf16[2,4,16,256]{3,2,1,0:T(8,128)(2,1)S(1)} %get-tuple-element.42), channel_id=1, source_target_pairs={{0,3},{1,2},{2,1},{3,0},{4,7},{5,6},{6,5},{7,4},{8,11},{9,10},{10,... | collective-permute-start | bytes 196616 | tf_op jit(solution)/shard_map/ppermute | solution.py:40
  6.5 1.1 %collective-permute-start.4 = (bf16[2,16,256]{2,1,0:T(8,128)(2,1)S(1)}, bf16[2,16,256]{2,1,0:T(8,128)(2,1)S(1)}, u32[]{:S(2)}, u32[]{:S(2)}) collective-permute-start(bf16[2,16,256]{2,1,0:T(8,128)(2,1)S(1)} %get-tuple-element.44), channel_id=1, source_target_pairs={{0,7},{1,6},{2,5},{3,4},{4,3},{5,2},{6,1},{7,0},{8,15},{9,14},{10,... | collective-permute-start | bytes 49160 | tf_op jit(solution)/shard_map/ppermute | solution.py:40
  8.2 2.7 %film.1 = (bf16[768,256]{1,0:T(8,128)(2,1)S(1)}, bf16[4,12,16,256]{3,2,1,0:T(8,128)(2,1)S(1)}, f32[768,256]{1,0:T(8,128)S(1)}, bf16[27,256,256]{2,1,0:T(8,128)(2,1)S(1)}) custom-call(s32[1]{0:T(128)S(6)} %copy.10.step, bf16[4,12,16,256]{3,2,1,0:T(8,128)(2,1)} %bitcast.19, bf16[4,12,16,256]{3,2,1,0:T(8,128)(2,1)} %bitcast.23, f32[1000,512]{1,0:T(8,128)} %table.1, ...), custom_call_target="tpu_custom_call" | custom-call | tf_op jit(solution)/shard_map/film/pallas_call | solution.py:50
  11.4 2.3 %conv_two_back.1 = (bf16[4,14,16,768]{3,2,1,0:T(8,128)(2,1)S(1)}, bf16[4,12,16,256]{3,2,1,0:T(8,128)(2,1)S(1)}) custom-call(bf16[4,22,16,256]{3,2,1,0:T(8,128)(2,1)S(1)} %pad_cotangent.1.padded, f32[768,256]{1,0:T(8,128)S(1)} %get-tuple-element.46.slope, bf16[27,256,256]{2,1,0:T(8,128)(2,1)S(1)} %get-tuple-element.47.taps), custom_call_target="tpu_custom_call" | custom-call | tf_op jit(solution)/shard_map/conv_two_back/pallas_call | solution.py:50
  13.7 3.1 %grad_one.1 = (f32[4,27,64,128]{3,2,1,0:T(8,128)S(1)}, f32[4,28,64,128]{3,2,1,0:T(8,128)S(1)}) custom-call(bf16[4,12,16,256]{3,2,1,0:T(8,128)(2,1)S(1)} %get-tuple-element.48.hid, bf16[4,12,16,256]{3,2,1,0:T(8,128)(2,1)S(1)} %get-tuple-element.50.inp, bf16[2,4,16,256]{3,2,1,0:T(8,128)(2,1)S(1)} %collective-permute-done.row, ...), custom_call_target="tpu_custom_call" | custom-call | tf_op jit(solution)/shard_map/grad_one/pallas_call | solution.py:50
  17.1 2.7 %grad_two.1 = (f32[9,32,768]{2,1,0:T(8,128)S(1)}, bf16[9,32,768]{2,1,0:T(8,128)(2,1)S(1)}, bf16[9,32,768]{2,1,0:T(8,128)(2,1)S(1)}, bf16[9,32,768]{2,1,0:T(8,128)(2,1)S(1)}) custom-call(bf16[4,14,16,768]{3,2,1,0:T(8,128)(2,1)S(1)} %get-tuple-element.49.wide, bf16[768,256]{1,0:T(8,128)(2,1)S(1)} %get-tuple-element.45.act, ...), custom_call_target="tpu_custom_call" | custom-call | tf_op jit(solution)/shard_map/grad_two/pallas_call | solution.py:50
  19.8 3.0 %collective-permute-start.6 = (bf16[9,32,768]{2,1,0:T(8,128)(2,1)S(1)}, bf16[9,32,768]{2,1,0:T(8,128)(2,1)S(1)}, u32[]{:S(2)}, u32[]{:S(2)}) collective-permute-start(bf16[9,32,768]{2,1,0:T(8,128)(2,1)S(1)} %get-tuple-element.52), channel_id=1, source_target_pairs={{0,2},{1,3},{2,0},{3,1},{4,6},{5,7},{6,4},{7,5},{8,10},{9,11},{10,... | collective-permute-start | bytes 1327112 | tf_op jit(solution)/shard_map/ppermute | solution.py:40
  23.9 1.3 %collective-permute-start.13 = (bf16[27,64,128]{2,1,0:T(8,128)(2,1)S(1)}, bf16[27,64,128]{2,1,0:T(8,128)(2,1)S(1)}, u32[]{:S(2)}, u32[]{:S(2)}) collective-permute-start(bf16[27,64,128]{2,1,0:T(8,128)(2,1)S(1)} %get-tuple-element.61), channel_id=1, source_target_pairs={{0,16},{1,17},{2,18},{3,19},{4,20},{5,21},{6,22},{7,23},{8,24},{9,... | collective-permute-start | bytes 1327112 | tf_op jit(solution)/shard_map/ppermute | solution.py:40
  25.2 1.3 %collective-permute-start.14 = (bf16[27,64,128]{2,1,0:T(8,128)(2,1)S(1)}, bf16[27,64,128]{2,1,0:T(8,128)(2,1)S(1)}, u32[]{:S(2)}, u32[]{:S(2)}) collective-permute-start(bf16[27,64,128]{2,1,0:T(8,128)(2,1)S(1)} %get-tuple-element.62), channel_id=1, source_target_pairs={{0,8},{1,9},{2,10},{3,11},{4,12},{5,13},{6,14},{7,15},{8,0},{9,1},... | collective-permute-start | bytes 1327112 | tf_op jit(solution)/shard_map/ppermute | solution.py:40
  26.5 8.1 %collective-permute-done.6.got1 = bf16[9,32,768]{2,1,0:T(8,128)(2,1)S(1)} collective-permute-done((bf16[9,32,768]{2,1,0:T(8,128)(2,1)S(1)}, bf16[9,32,768]{2,1,0:T(8,128)(2,1)S(1)}, u32[]{:S(2)}, u32[]{:S(2)}) %collective-permute-start.6) | collective-permute-done | bytes 442400 | tf_op jit(solution)/shard_map/ppermute | solution.py:40
  34.6 0.9 %collective-permute-start.15 = (bf16[27,64,128]{2,1,0:T(8,128)(2,1)S(1)}, bf16[27,64,128]{2,1,0:T(8,128)(2,1)S(1)}, u32[]{:S(2)}, u32[]{:S(2)}) collective-permute-start(bf16[27,64,128]{2,1,0:T(8,128)(2,1)S(1)} %get-tuple-element.63), channel_id=1, source_target_pairs={{0,24},{1,25},{2,26},{3,27},{4,28},{5,29},{6,30},{7,31},{8,16},{9,... | collective-permute-start | bytes 1327112 | tf_op jit(solution)/shard_map/ppermute | solution.py:40
  35.5 7.8 %collective-permute-done.8.got3 = bf16[9,32,768]{2,1,0:T(8,128)(2,1)S(1)} collective-permute-done((bf16[9,32,768]{2,1,0:T(8,128)(2,1)S(1)}, bf16[9,32,768]{2,1,0:T(8,128)(2,1)S(1)}, u32[]{:S(2)}, u32[]{:S(2)}) %collective-permute-start.8) | collective-permute-done | bytes 442400 | tf_op jit(solution)/shard_map/ppermute | solution.py:40
  43.8 1.3 %collective-permute-start.9 = (bf16[592,128]{1,0:T(8,128)(2,1)S(1)}, bf16[592,128]{1,0:T(8,128)(2,1)S(1)}, u32[]{:S(2)}, u32[]{:S(2)}) collective-permute-start(bf16[592,128]{1,0:T(8,128)(2,1)S(1)} %get-tuple-element.57), channel_id=1, source_target_pairs={{0,16},{1,17},{2,18},{3,19},{4,20},{5,21},{6,22},{7,23},{8,24},{9,... | collective-permute-start | bytes 454664 | tf_op jit(solution)/shard_map/ppermute | solution.py:40
  45.1 2.2 %collective-permute-start.11 = (bf16[592,128]{1,0:T(8,128)(2,1)S(1)}, bf16[592,128]{1,0:T(8,128)(2,1)S(1)}, u32[]{:S(2)}, u32[]{:S(2)}) collective-permute-start(bf16[592,128]{1,0:T(8,128)(2,1)S(1)} %get-tuple-element.59), channel_id=1, source_target_pairs={{0,24},{1,25},{2,26},{3,27},{4,28},{5,29},{6,30},{7,31},{8,16},{9,... | collective-permute-start | bytes 454664 | tf_op jit(solution)/shard_map/ppermute | solution.py:40
  47.9 2.3 %collective-permute-start.17 = (bf16[592,128]{1,0:T(8,128)(2,1)S(1)}, bf16[592,128]{1,0:T(8,128)(2,1)S(1)}, u32[]{:S(2)}, u32[]{:S(2)}) collective-permute-start(bf16[592,128]{1,0:T(8,128)(2,1)S(1)} %get-tuple-element.68), channel_id=1, source_target_pairs={{0,4},{1,5},{2,6},{3,7},{4,0},{5,1},{6,2},{7,3},{8,12},{9,13},{10,... | collective-permute-start | bytes 454664 | tf_op jit(solution)/shard_map/ppermute | solution.py:40
  50.2 5.1 %collective-permute-start.16 = (bf16[576,128]{1,0:T(8,128)(2,1)S(1)}, bf16[576,128]{1,0:T(8,128)(2,1)S(1)}, u32[]{:S(2)}, u32[]{:S(2)}) collective-permute-start(bf16[576,128]{1,0:T(8,128)(2,1)S(1)} %get-tuple-element.67), channel_id=1, source_target_pairs={{0,2},{1,3},{2,0},{3,1},{4,6},{5,7},{6,4},{7,5},{8,10},{9,11},{10,... | collective-permute-start | bytes 442376 | tf_op jit(solution)/shard_map/ppermute | solution.py:40
  55.7 5.6 %collective-permute-done.18.b3 = bf16[464,128]{1,0:T(8,128)(2,1)S(1)} collective-permute-done((bf16[464,128]{1,0:T(8,128)(2,1)S(1)}, bf16[464,128]{1,0:T(8,128)(2,1)S(1)}, u32[]{:S(2)}, u32[]{:S(2)}) %collective-permute-start.18) | collective-permute-done | bytes 118816 | tf_op jit(solution)/shard_map/ppermute | solution.py:40
  61.3 0.8 %last_stage.1 = (bf16[8,112,128]{2,1,0:T(8,128)(2,1)}, f32[112,128]{1,0:T(8,128)S(1)}, bf16[10,16,256]{2,1,0:T(8,128)(2,1)S(1)}) custom-call(f32[448,128]{1,0:T(8,128)S(1)} %get-tuple-element.56.own_two, bf16[592,128]{1,0:T(8,128)(2,1)S(1)} %collective-permute-done.9.a2, bf16[592,128]{1,0:T(8,128)(2,1)S(1)} %collective-permute-done.10.a1, ...), custom_call_target="tpu_custom_call" | custom-call | tf_op jit(solution)/shard_map/last_stage/pallas_call | solution.py:50
  62.1 8.5 %all-to-all-start = ((bf16[8,112,128]{2,1,0:T(8,128)(2,1)}), bf16[8,112,128]{2,1,0:T(8,128)(2,1)S(1)}, u32[]{:S(2)}, u32[]{:S(2)}) async-start(bf16[8,112,128]{2,1,0:T(8,128)(2,1)} %get-tuple-element.72), calls=%async_computation | async-start | bytes 458752 | tf_op jit(solution)/shard_map/all_to_all | solution.py:553
  70.6 5.1 %conv_one_back.1.after = bf16[4,12,16,256]{3,2,1,0:T(8,128)(2,1)} custom-call(bf16[4,12,16,256]{3,2,1,0:T(8,128)(2,1)S(1)} %get-tuple-element.48.hid, bf16[4,12,16,256]{3,2,1,0:T(8,128)(2,1)} %bitcast.21, bf16[10,16,256]{2,1,0:T(8,128)(2,1)S(1)} %get-tuple-element.70.border, bf16[2,4,16,256]{3,2,1,0:T(8,128)(2,1)S(1)} %get-tuple-element.65.cols, ...), custom_call_target="tpu_custom_call" | custom-call | tf_op jit(solution)/shard_map/conv_one_back/pallas_call | solution.py:50
  75.7 5.0 %all-to-all-done.got = bf16[8,112,128]{2,1,0:T(8,128)(2,1)S(1)} async-done(((bf16[8,112,128]{2,1,0:T(8,128)(2,1)}), bf16[8,112,128]{2,1,0:T(8,128)(2,1)S(1)}, u32[]{:S(2)}, u32[]{:S(2)}) %all-to-all-start) | async-done | bytes 229408 | tf_op jit(solution)/shard_map/all_to_all | solution.py:553
  80.7 0.8 final_sum.1
  (28 shorter events, 3.4 us)
Async XLA Ops:
  2.1 8.9 %collective-permute-start = (bf16[2,4,16,256]{3,2,1,0:T(8,128)(2,1)S(1)}, bf16[2,4,16,256]{3,2,1,0:T(8,128)(2,1)S(1)}, u32[]{:S(2)}, u32[]{:S(2)}) collective-permute-start(bf16[2,4,16,256]{3,2,1,0:T(8,128)(2,1)S(1)} %get-tuple-element.40), channel_id=1, source_target_pairs={{0,4},{1,5},{2,6},{3,7},{4,0},{5,1},{6,2},{7,3},{8,12},{9,13},{10,... | collective-permute-start | bytes 196616 | tf_op jit(solution)/shard_map/ppermute | solution.py:40
  3.6 7.3 %collective-permute-start.1 = (bf16[2,4,16,256]{3,2,1,0:T(8,128)(2,1)S(1)}, bf16[2,4,16,256]{3,2,1,0:T(8,128)(2,1)S(1)}, u32[]{:S(2)}, u32[]{:S(2)}) collective-permute-start(bf16[2,4,16,256]{3,2,1,0:T(8,128)(2,1)S(1)} %get-tuple-element.41), channel_id=1, source_target_pairs={{0,1},{1,0},{2,3},{3,2},{4,5},{5,4},{6,7},{7,6},{8,9},{9,8},{10,11... | collective-permute-start | bytes 196616 | tf_op jit(solution)/shard_map/ppermute | solution.py:40
  3.6 7.3 %collective-permute-start.2 = (bf16[2,4,16,256]{3,2,1,0:T(8,128)(2,1)S(1)}, bf16[2,4,16,256]{3,2,1,0:T(8,128)(2,1)S(1)}, u32[]{:S(2)}, u32[]{:S(2)}) collective-permute-start(bf16[2,4,16,256]{3,2,1,0:T(8,128)(2,1)S(1)} %get-tuple-element.42), channel_id=1, source_target_pairs={{0,3},{1,2},{2,1},{3,0},{4,7},{5,6},{6,5},{7,4},{8,11},{9,10},{10,... | collective-permute-start | bytes 196616 | tf_op jit(solution)/shard_map/ppermute | solution.py:40
  6.5 4.4 %collective-permute-start.3 = (bf16[2,16,256]{2,1,0:T(8,128)(2,1)S(1)}, bf16[2,16,256]{2,1,0:T(8,128)(2,1)S(1)}, u32[]{:S(2)}, u32[]{:S(2)}) collective-permute-start(bf16[2,16,256]{2,1,0:T(8,128)(2,1)S(1)} %get-tuple-element.43), channel_id=1, source_target_pairs={{0,5},{1,4},{2,7},{3,6},{4,1},{5,0},{6,3},{7,2},{8,13},{9,12},{10,... | collective-permute-start | bytes 49160 | tf_op jit(solution)/shard_map/ppermute | solution.py:40
  6.5 4.4 %collective-permute-start.4 = (bf16[2,16,256]{2,1,0:T(8,128)(2,1)S(1)}, bf16[2,16,256]{2,1,0:T(8,128)(2,1)S(1)}, u32[]{:S(2)}, u32[]{:S(2)}) collective-permute-start(bf16[2,16,256]{2,1,0:T(8,128)(2,1)S(1)} %get-tuple-element.44), channel_id=1, source_target_pairs={{0,7},{1,6},{2,5},{3,4},{4,3},{5,2},{6,1},{7,0},{8,15},{9,14},{10,... | collective-permute-start | bytes 49160 | tf_op jit(solution)/shard_map/ppermute | solution.py:40
  11.0 2.6 %collective-permute-start.5 = (bf16[4,22,16,256]{3,2,1,0:T(8,128)(2,1)S(1)}, bf16[4,22,16,256]{3,2,1,0:T(8,128)(2,1)S(1)}, u32[]{:S(2)}, u32[]{:S(2)}) collective-permute-start(bf16[4,22,16,256]{3,2,1,0:T(8,128)(2,1)S(1)} %pad_cotangent.1.padded), channel_id=1, source_target_pairs={{0,1},{1,0},{2,3},{3,2},{4,5},{5,4},{6,7},{7,6},{8,9},{9,8},{10,11... | collective-permute-start | bytes 2162696 | tf_op jit(solution)/shard_map/ppermute | solution.py:40
  16.7 6.8 %collective-permute-start.12 = (f32[4,28,64,128]{3,2,1,0:T(8,128)S(1)}, f32[4,28,64,128]{3,2,1,0:T(8,128)S(1)}, u32[]{:S(2)}, u32[]{:S(2)}) collective-permute-start(f32[4,28,64,128]{3,2,1,0:T(8,128)S(1)} %get-tuple-element.51.after), channel_id=1, source_target_pairs={{0,1},{1,0},{2,3},{3,2},{4,5},{5,4},{6,7},{7,6},{8,9},{9,8},{10,11... | collective-permute-start | bytes 11010056 | tf_op jit(solution)/shard_map/ppermute | solution.py:40
  19.8 14.8 %collective-permute-start.6 = (bf16[9,32,768]{2,1,0:T(8,128)(2,1)S(1)}, bf16[9,32,768]{2,1,0:T(8,128)(2,1)S(1)}, u32[]{:S(2)}, u32[]{:S(2)}) collective-permute-start(bf16[9,32,768]{2,1,0:T(8,128)(2,1)S(1)} %get-tuple-element.52), channel_id=1, source_target_pairs={{0,2},{1,3},{2,0},{3,1},{4,6},{5,7},{6,4},{7,5},{8,10},{9,11},{10,... | collective-permute-start | bytes 1327112 | tf_op jit(solution)/shard_map/ppermute | solution.py:40
  22.8 20.6 %collective-permute-start.8 = (bf16[9,32,768]{2,1,0:T(8,128)(2,1)S(1)}, bf16[9,32,768]{2,1,0:T(8,128)(2,1)S(1)}, u32[]{:S(2)}, u32[]{:S(2)}) collective-permute-start(bf16[9,32,768]{2,1,0:T(8,128)(2,1)S(1)} %get-tuple-element.54), channel_id=1, source_target_pairs={{0,6},{1,7},{2,4},{3,5},{4,2},{5,3},{6,0},{7,1},{8,14},{9,15},{10,... | collective-permute-start | bytes 1327112 | tf_op jit(solution)/shard_map/ppermute | solution.py:40
  23.3 20.1 %collective-permute-start.7 = (bf16[9,32,768]{2,1,0:T(8,128)(2,1)S(1)}, bf16[9,32,768]{2,1,0:T(8,128)(2,1)S(1)}, u32[]{:S(2)}, u32[]{:S(2)}) collective-permute-start(bf16[9,32,768]{2,1,0:T(8,128)(2,1)S(1)} %get-tuple-element.53.after), channel_id=1, source_target_pairs={{0,4},{1,5},{2,6},{3,7},{4,0},{5,1},{6,2},{7,3},{8,12},{9,13},{10,... | collective-permute-start | bytes 1327112 | tf_op jit(solution)/shard_map/ppermute | solution.py:40
  23.9 23.4 %collective-permute-start.13 = (bf16[27,64,128]{2,1,0:T(8,128)(2,1)S(1)}, bf16[27,64,128]{2,1,0:T(8,128)(2,1)S(1)}, u32[]{:S(2)}, u32[]{:S(2)}) collective-permute-start(bf16[27,64,128]{2,1,0:T(8,128)(2,1)S(1)} %get-tuple-element.61), channel_id=1, source_target_pairs={{0,16},{1,17},{2,18},{3,19},{4,20},{5,21},{6,22},{7,23},{8,24},{9,... | collective-permute-start | bytes 1327112 | tf_op jit(solution)/shard_map/ppermute | solution.py:40
  25.2 22.2 %collective-permute-start.14 = (bf16[27,64,128]{2,1,0:T(8,128)(2,1)S(1)}, bf16[27,64,128]{2,1,0:T(8,128)(2,1)S(1)}, u32[]{:S(2)}, u32[]{:S(2)}) collective-permute-start(bf16[27,64,128]{2,1,0:T(8,128)(2,1)S(1)} %get-tuple-element.62), channel_id=1, source_target_pairs={{0,8},{1,9},{2,10},{3,11},{4,12},{5,13},{6,14},{7,15},{8,0},{9,1},... | collective-permute-start | bytes 1327112 | tf_op jit(solution)/shard_map/ppermute | solution.py:40
  34.6 12.8 %collective-permute-start.15 = (bf16[27,64,128]{2,1,0:T(8,128)(2,1)S(1)}, bf16[27,64,128]{2,1,0:T(8,128)(2,1)S(1)}, u32[]{:S(2)}, u32[]{:S(2)}) collective-permute-start(bf16[27,64,128]{2,1,0:T(8,128)(2,1)S(1)} %get-tuple-element.63), channel_id=1, source_target_pairs={{0,24},{1,25},{2,26},{3,27},{4,28},{5,29},{6,30},{7,31},{8,16},{9,... | collective-permute-start | bytes 1327112 | tf_op jit(solution)/shard_map/ppermute | solution.py:40
  43.8 11.4 %collective-permute-start.9 = (bf16[592,128]{1,0:T(8,128)(2,1)S(1)}, bf16[592,128]{1,0:T(8,128)(2,1)S(1)}, u32[]{:S(2)}, u32[]{:S(2)}) collective-permute-start(bf16[592,128]{1,0:T(8,128)(2,1)S(1)} %get-tuple-element.57), channel_id=1, source_target_pairs={{0,16},{1,17},{2,18},{3,19},{4,20},{5,21},{6,22},{7,23},{8,24},{9,... | collective-permute-start | bytes 454664 | tf_op jit(solution)/shard_map/ppermute | solution.py:40
  45.1 10.6 %collective-permute-start.11 = (bf16[592,128]{1,0:T(8,128)(2,1)S(1)}, bf16[592,128]{1,0:T(8,128)(2,1)S(1)}, u32[]{:S(2)}, u32[]{:S(2)}) collective-permute-start(bf16[592,128]{1,0:T(8,128)(2,1)S(1)} %get-tuple-element.59), channel_id=1, source_target_pairs={{0,24},{1,25},{2,26},{3,27},{4,28},{5,29},{6,30},{7,31},{8,16},{9,... | collective-permute-start | bytes 454664 | tf_op jit(solution)/shard_map/ppermute | solution.py:40
  47.3 8.4 %collective-permute-start.10 = (bf16[592,128]{1,0:T(8,128)(2,1)S(1)}, bf16[592,128]{1,0:T(8,128)(2,1)S(1)}, u32[]{:S(2)}, u32[]{:S(2)}) collective-permute-start(bf16[592,128]{1,0:T(8,128)(2,1)S(1)} %get-tuple-element.58.after), channel_id=1, source_target_pairs={{0,8},{1,9},{2,10},{3,11},{4,12},{5,13},{6,14},{7,15},{8,0},{9,1},... | collective-permute-start | bytes 454664 | tf_op jit(solution)/shard_map/ppermute | solution.py:40
  47.9 13.4 %collective-permute-start.17 = (bf16[592,128]{1,0:T(8,128)(2,1)S(1)}, bf16[592,128]{1,0:T(8,128)(2,1)S(1)}, u32[]{:S(2)}, u32[]{:S(2)}) collective-permute-start(bf16[592,128]{1,0:T(8,128)(2,1)S(1)} %get-tuple-element.68), channel_id=1, source_target_pairs={{0,4},{1,5},{2,6},{3,7},{4,0},{5,1},{6,2},{7,3},{8,12},{9,13},{10,... | collective-permute-start | bytes 454664 | tf_op jit(solution)/shard_map/ppermute | solution.py:40
  50.2 11.1 %collective-permute-start.16 = (bf16[576,128]{1,0:T(8,128)(2,1)S(1)}, bf16[576,128]{1,0:T(8,128)(2,1)S(1)}, u32[]{:S(2)}, u32[]{:S(2)}) collective-permute-start(bf16[576,128]{1,0:T(8,128)(2,1)S(1)} %get-tuple-element.67), channel_id=1, source_target_pairs={{0,2},{1,3},{2,0},{3,1},{4,6},{5,7},{6,4},{7,5},{8,10},{9,11},{10,... | collective-permute-start | bytes 442376 | tf_op jit(solution)/shard_map/ppermute | solution.py:40
  55.2 6.0 %collective-permute-start.18 = (bf16[464,128]{1,0:T(8,128)(2,1)S(1)}, bf16[464,128]{1,0:T(8,128)(2,1)S(1)}, u32[]{:S(2)}, u32[]{:S(2)}) collective-permute-start(bf16[464,128]{1,0:T(8,128)(2,1)S(1)} %get-tuple-element.69), channel_id=1, source_target_pairs={{0,6},{1,7},{2,4},{3,5},{4,2},{5,3},{6,0},{7,1},{8,14},{9,15},{10,... | collective-permute-start | bytes 356360 | tf_op jit(solution)/shard_map/ppermute | solution.py:40
  62.1 18.6 %all-to-all-start = ((bf16[8,112,128]{2,1,0:T(8,128)(2,1)}), bf16[8,112,128]{2,1,0:T(8,128)(2,1)S(1)}, u32[]{:S(2)}, u32[]{:S(2)}) async-start(bf16[8,112,128]{2,1,0:T(8,128)(2,1)} %get-tuple-element.72), calls=%async_computation | async-start | bytes 458752 | tf_op jit(solution)/shard_map/all_to_all | solution.py:553

commit v13 on v12

--- a/solution.py
+++ b/solution.py
@@ -86,8 +86,12 @@
     return jnp.dot(chosen, block.reshape(768, 256), preferred_element_type=F32)
 
 
-def pack_kernel(one, two, row, face, outer, corner_face, corner_outer, same):
-    same[...] = one[...]
+def pack_kernel(
+    one, two, weight, row, face, outer, corner_face, corner_outer, same_one, same_two, taps, sem
+):
+    copy = pltpu.make_async_copy(weight.at[pl.ds(0, 9)], taps, sem)
+    copy.start()
+    same_one[...], same_two[...] = one[...], two[...]
     edge = 11 * (1 - lax.axis_index("ha"))
     for n, block in enumerate((one, two)):
         cells = border_cells(block[...], 160)
@@ -97,6 +101,7 @@
         corner_face[n], corner_outer[n] = by_core(lo, hi).astype(BF), by_core(hi, lo).astype(BF)
         for f in range(4):
             row[n, f] = block[f, edge]
+    copy.wait()
 
 
 def pad_block(put, block, row, left, right, corner_left, corner_right):
@@ -143,14 +148,16 @@
     return put
 
 
-def weight_copies(weight, held, sem):
+def weight_copies(weight, held, sem, first=0):
     return [
-        pltpu.make_async_copy(weight.at[pl.ds(a * 9, 9)], held.at[pl.ds(a * 9, 9)], sem.at[a])
-        for a in range(3)
+        pltpu.make_async_copy(
+            weight.at[pl.ds(a * 9, 9)], held.at[pl.ds((a - first) * 9, 9)], sem.at[a]
+        )
+        for a in range(first, 3)
     ]
 
 
-def conv_sum(wide, held, total):
+def conv_sum(wide, tap, total):
     for a in (2, 1, 0):
         frames = a + 2
         for b in range(3):
@@ -159,7 +166,7 @@
             for e in range(3):
                 one = lax.dot_general(
                     window[:, e * 256 : (e + 1) * 256],
-                    held[(a * 3 + b) * 3 + e],
+                    tap((a * 3 + b) * 3 + e),
                     NT,
                     preferred_element_type=F32,
                 )
@@ -179,30 +186,25 @@
 
 def film_kernel(
     step, inputs, hidden, table, weight, act_out, inp_out, slope, taps,
-    film, blocks, sem, block_sem, tap_sem,
+    film, block, sem, block_sem, tap_sem,
 ):
     start = step[0]
     whole = pl.multiple_of(start // 8 * 8, 8)
     film_copy = pltpu.make_async_copy(table.at[pl.ds(whole, 8)], film, sem)
     film_copy.start()
-    block_copies = [
-        pltpu.make_async_copy(ref, blocks.at[n], block_sem.at[n])
-        for n, ref in enumerate((inputs, hidden))
-    ]
-    for copy in block_copies:
-        copy.start()
-    copies = weight_copies(weight, taps, tap_sem)
+    block_copy = pltpu.make_async_copy(hidden, block, block_sem)
+    block_copy.start()
+    copies = weight_copies(weight, taps, tap_sem, 1)
     for copy in copies:
         copy.start()
     order = channel_order()
     sort = lambda v: jnp.dot(v, order, preferred_element_type=F32).astype(BF)
-    for copy in block_copies:
-        copy.wait()
-    inp_out[...] = sort(blocks[0].reshape(768, 256)).reshape(4, 12, 16, 256)
+    inp_out[...] = sort(inputs[...].reshape(768, 256)).reshape(4, 12, 16, 256)
+    block_copy.wait()
     film_copy.wait()
     line = film[pl.ds(start - whole, 1), :]
     scale, shift = 1.0 + line[:, 0:256], line[:, 256:512]
-    shifted = blocks[1].reshape(768, 256).astype(F32) * scale + shift
+    shifted = block[...].reshape(768, 256).astype(F32) * scale + shift
     sigma = jax.nn.sigmoid(shifted)
     act_out[...] = sort((shifted * sigma).astype(BF))
     slope[...] = scale * sigma * (1.0 + shifted * (1.0 - sigma))
@@ -228,9 +230,9 @@
             out[f, 16 + n % 6, :, n // 6 * 128 : n // 6 * 128 + 128] = cells
 
 
-def first_kernel(padded, slope, taps, wide, hid_out, total):
+def first_kernel(padded, slope, taps, more, wide, hid_out, total):
     build_shifted(put_back(wide), padded)
-    conv_sum(wide, taps, total)
+    conv_sum(wide, lambda t: taps[t] if t < 9 else more[t - 9], total)
     hid_out[...] = (total[...] * slope[...]).astype(BF).reshape(4, 12, 16, 256)
 
 
@@ -255,7 +257,7 @@
     build_shifted(put_back(wide), padded)
     for copy in copies:
         copy.wait()
-    conv_sum(wide, held, total)
+    conv_sum(wide, lambda t: held[t], total)
     grad = near_block[...].reshape(768, 256).astype(F32) + total[...]
     out[...] = grad.astype(BF).reshape(4, 12, 16, 256)
 
@@ -444,33 +446,35 @@
     def ring(parts, axis):
         return [send(parts[d - 1], ring_pairs(**{axis: d})) for d in (2, 1, 3)]
 
-    *packed, held_block = call(
+    *packed, held_block, held_inputs, held_two = call(
         pack_kernel,
         "pack_first",
-        (block, inputs),
-        "pp",
+        (block, inputs, taps_two),
+        "pph",
         [near((2, 4, 16, 256), BF)] * 3
         + [near((2, 16, 256), BF)] * 2
-        + [near((4, 12, 16, 256), BF)],
+        + [near((4, 12, 16, 256), BF)] * 2
+        + [near((9, 256, 256), BF)],
+        [pltpu.SemaphoreType.DMA],
     )
     ways = ((1, 0), (0, 1), (0, 3), (1, 1), (1, 3))
     sides = [send(p, block_pairs(*way)) for p, way in zip(packed, ways)]
-    act, inp, slope, held_two = call(
+    act, inp, slope, more_two = call(
         film_kernel,
         "film",
-        (timesteps, inputs, hidden, film_table, taps_two),
-        "shhhh",
+        (timesteps, held_inputs, hidden, film_table, taps_two),
+        "svhhh",
         [
             near((768, 256), BF),
             near((4, 12, 16, 256), BF),
             near((768, 256), F32),
-            near((27, 256, 256), BF),
+            near((18, 256, 256), BF),
         ],
         [
             pltpu.VMEM((8, 512), F32),
-            pltpu.VMEM((2, 4, 12, 16, 256), BF),
+            pltpu.VMEM((4, 12, 16, 256), BF),
             pltpu.SemaphoreType.DMA,
-            pltpu.SemaphoreType.DMA((2,)),
+            pltpu.SemaphoreType.DMA,
             pltpu.SemaphoreType.DMA((3,)),
         ],
     )
@@ -485,8 +489,8 @@
     wide_cot, grad_hidden = call(
         first_kernel,
         "conv_two_back",
-        (padded, slope, held_two),
-        "vvv",
+        (padded, slope, held_two, more_two),
+        "vvvv",
         [wide, near((4, 12, 16, 256), BF)],
         [pltpu.VMEM((768, 256), F32)],
     )

time: 81.8 us -> 81.5 us (level)
  starting transfers between devices: 33.3 us -> 30.4 us
  waiting for transfers between devices: 26.6 us -> 28.2 us
    ppermute x19, starting transfers between devices: 24.9 us -> 21.9 us  [send(): return lax.ppermute(value, AX, pairs)]
    ppermute x19, waiting for transfers between devices: 21.6 us -> 23.2 us  [send(): return lax.ppermute(value, AX, pairs)]
  transfers between devices with their start and end apart: 20 -> 20, of which waited for: 4 -> 6; matrix products, arithmetic and copies ran while one was open for 0% -> 0% of each run, Pallas kernels for 17% -> 17%
where the time goes in v13:
time: 81.5 us; the launch traced here: 80.7 us
  starting transfers between devices  30.4 us (37%)
  waiting for transfers between devices  28.2 us (35%)
  Pallas kernels  20.7 us (25%)
  between operations  1.39 us (2%)
    ppermute x19, waiting for transfers between devices, send(): return lax.ppermute(value, AX, pairs)  23.2 us
    ppermute x19, starting transfers between devices, send(): return lax.ppermute(value, AX, pairs)  21.9 us
    pallas_call x12, Pallas kernels, call(): pl.pallas_call(kernel, out_shape=tuple((o for o, _ in outs)), in_specs=[s...  20.7 us
    all_to_all x1, starting transfers between devices, shards(): planes = lax.all_to_all(out, 'z', 0, 0, tiled=True)  8.57 us
    all_to_all x1, waiting for transfers between devices, shards(): planes = lax.all_to_all(out, 'z', 0, 0, tiled=True)  5.02 us
  transfers between devices with their start and end apart: 20, of which 6 were waited for; matrix products, arithmetic and copies ran while one was open for 0% of the time, Pallas kernels for 17%

profile of v13, /device:TPU:24, one launch (start us, length us, event | category | flops | bytes accessed | tf_op | source)
XLA Modules:
  0.0 80.7 jit_solution(1624923495649677004)
XLA Ops:
  0.6 2.4 %pack_first.1 = (bf16[2,4,16,256]{3,2,1,0:T(8,128)(2,1)S(1)}, bf16[2,4,16,256]{3,2,1,0:T(8,128)(2,1)S(1)}, bf16[2,4,16,256]{3,2,1,0:T(8,128)(2,1)S(1)}, bf16[2,1...) custom-call(bf16[4,12,16,256]{3,2,1,0:T(8,128)(2,1)} %bitcast.19, ...), custom_call_target="tpu_custom_call" | custom-call | tf_op jit(solution)/shard_map/pack_first/pallas_call | solution.py:50
  3.0 1.6 %collective-permute-start = (bf16[2,4,16,256]{3,2,1,0:T(8,128)(2,1)S(1)}, bf16[2,4,16,256]{3,2,1,0:T(8,128)(2,1)S(1)}, u32[]{:S(2)}, u32[]{:S(2)}) collective-permute-start(bf16[2,4,16,256]{3,2,1,0:T(8,128)(2,1)S(1)} %get-tuple-element.42), channel_id=1, source_target_pairs={{0,4},{1,5},{2,6},{3,7},{4,0},{5,1},{6,2},{7,3},{8,12},{9,13},{10,... | collective-permute-start | bytes 196616 | tf_op jit(solution)/shard_map/ppermute | solution.py:40
  4.6 2.8 %collective-permute-start.2 = (bf16[2,4,16,256]{3,2,1,0:T(8,128)(2,1)S(1)}, bf16[2,4,16,256]{3,2,1,0:T(8,128)(2,1)S(1)}, u32[]{:S(2)}, u32[]{:S(2)}) collective-permute-start(bf16[2,4,16,256]{3,2,1,0:T(8,128)(2,1)S(1)} %get-tuple-element.44), channel_id=1, source_target_pairs={{0,3},{1,2},{2,1},{3,0},{4,7},{5,6},{6,5},{7,4},{8,11},{9,10},{10,... | collective-permute-start | bytes 196616 | tf_op jit(solution)/shard_map/ppermute | solution.py:40
  7.5 1.1 %collective-permute-start.4 = (bf16[2,16,256]{2,1,0:T(8,128)(2,1)S(1)}, bf16[2,16,256]{2,1,0:T(8,128)(2,1)S(1)}, u32[]{:S(2)}, u32[]{:S(2)}) collective-permute-start(bf16[2,16,256]{2,1,0:T(8,128)(2,1)S(1)} %get-tuple-element.46), channel_id=1, source_target_pairs={{0,7},{1,6},{2,5},{3,4},{4,3},{5,2},{6,1},{7,0},{8,15},{9,14},{10,... | collective-permute-start | bytes 49160 | tf_op jit(solution)/shard_map/ppermute | solution.py:40
  9.2 2.1 %film.1 = (bf16[768,256]{1,0:T(8,128)(2,1)S(1)}, bf16[4,12,16,256]{3,2,1,0:T(8,128)(2,1)S(1)}, f32[768,256]{1,0:T(8,128)S(1)}, bf16[18,256,256]{2,1,0:T(8,128)(2,1)S(1)}) custom-call(s32[1]{0:T(128)S(6)} %copy.10.step, bf16[4,12,16,256]{3,2,1,0:T(8,128)(2,1)S(1)} %get-tuple-element.47.inputs, bf16[4,12,16,256]{3,2,1,0:T(8,128)(2,1)} %bitcast.23, ...), custom_call_target="tpu_custom_call" | custom-call | tf_op jit(solution)/shard_map/film/pallas_call | solution.py:50
  12.4 2.3 %conv_two_back.1 = (bf16[4,14,16,768]{3,2,1,0:T(8,128)(2,1)S(1)}, bf16[4,12,16,256]{3,2,1,0:T(8,128)(2,1)S(1)}) custom-call(bf16[4,22,16,256]{3,2,1,0:T(8,128)(2,1)S(1)} %pad_cotangent.1.padded, f32[768,256]{1,0:T(8,128)S(1)} %get-tuple-element.49.slope, bf16[9,256,256]{2,1,0:T(8,128)(2,1)S(1)} %get-tuple-element.50.taps, ...), custom_call_target="tpu_custom_call" | custom-call | tf_op jit(solution)/shard_map/conv_two_back/pallas_call | solution.py:50
  14.6 3.1 %grad_one.1 = (f32[4,27,64,128]{3,2,1,0:T(8,128)S(1)}, f32[4,28,64,128]{3,2,1,0:T(8,128)S(1)}) custom-call(bf16[4,12,16,256]{3,2,1,0:T(8,128)(2,1)S(1)} %get-tuple-element.52.hid, bf16[4,12,16,256]{3,2,1,0:T(8,128)(2,1)S(1)} %get-tuple-element.54.inp, bf16[2,4,16,256]{3,2,1,0:T(8,128)(2,1)S(1)} %collective-permute-done.row, ...), custom_call_target="tpu_custom_call" | custom-call | tf_op jit(solution)/shard_map/grad_one/pallas_call | solution.py:50
  18.0 2.7 %grad_two.1 = (f32[9,32,768]{2,1,0:T(8,128)S(1)}, bf16[9,32,768]{2,1,0:T(8,128)(2,1)S(1)}, bf16[9,32,768]{2,1,0:T(8,128)(2,1)S(1)}, bf16[9,32,768]{2,1,0:T(8,128)(2,1)S(1)}) custom-call(bf16[4,14,16,768]{3,2,1,0:T(8,128)(2,1)S(1)} %get-tuple-element.53.wide, bf16[768,256]{1,0:T(8,128)(2,1)S(1)} %get-tuple-element.48.act, ...), custom_call_target="tpu_custom_call" | custom-call | tf_op jit(solution)/shard_map/grad_two/pallas_call | solution.py:50
  20.7 2.5 %collective-permute-start.6 = (bf16[9,32,768]{2,1,0:T(8,128)(2,1)S(1)}, bf16[9,32,768]{2,1,0:T(8,128)(2,1)S(1)}, u32[]{:S(2)}, u32[]{:S(2)}) collective-permute-start(bf16[9,32,768]{2,1,0:T(8,128)(2,1)S(1)} %get-tuple-element.56), channel_id=1, source_target_pairs={{0,2},{1,3},{2,0},{3,1},{4,6},{5,7},{6,4},{7,5},{8,10},{9,11},{10,... | collective-permute-start | bytes 1327112 | tf_op jit(solution)/shard_map/ppermute | solution.py:40
  23.2 0.8 %collective-permute-start.8 = (bf16[9,32,768]{2,1,0:T(8,128)(2,1)S(1)}, bf16[9,32,768]{2,1,0:T(8,128)(2,1)S(1)}, u32[]{:S(2)}, u32[]{:S(2)}) collective-permute-start(bf16[9,32,768]{2,1,0:T(8,128)(2,1)S(1)} %get-tuple-element.58), channel_id=1, source_target_pairs={{0,6},{1,7},{2,4},{3,5},{4,2},{5,3},{6,0},{7,1},{8,14},{9,15},{10,... | collective-permute-start | bytes 1327112 | tf_op jit(solution)/shard_map/ppermute | solution.py:40
  24.8 1.3 %collective-permute-start.13 = (bf16[27,64,128]{2,1,0:T(8,128)(2,1)S(1)}, bf16[27,64,128]{2,1,0:T(8,128)(2,1)S(1)}, u32[]{:S(2)}, u32[]{:S(2)}) collective-permute-start(bf16[27,64,128]{2,1,0:T(8,128)(2,1)S(1)} %get-tuple-element.65), channel_id=1, source_target_pairs={{0,16},{1,17},{2,18},{3,19},{4,20},{5,21},{6,22},{7,23},{8,24},{9,... | collective-permute-start | bytes 1327112 | tf_op jit(solution)/shard_map/ppermute | solution.py:40
  26.1 0.8 collective-permute-start.14
  26.9 8.6 %collective-permute-done.6.got1 = bf16[9,32,768]{2,1,0:T(8,128)(2,1)S(1)} collective-permute-done((bf16[9,32,768]{2,1,0:T(8,128)(2,1)S(1)}, bf16[9,32,768]{2,1,0:T(8,128)(2,1)S(1)}, u32[]{:S(2)}, u32[]{:S(2)}) %collective-permute-start.6) | collective-permute-done | bytes 442400 | tf_op jit(solution)/shard_map/ppermute | solution.py:40
  35.9 8.4 %collective-permute-done.8.got3 = bf16[9,32,768]{2,1,0:T(8,128)(2,1)S(1)} collective-permute-done((bf16[9,32,768]{2,1,0:T(8,128)(2,1)S(1)}, bf16[9,32,768]{2,1,0:T(8,128)(2,1)S(1)}, u32[]{:S(2)}, u32[]{:S(2)}) %collective-permute-start.8) | collective-permute-done | bytes 442400 | tf_op jit(solution)/shard_map/ppermute | solution.py:40
  44.8 1.3 %collective-permute-start.9 = (bf16[592,128]{1,0:T(8,128)(2,1)S(1)}, bf16[592,128]{1,0:T(8,128)(2,1)S(1)}, u32[]{:S(2)}, u32[]{:S(2)}) collective-permute-start(bf16[592,128]{1,0:T(8,128)(2,1)S(1)} %get-tuple-element.61), channel_id=1, source_target_pairs={{0,16},{1,17},{2,18},{3,19},{4,20},{5,21},{6,22},{7,23},{8,24},{9,... | collective-permute-start | bytes 454664 | tf_op jit(solution)/shard_map/ppermute | solution.py:40
  46.1 2.2 %collective-permute-start.11 = (bf16[592,128]{1,0:T(8,128)(2,1)S(1)}, bf16[592,128]{1,0:T(8,128)(2,1)S(1)}, u32[]{:S(2)}, u32[]{:S(2)}) collective-permute-start(bf16[592,128]{1,0:T(8,128)(2,1)S(1)} %get-tuple-element.63), channel_id=1, source_target_pairs={{0,24},{1,25},{2,26},{3,27},{4,28},{5,29},{6,30},{7,31},{8,16},{9,... | collective-permute-start | bytes 454664 | tf_op jit(solution)/shard_map/ppermute | solution.py:40
  48.9 1.8 %collective-permute-start.17 = (bf16[592,128]{1,0:T(8,128)(2,1)S(1)}, bf16[592,128]{1,0:T(8,128)(2,1)S(1)}, u32[]{:S(2)}, u32[]{:S(2)}) collective-permute-start(bf16[592,128]{1,0:T(8,128)(2,1)S(1)} %get-tuple-element.72), channel_id=1, source_target_pairs={{0,4},{1,5},{2,6},{3,7},{4,0},{5,1},{6,2},{7,3},{8,12},{9,13},{10,... | collective-permute-start | bytes 454664 | tf_op jit(solution)/shard_map/ppermute | solution.py:40
  50.7 3.6 %collective-permute-start.16 = (bf16[576,128]{1,0:T(8,128)(2,1)S(1)}, bf16[576,128]{1,0:T(8,128)(2,1)S(1)}, u32[]{:S(2)}, u32[]{:S(2)}) collective-permute-start(bf16[576,128]{1,0:T(8,128)(2,1)S(1)} %get-tuple-element.71), channel_id=1, source_target_pairs={{0,2},{1,3},{2,0},{3,1},{4,6},{5,7},{6,4},{7,5},{8,10},{9,11},{10,... | collective-permute-start | bytes 442376 | tf_op jit(solution)/shard_map/ppermute | solution.py:40
  55.5 4.9 %collective-permute-done.18.b3 = bf16[464,128]{1,0:T(8,128)(2,1)S(1)} collective-permute-done((bf16[464,128]{1,0:T(8,128)(2,1)S(1)}, bf16[464,128]{1,0:T(8,128)(2,1)S(1)}, u32[]{:S(2)}, u32[]{:S(2)}) %collective-permute-start.18) | collective-permute-done | bytes 118816 | tf_op jit(solution)/shard_map/ppermute | solution.py:40
  60.4 0.8 %last_stage.1 = (bf16[8,112,128]{2,1,0:T(8,128)(2,1)}, f32[112,128]{1,0:T(8,128)S(1)}, bf16[10,16,256]{2,1,0:T(8,128)(2,1)S(1)}) custom-call(f32[448,128]{1,0:T(8,128)S(1)} %get-tuple-element.60.own_two, bf16[592,128]{1,0:T(8,128)(2,1)S(1)} %collective-permute-done.9.a2, bf16[592,128]{1,0:T(8,128)(2,1)S(1)} %collective-permute-done.10.a1, ...), custom_call_target="tpu_custom_call" | custom-call | tf_op jit(solution)/shard_map/last_stage/pallas_call | solution.py:50
  61.2 8.6 %all-to-all-start = ((bf16[8,112,128]{2,1,0:T(8,128)(2,1)}), bf16[8,112,128]{2,1,0:T(8,128)(2,1)S(1)}, u32[]{:S(2)}, u32[]{:S(2)}) async-start(bf16[8,112,128]{2,1,0:T(8,128)(2,1)} %get-tuple-element.76), calls=%async_computation | async-start | bytes 458752 | tf_op jit(solution)/shard_map/all_to_all | solution.py:557
  69.8 5.1 %conv_one_back.1.after = bf16[4,12,16,256]{3,2,1,0:T(8,128)(2,1)} custom-call(bf16[4,12,16,256]{3,2,1,0:T(8,128)(2,1)S(1)} %get-tuple-element.52.hid, bf16[4,12,16,256]{3,2,1,0:T(8,128)(2,1)} %bitcast.20, bf16[10,16,256]{2,1,0:T(8,128)(2,1)S(1)} %get-tuple-element.74.border, bf16[2,4,16,256]{3,2,1,0:T(8,128)(2,1)S(1)} %get-tuple-element.69.cols, ...), custom_call_target="tpu_custom_call" | custom-call | tf_op jit(solution)/shard_map/conv_one_back/pallas_call | solution.py:50
  74.9 5.0 %all-to-all-done.got = bf16[8,112,128]{2,1,0:T(8,128)(2,1)S(1)} async-done(((bf16[8,112,128]{2,1,0:T(8,128)(2,1)}), bf16[8,112,128]{2,1,0:T(8,128)(2,1)S(1)}, u32[]{:S(2)}, u32[]{:S(2)}) %all-to-all-start) | async-done | bytes 229408 | tf_op jit(solution)/shard_map/all_to_all | solution.py:557
  79.9 0.8 final_sum.1
  (28 shorter events, 4.6 us)
Async XLA Ops:
  3.0 8.8 %collective-permute-start = (bf16[2,4,16,256]{3,2,1,0:T(8,128)(2,1)S(1)}, bf16[2,4,16,256]{3,2,1,0:T(8,128)(2,1)S(1)}, u32[]{:S(2)}, u32[]{:S(2)}) collective-permute-start(bf16[2,4,16,256]{3,2,1,0:T(8,128)(2,1)S(1)} %get-tuple-element.42), channel_id=1, source_target_pairs={{0,4},{1,5},{2,6},{3,7},{4,0},{5,1},{6,2},{7,3},{8,12},{9,13},{10,... | collective-permute-start | bytes 196616 | tf_op jit(solution)/shard_map/ppermute | solution.py:40
  4.6 7.2 %collective-permute-start.1 = (bf16[2,4,16,256]{3,2,1,0:T(8,128)(2,1)S(1)}, bf16[2,4,16,256]{3,2,1,0:T(8,128)(2,1)S(1)}, u32[]{:S(2)}, u32[]{:S(2)}) collective-permute-start(bf16[2,4,16,256]{3,2,1,0:T(8,128)(2,1)S(1)} %get-tuple-element.43), channel_id=1, source_target_pairs={{0,1},{1,0},{2,3},{3,2},{4,5},{5,4},{6,7},{7,6},{8,9},{9,8},{10,11... | collective-permute-start | bytes 196616 | tf_op jit(solution)/shard_map/ppermute | solution.py:40
  4.6 7.2 %collective-permute-start.2 = (bf16[2,4,16,256]{3,2,1,0:T(8,128)(2,1)S(1)}, bf16[2,4,16,256]{3,2,1,0:T(8,128)(2,1)S(1)}, u32[]{:S(2)}, u32[]{:S(2)}) collective-permute-start(bf16[2,4,16,256]{3,2,1,0:T(8,128)(2,1)S(1)} %get-tuple-element.44), channel_id=1, source_target_pairs={{0,3},{1,2},{2,1},{3,0},{4,7},{5,6},{6,5},{7,4},{8,11},{9,10},{10,... | collective-permute-start | bytes 196616 | tf_op jit(solution)/shard_map/ppermute | solution.py:40
  7.5 3.9 %collective-permute-start.3 = (bf16[2,16,256]{2,1,0:T(8,128)(2,1)S(1)}, bf16[2,16,256]{2,1,0:T(8,128)(2,1)S(1)}, u32[]{:S(2)}, u32[]{:S(2)}) collective-permute-start(bf16[2,16,256]{2,1,0:T(8,128)(2,1)S(1)} %get-tuple-element.45), channel_id=1, source_target_pairs={{0,5},{1,4},{2,7},{3,6},{4,1},{5,0},{6,3},{7,2},{8,13},{9,12},{10,... | collective-permute-start | bytes 49160 | tf_op jit(solution)/shard_map/ppermute | solution.py:40
  7.5 4.4 %collective-permute-start.4 = (bf16[2,16,256]{2,1,0:T(8,128)(2,1)S(1)}, bf16[2,16,256]{2,1,0:T(8,128)(2,1)S(1)}, u32[]{:S(2)}, u32[]{:S(2)}) collective-permute-start(bf16[2,16,256]{2,1,0:T(8,128)(2,1)S(1)} %get-tuple-element.46), channel_id=1, source_target_pairs={{0,7},{1,6},{2,5},{3,4},{4,3},{5,2},{6,1},{7,0},{8,15},{9,14},{10,... | collective-permute-start | bytes 49160 | tf_op jit(solution)/shard_map/ppermute | solution.py:40
  11.9 2.7 %collective-permute-start.5 = (bf16[4,22,16,256]{3,2,1,0:T(8,128)(2,1)S(1)}, bf16[4,22,16,256]{3,2,1,0:T(8,128)(2,1)S(1)}, u32[]{:S(2)}, u32[]{:S(2)}) collective-permute-start(bf16[4,22,16,256]{3,2,1,0:T(8,128)(2,1)S(1)} %pad_cotangent.1.padded), channel_id=1, source_target_pairs={{0,1},{1,0},{2,3},{3,2},{4,5},{5,4},{6,7},{7,6},{8,9},{9,8},{10,11... | collective-permute-start | bytes 2162696 | tf_op jit(solution)/shard_map/ppermute | solution.py:40
  17.7 6.7 %collective-permute-start.12 = (f32[4,28,64,128]{3,2,1,0:T(8,128)S(1)}, f32[4,28,64,128]{3,2,1,0:T(8,128)S(1)}, u32[]{:S(2)}, u32[]{:S(2)}) collective-permute-start(f32[4,28,64,128]{3,2,1,0:T(8,128)S(1)} %get-tuple-element.55.after), channel_id=1, source_target_pairs={{0,1},{1,0},{2,3},{3,2},{4,5},{5,4},{6,7},{7,6},{8,9},{9,8},{10,11... | collective-permute-start | bytes 11010056 | tf_op jit(solution)/shard_map/ppermute | solution.py:40
  20.7 14.8 %collective-permute-start.6 = (bf16[9,32,768]{2,1,0:T(8,128)(2,1)S(1)}, bf16[9,32,768]{2,1,0:T(8,128)(2,1)S(1)}, u32[]{:S(2)}, u32[]{:S(2)}) collective-permute-start(bf16[9,32,768]{2,1,0:T(8,128)(2,1)S(1)} %get-tuple-element.56), channel_id=1, source_target_pairs={{0,2},{1,3},{2,0},{3,1},{4,6},{5,7},{6,4},{7,5},{8,10},{9,11},{10,... | collective-permute-start | bytes 1327112 | tf_op jit(solution)/shard_map/ppermute | solution.py:40
  23.2 21.1 %collective-permute-start.8 = (bf16[9,32,768]{2,1,0:T(8,128)(2,1)S(1)}, bf16[9,32,768]{2,1,0:T(8,128)(2,1)S(1)}, u32[]{:S(2)}, u32[]{:S(2)}) collective-permute-start(bf16[9,32,768]{2,1,0:T(8,128)(2,1)S(1)} %get-tuple-element.58), channel_id=1, source_target_pairs={{0,6},{1,7},{2,4},{3,5},{4,2},{5,3},{6,0},{7,1},{8,14},{9,15},{10,... | collective-permute-start | bytes 1327112 | tf_op jit(solution)/shard_map/ppermute | solution.py:40
  24.1 20.3 %collective-permute-start.7 = (bf16[9,32,768]{2,1,0:T(8,128)(2,1)S(1)}, bf16[9,32,768]{2,1,0:T(8,128)(2,1)S(1)}, u32[]{:S(2)}, u32[]{:S(2)}) collective-permute-start(bf16[9,32,768]{2,1,0:T(8,128)(2,1)S(1)} %get-tuple-element.57.after), channel_id=1, source_target_pairs={{0,4},{1,5},{2,6},{3,7},{4,0},{5,1},{6,2},{7,3},{8,12},{9,13},{10,... | collective-permute-start | bytes 1327112 | tf_op jit(solution)/shard_map/ppermute | solution.py:40
  24.8 23.5 %collective-permute-start.13 = (bf16[27,64,128]{2,1,0:T(8,128)(2,1)S(1)}, bf16[27,64,128]{2,1,0:T(8,128)(2,1)S(1)}, u32[]{:S(2)}, u32[]{:S(2)}) collective-permute-start(bf16[27,64,128]{2,1,0:T(8,128)(2,1)S(1)} %get-tuple-element.65), channel_id=1, source_target_pairs={{0,16},{1,17},{2,18},{3,19},{4,20},{5,21},{6,22},{7,23},{8,24},{9,... | collective-permute-start | bytes 1327112 | tf_op jit(solution)/shard_map/ppermute | solution.py:40
  26.1 22.3 %collective-permute-start.14 = (bf16[27,64,128]{2,1,0:T(8,128)(2,1)S(1)}, bf16[27,64,128]{2,1,0:T(8,128)(2,1)S(1)}, u32[]{:S(2)}, u32[]{:S(2)}) collective-permute-start(bf16[27,64,128]{2,1,0:T(8,128)(2,1)S(1)} %get-tuple-element.66), channel_id=1, source_target_pairs={{0,8},{1,9},{2,10},{3,11},{4,12},{5,13},{6,14},{7,15},{8,0},{9,1},... | collective-permute-start | bytes 1327112 | tf_op jit(solution)/shard_map/ppermute | solution.py:40
  35.5 12.9 %collective-permute-start.15 = (bf16[27,64,128]{2,1,0:T(8,128)(2,1)S(1)}, bf16[27,64,128]{2,1,0:T(8,128)(2,1)S(1)}, u32[]{:S(2)}, u32[]{:S(2)}) collective-permute-start(bf16[27,64,128]{2,1,0:T(8,128)(2,1)S(1)} %get-tuple-element.67), channel_id=1, source_target_pairs={{0,24},{1,25},{2,26},{3,27},{4,28},{5,29},{6,30},{7,31},{8,16},{9,... | collective-permute-start | bytes 1327112 | tf_op jit(solution)/shard_map/ppermute | solution.py:40
  44.8 9.5 %collective-permute-start.9 = (bf16[592,128]{1,0:T(8,128)(2,1)S(1)}, bf16[592,128]{1,0:T(8,128)(2,1)S(1)}, u32[]{:S(2)}, u32[]{:S(2)}) collective-permute-start(bf16[592,128]{1,0:T(8,128)(2,1)S(1)} %get-tuple-element.61), channel_id=1, source_target_pairs={{0,16},{1,17},{2,18},{3,19},{4,20},{5,21},{6,22},{7,23},{8,24},{9,... | collective-permute-start | bytes 454664 | tf_op jit(solution)/shard_map/ppermute | solution.py:40
  46.1 9.4 %collective-permute-start.11 = (bf16[592,128]{1,0:T(8,128)(2,1)S(1)}, bf16[592,128]{1,0:T(8,128)(2,1)S(1)}, u32[]{:S(2)}, u32[]{:S(2)}) collective-permute-start(bf16[592,128]{1,0:T(8,128)(2,1)S(1)} %get-tuple-element.63), channel_id=1, source_target_pairs={{0,24},{1,25},{2,26},{3,27},{4,28},{5,29},{6,30},{7,31},{8,16},{9,... | collective-permute-start | bytes 454664 | tf_op jit(solution)/shard_map/ppermute | solution.py:40
  48.3 7.2 %collective-permute-start.10 = (bf16[592,128]{1,0:T(8,128)(2,1)S(1)}, bf16[592,128]{1,0:T(8,128)(2,1)S(1)}, u32[]{:S(2)}, u32[]{:S(2)}) collective-permute-start(bf16[592,128]{1,0:T(8,128)(2,1)S(1)} %get-tuple-element.62.after), channel_id=1, source_target_pairs={{0,8},{1,9},{2,10},{3,11},{4,12},{5,13},{6,14},{7,15},{8,0},{9,1},... | collective-permute-start | bytes 454664 | tf_op jit(solution)/shard_map/ppermute | solution.py:40
  48.9 11.4 %collective-permute-start.17 = (bf16[592,128]{1,0:T(8,128)(2,1)S(1)}, bf16[592,128]{1,0:T(8,128)(2,1)S(1)}, u32[]{:S(2)}, u32[]{:S(2)}) collective-permute-start(bf16[592,128]{1,0:T(8,128)(2,1)S(1)} %get-tuple-element.72), channel_id=1, source_target_pairs={{0,4},{1,5},{2,6},{3,7},{4,0},{5,1},{6,2},{7,3},{8,12},{9,13},{10,... | collective-permute-start | bytes 454664 | tf_op jit(solution)/shard_map/ppermute | solution.py:40
  50.7 9.7 %collective-permute-start.16 = (bf16[576,128]{1,0:T(8,128)(2,1)S(1)}, bf16[576,128]{1,0:T(8,128)(2,1)S(1)}, u32[]{:S(2)}, u32[]{:S(2)}) collective-permute-start(bf16[576,128]{1,0:T(8,128)(2,1)S(1)} %get-tuple-element.71), channel_id=1, source_target_pairs={{0,2},{1,3},{2,0},{3,1},{4,6},{5,7},{6,4},{7,5},{8,10},{9,11},{10,... | collective-permute-start | bytes 442376 | tf_op jit(solution)/shard_map/ppermute | solution.py:40
  54.3 6.0 %collective-permute-start.18 = (bf16[464,128]{1,0:T(8,128)(2,1)S(1)}, bf16[464,128]{1,0:T(8,128)(2,1)S(1)}, u32[]{:S(2)}, u32[]{:S(2)}) collective-permute-start(bf16[464,128]{1,0:T(8,128)(2,1)S(1)} %get-tuple-element.73), channel_id=1, source_target_pairs={{0,6},{1,7},{2,4},{3,5},{4,2},{5,3},{6,0},{7,1},{8,14},{9,15},{10,... | collective-permute-start | bytes 356360 | tf_op jit(solution)/shard_map/ppermute | solution.py:40
  61.2 18.7 %all-to-all-start = ((bf16[8,112,128]{2,1,0:T(8,128)(2,1)}), bf16[8,112,128]{2,1,0:T(8,128)(2,1)S(1)}, u32[]{:S(2)}, u32[]{:S(2)}) async-start(bf16[8,112,128]{2,1,0:T(8,128)(2,1)} %get-tuple-element.76), calls=%async_computation | async-start | bytes 458752 | tf_op jit(solution)/shard_map/all_to_all | solution.py:557

commit v14 on v13

--- a/solution.py
+++ b/solution.py
@@ -86,11 +86,7 @@
     return jnp.dot(chosen, block.reshape(768, 256), preferred_element_type=F32)
 
 
-def pack_kernel(
-    one, two, weight, row, face, outer, corner_face, corner_outer, same_one, same_two, taps, sem
-):
-    copy = pltpu.make_async_copy(weight.at[pl.ds(0, 9)], taps, sem)
-    copy.start()
+def pack_kernel(one, two, row, face, outer, corner_face, corner_outer, same_one, same_two):
     same_one[...], same_two[...] = one[...], two[...]
     edge = 11 * (1 - lax.axis_index("ha"))
     for n, block in enumerate((one, two)):
@@ -101,7 +97,6 @@
         corner_face[n], corner_outer[n] = by_core(lo, hi).astype(BF), by_core(hi, lo).astype(BF)
         for f in range(4):
             row[n, f] = block[f, edge]
-    copy.wait()
 
 
 def pad_block(put, block, row, left, right, corner_left, corner_right):
@@ -148,12 +143,10 @@
     return put
 
 
-def weight_copies(weight, held, sem, first=0):
+def weight_copies(weight, held, sem):
     return [
-        pltpu.make_async_copy(
-            weight.at[pl.ds(a * 9, 9)], held.at[pl.ds((a - first) * 9, 9)], sem.at[a]
-        )
-        for a in range(first, 3)
+        pltpu.make_async_copy(weight.at[pl.ds(a * 9, 9)], held.at[pl.ds(a * 9, 9)], sem.at[a])
+        for a in range(3)
     ]
 
 
@@ -194,7 +187,7 @@
     film_copy.start()
     block_copy = pltpu.make_async_copy(hidden, block, block_sem)
     block_copy.start()
-    copies = weight_copies(weight, taps, tap_sem, 1)
+    copies = weight_copies(weight, taps, tap_sem)
     for copy in copies:
         copy.start()
     order = channel_order()
@@ -230,9 +223,9 @@
             out[f, 16 + n % 6, :, n // 6 * 128 : n // 6 * 128 + 128] = cells
 
 
-def first_kernel(padded, slope, taps, more, wide, hid_out, total):
+def first_kernel(padded, slope, taps, wide, hid_out, total):
     build_shifted(put_back(wide), padded)
-    conv_sum(wide, lambda t: taps[t] if t < 9 else more[t - 9], total)
+    conv_sum(wide, lambda t: taps[t], total)
     hid_out[...] = (total[...] * slope[...]).astype(BF).reshape(4, 12, 16, 256)
 
 
@@ -400,7 +393,7 @@
         out[rows] = jnp.concatenate(halves + rest, axis=0).astype(BF)
 
 
-def last_kernel(own_two, a2, a1, a3, own_one, b2, b1, b3, out, keep, border, held):
+def last_kernel(own_two, a1, a2, a3, own_one, b1, b2, b3, out, keep, border, held):
     for f in range(4):
         for h in range(2):
             lanes = slice(h * 128, h * 128 + 128)
@@ -444,22 +437,20 @@
     taps_two = conv_two.transpose(1, 2, 3, 0, 4).reshape(27, 256, 256)
     wide = near((4, 14, 16, 768), BF)
     def ring(parts, axis):
-        return [send(parts[d - 1], ring_pairs(**{axis: d})) for d in (2, 1, 3)]
-
-    *packed, held_block, held_inputs, held_two = call(
+        return [send(parts[d - 1], ring_pairs(**{axis: d})) for d in (1, 2, 3)]
+
+    *packed, held_block, held_inputs = call(
         pack_kernel,
         "pack_first",
-        (block, inputs, taps_two),
-        "pph",
+        (block, inputs),
+        "pp",
         [near((2, 4, 16, 256), BF)] * 3
         + [near((2, 16, 256), BF)] * 2
-        + [near((4, 12, 16, 256), BF)] * 2
-        + [near((9, 256, 256), BF)],
-        [pltpu.SemaphoreType.DMA],
+        + [near((4, 12, 16, 256), BF)] * 2,
     )
     ways = ((1, 0), (0, 1), (0, 3), (1, 1), (1, 3))
     sides = [send(p, block_pairs(*way)) for p, way in zip(packed, ways)]
-    act, inp, slope, more_two = call(
+    act, inp, slope, held_two = call(
         film_kernel,
         "film",
         (timesteps, held_inputs, hidden, film_table, taps_two),
@@ -468,7 +459,7 @@
             near((768, 256), BF),
             near((4, 12, 16, 256), BF),
             near((768, 256), F32),
-            near((18, 256, 256), BF),
+            near((27, 256, 256), BF),
         ],
         [
             pltpu.VMEM((8, 512), F32),
@@ -489,8 +480,8 @@
     wide_cot, grad_hidden = call(
         first_kernel,
         "conv_two_back",
-        (padded, slope, held_two, more_two),
-        "vvvv",
+        (padded, slope, held_two),
+        "vvv",
         [wide, near((4, 12, 16, 256), BF)],
         [pltpu.VMEM((768, 256), F32)],
     )

time: 81.5 us -> 91 us (1.12)
  waiting for transfers between devices: 28.2 us -> 39.8 us
    ppermute x19, waiting for transfers between devices: 23.2 us -> 34.4 us  [send(): return lax.ppermute(value, AX, pairs)]
    pallas_call x12, Pallas kernels: 20.7 us -> 19.8 us  [call(): pl.pallas_call(kernel, out_shape=tuple((o for o, _ in outs)), in_specs=[s...]
  transfers between devices with their start and end apart: 20 -> 20, of which waited for: 6 -> 6; matrix products, arithmetic and copies ran while one was open for 0% -> 0% of each run, Pallas kernels for 17% -> 15%
where the time goes in v14:
time: 91 us; the launch traced here: 90.8 us
  waiting for transfers between devices  39.8 us (44%)
  starting transfers between devices  29.8 us (33%)
  Pallas kernels  19.8 us (22%)
  between operations  1.39 us (2%)
    ppermute x19, waiting for transfers between devices, send(): return lax.ppermute(value, AX, pairs)  34.4 us
    ppermute x19, starting transfers between devices, send(): return lax.ppermute(value, AX, pairs)  21.7 us
    pallas_call x12, Pallas kernels, call(): pl.pallas_call(kernel, out_shape=tuple((o for o, _ in outs)), in_specs=[s...  19.8 us
    all_to_all x1, starting transfers between devices, shards(): planes = lax.all_to_all(out, 'z', 0, 0, tiled=True)  8.09 us
    all_to_all x1, waiting for transfers between devices, shards(): planes = lax.all_to_all(out, 'z', 0, 0, tiled=True)  5.43 us
  transfers between devices with their start and end apart: 20, of which 6 were waited for; matrix products, arithmetic and copies ran while one was open for 0% of the time, Pallas kernels for 15%

profile of v14, /device:TPU:24, one launch (start us, length us, event | category | flops | bytes accessed | tf_op | source)
XLA Modules:
  0.0 90.8 jit_solution(7081011669160099945)
XLA Ops:
  0.6 1.4 %pack_first.1 = (bf16[2,4,16,256]{3,2,1,0:T(8,128)(2,1)S(1)}, bf16[2,4,16,256]{3,2,1,0:T(8,128)(2,1)S(1)}, bf16[2,4,16,256]{3,2,1,0:T(8,128)(2,1)S(1)}, bf16[2,1...) custom-call(bf16[4,12,16,256]{3,2,1,0:T(8,128)(2,1)} %bitcast.18, ...), custom_call_target="tpu_custom_call" | custom-call | tf_op jit(solution)/shard_map/pack_first/pallas_call | solution.py:50
  2.1 1.6 %collective-permute-start = (bf16[2,4,16,256]{3,2,1,0:T(8,128)(2,1)S(1)}, bf16[2,4,16,256]{3,2,1,0:T(8,128)(2,1)S(1)}, u32[]{:S(2)}, u32[]{:S(2)}) collective-permute-start(bf16[2,4,16,256]{3,2,1,0:T(8,128)(2,1)S(1)} %get-tuple-element.41), channel_id=1, source_target_pairs={{0,4},{1,5},{2,6},{3,7},{4,0},{5,1},{6,2},{7,3},{8,12},{9,13},{10,... | collective-permute-start | bytes 196616 | tf_op jit(solution)/shard_map/ppermute | solution.py:40
  3.7 2.8 %collective-permute-start.2 = (bf16[2,4,16,256]{3,2,1,0:T(8,128)(2,1)S(1)}, bf16[2,4,16,256]{3,2,1,0:T(8,128)(2,1)S(1)}, u32[]{:S(2)}, u32[]{:S(2)}) collective-permute-start(bf16[2,4,16,256]{3,2,1,0:T(8,128)(2,1)S(1)} %get-tuple-element.43), channel_id=1, source_target_pairs={{0,3},{1,2},{2,1},{3,0},{4,7},{5,6},{6,5},{7,4},{8,11},{9,10},{10,... | collective-permute-start | bytes 196616 | tf_op jit(solution)/shard_map/ppermute | solution.py:40
  6.5 1.1 %collective-permute-start.4 = (bf16[2,16,256]{2,1,0:T(8,128)(2,1)S(1)}, bf16[2,16,256]{2,1,0:T(8,128)(2,1)S(1)}, u32[]{:S(2)}, u32[]{:S(2)}) collective-permute-start(bf16[2,16,256]{2,1,0:T(8,128)(2,1)S(1)} %get-tuple-element.45), channel_id=1, source_target_pairs={{0,7},{1,6},{2,5},{3,4},{4,3},{5,2},{6,1},{7,0},{8,15},{9,14},{10,... | collective-permute-start | bytes 49160 | tf_op jit(solution)/shard_map/ppermute | solution.py:40
  8.2 2.2 %film.1 = (bf16[768,256]{1,0:T(8,128)(2,1)S(1)}, bf16[4,12,16,256]{3,2,1,0:T(8,128)(2,1)S(1)}, f32[768,256]{1,0:T(8,128)S(1)}, bf16[27,256,256]{2,1,0:T(8,128)(2,1)S(1)}) custom-call(s32[1]{0:T(128)S(6)} %copy.10.step, bf16[4,12,16,256]{3,2,1,0:T(8,128)(2,1)S(1)} %get-tuple-element.46.inputs, bf16[4,12,16,256]{3,2,1,0:T(8,128)(2,1)} %bitcast.21, ...), custom_call_target="tpu_custom_call" | custom-call | tf_op jit(solution)/shard_map/film/pallas_call | solution.py:50
  11.4 2.3 %conv_two_back.1 = (bf16[4,14,16,768]{3,2,1,0:T(8,128)(2,1)S(1)}, bf16[4,12,16,256]{3,2,1,0:T(8,128)(2,1)S(1)}) custom-call(bf16[4,22,16,256]{3,2,1,0:T(8,128)(2,1)S(1)} %pad_cotangent.1.padded, f32[768,256]{1,0:T(8,128)S(1)} %get-tuple-element.48.slope, bf16[27,256,256]{2,1,0:T(8,128)(2,1)S(1)} %get-tuple-element.49.taps), custom_call_target="tpu_custom_call" | custom-call | tf_op jit(solution)/shard_map/conv_two_back/pallas_call | solution.py:50
  13.7 3.1 %grad_one.1 = (f32[4,27,64,128]{3,2,1,0:T(8,128)S(1)}, f32[4,28,64,128]{3,2,1,0:T(8,128)S(1)}) custom-call(bf16[4,12,16,256]{3,2,1,0:T(8,128)(2,1)S(1)} %get-tuple-element.50.hid, bf16[4,12,16,256]{3,2,1,0:T(8,128)(2,1)S(1)} %get-tuple-element.52.inp, bf16[2,4,16,256]{3,2,1,0:T(8,128)(2,1)S(1)} %collective-permute-done.row, ...), custom_call_target="tpu_custom_call" | custom-call | tf_op jit(solution)/shard_map/grad_one/pallas_call | solution.py:50
  17.0 2.7 %grad_two.1 = (f32[9,32,768]{2,1,0:T(8,128)S(1)}, bf16[9,32,768]{2,1,0:T(8,128)(2,1)S(1)}, bf16[9,32,768]{2,1,0:T(8,128)(2,1)S(1)}, bf16[9,32,768]{2,1,0:T(8,128)(2,1)S(1)}) custom-call(bf16[4,14,16,768]{3,2,1,0:T(8,128)(2,1)S(1)} %get-tuple-element.51.wide, bf16[768,256]{1,0:T(8,128)(2,1)S(1)} %get-tuple-element.47.act, ...), custom_call_target="tpu_custom_call" | custom-call | tf_op jit(solution)/shard_map/grad_two/pallas_call | solution.py:50
  19.7 2.6 %collective-permute-start.7 = (bf16[9,32,768]{2,1,0:T(8,128)(2,1)S(1)}, bf16[9,32,768]{2,1,0:T(8,128)(2,1)S(1)}, u32[]{:S(2)}, u32[]{:S(2)}) collective-permute-start(bf16[9,32,768]{2,1,0:T(8,128)(2,1)S(1)} %get-tuple-element.55), channel_id=1, source_target_pairs={{0,2},{1,3},{2,0},{3,1},{4,6},{5,7},{6,4},{7,5},{8,10},{9,11},{10,... | collective-permute-start | bytes 1327112 | tf_op jit(solution)/shard_map/ppermute | solution.py:40
  23.8 0.8 collective-permute-start.13
  24.6 2.0 %collective-permute-start.14 = (bf16[27,64,128]{2,1,0:T(8,128)(2,1)S(1)}, bf16[27,64,128]{2,1,0:T(8,128)(2,1)S(1)}, u32[]{:S(2)}, u32[]{:S(2)}) collective-permute-start(bf16[27,64,128]{2,1,0:T(8,128)(2,1)S(1)} %get-tuple-element.64), channel_id=1, source_target_pairs={{0,16},{1,17},{2,18},{3,19},{4,20},{5,21},{6,22},{7,23},{8,24},{9,... | collective-permute-start | bytes 1327112 | tf_op jit(solution)/shard_map/ppermute | solution.py:40
  26.7 7.9 %collective-permute-done.7.got2 = bf16[9,32,768]{2,1,0:T(8,128)(2,1)S(1)} collective-permute-done((bf16[9,32,768]{2,1,0:T(8,128)(2,1)S(1)}, bf16[9,32,768]{2,1,0:T(8,128)(2,1)S(1)}, u32[]{:S(2)}, u32[]{:S(2)}) %collective-permute-start.7) | collective-permute-done | bytes 442400 | tf_op jit(solution)/shard_map/ppermute | solution.py:40
  35.1 8.3 %collective-permute-done.8.got3 = bf16[9,32,768]{2,1,0:T(8,128)(2,1)S(1)} collective-permute-done((bf16[9,32,768]{2,1,0:T(8,128)(2,1)S(1)}, bf16[9,32,768]{2,1,0:T(8,128)(2,1)S(1)}, u32[]{:S(2)}, u32[]{:S(2)}) %collective-permute-start.8) | collective-permute-done | bytes 442400 | tf_op jit(solution)/shard_map/ppermute | solution.py:40
  43.8 1.3 %collective-permute-start.10 = (bf16[592,128]{1,0:T(8,128)(2,1)S(1)}, bf16[592,128]{1,0:T(8,128)(2,1)S(1)}, u32[]{:S(2)}, u32[]{:S(2)}) collective-permute-start(bf16[592,128]{1,0:T(8,128)(2,1)S(1)} %get-tuple-element.60), channel_id=1, source_target_pairs={{0,16},{1,17},{2,18},{3,19},{4,20},{5,21},{6,22},{7,23},{8,24},{9,... | collective-permute-start | bytes 454664 | tf_op jit(solution)/shard_map/ppermute | solution.py:40
  45.1 2.2 %collective-permute-start.11 = (bf16[592,128]{1,0:T(8,128)(2,1)S(1)}, bf16[592,128]{1,0:T(8,128)(2,1)S(1)}, u32[]{:S(2)}, u32[]{:S(2)}) collective-permute-start(bf16[592,128]{1,0:T(8,128)(2,1)S(1)} %get-tuple-element.61), channel_id=1, source_target_pairs={{0,24},{1,25},{2,26},{3,27},{4,28},{5,29},{6,30},{7,31},{8,16},{9,... | collective-permute-start | bytes 454664 | tf_op jit(solution)/shard_map/ppermute | solution.py:40
  47.4 11.1 %collective-permute-done.15.got3 = bf16[27,64,128]{2,1,0:T(8,128)(2,1)S(1)} collective-permute-done((bf16[27,64,128]{2,1,0:T(8,128)(2,1)S(1)}, bf16[27,64,128]{2,1,0:T(8,128)(2,1)S(1)}, u32[]{:S(2)}, u32[]{:S(2)}) %collective-permute-start.15) | collective-permute-done | bytes 442400 | tf_op jit(solution)/shard_map/ppermute | solution.py:40
  59.0 1.8 %collective-permute-start.16 = (bf16[592,128]{1,0:T(8,128)(2,1)S(1)}, bf16[592,128]{1,0:T(8,128)(2,1)S(1)}, u32[]{:S(2)}, u32[]{:S(2)}) collective-permute-start(bf16[592,128]{1,0:T(8,128)(2,1)S(1)} %get-tuple-element.69), channel_id=1, source_target_pairs={{0,4},{1,5},{2,6},{3,7},{4,0},{5,1},{6,2},{7,3},{8,12},{9,13},{10,... | collective-permute-start | bytes 454664 | tf_op jit(solution)/shard_map/ppermute | solution.py:40
  60.8 1.4 %collective-permute-start.17 = (bf16[576,128]{1,0:T(8,128)(2,1)S(1)}, bf16[576,128]{1,0:T(8,128)(2,1)S(1)}, u32[]{:S(2)}, u32[]{:S(2)}) collective-permute-start(bf16[576,128]{1,0:T(8,128)(2,1)S(1)} %get-tuple-element.70), channel_id=1, source_target_pairs={{0,2},{1,3},{2,0},{3,1},{4,6},{5,7},{6,4},{7,5},{8,10},{9,11},{10,... | collective-permute-start | bytes 442376 | tf_op jit(solution)/shard_map/ppermute | solution.py:40
  62.2 1.6 %collective-permute-start.18 = (bf16[464,128]{1,0:T(8,128)(2,1)S(1)}, bf16[464,128]{1,0:T(8,128)(2,1)S(1)}, u32[]{:S(2)}, u32[]{:S(2)}) collective-permute-start(bf16[464,128]{1,0:T(8,128)(2,1)S(1)} %get-tuple-element.71), channel_id=1, source_target_pairs={{0,6},{1,7},{2,4},{3,5},{4,2},{5,3},{6,0},{7,1},{8,14},{9,15},{10,... | collective-permute-start | bytes 356360 | tf_op jit(solution)/shard_map/ppermute | solution.py:40
  63.8 6.7 %collective-permute-done.18.b3 = bf16[464,128]{1,0:T(8,128)(2,1)S(1)} collective-permute-done((bf16[464,128]{1,0:T(8,128)(2,1)S(1)}, bf16[464,128]{1,0:T(8,128)(2,1)S(1)}, u32[]{:S(2)}, u32[]{:S(2)}) %collective-permute-start.18) | collective-permute-done | bytes 118816 | tf_op jit(solution)/shard_map/ppermute | solution.py:40
  70.5 0.8 last_stage.1
  71.4 8.1 %all-to-all-start = ((bf16[8,112,128]{2,1,0:T(8,128)(2,1)}), bf16[8,112,128]{2,1,0:T(8,128)(2,1)S(1)}, u32[]{:S(2)}, u32[]{:S(2)}) async-start(bf16[8,112,128]{2,1,0:T(8,128)(2,1)} %get-tuple-element.74), calls=%async_computation | async-start | bytes 458752 | tf_op jit(solution)/shard_map/all_to_all | solution.py:548
  79.5 5.1 %conv_one_back.1.after = bf16[4,12,16,256]{3,2,1,0:T(8,128)(2,1)} custom-call(bf16[4,12,16,256]{3,2,1,0:T(8,128)(2,1)S(1)} %get-tuple-element.50.hid, bf16[4,12,16,256]{3,2,1,0:T(8,128)(2,1)} %bitcast.19, bf16[10,16,256]{2,1,0:T(8,128)(2,1)S(1)} %get-tuple-element.72.border, bf16[2,4,16,256]{3,2,1,0:T(8,128)(2,1)S(1)} %get-tuple-element.67.cols, ...), custom_call_target="tpu_custom_call" | custom-call | tf_op jit(solution)/shard_map/conv_one_back/pallas_call | solution.py:50
  84.6 5.4 %all-to-all-done.got = bf16[8,112,128]{2,1,0:T(8,128)(2,1)S(1)} async-done(((bf16[8,112,128]{2,1,0:T(8,128)(2,1)}), bf16[8,112,128]{2,1,0:T(8,128)(2,1)S(1)}, u32[]{:S(2)}, u32[]{:S(2)}) %all-to-all-start) | async-done | bytes 229408 | tf_op jit(solution)/shard_map/all_to_all | solution.py:548
  (28 shorter events, 5.1 us)
Async XLA Ops:
  2.1 8.8 %collective-permute-start = (bf16[2,4,16,256]{3,2,1,0:T(8,128)(2,1)S(1)}, bf16[2,4,16,256]{3,2,1,0:T(8,128)(2,1)S(1)}, u32[]{:S(2)}, u32[]{:S(2)}) collective-permute-start(bf16[2,4,16,256]{3,2,1,0:T(8,128)(2,1)S(1)} %get-tuple-element.41), channel_id=1, source_target_pairs={{0,4},{1,5},{2,6},{3,7},{4,0},{5,1},{6,2},{7,3},{8,12},{9,13},{10,... | collective-permute-start | bytes 196616 | tf_op jit(solution)/shard_map/ppermute | solution.py:40
  3.7 7.2 %collective-permute-start.1 = (bf16[2,4,16,256]{3,2,1,0:T(8,128)(2,1)S(1)}, bf16[2,4,16,256]{3,2,1,0:T(8,128)(2,1)S(1)}, u32[]{:S(2)}, u32[]{:S(2)}) collective-permute-start(bf16[2,4,16,256]{3,2,1,0:T(8,128)(2,1)S(1)} %get-tuple-element.42), channel_id=1, source_target_pairs={{0,1},{1,0},{2,3},{3,2},{4,5},{5,4},{6,7},{7,6},{8,9},{9,8},{10,11... | collective-permute-start | bytes 196616 | tf_op jit(solution)/shard_map/ppermute | solution.py:40
  3.7 7.2 %collective-permute-start.2 = (bf16[2,4,16,256]{3,2,1,0:T(8,128)(2,1)S(1)}, bf16[2,4,16,256]{3,2,1,0:T(8,128)(2,1)S(1)}, u32[]{:S(2)}, u32[]{:S(2)}) collective-permute-start(bf16[2,4,16,256]{3,2,1,0:T(8,128)(2,1)S(1)} %get-tuple-element.43), channel_id=1, source_target_pairs={{0,3},{1,2},{2,1},{3,0},{4,7},{5,6},{6,5},{7,4},{8,11},{9,10},{10,... | collective-permute-start | bytes 196616 | tf_op jit(solution)/shard_map/ppermute | solution.py:40
  6.5 4.0 %collective-permute-start.3 = (bf16[2,16,256]{2,1,0:T(8,128)(2,1)S(1)}, bf16[2,16,256]{2,1,0:T(8,128)(2,1)S(1)}, u32[]{:S(2)}, u32[]{:S(2)}) collective-permute-start(bf16[2,16,256]{2,1,0:T(8,128)(2,1)S(1)} %get-tuple-element.44), channel_id=1, source_target_pairs={{0,5},{1,4},{2,7},{3,6},{4,1},{5,0},{6,3},{7,2},{8,13},{9,12},{10,... | collective-permute-start | bytes 49160 | tf_op jit(solution)/shard_map/ppermute | solution.py:40
  6.5 4.4 %collective-permute-start.4 = (bf16[2,16,256]{2,1,0:T(8,128)(2,1)S(1)}, bf16[2,16,256]{2,1,0:T(8,128)(2,1)S(1)}, u32[]{:S(2)}, u32[]{:S(2)}) collective-permute-start(bf16[2,16,256]{2,1,0:T(8,128)(2,1)S(1)} %get-tuple-element.45), channel_id=1, source_target_pairs={{0,7},{1,6},{2,5},{3,4},{4,3},{5,2},{6,1},{7,0},{8,15},{9,14},{10,... | collective-permute-start | bytes 49160 | tf_op jit(solution)/shard_map/ppermute | solution.py:40
  11.0 2.7 %collective-permute-start.5 = (bf16[4,22,16,256]{3,2,1,0:T(8,128)(2,1)S(1)}, bf16[4,22,16,256]{3,2,1,0:T(8,128)(2,1)S(1)}, u32[]{:S(2)}, u32[]{:S(2)}) collective-permute-start(bf16[4,22,16,256]{3,2,1,0:T(8,128)(2,1)S(1)} %pad_cotangent.1.padded), channel_id=1, source_target_pairs={{0,1},{1,0},{2,3},{3,2},{4,5},{5,4},{6,7},{7,6},{8,9},{9,8},{10,11... | collective-permute-start | bytes 2162696 | tf_op jit(solution)/shard_map/ppermute | solution.py:40
  16.8 6.7 %collective-permute-start.12 = (f32[4,28,64,128]{3,2,1,0:T(8,128)S(1)}, f32[4,28,64,128]{3,2,1,0:T(8,128)S(1)}, u32[]{:S(2)}, u32[]{:S(2)}) collective-permute-start(f32[4,28,64,128]{3,2,1,0:T(8,128)S(1)} %get-tuple-element.53.after), channel_id=1, source_target_pairs={{0,1},{1,0},{2,3},{3,2},{4,5},{5,4},{6,7},{7,6},{8,9},{9,8},{10,11... | collective-permute-start | bytes 11010056 | tf_op jit(solution)/shard_map/ppermute | solution.py:40
  19.7 14.8 %collective-permute-start.7 = (bf16[9,32,768]{2,1,0:T(8,128)(2,1)S(1)}, bf16[9,32,768]{2,1,0:T(8,128)(2,1)S(1)}, u32[]{:S(2)}, u32[]{:S(2)}) collective-permute-start(bf16[9,32,768]{2,1,0:T(8,128)(2,1)S(1)} %get-tuple-element.55), channel_id=1, source_target_pairs={{0,2},{1,3},{2,0},{3,1},{4,6},{5,7},{6,4},{7,5},{8,10},{9,11},{10,... | collective-permute-start | bytes 1327112 | tf_op jit(solution)/shard_map/ppermute | solution.py:40
  22.3 21.1 %collective-permute-start.8 = (bf16[9,32,768]{2,1,0:T(8,128)(2,1)S(1)}, bf16[9,32,768]{2,1,0:T(8,128)(2,1)S(1)}, u32[]{:S(2)}, u32[]{:S(2)}) collective-permute-start(bf16[9,32,768]{2,1,0:T(8,128)(2,1)S(1)} %get-tuple-element.56), channel_id=1, source_target_pairs={{0,6},{1,7},{2,4},{3,5},{4,2},{5,3},{6,0},{7,1},{8,14},{9,15},{10,... | collective-permute-start | bytes 1327112 | tf_op jit(solution)/shard_map/ppermute | solution.py:40
  23.1 20.3 %collective-permute-start.6 = (bf16[9,32,768]{2,1,0:T(8,128)(2,1)S(1)}, bf16[9,32,768]{2,1,0:T(8,128)(2,1)S(1)}, u32[]{:S(2)}, u32[]{:S(2)}) collective-permute-start(bf16[9,32,768]{2,1,0:T(8,128)(2,1)S(1)} %get-tuple-element.54.after), channel_id=1, source_target_pairs={{0,4},{1,5},{2,6},{3,7},{4,0},{5,1},{6,2},{7,3},{8,12},{9,13},{10,... | collective-permute-start | bytes 1327112 | tf_op jit(solution)/shard_map/ppermute | solution.py:40
  23.8 23.5 %collective-permute-start.13 = (bf16[27,64,128]{2,1,0:T(8,128)(2,1)S(1)}, bf16[27,64,128]{2,1,0:T(8,128)(2,1)S(1)}, u32[]{:S(2)}, u32[]{:S(2)}) collective-permute-start(bf16[27,64,128]{2,1,0:T(8,128)(2,1)S(1)} %get-tuple-element.63), channel_id=1, source_target_pairs={{0,8},{1,9},{2,10},{3,11},{4,12},{5,13},{6,14},{7,15},{8,0},{9,1},... | collective-permute-start | bytes 1327112 | tf_op jit(solution)/shard_map/ppermute | solution.py:40
  24.6 22.8 %collective-permute-start.14 = (bf16[27,64,128]{2,1,0:T(8,128)(2,1)S(1)}, bf16[27,64,128]{2,1,0:T(8,128)(2,1)S(1)}, u32[]{:S(2)}, u32[]{:S(2)}) collective-permute-start(bf16[27,64,128]{2,1,0:T(8,128)(2,1)S(1)} %get-tuple-element.64), channel_id=1, source_target_pairs={{0,16},{1,17},{2,18},{3,19},{4,20},{5,21},{6,22},{7,23},{8,24},{9,... | collective-permute-start | bytes 1327112 | tf_op jit(solution)/shard_map/ppermute | solution.py:40
  34.5 23.9 %collective-permute-start.15 = (bf16[27,64,128]{2,1,0:T(8,128)(2,1)S(1)}, bf16[27,64,128]{2,1,0:T(8,128)(2,1)S(1)}, u32[]{:S(2)}, u32[]{:S(2)}) collective-permute-start(bf16[27,64,128]{2,1,0:T(8,128)(2,1)S(1)} %get-tuple-element.65), channel_id=1, source_target_pairs={{0,24},{1,25},{2,26},{3,27},{4,28},{5,29},{6,30},{7,31},{8,16},{9,... | collective-permute-start | bytes 1327112 | tf_op jit(solution)/shard_map/ppermute | solution.py:40
  43.8 18.4 %collective-permute-start.10 = (bf16[592,128]{1,0:T(8,128)(2,1)S(1)}, bf16[592,128]{1,0:T(8,128)(2,1)S(1)}, u32[]{:S(2)}, u32[]{:S(2)}) collective-permute-start(bf16[592,128]{1,0:T(8,128)(2,1)S(1)} %get-tuple-element.60), channel_id=1, source_target_pairs={{0,16},{1,17},{2,18},{3,19},{4,20},{5,21},{6,22},{7,23},{8,24},{9,... | collective-permute-start | bytes 454664 | tf_op jit(solution)/shard_map/ppermute | solution.py:40
  45.1 18.7 %collective-permute-start.11 = (bf16[592,128]{1,0:T(8,128)(2,1)S(1)}, bf16[592,128]{1,0:T(8,128)(2,1)S(1)}, u32[]{:S(2)}, u32[]{:S(2)}) collective-permute-start(bf16[592,128]{1,0:T(8,128)(2,1)S(1)} %get-tuple-element.61), channel_id=1, source_target_pairs={{0,24},{1,25},{2,26},{3,27},{4,28},{5,29},{6,30},{7,31},{8,16},{9,... | collective-permute-start | bytes 454664 | tf_op jit(solution)/shard_map/ppermute | solution.py:40
  47.3 16.5 %collective-permute-start.9 = (bf16[592,128]{1,0:T(8,128)(2,1)S(1)}, bf16[592,128]{1,0:T(8,128)(2,1)S(1)}, u32[]{:S(2)}, u32[]{:S(2)}) collective-permute-start(bf16[592,128]{1,0:T(8,128)(2,1)S(1)} %get-tuple-element.59.after), channel_id=1, source_target_pairs={{0,8},{1,9},{2,10},{3,11},{4,12},{5,13},{6,14},{7,15},{8,0},{9,1},... | collective-permute-start | bytes 454664 | tf_op jit(solution)/shard_map/ppermute | solution.py:40
  59.0 11.5 %collective-permute-start.16 = (bf16[592,128]{1,0:T(8,128)(2,1)S(1)}, bf16[592,128]{1,0:T(8,128)(2,1)S(1)}, u32[]{:S(2)}, u32[]{:S(2)}) collective-permute-start(bf16[592,128]{1,0:T(8,128)(2,1)S(1)} %get-tuple-element.69), channel_id=1, source_target_pairs={{0,4},{1,5},{2,6},{3,7},{4,0},{5,1},{6,2},{7,3},{8,12},{9,13},{10,... | collective-permute-start | bytes 454664 | tf_op jit(solution)/shard_map/ppermute | solution.py:40
  60.8 9.8 %collective-permute-start.17 = (bf16[576,128]{1,0:T(8,128)(2,1)S(1)}, bf16[576,128]{1,0:T(8,128)(2,1)S(1)}, u32[]{:S(2)}, u32[]{:S(2)}) collective-permute-start(bf16[576,128]{1,0:T(8,128)(2,1)S(1)} %get-tuple-element.70), channel_id=1, source_target_pairs={{0,2},{1,3},{2,0},{3,1},{4,6},{5,7},{6,4},{7,5},{8,10},{9,11},{10,... | collective-permute-start | bytes 442376 | tf_op jit(solution)/shard_map/ppermute | solution.py:40
  62.2 8.3 %collective-permute-start.18 = (bf16[464,128]{1,0:T(8,128)(2,1)S(1)}, bf16[464,128]{1,0:T(8,128)(2,1)S(1)}, u32[]{:S(2)}, u32[]{:S(2)}) collective-permute-start(bf16[464,128]{1,0:T(8,128)(2,1)S(1)} %get-tuple-element.71), channel_id=1, source_target_pairs={{0,6},{1,7},{2,4},{3,5},{4,2},{5,3},{6,0},{7,1},{8,14},{9,15},{10,... | collective-permute-start | bytes 356360 | tf_op jit(solution)/shard_map/ppermute | solution.py:40
  71.4 18.6 %all-to-all-start = ((bf16[8,112,128]{2,1,0:T(8,128)(2,1)}), bf16[8,112,128]{2,1,0:T(8,128)(2,1)S(1)}, u32[]{:S(2)}, u32[]{:S(2)}) async-start(bf16[8,112,128]{2,1,0:T(8,128)(2,1)} %get-tuple-element.74), calls=%async_computation | async-start | bytes 458752 | tf_op jit(solution)/shard_map/all_to_all | solution.py:548

commit v15 on v14

--- a/solution.py
+++ b/solution.py
@@ -393,7 +393,7 @@
         out[rows] = jnp.concatenate(halves + rest, axis=0).astype(BF)
 
 
-def last_kernel(own_two, a1, a2, a3, own_one, b1, b2, b3, out, keep, border, held):
+def last_kernel(own_two, a2, a1, a3, own_one, b2, b1, b3, out, keep, border, held):
     for f in range(4):
         for h in range(2):
             lanes = slice(h * 128, h * 128 + 128)
@@ -437,7 +437,7 @@
     taps_two = conv_two.transpose(1, 2, 3, 0, 4).reshape(27, 256, 256)
     wide = near((4, 14, 16, 768), BF)
     def ring(parts, axis):
-        return [send(parts[d - 1], ring_pairs(**{axis: d})) for d in (1, 2, 3)]
+        return [send(parts[d - 1], ring_pairs(**{axis: d})) for d in (2, 1, 3)]
 
     *packed, held_block, held_inputs = call(
         pack_kernel,

time: 91 us -> 80.9 us (0.89); the launches traced: 90.8 us -> 79.7 us
  waiting for transfers between devices: 39.8 us -> 27.8 us
    ppermute x19, waiting for transfers between devices: 34.4 us -> 22.8 us  [send(): return lax.ppermute(value, AX, pairs)]
  transfers between devices with their start and end apart: 20 -> 20, of which waited for: 6 -> 6; matrix products, arithmetic and copies ran while one was open for 0% -> 0% of each run, Pallas kernels for 15% -> 17%
where the time goes in v15:
time: 80.9 us; the launch traced here: 79.7 us
  starting transfers between devices  30.7 us (38%)
  waiting for transfers between devices  27.8 us (34%)
  Pallas kernels  19.8 us (24%)
  between operations  1.39 us (2%)
    ppermute x19, waiting for transfers between devices, send(): return lax.ppermute(value, AX, pairs)  22.8 us
    ppermute x19, starting transfers between devices, send(): return lax.ppermute(value, AX, pairs)  22.3 us
    pallas_call x12, Pallas kernels, call(): pl.pallas_call(kernel, out_shape=tuple((o for o, _ in outs)), in_specs=[s...  19.8 us
    all_to_all x1, starting transfers between devices, shards(): planes = lax.all_to_all(out, 'z', 0, 0, tiled=True)  8.48 us
    all_to_all x1, waiting for transfers between devices, shards(): planes = lax.all_to_all(out, 'z', 0, 0, tiled=True)  5.01 us
  transfers between devices with their start and end apart: 20, of which 6 were waited for; matrix products, arithmetic and copies ran while one was open for 0% of the time, Pallas kernels for 17%

profile of v15, /device:TPU:24, one launch (start us, length us, event | category | flops | bytes accessed | tf_op | source)
XLA Modules:
  0.0 79.7 jit_solution(13014257074733506038)
XLA Ops:
  0.6 1.4 %pack_first.1 = (bf16[2,4,16,256]{3,2,1,0:T(8,128)(2,1)S(1)}, bf16[2,4,16,256]{3,2,1,0:T(8,128)(2,1)S(1)}, bf16[2,4,16,256]{3,2,1,0:T(8,128)(2,1)S(1)}, bf16[2,1...) custom-call(bf16[4,12,16,256]{3,2,1,0:T(8,128)(2,1)} %bitcast.18, ...), custom_call_target="tpu_custom_call" | custom-call | tf_op jit(solution)/shard_map/pack_first/pallas_call | solution.py:50
  2.1 1.6 %collective-permute-start = (bf16[2,4,16,256]{3,2,1,0:T(8,128)(2,1)S(1)}, bf16[2,4,16,256]{3,2,1,0:T(8,128)(2,1)S(1)}, u32[]{:S(2)}, u32[]{:S(2)}) collective-permute-start(bf16[2,4,16,256]{3,2,1,0:T(8,128)(2,1)S(1)} %get-tuple-element.41), channel_id=1, source_target_pairs={{0,4},{1,5},{2,6},{3,7},{4,0},{5,1},{6,2},{7,3},{8,12},{9,13},{10,... | collective-permute-start | bytes 196616 | tf_op jit(solution)/shard_map/ppermute | solution.py:40
  3.7 2.8 %collective-permute-start.2 = (bf16[2,4,16,256]{3,2,1,0:T(8,128)(2,1)S(1)}, bf16[2,4,16,256]{3,2,1,0:T(8,128)(2,1)S(1)}, u32[]{:S(2)}, u32[]{:S(2)}) collective-permute-start(bf16[2,4,16,256]{3,2,1,0:T(8,128)(2,1)S(1)} %get-tuple-element.43), channel_id=1, source_target_pairs={{0,3},{1,2},{2,1},{3,0},{4,7},{5,6},{6,5},{7,4},{8,11},{9,10},{10,... | collective-permute-start | bytes 196616 | tf_op jit(solution)/shard_map/ppermute | solution.py:40
  6.5 1.1 %collective-permute-start.4 = (bf16[2,16,256]{2,1,0:T(8,128)(2,1)S(1)}, bf16[2,16,256]{2,1,0:T(8,128)(2,1)S(1)}, u32[]{:S(2)}, u32[]{:S(2)}) collective-permute-start(bf16[2,16,256]{2,1,0:T(8,128)(2,1)S(1)} %get-tuple-element.45), channel_id=1, source_target_pairs={{0,7},{1,6},{2,5},{3,4},{4,3},{5,2},{6,1},{7,0},{8,15},{9,14},{10,... | collective-permute-start | bytes 49160 | tf_op jit(solution)/shard_map/ppermute | solution.py:40
  8.2 2.2 %film.1 = (bf16[768,256]{1,0:T(8,128)(2,1)S(1)}, bf16[4,12,16,256]{3,2,1,0:T(8,128)(2,1)S(1)}, f32[768,256]{1,0:T(8,128)S(1)}, bf16[27,256,256]{2,1,0:T(8,128)(2,1)S(1)}) custom-call(s32[1]{0:T(128)S(6)} %copy.10.step, bf16[4,12,16,256]{3,2,1,0:T(8,128)(2,1)S(1)} %get-tuple-element.46.inputs, bf16[4,12,16,256]{3,2,1,0:T(8,128)(2,1)} %bitcast.21, ...), custom_call_target="tpu_custom_call" | custom-call | tf_op jit(solution)/shard_map/film/pallas_call | solution.py:50
  11.4 2.3 %conv_two_back.1 = (bf16[4,14,16,768]{3,2,1,0:T(8,128)(2,1)S(1)}, bf16[4,12,16,256]{3,2,1,0:T(8,128)(2,1)S(1)}) custom-call(bf16[4,22,16,256]{3,2,1,0:T(8,128)(2,1)S(1)} %pad_cotangent.1.padded, f32[768,256]{1,0:T(8,128)S(1)} %get-tuple-element.48.slope, bf16[27,256,256]{2,1,0:T(8,128)(2,1)S(1)} %get-tuple-element.49.taps), custom_call_target="tpu_custom_call" | custom-call | tf_op jit(solution)/shard_map/conv_two_back/pallas_call | solution.py:50
  13.7 3.1 %grad_one.1 = (f32[4,27,64,128]{3,2,1,0:T(8,128)S(1)}, f32[4,28,64,128]{3,2,1,0:T(8,128)S(1)}) custom-call(bf16[4,12,16,256]{3,2,1,0:T(8,128)(2,1)S(1)} %get-tuple-element.50.hid, bf16[4,12,16,256]{3,2,1,0:T(8,128)(2,1)S(1)} %get-tuple-element.52.inp, bf16[2,4,16,256]{3,2,1,0:T(8,128)(2,1)S(1)} %collective-permute-done.row, ...), custom_call_target="tpu_custom_call" | custom-call | tf_op jit(solution)/shard_map/grad_one/pallas_call | solution.py:50
  17.0 2.7 %grad_two.1 = (f32[9,32,768]{2,1,0:T(8,128)S(1)}, bf16[9,32,768]{2,1,0:T(8,128)(2,1)S(1)}, bf16[9,32,768]{2,1,0:T(8,128)(2,1)S(1)}, bf16[9,32,768]{2,1,0:T(8,128)(2,1)S(1)}) custom-call(bf16[4,14,16,768]{3,2,1,0:T(8,128)(2,1)S(1)} %get-tuple-element.51.wide, bf16[768,256]{1,0:T(8,128)(2,1)S(1)} %get-tuple-element.47.act, ...), custom_call_target="tpu_custom_call" | custom-call | tf_op jit(solution)/shard_map/grad_two/pallas_call | solution.py:50
  19.7 2.6 %collective-permute-start.6 = (bf16[9,32,768]{2,1,0:T(8,128)(2,1)S(1)}, bf16[9,32,768]{2,1,0:T(8,128)(2,1)S(1)}, u32[]{:S(2)}, u32[]{:S(2)}) collective-permute-start(bf16[9,32,768]{2,1,0:T(8,128)(2,1)S(1)} %get-tuple-element.54), channel_id=1, source_target_pairs={{0,2},{1,3},{2,0},{3,1},{4,6},{5,7},{6,4},{7,5},{8,10},{9,11},{10,... | collective-permute-start | bytes 1327112 | tf_op jit(solution)/shard_map/ppermute | solution.py:40
  22.3 0.8 collective-permute-start.8
  23.8 1.3 %collective-permute-start.13 = (bf16[27,64,128]{2,1,0:T(8,128)(2,1)S(1)}, bf16[27,64,128]{2,1,0:T(8,128)(2,1)S(1)}, u32[]{:S(2)}, u32[]{:S(2)}) collective-permute-start(bf16[27,64,128]{2,1,0:T(8,128)(2,1)S(1)} %get-tuple-element.63), channel_id=1, source_target_pairs={{0,16},{1,17},{2,18},{3,19},{4,20},{5,21},{6,22},{7,23},{8,24},{9,... | collective-permute-start | bytes 1327112 | tf_op jit(solution)/shard_map/ppermute | solution.py:40
  25.1 0.9 %collective-permute-start.14 = (bf16[27,64,128]{2,1,0:T(8,128)(2,1)S(1)}, bf16[27,64,128]{2,1,0:T(8,128)(2,1)S(1)}, u32[]{:S(2)}, u32[]{:S(2)}) collective-permute-start(bf16[27,64,128]{2,1,0:T(8,128)(2,1)S(1)} %get-tuple-element.64), channel_id=1, source_target_pairs={{0,8},{1,9},{2,10},{3,11},{4,12},{5,13},{6,14},{7,15},{8,0},{9,1},... | collective-permute-start | bytes 1327112 | tf_op jit(solution)/shard_map/ppermute | solution.py:40
  26.1 8.5 %collective-permute-done.6.got1 = bf16[9,32,768]{2,1,0:T(8,128)(2,1)S(1)} collective-permute-done((bf16[9,32,768]{2,1,0:T(8,128)(2,1)S(1)}, bf16[9,32,768]{2,1,0:T(8,128)(2,1)S(1)}, u32[]{:S(2)}, u32[]{:S(2)}) %collective-permute-start.6) | collective-permute-done | bytes 442400 | tf_op jit(solution)/shard_map/ppermute | solution.py:40
  35.1 8.3 %collective-permute-done.8.got3 = bf16[9,32,768]{2,1,0:T(8,128)(2,1)S(1)} collective-permute-done((bf16[9,32,768]{2,1,0:T(8,128)(2,1)S(1)}, bf16[9,32,768]{2,1,0:T(8,128)(2,1)S(1)}, u32[]{:S(2)}, u32[]{:S(2)}) %collective-permute-start.8) | collective-permute-done | bytes 442400 | tf_op jit(solution)/shard_map/ppermute | solution.py:40
  43.8 1.3 %collective-permute-start.9 = (bf16[592,128]{1,0:T(8,128)(2,1)S(1)}, bf16[592,128]{1,0:T(8,128)(2,1)S(1)}, u32[]{:S(2)}, u32[]{:S(2)}) collective-permute-start(bf16[592,128]{1,0:T(8,128)(2,1)S(1)} %get-tuple-element.59), channel_id=1, source_target_pairs={{0,16},{1,17},{2,18},{3,19},{4,20},{5,21},{6,22},{7,23},{8,24},{9,... | collective-permute-start | bytes 454664 | tf_op jit(solution)/shard_map/ppermute | solution.py:40
  45.1 2.2 %collective-permute-start.11 = (bf16[592,128]{1,0:T(8,128)(2,1)S(1)}, bf16[592,128]{1,0:T(8,128)(2,1)S(1)}, u32[]{:S(2)}, u32[]{:S(2)}) collective-permute-start(bf16[592,128]{1,0:T(8,128)(2,1)S(1)} %get-tuple-element.61), channel_id=1, source_target_pairs={{0,24},{1,25},{2,26},{3,27},{4,28},{5,29},{6,30},{7,31},{8,16},{9,... | collective-permute-start | bytes 454664 | tf_op jit(solution)/shard_map/ppermute | solution.py:40
  47.9 2.0 %collective-permute-start.17 = (bf16[592,128]{1,0:T(8,128)(2,1)S(1)}, bf16[592,128]{1,0:T(8,128)(2,1)S(1)}, u32[]{:S(2)}, u32[]{:S(2)}) collective-permute-start(bf16[592,128]{1,0:T(8,128)(2,1)S(1)} %get-tuple-element.70), channel_id=1, source_target_pairs={{0,4},{1,5},{2,6},{3,7},{4,0},{5,1},{6,2},{7,3},{8,12},{9,13},{10,... | collective-permute-start | bytes 454664 | tf_op jit(solution)/shard_map/ppermute | solution.py:40
  50.0 3.4 %collective-permute-start.16 = (bf16[576,128]{1,0:T(8,128)(2,1)S(1)}, bf16[576,128]{1,0:T(8,128)(2,1)S(1)}, u32[]{:S(2)}, u32[]{:S(2)}) collective-permute-start(bf16[576,128]{1,0:T(8,128)(2,1)S(1)} %get-tuple-element.69), channel_id=1, source_target_pairs={{0,2},{1,3},{2,0},{3,1},{4,6},{5,7},{6,4},{7,5},{8,10},{9,11},{10,... | collective-permute-start | bytes 442376 | tf_op jit(solution)/shard_map/ppermute | solution.py:40
  54.5 4.9 %collective-permute-done.18.b3 = bf16[464,128]{1,0:T(8,128)(2,1)S(1)} collective-permute-done((bf16[464,128]{1,0:T(8,128)(2,1)S(1)}, bf16[464,128]{1,0:T(8,128)(2,1)S(1)}, u32[]{:S(2)}, u32[]{:S(2)}) %collective-permute-start.18) | collective-permute-done | bytes 118816 | tf_op jit(solution)/shard_map/ppermute | solution.py:40
  59.5 0.8 %last_stage.1 = (bf16[8,112,128]{2,1,0:T(8,128)(2,1)}, f32[112,128]{1,0:T(8,128)S(1)}, bf16[10,16,256]{2,1,0:T(8,128)(2,1)S(1)}) custom-call(f32[448,128]{1,0:T(8,128)S(1)} %get-tuple-element.58.own_two, bf16[592,128]{1,0:T(8,128)(2,1)S(1)} %collective-permute-done.9.a2, bf16[592,128]{1,0:T(8,128)(2,1)S(1)} %collective-permute-done.10.a1, ...), custom_call_target="tpu_custom_call" | custom-call | tf_op jit(solution)/shard_map/last_stage/pallas_call | solution.py:50
  60.3 8.5 %all-to-all-start = ((bf16[8,112,128]{2,1,0:T(8,128)(2,1)}), bf16[8,112,128]{2,1,0:T(8,128)(2,1)S(1)}, u32[]{:S(2)}, u32[]{:S(2)}) async-start(bf16[8,112,128]{2,1,0:T(8,128)(2,1)} %get-tuple-element.74), calls=%async_computation | async-start | bytes 458752 | tf_op jit(solution)/shard_map/all_to_all | solution.py:548
  68.8 5.1 %conv_one_back.1.after = bf16[4,12,16,256]{3,2,1,0:T(8,128)(2,1)} custom-call(bf16[4,12,16,256]{3,2,1,0:T(8,128)(2,1)S(1)} %get-tuple-element.50.hid, bf16[4,12,16,256]{3,2,1,0:T(8,128)(2,1)} %bitcast.19, bf16[10,16,256]{2,1,0:T(8,128)(2,1)S(1)} %get-tuple-element.72.border, bf16[2,4,16,256]{3,2,1,0:T(8,128)(2,1)S(1)} %get-tuple-element.67.cols, ...), custom_call_target="tpu_custom_call" | custom-call | tf_op jit(solution)/shard_map/conv_one_back/pallas_call | solution.py:50
  73.9 5.0 %all-to-all-done.got = bf16[8,112,128]{2,1,0:T(8,128)(2,1)S(1)} async-done(((bf16[8,112,128]{2,1,0:T(8,128)(2,1)}), bf16[8,112,128]{2,1,0:T(8,128)(2,1)S(1)}, u32[]{:S(2)}, u32[]{:S(2)}) %all-to-all-start) | async-done | bytes 229408 | tf_op jit(solution)/shard_map/all_to_all | solution.py:548
  78.9 0.8 final_sum.1
  (28 shorter events, 4.7 us)
Async XLA Ops:
  2.1 8.8 %collective-permute-start = (bf16[2,4,16,256]{3,2,1,0:T(8,128)(2,1)S(1)}, bf16[2,4,16,256]{3,2,1,0:T(8,128)(2,1)S(1)}, u32[]{:S(2)}, u32[]{:S(2)}) collective-permute-start(bf16[2,4,16,256]{3,2,1,0:T(8,128)(2,1)S(1)} %get-tuple-element.41), channel_id=1, source_target_pairs={{0,4},{1,5},{2,6},{3,7},{4,0},{5,1},{6,2},{7,3},{8,12},{9,13},{10,... | collective-permute-start | bytes 196616 | tf_op jit(solution)/shard_map/ppermute | solution.py:40
  3.7 7.2 %collective-permute-start.1 = (bf16[2,4,16,256]{3,2,1,0:T(8,128)(2,1)S(1)}, bf16[2,4,16,256]{3,2,1,0:T(8,128)(2,1)S(1)}, u32[]{:S(2)}, u32[]{:S(2)}) collective-permute-start(bf16[2,4,16,256]{3,2,1,0:T(8,128)(2,1)S(1)} %get-tuple-element.42), channel_id=1, source_target_pairs={{0,1},{1,0},{2,3},{3,2},{4,5},{5,4},{6,7},{7,6},{8,9},{9,8},{10,11... | collective-permute-start | bytes 196616 | tf_op jit(solution)/shard_map/ppermute | solution.py:40
  3.7 7.2 %collective-permute-start.2 = (bf16[2,4,16,256]{3,2,1,0:T(8,128)(2,1)S(1)}, bf16[2,4,16,256]{3,2,1,0:T(8,128)(2,1)S(1)}, u32[]{:S(2)}, u32[]{:S(2)}) collective-permute-start(bf16[2,4,16,256]{3,2,1,0:T(8,128)(2,1)S(1)} %get-tuple-element.43), channel_id=1, source_target_pairs={{0,3},{1,2},{2,1},{3,0},{4,7},{5,6},{6,5},{7,4},{8,11},{9,10},{10,... | collective-permute-start | bytes 196616 | tf_op jit(solution)/shard_map/ppermute | solution.py:40
  6.5 4.0 %collective-permute-start.3 = (bf16[2,16,256]{2,1,0:T(8,128)(2,1)S(1)}, bf16[2,16,256]{2,1,0:T(8,128)(2,1)S(1)}, u32[]{:S(2)}, u32[]{:S(2)}) collective-permute-start(bf16[2,16,256]{2,1,0:T(8,128)(2,1)S(1)} %get-tuple-element.44), channel_id=1, source_target_pairs={{0,5},{1,4},{2,7},{3,6},{4,1},{5,0},{6,3},{7,2},{8,13},{9,12},{10,... | collective-permute-start | bytes 49160 | tf_op jit(solution)/shard_map/ppermute | solution.py:40
  6.5 4.4 %collective-permute-start.4 = (bf16[2,16,256]{2,1,0:T(8,128)(2,1)S(1)}, bf16[2,16,256]{2,1,0:T(8,128)(2,1)S(1)}, u32[]{:S(2)}, u32[]{:S(2)}) collective-permute-start(bf16[2,16,256]{2,1,0:T(8,128)(2,1)S(1)} %get-tuple-element.45), channel_id=1, source_target_pairs={{0,7},{1,6},{2,5},{3,4},{4,3},{5,2},{6,1},{7,0},{8,15},{9,14},{10,... | collective-permute-start | bytes 49160 | tf_op jit(solution)/shard_map/ppermute | solution.py:40
  11.0 2.7 %collective-permute-start.5 = (bf16[4,22,16,256]{3,2,1,0:T(8,128)(2,1)S(1)}, bf16[4,22,16,256]{3,2,1,0:T(8,128)(2,1)S(1)}, u32[]{:S(2)}, u32[]{:S(2)}) collective-permute-start(bf16[4,22,16,256]{3,2,1,0:T(8,128)(2,1)S(1)} %pad_cotangent.1.padded), channel_id=1, source_target_pairs={{0,1},{1,0},{2,3},{3,2},{4,5},{5,4},{6,7},{7,6},{8,9},{9,8},{10,11... | collective-permute-start | bytes 2162696 | tf_op jit(solution)/shard_map/ppermute | solution.py:40
  16.8 6.7 %collective-permute-start.12 = (f32[4,28,64,128]{3,2,1,0:T(8,128)S(1)}, f32[4,28,64,128]{3,2,1,0:T(8,128)S(1)}, u32[]{:S(2)}, u32[]{:S(2)}) collective-permute-start(f32[4,28,64,128]{3,2,1,0:T(8,128)S(1)} %get-tuple-element.53.after), channel_id=1, source_target_pairs={{0,1},{1,0},{2,3},{3,2},{4,5},{5,4},{6,7},{7,6},{8,9},{9,8},{10,11... | collective-permute-start | bytes 11010056 | tf_op jit(solution)/shard_map/ppermute | solution.py:40
  19.7 14.8 %collective-permute-start.6 = (bf16[9,32,768]{2,1,0:T(8,128)(2,1)S(1)}, bf16[9,32,768]{2,1,0:T(8,128)(2,1)S(1)}, u32[]{:S(2)}, u32[]{:S(2)}) collective-permute-start(bf16[9,32,768]{2,1,0:T(8,128)(2,1)S(1)} %get-tuple-element.54), channel_id=1, source_target_pairs={{0,2},{1,3},{2,0},{3,1},{4,6},{5,7},{6,4},{7,5},{8,10},{9,11},{10,... | collective-permute-start | bytes 1327112 | tf_op jit(solution)/shard_map/ppermute | solution.py:40
  22.3 21.1 %collective-permute-start.8 = (bf16[9,32,768]{2,1,0:T(8,128)(2,1)S(1)}, bf16[9,32,768]{2,1,0:T(8,128)(2,1)S(1)}, u32[]{:S(2)}, u32[]{:S(2)}) collective-permute-start(bf16[9,32,768]{2,1,0:T(8,128)(2,1)S(1)} %get-tuple-element.56), channel_id=1, source_target_pairs={{0,6},{1,7},{2,4},{3,5},{4,2},{5,3},{6,0},{7,1},{8,14},{9,15},{10,... | collective-permute-start | bytes 1327112 | tf_op jit(solution)/shard_map/ppermute | solution.py:40
  23.1 20.3 %collective-permute-start.7 = (bf16[9,32,768]{2,1,0:T(8,128)(2,1)S(1)}, bf16[9,32,768]{2,1,0:T(8,128)(2,1)S(1)}, u32[]{:S(2)}, u32[]{:S(2)}) collective-permute-start(bf16[9,32,768]{2,1,0:T(8,128)(2,1)S(1)} %get-tuple-element.55.after), channel_id=1, source_target_pairs={{0,4},{1,5},{2,6},{3,7},{4,0},{5,1},{6,2},{7,3},{8,12},{9,13},{10,... | collective-permute-start | bytes 1327112 | tf_op jit(solution)/shard_map/ppermute | solution.py:40
  23.8 23.5 %collective-permute-start.13 = (bf16[27,64,128]{2,1,0:T(8,128)(2,1)S(1)}, bf16[27,64,128]{2,1,0:T(8,128)(2,1)S(1)}, u32[]{:S(2)}, u32[]{:S(2)}) collective-permute-start(bf16[27,64,128]{2,1,0:T(8,128)(2,1)S(1)} %get-tuple-element.63), channel_id=1, source_target_pairs={{0,16},{1,17},{2,18},{3,19},{4,20},{5,21},{6,22},{7,23},{8,24},{9,... | collective-permute-start | bytes 1327112 | tf_op jit(solution)/shard_map/ppermute | solution.py:40
  25.1 22.3 %collective-permute-start.14 = (bf16[27,64,128]{2,1,0:T(8,128)(2,1)S(1)}, bf16[27,64,128]{2,1,0:T(8,128)(2,1)S(1)}, u32[]{:S(2)}, u32[]{:S(2)}) collective-permute-start(bf16[27,64,128]{2,1,0:T(8,128)(2,1)S(1)} %get-tuple-element.64), channel_id=1, source_target_pairs={{0,8},{1,9},{2,10},{3,11},{4,12},{5,13},{6,14},{7,15},{8,0},{9,1},... | collective-permute-start | bytes 1327112 | tf_op jit(solution)/shard_map/ppermute | solution.py:40
  34.5 12.9 %collective-permute-start.15 = (bf16[27,64,128]{2,1,0:T(8,128)(2,1)S(1)}, bf16[27,64,128]{2,1,0:T(8,128)(2,1)S(1)}, u32[]{:S(2)}, u32[]{:S(2)}) collective-permute-start(bf16[27,64,128]{2,1,0:T(8,128)(2,1)S(1)} %get-tuple-element.65), channel_id=1, source_target_pairs={{0,24},{1,25},{2,26},{3,27},{4,28},{5,29},{6,30},{7,31},{8,16},{9,... | collective-permute-start | bytes 1327112 | tf_op jit(solution)/shard_map/ppermute | solution.py:40
  43.8 9.6 %collective-permute-start.9 = (bf16[592,128]{1,0:T(8,128)(2,1)S(1)}, bf16[592,128]{1,0:T(8,128)(2,1)S(1)}, u32[]{:S(2)}, u32[]{:S(2)}) collective-permute-start(bf16[592,128]{1,0:T(8,128)(2,1)S(1)} %get-tuple-element.59), channel_id=1, source_target_pairs={{0,16},{1,17},{2,18},{3,19},{4,20},{5,21},{6,22},{7,23},{8,24},{9,... | collective-permute-start | bytes 454664 | tf_op jit(solution)/shard_map/ppermute | solution.py:40
  45.1 9.4 %collective-permute-start.11 = (bf16[592,128]{1,0:T(8,128)(2,1)S(1)}, bf16[592,128]{1,0:T(8,128)(2,1)S(1)}, u32[]{:S(2)}, u32[]{:S(2)}) collective-permute-start(bf16[592,128]{1,0:T(8,128)(2,1)S(1)} %get-tuple-element.61), channel_id=1, source_target_pairs={{0,24},{1,25},{2,26},{3,27},{4,28},{5,29},{6,30},{7,31},{8,16},{9,... | collective-permute-start | bytes 454664 | tf_op jit(solution)/shard_map/ppermute | solution.py:40
  47.3 7.2 %collective-permute-start.10 = (bf16[592,128]{1,0:T(8,128)(2,1)S(1)}, bf16[592,128]{1,0:T(8,128)(2,1)S(1)}, u32[]{:S(2)}, u32[]{:S(2)}) collective-permute-start(bf16[592,128]{1,0:T(8,128)(2,1)S(1)} %get-tuple-element.60.after), channel_id=1, source_target_pairs={{0,8},{1,9},{2,10},{3,11},{4,12},{5,13},{6,14},{7,15},{8,0},{9,1},... | collective-permute-start | bytes 454664 | tf_op jit(solution)/shard_map/ppermute | solution.py:40
  47.9 11.5 %collective-permute-start.17 = (bf16[592,128]{1,0:T(8,128)(2,1)S(1)}, bf16[592,128]{1,0:T(8,128)(2,1)S(1)}, u32[]{:S(2)}, u32[]{:S(2)}) collective-permute-start(bf16[592,128]{1,0:T(8,128)(2,1)S(1)} %get-tuple-element.70), channel_id=1, source_target_pairs={{0,4},{1,5},{2,6},{3,7},{4,0},{5,1},{6,2},{7,3},{8,12},{9,13},{10,... | collective-permute-start | bytes 454664 | tf_op jit(solution)/shard_map/ppermute | solution.py:40
  50.0 9.5 %collective-permute-start.16 = (bf16[576,128]{1,0:T(8,128)(2,1)S(1)}, bf16[576,128]{1,0:T(8,128)(2,1)S(1)}, u32[]{:S(2)}, u32[]{:S(2)}) collective-permute-start(bf16[576,128]{1,0:T(8,128)(2,1)S(1)} %get-tuple-element.69), channel_id=1, source_target_pairs={{0,2},{1,3},{2,0},{3,1},{4,6},{5,7},{6,4},{7,5},{8,10},{9,11},{10,... | collective-permute-start | bytes 442376 | tf_op jit(solution)/shard_map/ppermute | solution.py:40
  53.4 6.0 %collective-permute-start.18 = (bf16[464,128]{1,0:T(8,128)(2,1)S(1)}, bf16[464,128]{1,0:T(8,128)(2,1)S(1)}, u32[]{:S(2)}, u32[]{:S(2)}) collective-permute-start(bf16[464,128]{1,0:T(8,128)(2,1)S(1)} %get-tuple-element.71), channel_id=1, source_target_pairs={{0,6},{1,7},{2,4},{3,5},{4,2},{5,3},{6,0},{7,1},{8,14},{9,15},{10,... | collective-permute-start | bytes 356360 | tf_op jit(solution)/shard_map/ppermute | solution.py:40
  60.3 18.6 %all-to-all-start = ((bf16[8,112,128]{2,1,0:T(8,128)(2,1)}), bf16[8,112,128]{2,1,0:T(8,128)(2,1)S(1)}, u32[]{:S(2)}, u32[]{:S(2)}) async-start(bf16[8,112,128]{2,1,0:T(8,128)(2,1)} %get-tuple-element.74), calls=%async_computation | async-start | bytes 458752 | tf_op jit(solution)/shard_map/all_to_all | solution.py:548

commit v16 on v15

--- a/solution.py
+++ b/solution.py
@@ -289,8 +289,8 @@
         held[...] = jnp.concatenate(parts, axis=0).T.reshape(8, 4, 8, 128)
         for d, out in enumerate((keep, one, two, three)):
             out[g * 64 : g * 64 + 64] = held[:, y ^ d].reshape(64, 128).astype(out.dtype)
-    for out in (one, two, three):
-        out[448:592] = jnp.zeros((144, 128), BF)
+    for out, rows in ((one, 144), (two, 144), (three, 16)):
+        out[448 : 448 + rows] = jnp.zeros((rows, 128), BF)
 
 
 def border_at(n, h):
@@ -524,7 +524,7 @@
         "grad_two_x",
         (*got_two, own_two),
         "vvvv",
-        [near((448, 128), F32)] + [near((592, 128), BF)] * 3,
+        [near((448, 128), F32), near((592, 128), BF), near((592, 128), BF), near((464, 128), BF)],
         [pltpu.VMEM((8, 4, 8, 128), F32)],
     )
     got_two = ring(parts, "dy")

time: 80.9 us -> 82.1 us (1.015); the launches traced: 79.7 us -> 81.9 us
  starting transfers between devices: 30.7 us -> 32.6 us
    ppermute x19, starting transfers between devices: 22.3 us -> 23.5 us  [send(): return lax.ppermute(value, AX, pairs)]
  transfers between devices with their start and end apart: 20 -> 20, of which waited for: 6 -> 5; matrix products, arithmetic and copies ran while one was open for 0% -> 0% of each run, Pallas kernels for 17% -> 17%
where the time goes in v16:
time: 82.1 us; the launch traced here: 81.9 us
  starting transfers between devices  32.6 us (40%)
  waiting for transfers between devices  28.2 us (34%)
  Pallas kernels  19.8 us (24%)
  between operations  1.39 us (2%)
    ppermute x19, starting transfers between devices, send(): return lax.ppermute(value, AX, pairs)  23.5 us
    ppermute x19, waiting for transfers between devices, send(): return lax.ppermute(value, AX, pairs)  22.6 us
    pallas_call x12, Pallas kernels, call(): pl.pallas_call(kernel, out_shape=tuple((o for o, _ in outs)), in_specs=[s...  19.8 us
    all_to_all x1, starting transfers between devices, shards(): planes = lax.all_to_all(out, 'z', 0, 0, tiled=True)  9.08 us
    all_to_all x1, waiting for transfers between devices, shards(): planes = lax.all_to_all(out, 'z', 0, 0, tiled=True)  5.59 us
  transfers between devices with their start and end apart: 20, of which 5 were waited for; matrix products, arithmetic and copies ran while one was open for 0% of the time, Pallas kernels for 17%

profile of v16, /device:TPU:24, one launch (start us, length us, event | category | flops | bytes accessed | tf_op | source)
XLA Modules:
  0.0 81.9 jit_solution(18158990729798297928)
XLA Ops:
  0.6 1.4 %pack_first.1 = (bf16[2,4,16,256]{3,2,1,0:T(8,128)(2,1)S(1)}, bf16[2,4,16,256]{3,2,1,0:T(8,128)(2,1)S(1)}, bf16[2,4,16,256]{3,2,1,0:T(8,128)(2,1)S(1)}, bf16[2,1...) custom-call(bf16[4,12,16,256]{3,2,1,0:T(8,128)(2,1)} %bitcast.18, ...), custom_call_target="tpu_custom_call" | custom-call | tf_op jit(solution)/shard_map/pack_first/pallas_call | solution.py:50
  2.1 1.6 %collective-permute-start = (bf16[2,4,16,256]{3,2,1,0:T(8,128)(2,1)S(1)}, bf16[2,4,16,256]{3,2,1,0:T(8,128)(2,1)S(1)}, u32[]{:S(2)}, u32[]{:S(2)}) collective-permute-start(bf16[2,4,16,256]{3,2,1,0:T(8,128)(2,1)S(1)} %get-tuple-element.41), channel_id=1, source_target_pairs={{0,4},{1,5},{2,6},{3,7},{4,0},{5,1},{6,2},{7,3},{8,12},{9,13},{10,... | collective-permute-start | bytes 196616 | tf_op jit(solution)/shard_map/ppermute | solution.py:40
  3.7 2.8 %collective-permute-start.2 = (bf16[2,4,16,256]{3,2,1,0:T(8,128)(2,1)S(1)}, bf16[2,4,16,256]{3,2,1,0:T(8,128)(2,1)S(1)}, u32[]{:S(2)}, u32[]{:S(2)}) collective-permute-start(bf16[2,4,16,256]{3,2,1,0:T(8,128)(2,1)S(1)} %get-tuple-element.43), channel_id=1, source_target_pairs={{0,3},{1,2},{2,1},{3,0},{4,7},{5,6},{6,5},{7,4},{8,11},{9,10},{10,... | collective-permute-start | bytes 196616 | tf_op jit(solution)/shard_map/ppermute | solution.py:40
  6.5 1.1 %collective-permute-start.4 = (bf16[2,16,256]{2,1,0:T(8,128)(2,1)S(1)}, bf16[2,16,256]{2,1,0:T(8,128)(2,1)S(1)}, u32[]{:S(2)}, u32[]{:S(2)}) collective-permute-start(bf16[2,16,256]{2,1,0:T(8,128)(2,1)S(1)} %get-tuple-element.45), channel_id=1, source_target_pairs={{0,7},{1,6},{2,5},{3,4},{4,3},{5,2},{6,1},{7,0},{8,15},{9,14},{10,... | collective-permute-start | bytes 49160 | tf_op jit(solution)/shard_map/ppermute | solution.py:40
  8.2 2.2 %film.1 = (bf16[768,256]{1,0:T(8,128)(2,1)S(1)}, bf16[4,12,16,256]{3,2,1,0:T(8,128)(2,1)S(1)}, f32[768,256]{1,0:T(8,128)S(1)}, bf16[27,256,256]{2,1,0:T(8,128)(2,1)S(1)}) custom-call(s32[1]{0:T(128)S(6)} %copy.10.step, bf16[4,12,16,256]{3,2,1,0:T(8,128)(2,1)S(1)} %get-tuple-element.46.inputs, bf16[4,12,16,256]{3,2,1,0:T(8,128)(2,1)} %bitcast.21, ...), custom_call_target="tpu_custom_call" | custom-call | tf_op jit(solution)/shard_map/film/pallas_call | solution.py:50
  11.4 2.3 %conv_two_back.1 = (bf16[4,14,16,768]{3,2,1,0:T(8,128)(2,1)S(1)}, bf16[4,12,16,256]{3,2,1,0:T(8,128)(2,1)S(1)}) custom-call(bf16[4,22,16,256]{3,2,1,0:T(8,128)(2,1)S(1)} %pad_cotangent.1.padded, f32[768,256]{1,0:T(8,128)S(1)} %get-tuple-element.48.slope, bf16[27,256,256]{2,1,0:T(8,128)(2,1)S(1)} %get-tuple-element.49.taps), custom_call_target="tpu_custom_call" | custom-call | tf_op jit(solution)/shard_map/conv_two_back/pallas_call | solution.py:50
  13.7 3.1 %grad_one.1 = (f32[4,27,64,128]{3,2,1,0:T(8,128)S(1)}, f32[4,28,64,128]{3,2,1,0:T(8,128)S(1)}) custom-call(bf16[4,12,16,256]{3,2,1,0:T(8,128)(2,1)S(1)} %get-tuple-element.50.hid, bf16[4,12,16,256]{3,2,1,0:T(8,128)(2,1)S(1)} %get-tuple-element.52.inp, bf16[2,4,16,256]{3,2,1,0:T(8,128)(2,1)S(1)} %collective-permute-done.row, ...), custom_call_target="tpu_custom_call" | custom-call | tf_op jit(solution)/shard_map/grad_one/pallas_call | solution.py:50
  17.0 2.7 %grad_two.1 = (f32[9,32,768]{2,1,0:T(8,128)S(1)}, bf16[9,32,768]{2,1,0:T(8,128)(2,1)S(1)}, bf16[9,32,768]{2,1,0:T(8,128)(2,1)S(1)}, bf16[9,32,768]{2,1,0:T(8,128)(2,1)S(1)}) custom-call(bf16[4,14,16,768]{3,2,1,0:T(8,128)(2,1)S(1)} %get-tuple-element.51.wide, bf16[768,256]{1,0:T(8,128)(2,1)S(1)} %get-tuple-element.47.act, ...), custom_call_target="tpu_custom_call" | custom-call | tf_op jit(solution)/shard_map/grad_two/pallas_call | solution.py:50
  19.7 2.6 %collective-permute-start.6 = (bf16[9,32,768]{2,1,0:T(8,128)(2,1)S(1)}, bf16[9,32,768]{2,1,0:T(8,128)(2,1)S(1)}, u32[]{:S(2)}, u32[]{:S(2)}) collective-permute-start(bf16[9,32,768]{2,1,0:T(8,128)(2,1)S(1)} %get-tuple-element.54), channel_id=1, source_target_pairs={{0,2},{1,3},{2,0},{3,1},{4,6},{5,7},{6,4},{7,5},{8,10},{9,11},{10,... | collective-permute-start | bytes 1327112 | tf_op jit(solution)/shard_map/ppermute | solution.py:40
  23.8 1.3 %collective-permute-start.13 = (bf16[27,64,128]{2,1,0:T(8,128)(2,1)S(1)}, bf16[27,64,128]{2,1,0:T(8,128)(2,1)S(1)}, u32[]{:S(2)}, u32[]{:S(2)}) collective-permute-start(bf16[27,64,128]{2,1,0:T(8,128)(2,1)S(1)} %get-tuple-element.63), channel_id=1, source_target_pairs={{0,16},{1,17},{2,18},{3,19},{4,20},{5,21},{6,22},{7,23},{8,24},{9,... | collective-permute-start | bytes 1327112 | tf_op jit(solution)/shard_map/ppermute | solution.py:40
  25.1 0.9 %collective-permute-start.14 = (bf16[27,64,128]{2,1,0:T(8,128)(2,1)S(1)}, bf16[27,64,128]{2,1,0:T(8,128)(2,1)S(1)}, u32[]{:S(2)}, u32[]{:S(2)}) collective-permute-start(bf16[27,64,128]{2,1,0:T(8,128)(2,1)S(1)} %get-tuple-element.64), channel_id=1, source_target_pairs={{0,8},{1,9},{2,10},{3,11},{4,12},{5,13},{6,14},{7,15},{8,0},{9,1},... | collective-permute-start | bytes 1327112 | tf_op jit(solution)/shard_map/ppermute | solution.py:40
  26.1 8.5 %collective-permute-done.6.got1 = bf16[9,32,768]{2,1,0:T(8,128)(2,1)S(1)} collective-permute-done((bf16[9,32,768]{2,1,0:T(8,128)(2,1)S(1)}, bf16[9,32,768]{2,1,0:T(8,128)(2,1)S(1)}, u32[]{:S(2)}, u32[]{:S(2)}) %collective-permute-start.6) | collective-permute-done | bytes 442400 | tf_op jit(solution)/shard_map/ppermute | solution.py:40
  35.1 8.3 %collective-permute-done.8.got3 = bf16[9,32,768]{2,1,0:T(8,128)(2,1)S(1)} collective-permute-done((bf16[9,32,768]{2,1,0:T(8,128)(2,1)S(1)}, bf16[9,32,768]{2,1,0:T(8,128)(2,1)S(1)}, u32[]{:S(2)}, u32[]{:S(2)}) %collective-permute-start.8) | collective-permute-done | bytes 442400 | tf_op jit(solution)/shard_map/ppermute | solution.py:40
  43.8 0.8 collective-permute-start.11
  44.6 2.1 %collective-permute-start.9 = (bf16[592,128]{1,0:T(8,128)(2,1)S(1)}, bf16[592,128]{1,0:T(8,128)(2,1)S(1)}, u32[]{:S(2)}, u32[]{:S(2)}) collective-permute-start(bf16[592,128]{1,0:T(8,128)(2,1)S(1)} %get-tuple-element.59), channel_id=1, source_target_pairs={{0,16},{1,17},{2,18},{3,19},{4,20},{5,21},{6,22},{7,23},{8,24},{9,... | collective-permute-start | bytes 454664 | tf_op jit(solution)/shard_map/ppermute | solution.py:40
  46.7 1.3 %collective-permute-start.10 = (bf16[592,128]{1,0:T(8,128)(2,1)S(1)}, bf16[592,128]{1,0:T(8,128)(2,1)S(1)}, u32[]{:S(2)}, u32[]{:S(2)}) collective-permute-start(bf16[592,128]{1,0:T(8,128)(2,1)S(1)} %get-tuple-element.60.after), channel_id=1, source_target_pairs={{0,8},{1,9},{2,10},{3,11},{4,12},{5,13},{6,14},{7,15},{8,0},{9,1},... | collective-permute-start | bytes 454664 | tf_op jit(solution)/shard_map/ppermute | solution.py:40
  48.5 0.9 %collective-permute-start.17 = (bf16[592,128]{1,0:T(8,128)(2,1)S(1)}, bf16[592,128]{1,0:T(8,128)(2,1)S(1)}, u32[]{:S(2)}, u32[]{:S(2)}) collective-permute-start(bf16[592,128]{1,0:T(8,128)(2,1)S(1)} %get-tuple-element.70), channel_id=1, source_target_pairs={{0,4},{1,5},{2,6},{3,7},{4,0},{5,1},{6,2},{7,3},{8,12},{9,13},{10,... | collective-permute-start | bytes 454664 | tf_op jit(solution)/shard_map/ppermute | solution.py:40
  49.4 4.5 %collective-permute-start.16 = (bf16[576,128]{1,0:T(8,128)(2,1)S(1)}, bf16[576,128]{1,0:T(8,128)(2,1)S(1)}, u32[]{:S(2)}, u32[]{:S(2)}) collective-permute-start(bf16[576,128]{1,0:T(8,128)(2,1)S(1)} %get-tuple-element.69), channel_id=1, source_target_pairs={{0,2},{1,3},{2,0},{3,1},{4,6},{5,7},{6,4},{7,5},{8,10},{9,11},{10,... | collective-permute-start | bytes 442376 | tf_op jit(solution)/shard_map/ppermute | solution.py:40
  53.9 1.2 %collective-permute-start.18 = (bf16[464,128]{1,0:T(8,128)(2,1)S(1)}, bf16[464,128]{1,0:T(8,128)(2,1)S(1)}, u32[]{:S(2)}, u32[]{:S(2)}) collective-permute-start(bf16[464,128]{1,0:T(8,128)(2,1)S(1)} %get-tuple-element.71), channel_id=1, source_target_pairs={{0,6},{1,7},{2,4},{3,5},{4,2},{5,3},{6,0},{7,1},{8,14},{9,15},{10,... | collective-permute-start | bytes 356360 | tf_op jit(solution)/shard_map/ppermute | solution.py:40
  55.1 5.4 %collective-permute-done.18.b3 = bf16[464,128]{1,0:T(8,128)(2,1)S(1)} collective-permute-done((bf16[464,128]{1,0:T(8,128)(2,1)S(1)}, bf16[464,128]{1,0:T(8,128)(2,1)S(1)}, u32[]{:S(2)}, u32[]{:S(2)}) %collective-permute-start.18) | collective-permute-done | bytes 118816 | tf_op jit(solution)/shard_map/ppermute | solution.py:40
  60.5 0.8 %last_stage.1 = (bf16[8,112,128]{2,1,0:T(8,128)(2,1)}, f32[112,128]{1,0:T(8,128)S(1)}, bf16[10,16,256]{2,1,0:T(8,128)(2,1)S(1)}) custom-call(f32[448,128]{1,0:T(8,128)S(1)} %get-tuple-element.58.own_two, bf16[592,128]{1,0:T(8,128)(2,1)S(1)} %collective-permute-done.9.a2, bf16[592,128]{1,0:T(8,128)(2,1)S(1)} %collective-permute-done.10.a1, ...), custom_call_target="tpu_custom_call" | custom-call | tf_op jit(solution)/shard_map/last_stage/pallas_call | solution.py:50
  61.3 9.1 %all-to-all-start = ((bf16[8,112,128]{2,1,0:T(8,128)(2,1)}), bf16[8,112,128]{2,1,0:T(8,128)(2,1)S(1)}, u32[]{:S(2)}, u32[]{:S(2)}) async-start(bf16[8,112,128]{2,1,0:T(8,128)(2,1)} %get-tuple-element.74), calls=%async_computation | async-start | bytes 458752 | tf_op jit(solution)/shard_map/all_to_all | solution.py:548
  70.4 5.1 %conv_one_back.1.after = bf16[4,12,16,256]{3,2,1,0:T(8,128)(2,1)} custom-call(bf16[4,12,16,256]{3,2,1,0:T(8,128)(2,1)S(1)} %get-tuple-element.50.hid, bf16[4,12,16,256]{3,2,1,0:T(8,128)(2,1)} %bitcast.19, bf16[10,16,256]{2,1,0:T(8,128)(2,1)S(1)} %get-tuple-element.72.border, bf16[2,4,16,256]{3,2,1,0:T(8,128)(2,1)S(1)} %get-tuple-element.67.cols, ...), custom_call_target="tpu_custom_call" | custom-call | tf_op jit(solution)/shard_map/conv_one_back/pallas_call | solution.py:50
  75.5 5.6 %all-to-all-done.got = bf16[8,112,128]{2,1,0:T(8,128)(2,1)S(1)} async-done(((bf16[8,112,128]{2,1,0:T(8,128)(2,1)}), bf16[8,112,128]{2,1,0:T(8,128)(2,1)S(1)}, u32[]{:S(2)}, u32[]{:S(2)}) %all-to-all-start) | async-done | bytes 229408 | tf_op jit(solution)/shard_map/all_to_all | solution.py:548
  (28 shorter events, 5.0 us)
Async XLA Ops:
  2.1 8.8 %collective-permute-start = (bf16[2,4,16,256]{3,2,1,0:T(8,128)(2,1)S(1)}, bf16[2,4,16,256]{3,2,1,0:T(8,128)(2,1)S(1)}, u32[]{:S(2)}, u32[]{:S(2)}) collective-permute-start(bf16[2,4,16,256]{3,2,1,0:T(8,128)(2,1)S(1)} %get-tuple-element.41), channel_id=1, source_target_pairs={{0,4},{1,5},{2,6},{3,7},{4,0},{5,1},{6,2},{7,3},{8,12},{9,13},{10,... | collective-permute-start | bytes 196616 | tf_op jit(solution)/shard_map/ppermute | solution.py:40
  3.7 7.2 %collective-permute-start.1 = (bf16[2,4,16,256]{3,2,1,0:T(8,128)(2,1)S(1)}, bf16[2,4,16,256]{3,2,1,0:T(8,128)(2,1)S(1)}, u32[]{:S(2)}, u32[]{:S(2)}) collective-permute-start(bf16[2,4,16,256]{3,2,1,0:T(8,128)(2,1)S(1)} %get-tuple-element.42), channel_id=1, source_target_pairs={{0,1},{1,0},{2,3},{3,2},{4,5},{5,4},{6,7},{7,6},{8,9},{9,8},{10,11... | collective-permute-start | bytes 196616 | tf_op jit(solution)/shard_map/ppermute | solution.py:40
  3.7 7.2 %collective-permute-start.2 = (bf16[2,4,16,256]{3,2,1,0:T(8,128)(2,1)S(1)}, bf16[2,4,16,256]{3,2,1,0:T(8,128)(2,1)S(1)}, u32[]{:S(2)}, u32[]{:S(2)}) collective-permute-start(bf16[2,4,16,256]{3,2,1,0:T(8,128)(2,1)S(1)} %get-tuple-element.43), channel_id=1, source_target_pairs={{0,3},{1,2},{2,1},{3,0},{4,7},{5,6},{6,5},{7,4},{8,11},{9,10},{10,... | collective-permute-start | bytes 196616 | tf_op jit(solution)/shard_map/ppermute | solution.py:40
  6.5 4.0 %collective-permute-start.3 = (bf16[2,16,256]{2,1,0:T(8,128)(2,1)S(1)}, bf16[2,16,256]{2,1,0:T(8,128)(2,1)S(1)}, u32[]{:S(2)}, u32[]{:S(2)}) collective-permute-start(bf16[2,16,256]{2,1,0:T(8,128)(2,1)S(1)} %get-tuple-element.44), channel_id=1, source_target_pairs={{0,5},{1,4},{2,7},{3,6},{4,1},{5,0},{6,3},{7,2},{8,13},{9,12},{10,... | collective-permute-start | bytes 49160 | tf_op jit(solution)/shard_map/ppermute | solution.py:40
  6.5 4.4 %collective-permute-start.4 = (bf16[2,16,256]{2,1,0:T(8,128)(2,1)S(1)}, bf16[2,16,256]{2,1,0:T(8,128)(2,1)S(1)}, u32[]{:S(2)}, u32[]{:S(2)}) collective-permute-start(bf16[2,16,256]{2,1,0:T(8,128)(2,1)S(1)} %get-tuple-element.45), channel_id=1, source_target_pairs={{0,7},{1,6},{2,5},{3,4},{4,3},{5,2},{6,1},{7,0},{8,15},{9,14},{10,... | collective-permute-start | bytes 49160 | tf_op jit(solution)/shard_map/ppermute | solution.py:40
  11.0 2.7 %collective-permute-start.5 = (bf16[4,22,16,256]{3,2,1,0:T(8,128)(2,1)S(1)}, bf16[4,22,16,256]{3,2,1,0:T(8,128)(2,1)S(1)}, u32[]{:S(2)}, u32[]{:S(2)}) collective-permute-start(bf16[4,22,16,256]{3,2,1,0:T(8,128)(2,1)S(1)} %pad_cotangent.1.padded), channel_id=1, source_target_pairs={{0,1},{1,0},{2,3},{3,2},{4,5},{5,4},{6,7},{7,6},{8,9},{9,8},{10,11... | collective-permute-start | bytes 2162696 | tf_op jit(solution)/shard_map/ppermute | solution.py:40
  16.8 6.7 %collective-permute-start.12 = (f32[4,28,64,128]{3,2,1,0:T(8,128)S(1)}, f32[4,28,64,128]{3,2,1,0:T(8,128)S(1)}, u32[]{:S(2)}, u32[]{:S(2)}) collective-permute-start(f32[4,28,64,128]{3,2,1,0:T(8,128)S(1)} %get-tuple-element.53.after), channel_id=1, source_target_pairs={{0,1},{1,0},{2,3},{3,2},{4,5},{5,4},{6,7},{7,6},{8,9},{9,8},{10,11... | collective-permute-start | bytes 11010056 | tf_op jit(solution)/shard_map/ppermute | solution.py:40
  19.7 14.8 %collective-permute-start.6 = (bf16[9,32,768]{2,1,0:T(8,128)(2,1)S(1)}, bf16[9,32,768]{2,1,0:T(8,128)(2,1)S(1)}, u32[]{:S(2)}, u32[]{:S(2)}) collective-permute-start(bf16[9,32,768]{2,1,0:T(8,128)(2,1)S(1)} %get-tuple-element.54), channel_id=1, source_target_pairs={{0,2},{1,3},{2,0},{3,1},{4,6},{5,7},{6,4},{7,5},{8,10},{9,11},{10,... | collective-permute-start | bytes 1327112 | tf_op jit(solution)/shard_map/ppermute | solution.py:40
  22.3 21.1 %collective-permute-start.8 = (bf16[9,32,768]{2,1,0:T(8,128)(2,1)S(1)}, bf16[9,32,768]{2,1,0:T(8,128)(2,1)S(1)}, u32[]{:S(2)}, u32[]{:S(2)}) collective-permute-start(bf16[9,32,768]{2,1,0:T(8,128)(2,1)S(1)} %get-tuple-element.56), channel_id=1, source_target_pairs={{0,6},{1,7},{2,4},{3,5},{4,2},{5,3},{6,0},{7,1},{8,14},{9,15},{10,... | collective-permute-start | bytes 1327112 | tf_op jit(solution)/shard_map/ppermute | solution.py:40
  23.1 20.3 %collective-permute-start.7 = (bf16[9,32,768]{2,1,0:T(8,128)(2,1)S(1)}, bf16[9,32,768]{2,1,0:T(8,128)(2,1)S(1)}, u32[]{:S(2)}, u32[]{:S(2)}) collective-permute-start(bf16[9,32,768]{2,1,0:T(8,128)(2,1)S(1)} %get-tuple-element.55.after), channel_id=1, source_target_pairs={{0,4},{1,5},{2,6},{3,7},{4,0},{5,1},{6,2},{7,3},{8,12},{9,13},{10,... | collective-permute-start | bytes 1327112 | tf_op jit(solution)/shard_map/ppermute | solution.py:40
  23.8 22.9 %collective-permute-start.13 = (bf16[27,64,128]{2,1,0:T(8,128)(2,1)S(1)}, bf16[27,64,128]{2,1,0:T(8,128)(2,1)S(1)}, u32[]{:S(2)}, u32[]{:S(2)}) collective-permute-start(bf16[27,64,128]{2,1,0:T(8,128)(2,1)S(1)} %get-tuple-element.63), channel_id=1, source_target_pairs={{0,16},{1,17},{2,18},{3,19},{4,20},{5,21},{6,22},{7,23},{8,24},{9,... | collective-permute-start | bytes 1327112 | tf_op jit(solution)/shard_map/ppermute | solution.py:40
  25.1 22.9 %collective-permute-start.14 = (bf16[27,64,128]{2,1,0:T(8,128)(2,1)S(1)}, bf16[27,64,128]{2,1,0:T(8,128)(2,1)S(1)}, u32[]{:S(2)}, u32[]{:S(2)}) collective-permute-start(bf16[27,64,128]{2,1,0:T(8,128)(2,1)S(1)} %get-tuple-element.64), channel_id=1, source_target_pairs={{0,8},{1,9},{2,10},{3,11},{4,12},{5,13},{6,14},{7,15},{8,0},{9,1},... | collective-permute-start | bytes 1327112 | tf_op jit(solution)/shard_map/ppermute | solution.py:40
  34.5 13.5 %collective-permute-start.15 = (bf16[27,64,128]{2,1,0:T(8,128)(2,1)S(1)}, bf16[27,64,128]{2,1,0:T(8,128)(2,1)S(1)}, u32[]{:S(2)}, u32[]{:S(2)}) collective-permute-start(bf16[27,64,128]{2,1,0:T(8,128)(2,1)S(1)} %get-tuple-element.65), channel_id=1, source_target_pairs={{0,24},{1,25},{2,26},{3,27},{4,28},{5,29},{6,30},{7,31},{8,16},{9,... | collective-permute-start | bytes 1327112 | tf_op jit(solution)/shard_map/ppermute | solution.py:40
  43.8 10.1 %collective-permute-start.11 = (bf16[464,128]{1,0:T(8,128)(2,1)S(1)}, bf16[464,128]{1,0:T(8,128)(2,1)S(1)}, u32[]{:S(2)}, u32[]{:S(2)}) collective-permute-start(bf16[464,128]{1,0:T(8,128)(2,1)S(1)} %get-tuple-element.61), channel_id=1, source_target_pairs={{0,24},{1,25},{2,26},{3,27},{4,28},{5,29},{6,30},{7,31},{8,16},{9,... | collective-permute-start | bytes 356360 | tf_op jit(solution)/shard_map/ppermute | solution.py:40
  44.6 10.5 %collective-permute-start.9 = (bf16[592,128]{1,0:T(8,128)(2,1)S(1)}, bf16[592,128]{1,0:T(8,128)(2,1)S(1)}, u32[]{:S(2)}, u32[]{:S(2)}) collective-permute-start(bf16[592,128]{1,0:T(8,128)(2,1)S(1)} %get-tuple-element.59), channel_id=1, source_target_pairs={{0,16},{1,17},{2,18},{3,19},{4,20},{5,21},{6,22},{7,23},{8,24},{9,... | collective-permute-start | bytes 454664 | tf_op jit(solution)/shard_map/ppermute | solution.py:40
  46.7 8.4 %collective-permute-start.10 = (bf16[592,128]{1,0:T(8,128)(2,1)S(1)}, bf16[592,128]{1,0:T(8,128)(2,1)S(1)}, u32[]{:S(2)}, u32[]{:S(2)}) collective-permute-start(bf16[592,128]{1,0:T(8,128)(2,1)S(1)} %get-tuple-element.60.after), channel_id=1, source_target_pairs={{0,8},{1,9},{2,10},{3,11},{4,12},{5,13},{6,14},{7,15},{8,0},{9,1},... | collective-permute-start | bytes 454664 | tf_op jit(solution)/shard_map/ppermute | solution.py:40
  48.5 11.9 %collective-permute-start.17 = (bf16[592,128]{1,0:T(8,128)(2,1)S(1)}, bf16[592,128]{1,0:T(8,128)(2,1)S(1)}, u32[]{:S(2)}, u32[]{:S(2)}) collective-permute-start(bf16[592,128]{1,0:T(8,128)(2,1)S(1)} %get-tuple-element.70), channel_id=1, source_target_pairs={{0,4},{1,5},{2,6},{3,7},{4,0},{5,1},{6,2},{7,3},{8,12},{9,13},{10,... | collective-permute-start | bytes 454664 | tf_op jit(solution)/shard_map/ppermute | solution.py:40
  49.4 11.1 %collective-permute-start.16 = (bf16[576,128]{1,0:T(8,128)(2,1)S(1)}, bf16[576,128]{1,0:T(8,128)(2,1)S(1)}, u32[]{:S(2)}, u32[]{:S(2)}) collective-permute-start(bf16[576,128]{1,0:T(8,128)(2,1)S(1)} %get-tuple-element.69), channel_id=1, source_target_pairs={{0,2},{1,3},{2,0},{3,1},{4,6},{5,7},{6,4},{7,5},{8,10},{9,11},{10,... | collective-permute-start | bytes 442376 | tf_op jit(solution)/shard_map/ppermute | solution.py:40
  53.9 6.5 %collective-permute-start.18 = (bf16[464,128]{1,0:T(8,128)(2,1)S(1)}, bf16[464,128]{1,0:T(8,128)(2,1)S(1)}, u32[]{:S(2)}, u32[]{:S(2)}) collective-permute-start(bf16[464,128]{1,0:T(8,128)(2,1)S(1)} %get-tuple-element.71), channel_id=1, source_target_pairs={{0,6},{1,7},{2,4},{3,5},{4,2},{5,3},{6,0},{7,1},{8,14},{9,15},{10,... | collective-permute-start | bytes 356360 | tf_op jit(solution)/shard_map/ppermute | solution.py:40
  61.3 19.8 %all-to-all-start = ((bf16[8,112,128]{2,1,0:T(8,128)(2,1)}), bf16[8,112,128]{2,1,0:T(8,128)(2,1)S(1)}, u32[]{:S(2)}, u32[]{:S(2)}) async-start(bf16[8,112,128]{2,1,0:T(8,128)(2,1)} %get-tuple-element.74), calls=%async_computation | async-start | bytes 458752 | tf_op jit(solution)/shard_map/all_to_all | solution.py:548
